TPU v7x, 32 devices: a whole 2x2x4 slice. The times are simulated.
32 devices in a mesh: query: 8 (over y, x, core), feat: 4 (over z).
Axes of the slice: x: 2, y: 2, z: 4, core: 2. Of those that a mesh axis runs over, the one named last changes fastest.
Arguments:
- scores: float32 [32768], P(('query', 'feat')), may hold values from -6 to 6
- labels: int32 [32768], P('query'), may hold values from 0 to 4
- leaves: int32 [32768], P(('query', 'feat')), may hold values from 0 to 1023
- bins: int32 [32768, 256], P(('query', 'feat')), may hold values from 0 to 255
- lengths: int32 [8, 16], P('query'), may hold values from 1 to 1024, 4096 in all within a row
- owner: int32 [256], replicated, may hold values from 0 to 255, each once
Outputs:
- lambdas: float32 [2, 32768], P(None, ('query', 'feat'))
- leaf_values: float32 [1024], replicated
- score_step: float32 [32768], P(('query', 'feat'))
- histograms: float32 [3, 65536], P(None, ('query', 'feat'))
Inputs may be any that keep to these rules, and one draw needn't show every extreme that they name: `lengths`: each row sums to 4096. `owner`: a permutation; the p-th device of query+feat, in that order, holds the histograms of the features owner[j] for p * 8 <= j < (p + 1) * 8.
All inputs are finite; a program needn't handle non-finite values.
Results may differ from a plain program's by a relative error of at most 0.0003.
Values sent between devices are 32-bit elements; how exact they have to be, the bound alone decides.
No kernel may reach another device: no remote copies, remote signals or barrier semaphores. Data moves between devices by JAX's collectives and lax.ppermute only.
A program may use at most 128 MiB of HBM per device.

v0:
```python
import jax
import jax.numpy as jnp
from jax import lax
from jax.sharding import PartitionSpec as P

BINS = 256
LEAVES = 1024
TILE_ROWS = 512
WINDOW = 1536


lasso_penalty = 1.0
ridge_penalty = 1.0
shrinkage = 0.1
group_width = 8


def query_of(lengths_row, count):
    bounds = jnp.cumsum(lengths_row)
    places = jnp.arange(count, dtype=jnp.int32)
    return jnp.searchsorted(bounds, places, side="right")


def place_in_query(sorted_ids):
    places = jnp.arange(sorted_ids.shape[0], dtype=jnp.int32)
    first = jnp.concatenate([jnp.ones((1,), dtype=jnp.bool_), sorted_ids[1:] != sorted_ids[:-1]])
    starts = lax.cummax(jnp.where(first, places, 0), axis=0)
    return places - starts


def query_stats(values, grades, query_ids, count):
    order = jnp.lexsort((-values, query_ids))
    ranked = place_in_query(query_ids[order])
    standing = jnp.zeros(values.shape, jnp.int32).at[order].set(ranked)
    discount = 1.0 / jnp.log2(2.0 + standing.astype(jnp.float32))
    ideal_order = jnp.lexsort((-grades, query_ids))
    ideal_ids = query_ids[ideal_order]
    ideal_place = place_in_query(ideal_ids)
    worth = jnp.exp2(grades[ideal_order].astype(jnp.float32)) - 1.0
    terms = worth / jnp.log2(2.0 + ideal_place.astype(jnp.float32))
    slots = jnp.where(ideal_ids >= 0, ideal_ids, count)
    ideal = jax.ops.segment_sum(terms, slots, num_segments=count + 1)
    usable = ideal > 0.5
    inverse = jnp.where(usable, 1.0 / jnp.where(usable, ideal, 1.0), 0.0)
    return (discount, inverse[jnp.where(query_ids >= 0, query_ids, count)])


def pair_block(row_part, col_part):
    row_score, row_grade, row_query, row_discount, row_inverse, row_place = row_part
    col_score, col_grade, col_query, col_discount, col_place = col_part
    keep = (row_query[:, None] == col_query[None, :]) & (row_query[:, None] >= 0)
    keep = keep & (col_place[None, :] > row_place[:, None])
    row_worth = jnp.exp2(row_grade.astype(jnp.float32))
    col_worth = jnp.exp2(col_grade.astype(jnp.float32))
    signs = jnp.sign(row_grade[:, None] - col_grade[None, :]).astype(jnp.float32)
    change = (
        jnp.abs(row_worth[:, None] - col_worth[None, :])
        * jnp.abs(row_discount[:, None] - col_discount[None, :])
        * row_inverse[:, None]
    )
    chance = jax.nn.sigmoid(-signs * (row_score[:, None] - col_score[None, :]))
    push = jnp.where(keep, change * chance, 0.0) * signs
    bend = jnp.where(keep, change * chance * (1.0 - chance), 0.0)
    return (
        -jnp.sum(push, axis=1),
        jnp.sum(bend, axis=1),
        jnp.sum(push, axis=0),
        jnp.sum(bend, axis=0),
    )


def add_into(total, piece, start):
    current = lax.dynamic_slice_in_dim(total, start, piece.shape[0])
    return lax.dynamic_update_slice_in_dim(total, current + piece, start, 0)


def leaf_newton(sums):
    total_grad = sums[0]
    total_curv = sums[1]
    return (
        -jnp.sign(total_grad)
        * jnp.maximum(jnp.abs(total_grad) - lasso_penalty, 0.0)
        / (total_curv + ridge_penalty)
    )


def histogram_of(gradient, curvature, bins, owner):
    weights = jnp.stack([gradient, curvature, jnp.ones_like(gradient)])
    ordered = jnp.take(bins, owner, axis=1)
    groups = ordered.shape[1] // group_width
    grouped = ordered.reshape(ordered.shape[0], groups, group_width).transpose(1, 0, 2)
    levels = jnp.arange(BINS, dtype=jnp.int32)

    def one_group(group_bins):
        onehot = (group_bins[:, :, None] == levels[None, None, :]).astype(jnp.bfloat16)
        return jnp.einsum(
            "cd,dgb->cgb", weights, onehot.astype(jnp.float32), precision=lax.Precision.HIGHEST
        )

    parts = lax.map(one_group, grouped)
    return parts.transpose(1, 0, 2, 3).reshape(3, -1)


def local(scores, labels, leaves, bins, lengths, owner):
    feat_count = lax.axis_size("feat")
    feat_pos = lax.axis_index("feat")
    own_rows = scores.shape[0]
    block_rows = labels.shape[0]
    lengths_row = lengths[0]
    queries = lengths_row.shape[0]
    block_ids = query_of(lengths_row, block_rows)
    whole = lax.all_gather(scores, "feat", axis=0, tiled=True)
    discount, inverse = query_stats(whole, labels, block_ids, queries)
    padded = (
        jnp.pad(whole, (0, WINDOW)),
        jnp.pad(labels, (0, WINDOW)),
        jnp.pad(block_ids, (0, WINDOW), constant_values=-1),
        jnp.pad(discount, (0, WINDOW)),
        jnp.pad(inverse, (0, WINDOW)),
        jnp.arange(block_rows + WINDOW, dtype=jnp.int32),
    )

    def visit(tile_index, carry):
        acc_grad, acc_curv = carry
        start = (tile_index * feat_count + feat_pos) * TILE_ROWS
        row_part = tuple((lax.dynamic_slice_in_dim(item, start, TILE_ROWS) for item in padded))
        col_part = tuple(
            (lax.dynamic_slice_in_dim(padded[which], start, WINDOW) for which in (0, 1, 2, 3, 5))
        )
        row_grad, row_curv, col_grad, col_curv = pair_block(row_part, col_part)
        acc_grad = add_into(add_into(acc_grad, col_grad, start), row_grad, start)
        acc_curv = add_into(add_into(acc_curv, col_curv, start), row_curv, start)
        return (acc_grad, acc_curv)

    empty = jnp.zeros((block_rows + WINDOW,), jnp.float32)
    acc_grad, acc_curv = lax.fori_loop(0, own_rows // TILE_ROWS, visit, (empty, empty))
    partial_sums = jnp.stack([acc_grad[:block_rows], acc_curv[:block_rows]])
    lambdas = lax.psum_scatter(partial_sums, "feat", scatter_dimension=1, tiled=True)
    table = (leaves[:, None] == jnp.arange(LEAVES, dtype=jnp.int32)[None, :]).astype(jnp.float32)
    leaf_part = jnp.dot(lambdas, table, precision=lax.Precision.HIGHEST)
    leaf_values = leaf_newton(lax.psum(leaf_part, ("query", "feat")))
    score_step = shrinkage * leaf_values[leaves]
    partial_hist = histogram_of(lambdas[0], lambdas[1], bins, owner)
    histograms = lax.psum_scatter(partial_hist, ("query", "feat"), scatter_dimension=1, tiled=True)
    return (lambdas, leaf_values, score_step, histograms)


def solution(mesh):
    in_specs = (
        P(("query", "feat")),
        P("query"),
        P(("query", "feat")),
        P(("query", "feat"), None),
        P("query", None),
        P(),
    )
    out_specs = (P(None, ("query", "feat")), P(), P(("query", "feat")), P(None, ("query", "feat")))
    return jax.shard_map(local, mesh=mesh, in_specs=in_specs, out_specs=out_specs, check_vma=False)
```

profile of v0, /device:TPU:0, one launch (start us, length us, event | category | flops | bytes accessed | tf_op | source)
XLA Modules:
  0.0 1117.8 jit_solution(8969469040733795026)
XLA Ops:
  8.8 53.5 %while.53 = (s32[]{:T(128)}, u32[4096]{0:T(1024)S(1)}, u32[4096]{0:T(1024)S(1)}, s32[16]{0:T(128)S(1)}, s32[]{:T(128)}, /*index=5*/s32[]{:T(128)}) while((s32[]{:T(128)}, u32[4096]{0:T(1024)S(1)}, u32[4096]{0:T(1024)S(1)}, s32[16]{0:T(128)S(1)}, s32[]{:T(128)}, /*index=5*/s32[]{:T(128)}) %tuple.134), condition=%wide.region_2.3_spmd.clone, body=%wide.region_1.2_spmd.clone.sunk | while | flops 155651 | bytes 65807 | solution.py:21
  9.6 10.0 fusion.46
  20.3 10.0 fusion.46
  31.0 10.0 fusion.46
  41.7 10.0 fusion.46
  52.4 10.0 fusion.46
  62.4 6.1 sort.47
  68.5 23.0 %gather_fusion.1 = s32[4096]{0:T(1024)S(1)} fusion(s32[4096]{0:T(1024)S(1)} %convert_element_type.47, s32[4096]{0:T(1024)S(1)} %fusion.18), kind=kCustom, calls=%fused_computation.1 | custom fusion | bytes 49152 | tf_op jit(solution)/shard_map/gather | solution.py:37
  91.5 23.0 %gather_fusion.2 = s32[4096]{0:T(1024)S(1)} fusion(s32[4096]{0:T(1024)S(1)} %copy-done, s32[4096]{0:T(1024)S(1)} %fusion.18), kind=kCustom, calls=%fused_computation.2 | custom fusion | bytes 49152 | tf_op jit(solution)/shard_map/gather | solution.py:39
  114.6 14.8 %all_gather.3 = f32[4096]{0:T(1024)S(1)} all-gather(f32[1024]{0:T(1024)S(1)} %copy-done.5), channel_id=1, replica_groups=mesh['query'=8,'feat'=4] {'feat'}, dimensions={0}, use_global_device_ids=true | all-gather | bytes 20480 | tf_op jit(solution)/shard_map/all_gather | solution.py:112
  129.4 6.3 sort.46
  135.7 23.0 %gather_fusion = s32[4096]{0:T(1024)S(1)} fusion(s32[4096]{0:T(1024)S(1)} %convert_element_type.47, s32[4096]{0:T(1024)S(1)} %get-tuple-element.400), kind=kCustom, calls=%fused_computation | custom fusion | bytes 49152 | tf_op jit(solution)/shard_map/gather | solution.py:33
  159.9 15.5 %scatter_custom_fusion = s32[4096]{0:T(1024)S(1)} fusion(s32[4096]{0:T(1024)S(1)} %get-tuple-element.401, s32[4096]{0:T(1024)S(1)} %bitcast_subtract_fusion.1, s32[]{:T(128)} %copy.60), kind=kCustom, calls=%fused_computation.72 | custom fusion | bytes 16388 | tf_op jit(solution)/shard_map/scatter | solution.py:34
  175.8 29.0 %scatter_custom_fusion.1 = f32[17]{0:T(128)S(1)} fusion(s32[4096]{0:T(1024)S(1)} %bitcast.138, f32[4096]{0:T(1024)S(1)} %fusion.23, f32[]{:T(128)} %constant.151.clone.1), kind=kCustom, calls=%fused_computation.83 | custom fusion | flops 4096 | bytes 72 | tf_op jit(solution)/shard_map/scatter-add | solution.py:42
  205.6 10.6 select_select_fusion.1
  216.2 12.7 %while.51 = (s32[]{:T(128)}, f32[5632]{0:T(1024)S(1)}, f32[5632]{0:T(1024)S(1)}, s32[]{:T(128)}, s32[5632]{0:T(1024)S(1)}, /*index=5*/s32[5632]{0:T(1024)S(1)}, ...) while((s32[]{:T(128)}, f32[5632]{0:T(1024)S(1)}, ...), condition=%wide.region_16.17_spmd.clone, body=%wide.region_11.16_spmd.clone.sunk | while | flops 22811656 | bytes 224523 | solution.py:136
  217.1 4.9 fusion.42
  223.4 4.9 fusion.42
  232.8 43.3 %reduce-scatter.7.cloned.1.call-done = f32[1024,2]{1,0:T(8,128)} async-done(((f32[4096,2]{1,0:T(8,128)}), f32[1024,2]{1,0:T(8,128)}) %reduce-scatter.7.cloned.1.call-update) | async-done | bytes 8208
  277.9 102.5 %while.52 = (s32[]{:T(128)}, f32[32,3,8,256]{3,1,2,0:T(4,128)S(1)}, s32[32,1024,8]{1,2,0:T(8,128)S(1)}, f32[3,1024]{1,0:T(4,128)S(1)}, s32[]{:T(128)}) while((s32[]{:T(128)}, f32[32,3,8,256]{3,1,2,0:T(4,128)S(1)}, s32[32,1024,8]{1,2,0:T(8,128)S(1)}, f32[3,1024]{1,0:T(4,128)S(1)}, s32[]{:T(128)}) %tuple.140), condition=%wide.region_20.21_spmd.clone, body=%wide.region_19.20_spmd.clone.sunk | while | flops 77594624 | bytes 147533 | solution.py:100
  281.1 3.2 fusion.44
  284.3 3.2 fusion.44
  287.5 3.2 fusion.44
  290.7 3.2 fusion.44
  293.9 3.2 fusion.44
  297.1 3.2 fusion.44
  300.3 3.2 fusion.44
  342.0 3.2 fusion.44
  380.4 16.0 %copy.24 = f32[3,65536]{0,1:T(8,128)} copy(f32[3,65536]{1,0:T(4,128)S(1)} %bitcast.132) | data formatting | bytes 1572864
  398.9 43.7 %psum.7 = f32[2,1024]{1,0:T(2,128)S(1)} all-reduce(f32[2,1024]{1,0:T(2,128)S(1)} %fusion.15), channel_id=1, replica_groups=mesh['query'=8,'feat'=4] {'query','feat'}, use_global_device_ids=true, to_apply=%region_18.19 | all-reduce | flops 2048 | bytes 16384 | tf_op jit(solution)/shard_map/psum | solution.py:141
  442.7 4.5 gather_fusion.3
  447.8 661.0 %reduce-scatter.9.cloned.1.call-done = f32[2048,3]{1,0:T(8,128)} async-done(((f32[65536,3]{1,0:T(8,128)}), f32[2048,3]{1,0:T(8,128)}) %reduce-scatter.9.cloned.1.call-update) | async-done | bytes 24592
  (165 shorter events, 98.2 us)
Async XLA Ops:
  7.2 268.9 %reduce-scatter.7.cloned.1.call-start = ((), (), s32[]{:S(2)}) async-start(), calls=%async_computation.2 | async-start | bytes 2621440
  68.5 23.1 %copy-start = (s32[4096]{0:T(1024)S(1)}, s32[4096]{0:T(1024)}, u32[]{:S(2)}) copy-start(s32[4096]{0:T(1024)} %param.13) | copy-start | bytes 49156
  91.5 23.1 %copy-start.5 = (f32[1024]{0:T(1024)S(1)}, f32[1024]{0:T(1024)}, u32[]{:S(2)}) copy-start(f32[1024]{0:T(1024)} %param.12) | copy-start | bytes 12292
  228.9 2.2 copy-start.7
  228.9 2.3 copy-start.2
  231.0 877.8 %reduce-scatter.9.cloned.1.call-start = ((), (), s32[]{:S(2)}) async-start(), calls=%async_computation.3 | async-start | bytes 34603008
  277.3 0.6 copy-start.4
  396.4 0.7 copy-start.6
  396.4 1.1 copy-start.3
  442.7 668.3 %copy-start.1 = (f32[1,1024]{1,0:T(1,128)}, f32[1,1024]{1,0:T(1,128)S(1)}, u32[]{:S(2)}) copy-start(f32[1,1024]{1,0:T(1,128)S(1)} %fusion.31) | copy-start | bytes 12292
Sparse Core Ops, SparseCore 0:
  231.2 44.8 reduce-scatter.6
  396.6 712.1 reduce-scatter.8
where the time goes:
time: 1120 us
  waiting for transfers between devices  704 us (63%)
  local copies, waits for them, and re-layouts  120 us (11%)
  other arithmetic  116 us (10%)
  matrix products  104 us (9%)
  blocking collectives  58.5 us (5%)
  between operations  14.4 us (1%)
    unnamed x4, waiting for transfers between devices  704 us
    dot_general x32, matrix products, one_group(): jnp.einsum('cd,dgb->cgb', weights, onehot.astype(jnp.float32), precision=...  102 us
    select_n x5, other arithmetic, query_of(): return jnp.searchsorted(bounds, places, side='right')  49.8 us
    psum x1, blocking collectives, local(): leaf_values = leaf_newton(lax.psum(leaf_part, ('query', 'feat')))  43.7 us
    scatter-add x1, other arithmetic, query_stats(): ideal = jax.ops.segment_sum(terms, slots, num_segments=count + 1)  29 us
    unnamed x21, local copies, waits for them, and re-layouts  23.4 us
    gather x1, local copies, waits for them, and re-layouts, query_stats(): ideal_ids = query_ids[ideal_order]  23 us
    gather x1, local copies, waits for them, and re-layouts, query_stats(): worth = jnp.exp2(grades[ideal_order].astype(jnp.float32)) - 1.0  23 us
  transfers between devices with their start and end apart: 2, of which 2 were waited for; matrix products, arithmetic and copies ran while one was open for 1% of the time, Pallas kernels for 0%

commit v1 on v0

v1 whole, which is shorter than its diff:
```python
import functools

import jax
import jax.numpy as jnp
import numpy as np
from jax import lax
from jax.experimental import pallas as pl
from jax.experimental.pallas import tpu as pltpu
from jax.sharding import PartitionSpec as P

BINS = 256
LEAVES = 1024
LANES = 128
GRADES = 4
LOW = 32
HIGH = BINS // LOW
GROUP = 8
CHUNK = 64
MAX_LEN = 1024

lasso_penalty = 1.0
ridge_penalty = 1.0
shrinkage = 0.1

VMEM_LIMIT = 48 * 1024 * 1024
F32 = jnp.float32
BF16 = jnp.bfloat16
NT = (((1,), (1,)), ((), ()))


def iota(shape, axis):
    return lax.broadcasted_iota(jnp.int32, shape, axis)


def vmem():
    return pl.BlockSpec(memory_space=pltpu.VMEM)


def smem():
    return pl.BlockSpec(memory_space=pltpu.SMEM)


def prepare_kernel(len_ref, pos_ref, perm_ref, bins_ref, lab_ref, bins_t_ref, qid_ref, inv_ref, bounds_ref):
    queries = len_ref.shape[1]
    rows = lab_ref.shape[0]
    own = inv_ref.shape[0]
    bins = bins_ref[...].astype(F32).astype(BF16)
    bins_t_ref[...] = lax.dot_general(perm_ref[...], bins, NT, preferred_element_type=F32)

    place = iota((rows, LANES), 0) * LANES + iota((rows, LANES), 1)
    qid = jnp.zeros((rows, LANES), jnp.int32)
    begin = jnp.zeros((queries, LANES), jnp.int32)
    finish = jnp.zeros((queries, LANES), jnp.int32)
    which = iota((queries, LANES), 0)
    start = jnp.int32(0)
    for q in range(queries):
        end = start + len_ref[0, q]
        qid = qid + jnp.where(place >= end, 1, 0)
        begin = jnp.where(which == q, start, begin)
        finish = jnp.where(which == q, end, finish)

        def set_low(r, carry, start=start):
            bounds_ref[0, r] = start
            return carry

        def set_high(r, carry, end=end):
            bounds_ref[1, r] = end
            return carry

        lax.fori_loop((start + LANES - 1) // LANES, (end + LANES - 1) // LANES, set_low, 0)
        lax.fori_loop(start // LANES, end // LANES, set_high, 0)
        start = end
    qid_ref[...] = qid

    counts = [jnp.zeros((queries, LANES), F32) for _ in range(GRADES)]
    lane = iota((queries, LANES), 1)
    for r in range(rows):
        at = lane + r * LANES
        inside = (at >= begin) & (at < finish)
        grade = jnp.where(inside, jnp.broadcast_to(lab_ref[r:r + 1, :], (queries, LANES)), 0)
        for g in range(GRADES):
            counts[g] = counts[g] + jnp.where(grade > g, 1.0, 0.0)
    position = iota((queries, MAX_LEN), 1).astype(F32)
    worth = jnp.zeros((queries, MAX_LEN), F32)
    for g in range(GRADES):
        held = jnp.sum(counts[g], axis=1, keepdims=True)
        worth = worth + jnp.where(position < held, float(2 ** g), 0.0)
    ideal = jnp.sum(worth / jnp.log2(2.0 + position), axis=1, keepdims=True)
    usable = ideal > 0.5
    inverse = jnp.where(usable, 1.0 / jnp.where(usable, ideal, 1.0), 0.0)
    first = pos_ref[0] * own
    for t in range(own):
        at = lane + (first + t) * LANES
        inside = (at >= begin) & (at < finish)
        inv_ref[t:t + 1, :] = jnp.sum(jnp.where(inside, inverse, 0.0), axis=0, keepdims=True)


def prepare(lengths, pos, perm, bins, labels):
    rows = labels.shape[0]
    own = bins.shape[0] // LANES
    features = bins.shape[1]
    return pl.pallas_call(
        prepare_kernel,
        out_shape=(
            jax.ShapeDtypeStruct((features, bins.shape[0]), F32),
            jax.ShapeDtypeStruct((rows, LANES), jnp.int32),
            jax.ShapeDtypeStruct((own, LANES), F32),
            jax.ShapeDtypeStruct((2, rows), jnp.int32),
        ),
        in_specs=[smem(), smem(), vmem(), vmem(), vmem()],
        out_specs=(vmem(), vmem(), vmem(), smem()),
        compiler_params=pltpu.CompilerParams(vmem_limit_bytes=VMEM_LIMIT),
        cost_estimate=pl.CostEstimate(flops=200_000_000, bytes_accessed=3_000_000, transcendentals=20_000),
        name="prepare",
    )(lengths, pos, perm, bins, labels)


def split_terms(value, terms):
    parts = []
    rest = value
    for _ in range(terms):
        part = rest.astype(BF16)
        parts.append(part)
        rest = rest - part.astype(F32)
    return parts


def widen(ref, source, rows):
    turned = jnp.transpose(source)
    for r in range(rows):
        ref[r * LANES:(r + 1) * LANES, :] = jnp.broadcast_to(turned[:, r:r + 1], (LANES, LANES))


def pairs_kernel(parts, bounds_ref, pos_ref, *refs):
    score_refs = refs[:parts]
    (lab_ref, qid_ref, inv_ref, leaf_ref, lam_ref, sums_ref,
     s_row, a_row, w_row, d_row, s_col, a_col, w_col, q_col, d_col, grad, curv) = refs[parts:]
    rows = lab_ref.shape[0]
    own = inv_ref.shape[0]
    me = pos_ref[0]
    for k in range(parts):
        s_row[pl.ds(pl.multiple_of((me ^ k) * own, own), own), :] = score_refs[k][...]
    a_row[...] = jnp.exp(s_row[...])
    w_row[...] = jnp.left_shift(1, lab_ref[...]).astype(F32)
    d_row[...] = jnp.zeros((rows, LANES), F32)
    widen(s_col, s_row[...], rows)
    widen(q_col, qid_ref[...], rows)
    widen(a_col, a_row[...], rows)
    widen(w_col, w_row[...], rows)

    first = me * own
    window_low = bounds_ref[0, first] // LANES
    window_high = (bounds_ref[1, first + own - 1] + LANES - 1) // LANES

    def row_of(ref, r):
        return jnp.broadcast_to(ref[pl.ds(r, 1), :], (8, LANES))

    def rank_group(r, carry):
        score = row_of(s_row, r)
        query = row_of(qid_ref, r)

        def sweep(ahead):
            def step(c, acc):
                base = pl.multiple_of(c * CHUNK, CHUNK)
                acc = list(acc)
                for u in range(CHUNK // 8):
                    other = s_col[pl.ds(base + 8 * u, 8), :]
                    above = (other >= score) if ahead else (other > score)
                    hit = above & (q_col[pl.ds(base + 8 * u, 8), :] == query)
                    acc[u % 4] = acc[u % 4] + jnp.where(hit, 1.0, 0.0)
                return tuple(acc)
            return step

        acc = tuple(jnp.zeros((8, LANES), F32) for _ in range(4))
        low = bounds_ref[0, r] // CHUNK
        high = (bounds_ref[1, r] + CHUNK - 1) // CHUNK
        per = LANES // CHUNK
        acc = lax.fori_loop(low, r * per, sweep(True), acc)
        acc = list(lax.fori_loop((r + 1) * per, high, sweep(False), acc))
        base = pl.multiple_of(r * LANES, LANES)
        for u in range(LANES // 8):
            other = s_col[pl.ds(base + 8 * u, 8), :]
            earlier = iota((8, LANES), 0) + 8 * u < iota((8, LANES), 1)
            above = (other > score) | ((other == score) & earlier)
            hit = above & (q_col[pl.ds(base + 8 * u, 8), :] == query)
            acc[u % 4] = acc[u % 4] + jnp.where(hit, 1.0, 0.0)
        total = (acc[0] + acc[1]) + (acc[2] + acc[3])
        d_row[pl.ds(r, 1), :] = jnp.sum(total, axis=0, keepdims=True)
        return carry

    lax.fori_loop(window_low, window_high, rank_group, 0)
    d_row[...] = 1.0 / jnp.log2(2.0 + d_row[...])
    widen(d_col, d_row[...], rows)

    def pair_group(t, carry):
        r = first + t
        a_i = row_of(a_row, r)
        w_i = row_of(w_row, r)
        d_i = row_of(d_row, r)
        query = row_of(qid_ref, r)

        def step(c, acc):
            base = pl.multiple_of(c * CHUNK, CHUNK)
            push = list(acc[:2])
            bend = list(acc[2:])
            for u in range(CHUNK // 8):
                at = pl.ds(base + 8 * u, 8)
                a_j = a_col[at, :]
                total = a_i + a_j
                rough = pl.reciprocal(total, approx=True)
                recip = rough * (2.0 - total * rough)
                gap = jnp.abs(d_i - d_col[at, :])
                lift = w_i - w_col[at, :]
                weight = jnp.where(q_col[at, :] == query, gap * recip, 0.0) * lift
                push[u % 2] = push[u % 2] + weight * jnp.where(lift > 0.0, a_j, a_i)
                bend[u % 2] = bend[u % 2] + jnp.abs(weight) * (recip * a_j)
            return tuple(push + bend)

        acc = tuple(jnp.zeros((8, LANES), F32) for _ in range(4))
        low = bounds_ref[0, r] // CHUNK
        high = (bounds_ref[1, r] + CHUNK - 1) // CHUNK
        acc = lax.fori_loop(low, high, step, acc)
        inverse = inv_ref[pl.ds(t, 1), :]
        grad[pl.ds(t, 1), :] = -inverse * jnp.sum(acc[0] + acc[1], axis=0, keepdims=True)
        curv[pl.ds(t, 1), :] = inverse * a_row[pl.ds(r, 1), :] * jnp.sum(acc[2] + acc[3], axis=0, keepdims=True)
        return carry

    lax.fori_loop(0, own, pair_group, 0)
    for t in range(own):
        lam_ref[0:1, t * LANES:(t + 1) * LANES] = grad[t:t + 1, :]
        lam_ref[1:2, t * LANES:(t + 1) * LANES] = curv[t:t + 1, :]

    docs = own * LANES
    leaf = leaf_ref[...]
    highs = LEAVES // LANES
    top = jnp.broadcast_to(leaf // LANES, (highs, docs)) == iota((highs, docs), 0)
    spots = jnp.where(jnp.broadcast_to(leaf % LANES, (LANES, docs)) == iota((LANES, docs), 0), 1.0, 0.0).astype(BF16)
    pieces = []
    for c in range(2):
        for part in split_terms(lam_ref[c:c + 1, :], 3):
            pieces.append(jnp.where(top, jnp.broadcast_to(part.astype(F32), (highs, docs)), 0.0))
    stacked = jnp.concatenate(pieces, axis=0).astype(BF16)
    sums = lax.dot_general(stacked, spots, NT, preferred_element_type=F32)
    for c in range(2):
        base = c * 3 * highs
        sums_ref[c * highs:(c + 1) * highs, :] = (
            sums[base:base + highs] + (sums[base + highs:base + 2 * highs] + sums[base + 2 * highs:base + 3 * highs])
        )


def pair_terms(bounds, pos, scores, labels, qid, inverse, leaves):
    rows = labels.shape[0]
    own = inverse.shape[0]
    block = rows * LANES
    row = pltpu.VMEM((rows, LANES), F32)
    col = pltpu.VMEM((block, LANES), F32)
    return pl.pallas_call(
        functools.partial(pairs_kernel, len(scores)),
        out_shape=(
            jax.ShapeDtypeStruct((2, own * LANES), F32),
            jax.ShapeDtypeStruct((2 * LEAVES // LANES, LANES), F32),
        ),
        in_specs=[smem(), smem()] + [vmem()] * (len(scores) + 4),
        out_specs=(vmem(), vmem()),
        scratch_shapes=[row, row, row, row, col, col, col, pltpu.VMEM((block, LANES), jnp.int32), col,
                        pltpu.VMEM((own, LANES), F32), pltpu.VMEM((own, LANES), F32)],
        compiler_params=pltpu.CompilerParams(vmem_limit_bytes=VMEM_LIMIT),
        cost_estimate=pl.CostEstimate(flops=40_000_000, bytes_accessed=200_000, transcendentals=2_000_000),
        name="pair_terms",
    )(bounds, pos, *scores, labels, qid, inverse, leaves)


def histogram_kernel(first, groups, lam_ref, bins_ref, out_ref, weights):
    docs = lam_ref.shape[1]
    depth = 256
    rows = 16
    for c in range(2):
        fine = split_terms(lam_ref[c:c + 1, :], 2)
        tile = jnp.concatenate([jnp.broadcast_to(part.astype(F32), (HIGH, docs)) for part in fine], axis=0)
        weights[c * rows:(c + 1) * rows, :] = tile.astype(BF16)

    row = iota((rows, depth), 0)
    low_level = [(row + rows * k).astype(F32).astype(BF16) for k in range(LOW // rows)]
    high_level = (row % HIGH).astype(F32).astype(BF16)
    upper = row < HIGH
    zero = jnp.zeros((rows, depth), BF16)
    one = jnp.ones((rows, depth), BF16)
    lane_owner = iota((1, GROUP * LOW), 1) // LOW

    def one_group(g, carry):
        base = pl.multiple_of((first + g) * GROUP, GROUP)
        acc = None
        for k in range(docs // depth):
            span = slice(k * depth, (k + 1) * depth)
            code = bins_ref[pl.ds(base, GROUP), span]
            high = jnp.floor(code * (1.0 / LOW))
            low = code - high * LOW
            left, right, count = [], [], []
            wide = []
            for f in range(GROUP):
                high_f = jnp.broadcast_to(high[f:f + 1, :], (rows, depth))
                low_f = jnp.broadcast_to(low[f:f + 1, :], (rows, depth)).astype(BF16)
                wide.append(high_f)
                match = high_f.astype(BF16) == high_level
                for c in range(2):
                    left.append(jnp.where(match, weights[c * rows:(c + 1) * rows, span], zero))
                for level in low_level:
                    right.append(jnp.where(low_f == level, one, zero))
            for f in range(0, GROUP, 2):
                both = jnp.where(upper, wide[f], wide[f + 1]).astype(BF16)
                count.append(jnp.where(both == high_level, one, zero))
            part = lax.dot_general(
                jnp.concatenate(left + count, axis=0), jnp.concatenate(right, axis=0), NT,
                preferred_element_type=F32,
            )
            acc = part if acc is None else acc + part
        stats = jnp.zeros((2 * rows, GROUP * LOW), F32)
        counts = jnp.zeros((HIGH, GROUP * LOW), F32)
        for f in range(GROUP):
            mine = lane_owner == f
            stats = jnp.where(mine, acc[f * 2 * rows:(f + 1) * 2 * rows], stats)
            at = GROUP * 2 * rows + f * HIGH
            counts = jnp.where(mine, acc[at:at + HIGH], counts)
        out_ref[g] = jnp.concatenate(
            [stats[0:HIGH] + stats[HIGH:2 * HIGH], stats[2 * HIGH:3 * HIGH] + stats[3 * HIGH:4 * HIGH], counts], axis=0)
        return carry

    lax.fori_loop(0, groups, one_group, 0)


def histogram_part(first, groups, lambdas, bins_t):
    docs = lambdas.shape[1]
    return pl.pallas_call(
        functools.partial(histogram_kernel, first, groups),
        out_shape=jax.ShapeDtypeStruct((groups, 3 * HIGH, GROUP * LOW), F32),
        in_specs=[vmem(), vmem()],
        out_specs=vmem(),
        scratch_shapes=[pltpu.VMEM((4 * HIGH, docs), BF16)],
        compiler_params=pltpu.CompilerParams(vmem_limit_bytes=VMEM_LIMIT),
        cost_estimate=pl.CostEstimate(flops=groups * 330_000_000, bytes_accessed=groups * 60_000, transcendentals=0),
        name="histogram_part",
    )(lambdas, bins_t)


def finish_kernel(parts, per_dev, *refs):
    sum_refs = refs[:parts]
    leaf_ref = refs[parts]
    hist_refs = refs[parts + 1:parts + 1 + parts]
    value_ref, step_ref, hist_ref = refs[2 * parts + 1:]
    totals = add_up([ref[...] for ref in sum_refs])
    highs = LEAVES // LANES
    grad, curv = totals[:highs], totals[highs:]
    shrunk = jnp.maximum(jnp.abs(grad) - lasso_penalty, 0.0)
    values = jnp.where(grad > 0.0, -shrunk, shrunk) / (curv + ridge_penalty)
    value_ref[...] = values
    leaf = leaf_ref[...]
    top, spot = leaf // LANES, leaf % LANES
    step = jnp.zeros(leaf.shape, F32)
    for h in range(highs):
        row = jnp.broadcast_to(values[h:h + 1, :], leaf.shape)
        step = jnp.where(top == h, jnp.take_along_axis(row, spot, axis=1), step)
    step_ref[...] = shrinkage * step
    hist = add_up([ref[...] for ref in hist_refs])
    if per_dev == GROUP:
        for c in range(3):
            for f in range(GROUP):
                line = [hist[c * HIGH + h:c * HIGH + h + 1, f * LOW:(f + 1) * LOW] for h in range(HIGH)]
                hist_ref[c:c + 1, f * BINS:(f + 1) * BINS] = jnp.concatenate(line, axis=1)
    else:
        hist_ref[...] = hist


def finish(sums, leaves, hists, per_dev):
    out = (3, per_dev * BINS) if per_dev == GROUP else hists[0].shape
    return pl.pallas_call(
        functools.partial(finish_kernel, len(sums), per_dev),
        out_shape=(
            jax.ShapeDtypeStruct((LEAVES // LANES, LANES), F32),
            jax.ShapeDtypeStruct(leaves.shape, F32),
            jax.ShapeDtypeStruct(out, F32),
        ),
        in_specs=[vmem()] * (2 * len(sums) + 1),
        out_specs=(vmem(), vmem(), vmem()),
        compiler_params=pltpu.CompilerParams(vmem_limit_bytes=VMEM_LIMIT),
        name="finish",
    )(*sums, leaves, *hists)


def add_up(parts):
    while len(parts) > 1:
        parts = [parts[k] + parts[k + 1] for k in range(0, len(parts), 2)]
    return parts[0]


def exchange_rounds(query_count, feat_count):
    feat_bits = [1 << b for b in range(feat_count.bit_length() - 1)]
    query_bits = [feat_count << b for b in range(query_count.bit_length() - 1)]
    rounds = [query_bits[:1]] if query_bits else []
    for bits in (query_bits[1:], feat_bits):
        rounds += [bits[k:k + 2] for k in range(0, len(bits), 2)]
    return [[0] + bits if len(bits) == 1 else [0, bits[0], bits[1], bits[0] | bits[1]] for bits in rounds]


def local(scores, labels, leaves, bins, lengths, owner):
    query_count = lax.axis_size("query")
    feat_count = lax.axis_size("feat")
    count = query_count * feat_count
    feat_pos = lax.axis_index("feat").astype(jnp.int32)
    place = lax.axis_index("query").astype(jnp.int32) * feat_count + feat_pos
    docs = scores.shape[0]
    own = docs // LANES
    features = owner.shape[0]
    per_dev = features // count
    axes = ("query", "feat")
    rounds = exchange_rounds(query_count, feat_count)

    def swap(value, mask):
        return lax.ppermute(value, axes, [(p, p ^ mask) for p in range(count)])

    own_scores = scores.reshape(own, LANES)
    score_parts = [own_scores] + [
        lax.ppermute(own_scores, "feat", [(p, p ^ k) for p in range(feat_count)]) for k in range(1, feat_count)]

    order = [0]
    for masks in reversed(rounds):
        order = [mask | rest for mask in masks for rest in order]
    relative = jnp.asarray(np.array(order, np.int32)) ^ place
    held = owner.reshape(count, per_dev)
    pick = relative[:, None, None] == jnp.arange(count, dtype=jnp.int32)[None, :, None]
    turned = jnp.sum(jnp.where(pick, held[None], 0), axis=1).reshape(features)
    perm = (turned[:, None] == jnp.arange(features, dtype=jnp.int32)[None, :]).astype(BF16)

    pos = feat_pos.reshape(1)
    label_rows = labels.reshape(-1, LANES)
    bins_t, qid, inverse, bounds = prepare(lengths, pos, perm, bins, label_rows)
    lambdas, sums = pair_terms(bounds, pos, score_parts, label_rows, qid, inverse, leaves.reshape(1, docs))

    def blocks(part):
        if per_dev == GROUP:
            return part
        groups = part.shape[0]
        wide = part.reshape(groups, 3, HIGH, GROUP // per_dev, per_dev, LOW)
        return wide.transpose(0, 3, 1, 4, 2, 5).reshape(groups * GROUP // per_dev, 3, per_dev * BINS)

    total_groups = features // GROUP
    fan = len(rounds[1])
    cuts = [total_groups // 2, total_groups // (2 * fan), 0]
    tops = [total_groups, total_groups // 2, total_groups // (2 * fan)]
    pieces = [blocks(histogram_part(cut, top - cut, lambdas, bins_t)) for cut, top in zip(cuts, tops)]

    arrived = swap(pieces[0], rounds[0][1])
    edge = pieces[2].shape[0]
    current = [pieces[2] + arrived[:edge]]
    for k in range(fan - 1):
        span = slice(k * edge, (k + 1) * edge)
        current.append(pieces[1][span] + arrived[edge:][span])
    for k in range(1, len(rounds)):
        masks = rounds[k]
        received = [current[0]] + [swap(current[m], masks[m]) for m in range(1, len(masks))]
        if k + 1 < len(rounds):
            merged = add_up(received)
            step = merged.shape[0] // len(rounds[k + 1])
            current = [merged[m * step:(m + 1) * step] for m in range(len(rounds[k + 1]))]

    for k, masks in enumerate(rounds):
        sums_parts = [sums] + [swap(sums, mask) for mask in masks[1:]]
        if k + 1 < len(rounds):
            sums = add_up(sums_parts)

    values, step, histograms = finish(
        sums_parts, leaves.reshape(own, LANES), [part[0] for part in received], per_dev)
    return lambdas, values.reshape(LEAVES), step.reshape(docs), histograms


def solution(mesh):
    in_specs = (
        P(("query", "feat")),
        P("query"),
        P(("query", "feat")),
        P(("query", "feat"), None),
        P("query", None),
        P(),
    )
    out_specs = (P(None, ("query", "feat")), P(), P(("query", "feat")), P(None, ("query", "feat")))
    return jax.shard_map(local, mesh=mesh, in_specs=in_specs, out_specs=out_specs, check_vma=False)
```

time: 1120 us -> 58.9 us (0.05)
  waiting for transfers between devices: 704 us -> 5.49 us
  local copies, waits for them, and re-layouts: 120 us -> 4.72 us
  other arithmetic: 116 us -> 0.9 us
  matrix products: 104 us -> 0 us
  blocking collectives: 58.5 us -> 0 us
  starting transfers between devices: 0.08 us -> 23.6 us
  Pallas kernels: 0 us -> 23.2 us
  between operations: 14.4 us -> 0.81 us
    unnamed x4 -> x0, waiting for transfers between devices: 704 us -> none
    dot_general x33 -> x0, matrix products: 104 us -> none  [the longest x32 102 us: one_group(): jnp.einsum('cd,dgb->cgb', weights, onehot.astype(jnp.float32), precision=...]
    gather x11 -> x0, local copies, waits for them, and re-layouts: 79 us -> none  [the longest x1 23 us: query_stats(): ideal_ids = query_ids[ideal_order]]
    select_n x9 -> x0, other arithmetic: 49.9 us -> none  [the longest x5 49.8 us: query_of(): return jnp.searchsorted(bounds, places, side='right')]
    psum x1 -> x0, blocking collectives: 43.7 us -> none  [local(): leaf_values = leaf_newton(lax.psum(leaf_part, ('query', 'feat')))]
    scatter-add x1 -> x0, other arithmetic: 29 us -> none  [query_stats(): ideal = jax.ops.segment_sum(terms, slots, num_segments=count + 1)]
    ppermute x0 -> x17, starting transfers between devices: none -> 23.6 us  [the longest x14 17.8 us: swap(): return lax.ppermute(value, axes, [(p, p ^ mask) for p in range(count)])]
    pallas_call x0 -> x6, Pallas kernels: none -> 23.2 us  [the longest x3 12.5 us: histogram_part(): pl.pallas_call(functools.partial(histogram_kernel, first, groups), out_sh...]
  transfers between devices with their start and end apart: 2 -> 17, of which waited for: 2 -> 3; matrix products, arithmetic and copies ran while one was open for 1% -> 2% of each run, Pallas kernels for 0% -> 14%
where the time goes in v1:
time: 58.9 us; the launch traced here: 58.7 us
  starting transfers between devices  23.6 us (40%)
  Pallas kernels  23.2 us (39%)
  waiting for transfers between devices  5.49 us (9%)
  local copies, waits for them, and re-layouts  4.72 us (8%)
  other arithmetic  0.9 us (2%)
  between operations  0.81 us (1%)
    ppermute x14, starting transfers between devices, swap(): return lax.ppermute(value, axes, [(p, p ^ mask) for p in range(count)])  17.8 us
    pallas_call x3, Pallas kernels, histogram_part(): pl.pallas_call(functools.partial(histogram_kernel, first, groups), out_sh...  12.5 us
    pallas_call x1, Pallas kernels, pair_terms(): pl.pallas_call(functools.partial(pairs_kernel, len(scores)), out_shape=(j...  7.73 us
    ppermute x3, starting transfers between devices, local(): lax.ppermute(own_scores, 'feat', [(p, p ^ k) for p in range(feat_count)])  5.76 us
    ppermute x14, waiting for transfers between devices, swap(): return lax.ppermute(value, axes, [(p, p ^ mask) for p in range(count)])  5.48 us
    unnamed x16, local copies, waits for them, and re-layouts  4.48 us
    pallas_call x1, Pallas kernels, prepare(): pl.pallas_call(prepare_kernel, out_shape=(jax.ShapeDtypeStruct((features,...  2.13 us
  transfers between devices with their start and end apart: 17, of which 3 were waited for; matrix products, arithmetic and copies ran while one was open for 2% of the time, Pallas kernels for 14%

profile of v1, /device:TPU:0, one launch (start us, length us, event | category | flops | bytes accessed | tf_op | source)
XLA Modules:
  0.0 58.7 jit_solution(6037208442646137547)
XLA Ops:
  0.6 5.1 %collective-permute-start.2 = (f32[8,128]{1,0:T(8,128)}, f32[8,128]{1,0:T(8,128)S(1)}, u32[]{:S(2)}, u32[]{:S(2)}) collective-permute-start(f32[8,128]{1,0:T(8,128)} %bitcast.19), channel_id=1, source_target_pairs={{0,3},{1,2},{2,1},{3,0},{4,7},{5,6},{6,5},{7,4},{8,11},{9,10},{10,... | collective-permute-start | bytes 12296 | tf_op jit(solution)/shard_map/ppermute | solution.py:422
  5.7 0.6 %collective-permute-start = (f32[8,128]{1,0:T(8,128)}, f32[8,128]{1,0:T(8,128)S(1)}, u32[]{:S(2)}, u32[]{:S(2)}) collective-permute-start(f32[8,128]{1,0:T(8,128)} %bitcast.21), channel_id=1, source_target_pairs={{0,1},{1,0},{2,3},{3,2},{4,5},{5,4},{6,7},{7,6},{8,9},{9,8},{10,11... | collective-permute-start | bytes 12296 | tf_op jit(solution)/shard_map/ppermute | solution.py:422
  6.4 0.7 %copy-done.7 = s32[32]{0:T(128)S(1)} copy-done((s32[32]{0:T(128)S(1)}, s32[32]{0:T(128)}, u32[]{:S(2)}) %copy-start.7) | copy-done | bytes 152
  7.1 0.1 iota_compare_fusion.1
  7.1 0.6 %copy-done.6 = s32[256]{0:T(256)S(1)} copy-done((s32[256]{0:T(256)S(1)}, s32[256]{0:T(256)}, u32[]{:S(2)}) %copy-start.6) | copy-done | bytes 1048
  7.7 0.1 broadcast_in_dim.26
  7.8 0.1 copy.11
  7.9 0.6 %select_reduce_fusion = s32[32,8]{1,0:T(8,128)S(1)} fusion(s32[32,8]{0,1:T(8,128)S(1)} %copy.11, pred[32,32]{1,0:T(8,128)(4,1)S(1)} %iota_compare_fusion.1), kind=kLoop, calls=%fused_computation.2 | loop fusion | flops 16128 | bytes 3072 | tf_op jit(solution)/shard_map/reduce_sum | solution.py:430
  8.5 0.1 eq.36
  8.6 0.1 fusion.perm_ref
  8.7 0.6 %copy-done.1 = s32[4096]{0:T(1024)S(1)} copy-done((s32[4096]{0:T(1024)S(1)}, s32[4096]{0:T(1024)}, u32[]{:S(2)}) %copy-start.1) | copy-done | bytes 16408
  9.4 1.2 %copy-done = s32[1024,256]{1,0:T(8,128)S(1)} copy-done((s32[1024,256]{1,0:T(8,128)S(1)}, s32[1024,256]{1,0:T(8,128)}, u32[]{:S(2)}) %copy-start) | copy-done | bytes 1048600
  10.6 2.1 %prepare.1 = (f32[256,1024]{1,0:T(8,128)S(1)}, s32[32,128]{1,0:T(8,128)S(1)}, f32[8,128]{1,0:T(8,128)S(1)}, s32[2,32]{1,0:T(2,128)S(1)}) custom-call(s32[1,16]{1,0:T(1,128)S(1)} %copy-done.3, s32[1]{0:T(128)} %bitcast.pos_ref, bf16[256,256]{1,0:T(8,128)(2,1)S(1)} %fusion.perm_ref, s32[1024,256]{1,0:T(8,128)S(1)} %copy-done, s32[32,128]{1,0:T(8,128)S(1)} %bitcast.15), custom_call_target="tpu_custom_call" | custom-call | flops 200000000 | bytes 3000000 | tf_op jit(solution)/shard_map/prepare/pallas_call | solution.py:102
  12.8 0.6 %copy-done.2 = s32[1024]{0:T(1024)S(1)} copy-done((s32[1024]{0:T(1024)S(1)}, s32[1024]{0:T(1024)}, u32[]{:S(2)}) %copy-start.2) | copy-done | bytes 4120
  13.4 7.7 %pair_terms.1 = (f32[2,1024]{1,0:T(2,128)}, f32[16,128]{1,0:T(8,128)S(1)}) custom-call(s32[2,32]{1,0:T(2,128)S(1)} %get-tuple-element.13.bounds_ref, s32[1]{0:T(128)} %bitcast.pos_ref, f32[8,128]{1,0:T(8,128)S(1)} %bitcast.22, f32[8,128]{1,0:T(8,128)S(1)} %collective-permute-done.refs_1_, f32[8,128]{1,0:T(8,128)S(1)} %collective-permute-done.1.refs_2_, ...), custom_call_target="tpu_custom_call" | custom-call | flops 40000000 | bytes 200000 | tf_op jit(solution)/shard_map/pair_terms/pallas_call | solution.py:257
  21.2 0.7 %copy-done.5 = f32[2,1024]{1,0:T(2,128)S(1)} copy-done((f32[2,1024]{1,0:T(2,128)S(1)}, f32[2,1024]{1,0:T(2,128)}, u32[]{:S(2)}) %copy-start.5) | copy-done | bytes 8216
  21.9 6.2 %histogram_part.4 = f32[16,24,256]{2,1,0:T(8,128)S(1)} custom-call(f32[2,1024]{1,0:T(2,128)S(1)} %copy-done.5, f32[256,1024]{1,0:T(8,128)S(1)} %get-tuple-element.18.bins_ref), custom_call_target="tpu_custom_call" | custom-call | flops 5280000000 | bytes 960000 | tf_op jit(solution)/shard_map/histogram_part/pallas_call | solution.py:333
  28.1 0.1 collective-permute-start.10
  28.2 0.5 collective-permute-start.3
  28.7 4.7 %histogram_part.5 = f32[12,24,256]{2,1,0:T(8,128)S(1)} custom-call(f32[2,1024]{1,0:T(2,128)S(1)} %copy-done.5, f32[256,1024]{1,0:T(8,128)S(1)} %get-tuple-element.18.bins_ref), custom_call_target="tpu_custom_call" | custom-call | flops 3960000000 | bytes 720000 | tf_op jit(solution)/shard_map/histogram_part/pallas_call | solution.py:333
  33.4 2.5 %collective-permute-start.13 = (f32[4,24,256]{2,1,0:T(8,128)S(1)}, f32[4,24,256]{2,1,0:T(8,128)S(1)}, u32[]{:S(2)}, u32[]{:S(2)}) collective-permute-start(f32[4,24,256]{2,1,0:T(8,128)S(1)} %get-tuple-element.22), channel_id=1, source_target_pairs={{0,24},{1,25},{2,26},{3,27},{4,28},{5,29},{6,30},{7,31},{8,16},{9,... | collective-permute-start | bytes 294920 | tf_op jit(solution)/shard_map/ppermute | solution.py:418
  35.9 2.5 %collective-permute-start.12 = (f32[4,24,256]{2,1,0:T(8,128)S(1)}, f32[4,24,256]{2,1,0:T(8,128)S(1)}, u32[]{:S(2)}, u32[]{:S(2)}) collective-permute-start(f32[4,24,256]{2,1,0:T(8,128)S(1)} %get-tuple-element.23), channel_id=1, source_target_pairs={{0,16},{1,17},{2,18},{3,19},{4,20},{5,21},{6,22},{7,23},{8,24},{9,... | collective-permute-start | bytes 294920 | tf_op jit(solution)/shard_map/ppermute | solution.py:418
  38.4 1.6 %histogram_part.3 = f32[4,24,256]{2,1,0:T(8,128)S(1)} custom-call(f32[2,1024]{1,0:T(2,128)S(1)} %copy-done.5, f32[256,1024]{1,0:T(8,128)S(1)} %get-tuple-element.18.bins_ref), custom_call_target="tpu_custom_call" | custom-call | flops 1320000000 | bytes 240000 | tf_op jit(solution)/shard_map/histogram_part/pallas_call | solution.py:333
  40.0 1.5 %collective-permute-start.6 = (f32[16,128]{1,0:T(8,128)S(1)}, f32[16,128]{1,0:T(8,128)S(1)}, u32[]{:S(2)}, u32[]{:S(2)}) collective-permute-start(f32[16,128]{1,0:T(8,128)S(1)} %add.37), channel_id=1, source_target_pairs={{0,24},{1,25},{2,26},{3,27},{4,28},{5,29},{6,30},{7,31},{8,16},{9,... | collective-permute-start | bytes 24584 | tf_op jit(solution)/shard_map/ppermute | solution.py:418
  41.5 2.0 %collective-permute-start.5 = (f32[16,128]{1,0:T(8,128)S(1)}, f32[16,128]{1,0:T(8,128)S(1)}, u32[]{:S(2)}, u32[]{:S(2)}) collective-permute-start(f32[16,128]{1,0:T(8,128)S(1)} %add.37), channel_id=1, source_target_pairs={{0,16},{1,17},{2,18},{3,19},{4,20},{5,21},{6,22},{7,23},{8,24},{9,... | collective-permute-start | bytes 24584 | tf_op jit(solution)/shard_map/ppermute | solution.py:418
  43.7 4.2 %collective-permute-start.16 = (f32[1,24,256]{2,1,0:T(8,128)S(1)}, f32[1,24,256]{2,1,0:T(8,128)S(1)}, u32[]{:S(2)}, u32[]{:S(2)}) collective-permute-start(f32[1,24,256]{2,1,0:T(8,128)S(1)} %get-tuple-element.25), channel_id=1, source_target_pairs={{0,3},{1,2},{2,1},{3,0},{4,7},{5,6},{6,5},{7,4},{8,11},{9,10},{10,... | collective-permute-start | bytes 73736 | tf_op jit(solution)/shard_map/ppermute | solution.py:418
  47.9 0.6 %collective-permute-start.14 = (f32[1,24,256]{2,1,0:T(8,128)S(1)}, f32[1,24,256]{2,1,0:T(8,128)S(1)}, u32[]{:S(2)}, u32[]{:S(2)}) collective-permute-start(f32[1,24,256]{2,1,0:T(8,128)S(1)} %get-tuple-element.27), channel_id=1, source_target_pairs={{0,1},{1,0},{2,3},{3,2},{4,5},{5,4},{6,7},{7,6},{8,9},{9,8},{10,11... | collective-permute-start | bytes 73736 | tf_op jit(solution)/shard_map/ppermute | solution.py:418
  48.5 3.8 %collective-permute-start.9 = (f32[16,128]{1,0:T(8,128)S(1)}, f32[16,128]{1,0:T(8,128)S(1)}, u32[]{:S(2)}, u32[]{:S(2)}) collective-permute-start(f32[16,128]{1,0:T(8,128)S(1)} %add_add_fusion.refs_0_), channel_id=1, source_target_pairs={{0,3},{1,2},{2,1},{3,0},{4,7},{5,6},{6,5},{7,4},{8,11},{9,10},{10,... | collective-permute-start | bytes 24584 | tf_op jit(solution)/shard_map/ppermute | solution.py:418
  52.3 1.8 %collective-permute-done.9.refs_3_ = f32[16,128]{1,0:T(8,128)S(1)} collective-permute-done((f32[16,128]{1,0:T(8,128)S(1)}, f32[16,128]{1,0:T(8,128)S(1)}, u32[]{:S(2)}, u32[]{:S(2)}) %collective-permute-start.9) | collective-permute-done | bytes 8224 | tf_op jit(solution)/shard_map/ppermute | solution.py:418
  54.1 2.7 %collective-permute-done.8.refs_2_ = f32[16,128]{1,0:T(8,128)S(1)} collective-permute-done((f32[16,128]{1,0:T(8,128)S(1)}, f32[16,128]{1,0:T(8,128)S(1)}, u32[]{:S(2)}, u32[]{:S(2)}) %collective-permute-start.8) | collective-permute-done | bytes 8224 | tf_op jit(solution)/shard_map/ppermute | solution.py:418
  56.9 0.9 %collective-permute-done.7.refs_1_ = f32[16,128]{1,0:T(8,128)S(1)} collective-permute-done((f32[16,128]{1,0:T(8,128)S(1)}, f32[16,128]{1,0:T(8,128)S(1)}, u32[]{:S(2)}, u32[]{:S(2)}) %collective-permute-start.7) | collective-permute-done | bytes 8224 | tf_op jit(solution)/shard_map/ppermute | solution.py:418
  57.8 0.9 %finish.1 = (f32[8,128]{1,0:T(8,128)}, f32[8,128]{1,0:T(8,128)}, f32[3,2048]{1,0:T(4,128)}) custom-call(f32[16,128]{1,0:T(8,128)S(1)} %add_add_fusion.refs_0_, f32[16,128]{1,0:T(8,128)S(1)} %collective-permute-done.7.refs_1_, f32[16,128]{1,0:T(8,128)S(1)} %collective-permute-done.8.refs_2_, f32[16,128]{1,0:T(8,128)S(1)} %collective-permute-done.9.refs_3_, ...), custom_call_target="tpu_custom_call" | custom-call | tf_op jit(solution)/shard_map/finish/pallas_call | solution.py:375
  (36 shorter events, 0.2 us)
Async XLA Ops:
  0.6 12.1 %collective-permute-start.2 = (f32[8,128]{1,0:T(8,128)}, f32[8,128]{1,0:T(8,128)S(1)}, u32[]{:S(2)}, u32[]{:S(2)}) collective-permute-start(f32[8,128]{1,0:T(8,128)} %bitcast.19), channel_id=1, source_target_pairs={{0,3},{1,2},{2,1},{3,0},{4,7},{5,6},{6,5},{7,4},{8,11},{9,10},{10,... | collective-permute-start | bytes 12296 | tf_op jit(solution)/shard_map/ppermute | solution.py:422
  5.7 7.0 %collective-permute-start.1 = (f32[8,128]{1,0:T(8,128)}, f32[8,128]{1,0:T(8,128)S(1)}, u32[]{:S(2)}, u32[]{:S(2)}) collective-permute-start(f32[8,128]{1,0:T(8,128)} %bitcast.20), channel_id=1, source_target_pairs={{0,2},{1,3},{2,0},{3,1},{4,6},{5,7},{6,4},{7,5},{8,10},{9,11},{10,... | collective-permute-start | bytes 12296 | tf_op jit(solution)/shard_map/ppermute | solution.py:422
  5.7 7.0 %collective-permute-start = (f32[8,128]{1,0:T(8,128)}, f32[8,128]{1,0:T(8,128)S(1)}, u32[]{:S(2)}, u32[]{:S(2)}) collective-permute-start(f32[8,128]{1,0:T(8,128)} %bitcast.21), channel_id=1, source_target_pairs={{0,1},{1,0},{2,3},{3,2},{4,5},{5,4},{6,7},{7,6},{8,9},{9,8},{10,11... | collective-permute-start | bytes 12296 | tf_op jit(solution)/shard_map/ppermute | solution.py:422
  6.4 0.7 %copy-start.7 = (s32[32]{0:T(128)S(1)}, s32[32]{0:T(128)}, u32[]{:S(2)}) copy-start(s32[32]{0:T(128)} %constant.15.clone) | copy-start | bytes 388
  7.0 0.7 %copy-start.6 = (s32[256]{0:T(256)S(1)}, s32[256]{0:T(256)}, u32[]{:S(2)}) copy-start(s32[256]{0:T(256)} %param.12) | copy-start | bytes 3076
  8.6 0.7 %copy-start.1 = (s32[4096]{0:T(1024)S(1)}, s32[4096]{0:T(1024)}, u32[]{:S(2)}) copy-start(s32[4096]{0:T(1024)} %param.8) | copy-start | bytes 49156
  8.7 0.7 %copy-start.3 = (s32[1,16]{1,0:T(1,128)S(1)}, s32[1,16]{1,0:T(1,128)}, u32[]{:S(2)}) copy-start(s32[1,16]{1,0:T(1,128)} %len_ref.1) | copy-start | bytes 196
  9.4 1.2 %copy-start = (s32[1024,256]{1,0:T(8,128)S(1)}, s32[1024,256]{1,0:T(8,128)}, u32[]{:S(2)}) copy-start(s32[1024,256]{1,0:T(8,128)} %bins_ref.1) | copy-start | bytes 3145732
  10.6 2.2 %copy-start.4 = (f32[1024]{0:T(1024)S(1)}, f32[1024]{0:T(1024)}, u32[]{:S(2)}) copy-start(f32[1024]{0:T(1024)} %param.7) | copy-start | bytes 12292
  12.7 0.7 %copy-start.2 = (s32[1024]{0:T(1024)S(1)}, s32[1024]{0:T(1024)}, u32[]{:S(2)}) copy-start(s32[1024]{0:T(1024)} %param.9) | copy-start | bytes 12292
  21.2 0.7 %copy-start.5 = (f32[2,1024]{1,0:T(2,128)S(1)}, f32[2,1024]{1,0:T(2,128)}, u32[]{:S(2)}) copy-start(f32[2,1024]{1,0:T(2,128)} %get-tuple-element.9.lam_ref) | copy-start | bytes 24580
  28.1 5.3 %collective-permute-start.10 = (f32[16,24,256]{2,1,0:T(8,128)S(1)}, f32[16,24,256]{2,1,0:T(8,128)S(1)}, u32[]{:S(2)}, u32[]{:S(2)}) collective-permute-start(f32[16,24,256]{2,1,0:T(8,128)S(1)} %histogram_part.4), channel_id=1, source_target_pairs={{0,4},{1,5},{2,6},{3,7},{4,0},{5,1},{6,2},{7,3},{8,12},{9,13},{10,... | collective-permute-start | bytes 1179656 | tf_op jit(solution)/shard_map/ppermute | solution.py:418
  28.2 11.8 %collective-permute-start.3 = (f32[16,128]{1,0:T(8,128)S(1)}, f32[16,128]{1,0:T(8,128)S(1)}, u32[]{:S(2)}, u32[]{:S(2)}) collective-permute-start(f32[16,128]{1,0:T(8,128)S(1)} %get-tuple-element.17), channel_id=1, source_target_pairs={{0,4},{1,5},{2,6},{3,7},{4,0},{5,1},{6,2},{7,3},{8,12},{9,13},{10,... | collective-permute-start | bytes 24584 | tf_op jit(solution)/shard_map/ppermute | solution.py:418
  33.4 10.2 %collective-permute-start.13 = (f32[4,24,256]{2,1,0:T(8,128)S(1)}, f32[4,24,256]{2,1,0:T(8,128)S(1)}, u32[]{:S(2)}, u32[]{:S(2)}) collective-permute-start(f32[4,24,256]{2,1,0:T(8,128)S(1)} %get-tuple-element.22), channel_id=1, source_target_pairs={{0,24},{1,25},{2,26},{3,27},{4,28},{5,29},{6,30},{7,31},{8,16},{9,... | collective-permute-start | bytes 294920 | tf_op jit(solution)/shard_map/ppermute | solution.py:418
  35.9 7.7 %collective-permute-start.12 = (f32[4,24,256]{2,1,0:T(8,128)S(1)}, f32[4,24,256]{2,1,0:T(8,128)S(1)}, u32[]{:S(2)}, u32[]{:S(2)}) collective-permute-start(f32[4,24,256]{2,1,0:T(8,128)S(1)} %get-tuple-element.23), channel_id=1, source_target_pairs={{0,16},{1,17},{2,18},{3,19},{4,20},{5,21},{6,22},{7,23},{8,24},{9,... | collective-permute-start | bytes 294920 | tf_op jit(solution)/shard_map/ppermute | solution.py:418
  38.4 5.2 %collective-permute-start.11 = (f32[4,24,256]{2,1,0:T(8,128)S(1)}, f32[4,24,256]{2,1,0:T(8,128)S(1)}, u32[]{:S(2)}, u32[]{:S(2)}) collective-permute-start(f32[4,24,256]{2,1,0:T(8,128)S(1)} %get-tuple-element.24), channel_id=1, source_target_pairs={{0,8},{1,9},{2,10},{3,11},{4,12},{5,13},{6,14},{7,15},{8,0},{9,1},... | collective-permute-start | bytes 294920 | tf_op jit(solution)/shard_map/ppermute | solution.py:418
  40.0 7.8 %collective-permute-start.6 = (f32[16,128]{1,0:T(8,128)S(1)}, f32[16,128]{1,0:T(8,128)S(1)}, u32[]{:S(2)}, u32[]{:S(2)}) collective-permute-start(f32[16,128]{1,0:T(8,128)S(1)} %add.37), channel_id=1, source_target_pairs={{0,24},{1,25},{2,26},{3,27},{4,28},{5,29},{6,30},{7,31},{8,16},{9,... | collective-permute-start | bytes 24584 | tf_op jit(solution)/shard_map/ppermute | solution.py:418
  41.5 7.0 %collective-permute-start.5 = (f32[16,128]{1,0:T(8,128)S(1)}, f32[16,128]{1,0:T(8,128)S(1)}, u32[]{:S(2)}, u32[]{:S(2)}) collective-permute-start(f32[16,128]{1,0:T(8,128)S(1)} %add.37), channel_id=1, source_target_pairs={{0,16},{1,17},{2,18},{3,19},{4,20},{5,21},{6,22},{7,23},{8,24},{9,... | collective-permute-start | bytes 24584 | tf_op jit(solution)/shard_map/ppermute | solution.py:418
  43.6 4.9 %collective-permute-start.4 = (f32[16,128]{1,0:T(8,128)S(1)}, f32[16,128]{1,0:T(8,128)S(1)}, u32[]{:S(2)}, u32[]{:S(2)}) collective-permute-start(f32[16,128]{1,0:T(8,128)S(1)} %add.37), channel_id=1, source_target_pairs={{0,8},{1,9},{2,10},{3,11},{4,12},{5,13},{6,14},{7,15},{8,0},{9,1},... | collective-permute-start | bytes 24584 | tf_op jit(solution)/shard_map/ppermute | solution.py:418
  43.7 14.1 %collective-permute-start.16 = (f32[1,24,256]{2,1,0:T(8,128)S(1)}, f32[1,24,256]{2,1,0:T(8,128)S(1)}, u32[]{:S(2)}, u32[]{:S(2)}) collective-permute-start(f32[1,24,256]{2,1,0:T(8,128)S(1)} %get-tuple-element.25), channel_id=1, source_target_pairs={{0,3},{1,2},{2,1},{3,0},{4,7},{5,6},{6,5},{7,4},{8,11},{9,10},{10,... | collective-permute-start | bytes 73736 | tf_op jit(solution)/shard_map/ppermute | solution.py:418
  47.9 9.9 %collective-permute-start.15 = (f32[1,24,256]{2,1,0:T(8,128)S(1)}, f32[1,24,256]{2,1,0:T(8,128)S(1)}, u32[]{:S(2)}, u32[]{:S(2)}) collective-permute-start(f32[1,24,256]{2,1,0:T(8,128)S(1)} %get-tuple-element.26), channel_id=1, source_target_pairs={{0,2},{1,3},{2,0},{3,1},{4,6},{5,7},{6,4},{7,5},{8,10},{9,11},{10,... | collective-permute-start | bytes 73736 | tf_op jit(solution)/shard_map/ppermute | solution.py:418
  47.9 9.9 %collective-permute-start.14 = (f32[1,24,256]{2,1,0:T(8,128)S(1)}, f32[1,24,256]{2,1,0:T(8,128)S(1)}, u32[]{:S(2)}, u32[]{:S(2)}) collective-permute-start(f32[1,24,256]{2,1,0:T(8,128)S(1)} %get-tuple-element.27), channel_id=1, source_target_pairs={{0,1},{1,0},{2,3},{3,2},{4,5},{5,4},{6,7},{7,6},{8,9},{9,8},{10,11... | collective-permute-start | bytes 73736 | tf_op jit(solution)/shard_map/ppermute | solution.py:418
  48.5 5.6 %collective-permute-start.9 = (f32[16,128]{1,0:T(8,128)S(1)}, f32[16,128]{1,0:T(8,128)S(1)}, u32[]{:S(2)}, u32[]{:S(2)}) collective-permute-start(f32[16,128]{1,0:T(8,128)S(1)} %add_add_fusion.refs_0_), channel_id=1, source_target_pairs={{0,3},{1,2},{2,1},{3,0},{4,7},{5,6},{6,5},{7,4},{8,11},{9,10},{10,... | collective-permute-start | bytes 24584 | tf_op jit(solution)/shard_map/ppermute | solution.py:418
  52.3 4.5 %collective-permute-start.8 = (f32[16,128]{1,0:T(8,128)S(1)}, f32[16,128]{1,0:T(8,128)S(1)}, u32[]{:S(2)}, u32[]{:S(2)}) collective-permute-start(f32[16,128]{1,0:T(8,128)S(1)} %add_add_fusion.refs_0_), channel_id=1, source_target_pairs={{0,2},{1,3},{2,0},{3,1},{4,6},{5,7},{6,4},{7,5},{8,10},{9,11},{10,... | collective-permute-start | bytes 24584 | tf_op jit(solution)/shard_map/ppermute | solution.py:418
  54.1 3.7 %collective-permute-start.7 = (f32[16,128]{1,0:T(8,128)S(1)}, f32[16,128]{1,0:T(8,128)S(1)}, u32[]{:S(2)}, u32[]{:S(2)}) collective-permute-start(f32[16,128]{1,0:T(8,128)S(1)} %add_add_fusion.refs_0_), channel_id=1, source_target_pairs={{0,1},{1,0},{2,3},{3,2},{4,5},{5,4},{6,7},{7,6},{8,9},{9,8},{10,11... | collective-permute-start | bytes 24584 | tf_op jit(solution)/shard_map/ppermute | solution.py:418

commit v2 on v1

v2 whole, which is shorter than its diff:
```python
import functools

import jax
import jax.numpy as jnp
from jax import lax
from jax.experimental import pallas as pl
from jax.experimental.pallas import tpu as pltpu
from jax.sharding import PartitionSpec as P

BINS = 256
LEAVES = 1024
LANES = 128
GRADES = 4
LOW = 32
HIGH = BINS // LOW
GROUP = 8
CHUNK = 64
MAX_LEN = 1024

lasso_penalty = 1.0
ridge_penalty = 1.0
shrinkage = 0.1

VMEM_LIMIT = 48 * 1024 * 1024
F32 = jnp.float32
BF16 = jnp.bfloat16
NT = (((1,), (1,)), ((), ()))


def iota(shape, axis):
    return lax.broadcasted_iota(jnp.int32, shape, axis)


def vmem():
    return pl.BlockSpec(memory_space=pltpu.VMEM)


def smem():
    return pl.BlockSpec(memory_space=pltpu.SMEM)


def prepare_kernel(feat_count, masks, len_ref, pos_ref, owner_hbm, bins_hbm, lab_hbm, leaf_hbm,
                   bins_t_ref, qid_ref, worth_ref, inv_ref, leaf_ref, bounds_ref, bins_ref, lab_ref, owner_ref, sems):
    queries = len_ref.shape[1]
    rows = lab_ref.shape[0]
    own = inv_ref.shape[0]
    features = bins_ref.shape[1]
    place = pos_ref[0]
    copies = [pltpu.make_async_copy(source, target, sems.at[k]) for k, (source, target) in enumerate(
        ((lab_hbm, lab_ref), (owner_hbm, owner_ref), (bins_hbm, bins_ref), (leaf_hbm, leaf_ref)))]
    for copy in copies:
        copy.start()

    spot = iota((rows, LANES), 0) * LANES + iota((rows, LANES), 1)
    qid = jnp.zeros((rows, LANES), jnp.int32)
    begin = jnp.zeros((queries, LANES), jnp.int32)
    finish = jnp.zeros((queries, LANES), jnp.int32)
    which = iota((queries, LANES), 0)
    start = jnp.int32(0)
    for q in range(queries):
        end = start + len_ref[0, q]
        qid = qid + jnp.where(spot >= end, 1, 0)
        begin = jnp.where(which == q, start, begin)
        finish = jnp.where(which == q, end, finish)

        def set_low(r, carry, start=start):
            bounds_ref[0, r] = start
            return carry

        def set_high(r, carry, end=end):
            bounds_ref[1, r] = end
            return carry

        lax.fori_loop((start + LANES - 1) // LANES, (end + LANES - 1) // LANES, set_low, 0)
        lax.fori_loop(start // LANES, end // LANES, set_high, 0)
        start = end
    qid_ref[...] = qid

    copies[0].wait()
    worth_ref[...] = jnp.left_shift(1, lab_ref[...]).astype(F32)
    counts = [jnp.zeros((queries, LANES), F32) for _ in range(GRADES)]
    lane = iota((queries, LANES), 1)
    for r in range(rows):
        at = lane + r * LANES
        inside = (at >= begin) & (at < finish)
        grade = jnp.where(inside, jnp.broadcast_to(lab_ref[r:r + 1, :], (queries, LANES)), 0)
        for g in range(GRADES):
            counts[g] = counts[g] + jnp.where(grade > g, 1.0, 0.0)
    position = iota((queries, MAX_LEN), 1).astype(F32)
    gain = jnp.zeros((queries, MAX_LEN), F32)
    for g in range(GRADES):
        held = jnp.sum(counts[g], axis=1, keepdims=True)
        gain = gain + jnp.where(position < held, float(2 ** g), 0.0)
    level = 1.0 / jnp.log2(2.0 + position[0:1, :])
    ideal = jnp.sum(gain * level, axis=1, keepdims=True)
    usable = ideal > 0.5
    inverse = jnp.where(usable, 1.0 / jnp.where(usable, ideal, 1.0), 0.0)
    first = place % feat_count * own
    for t in range(own):
        at = lane + (first + t) * LANES
        inside = (at >= begin) & (at < finish)
        inv_ref[t:t + 1, :] = jnp.sum(jnp.where(inside, inverse, 0.0), axis=0, keepdims=True)

    copies[1].wait()
    per_dev = features >> len(masks)
    owner = jnp.concatenate([owner_ref[k:k + 1, :] for k in range(features // LANES)], axis=1)
    square = (features, features)
    down, across = iota(square, 0), iota(square, 1)
    index = down // per_dev
    target = jnp.zeros(square, jnp.int32)
    for b, mask in enumerate(masks):
        target = target + ((index >> b) & 1) * mask
    target = (target ^ place) * per_dev + down % per_dev
    pick = jnp.where(target == across, 1.0, 0.0).astype(BF16)
    holds = jnp.where(jnp.broadcast_to(owner, square) == down, 1.0, 0.0).astype(BF16)
    perm = lax.dot_general(pick, holds, NT, preferred_element_type=F32).astype(BF16)
    copies[2].wait()
    bins = bins_ref[...].astype(F32).astype(BF16)
    bins_t_ref[...] = lax.dot_general(perm, bins, NT, preferred_element_type=F32)
    copies[3].wait()


def prepare(feat_count, masks, lengths, pos, owner, bins, labels, leaves):
    rows = labels.shape[0]
    own = leaves.shape[0]
    docs, features = bins.shape
    hbm = pl.BlockSpec(memory_space=pltpu.HBM)
    return pl.pallas_call(
        functools.partial(prepare_kernel, feat_count, masks),
        out_shape=(
            jax.ShapeDtypeStruct((features, docs), F32),
            jax.ShapeDtypeStruct((rows, LANES), jnp.int32),
            jax.ShapeDtypeStruct((rows, LANES), F32),
            jax.ShapeDtypeStruct((own, LANES), F32),
            jax.ShapeDtypeStruct((own, LANES), jnp.int32),
            jax.ShapeDtypeStruct((2, rows), jnp.int32),
        ),
        in_specs=[smem(), smem(), hbm, hbm, hbm, hbm],
        out_specs=(vmem(), vmem(), vmem(), vmem(), vmem(), smem()),
        scratch_shapes=[pltpu.VMEM((docs, features), jnp.int32), pltpu.VMEM((rows, LANES), jnp.int32),
                        pltpu.VMEM((features // LANES, LANES), jnp.int32), pltpu.SemaphoreType.DMA((4,))],
        compiler_params=pltpu.CompilerParams(vmem_limit_bytes=VMEM_LIMIT),
        cost_estimate=pl.CostEstimate(flops=200_000_000, bytes_accessed=3_000_000, transcendentals=20_000),
        name="prepare",
    )(lengths, pos, owner, bins, labels, leaves)


def split_terms(value, terms):
    parts = []
    rest = value
    for _ in range(terms):
        part = rest.astype(BF16)
        parts.append(part)
        rest = rest - part.astype(F32)
    return parts


def widen(ref, source):
    turned = jnp.transpose(source)
    for r in range(source.shape[0]):
        ref[r * LANES:(r + 1) * LANES, :] = jnp.broadcast_to(turned[:, r:r + 1], (LANES, LANES))


def pairs_kernel(parts, bounds_ref, pos_ref, *refs):
    score_refs = refs[:parts]
    (worth_ref, qid_ref, inv_ref, leaf_ref, lam_ref, tile_ref, sums_ref,
     s_row, a_row, d_row, s_turn, q_turn, s_col, q_col, a_own, w_own, d_own, push_own, bend_own) = refs[parts:]
    rows = worth_ref.shape[0]
    own = inv_ref.shape[0]
    docs = own * LANES
    me = pos_ref[0] % parts
    for k in range(parts):
        s_row[pl.ds(pl.multiple_of((me ^ k) * own, own), own), :] = score_refs[k][...]
    a_row[...] = jnp.exp(s_row[...])
    d_row[...] = jnp.zeros((rows, LANES), F32)
    first = pl.multiple_of(me * own, own)
    window_low = bounds_ref[0, first] // LANES
    window_high = (bounds_ref[1, first + own - 1] + LANES - 1) // LANES
    s_turn[...] = jnp.transpose(s_row[...])
    q_turn[...] = jnp.transpose(qid_ref[...])
    for r in range(rows):
        @pl.when((r >= window_low) & (r < window_high))
        def _(r=r):
            at = slice(r * LANES, (r + 1) * LANES)
            s_col[at, :] = jnp.broadcast_to(s_turn[:, r:r + 1], (LANES, LANES))
            q_col[at, :] = jnp.broadcast_to(q_turn[:, r:r + 1], (LANES, LANES))
    widen(a_own, a_row[pl.ds(first, own), :])
    widen(w_own, worth_ref[pl.ds(first, own), :])

    def row_of(ref, r):
        return jnp.broadcast_to(ref[pl.ds(r, 1), :], (8, LANES))

    def rank_group(r, carry):
        score = row_of(s_row, r)
        query = row_of(qid_ref, r)

        def sweep(ahead):
            def step(c, acc):
                base = pl.multiple_of(c * CHUNK, CHUNK)
                acc = list(acc)
                for u in range(CHUNK // 8):
                    other = s_col[pl.ds(base + 8 * u, 8), :]
                    above = (other >= score) if ahead else (other > score)
                    hit = above & (q_col[pl.ds(base + 8 * u, 8), :] == query)
                    acc[u % 4] = acc[u % 4] + jnp.where(hit, 1.0, 0.0)
                return tuple(acc)
            return step

        acc = tuple(jnp.zeros((8, LANES), F32) for _ in range(4))
        per = LANES // CHUNK
        low = jnp.maximum(bounds_ref[0, r] // CHUNK, window_low * per)
        high = jnp.minimum((bounds_ref[1, r] + CHUNK - 1) // CHUNK, window_high * per)
        acc = lax.fori_loop(low, r * per, sweep(True), acc)
        acc = list(lax.fori_loop((r + 1) * per, high, sweep(False), acc))
        base = pl.multiple_of(r * LANES, LANES)
        for u in range(LANES // 8):
            other = s_col[pl.ds(base + 8 * u, 8), :]
            earlier = iota((8, LANES), 0) + 8 * u < iota((8, LANES), 1)
            above = (other > score) | ((other == score) & earlier)
            hit = above & (q_col[pl.ds(base + 8 * u, 8), :] == query)
            acc[u % 4] = acc[u % 4] + jnp.where(hit, 1.0, 0.0)
        total = (acc[0] + acc[1]) + (acc[2] + acc[3])
        d_row[pl.ds(r, 1), :] = jnp.sum(total, axis=0, keepdims=True)
        return carry

    lax.fori_loop(window_low, window_high, rank_group, 0)
    d_row[...] = 1.0 / jnp.log2(2.0 + d_row[...])
    widen(d_own, d_row[pl.ds(first, own), :])

    def pair_block(b, carry):
        base = pl.multiple_of(b * CHUNK, CHUNK)
        r = first + b // (LANES // CHUNK)
        count = CHUNK // 8
        queries = pl.multiple_of(first * LANES + base, CHUNK)

        def step(c, acc):
            acc = list(acc)
            a_j = row_of(a_row, c)
            w_j = row_of(worth_ref, c)
            d_j = row_of(d_row, c)
            query = row_of(qid_ref, c)
            for u in range(count):
                at = pl.ds(base + 8 * u, 8)
                a_i = a_own[at, :]
                total = a_i + a_j
                rough = pl.reciprocal(total, approx=True)
                recip = rough * (2.0 - total * rough)
                gap = jnp.abs(d_own[at, :] - d_j)
                lift = w_own[at, :] - w_j
                weight = jnp.where(q_col[pl.ds(queries + 8 * u, 8), :] == query, gap * recip, 0.0) * lift
                acc[u] = acc[u] + weight * jnp.where(lift > 0.0, a_j, a_i)
                acc[count + u] = acc[count + u] + jnp.abs(weight) * (recip * a_j)
            return tuple(acc)

        acc = tuple(jnp.zeros((8, LANES), F32) for _ in range(2 * count))
        acc = lax.fori_loop(bounds_ref[0, r] // LANES, (bounds_ref[1, r] + LANES - 1) // LANES, step, acc)
        for u in range(count):
            push_own[pl.ds(base + 8 * u, 8), :] = acc[u]
            bend_own[pl.ds(base + 8 * u, 8), :] = acc[count + u]
        return carry

    lax.fori_loop(0, docs // CHUNK, pair_block, 0)
    for t in range(own):
        at = slice(t * LANES, (t + 1) * LANES)
        inverse = inv_ref[t:t + 1, :]
        lam_ref[0:1, at] = -inverse * jnp.sum(jnp.transpose(push_own[at, :]), axis=0, keepdims=True)
        lam_ref[1:2, at] = (inverse * a_row[pl.ds(first + t, 1), :]
                            * jnp.sum(jnp.transpose(bend_own[at, :]), axis=0, keepdims=True))

    leaf = jnp.concatenate([leaf_ref[t:t + 1, :] for t in range(own)], axis=1)
    highs = LEAVES // LANES
    top = jnp.broadcast_to(leaf // LANES, (highs, docs)) == iota((highs, docs), 0)
    spots = jnp.where(jnp.broadcast_to(leaf % LANES, (LANES, docs)) == iota((LANES, docs), 0), 1.0, 0.0).astype(BF16)
    pieces, tiles = [], []
    for c in range(2):
        for k, part in enumerate(split_terms(lam_ref[c:c + 1, :], 3)):
            wide = jnp.broadcast_to(part.astype(F32), (highs, docs))
            pieces.append(jnp.where(top, wide, 0.0))
            if k < 2:
                tiles.append(wide)
    tile_ref[...] = jnp.concatenate(tiles, axis=0).astype(BF16)
    stacked = jnp.concatenate(pieces, axis=0).astype(BF16)
    sums = lax.dot_general(stacked, spots, NT, preferred_element_type=F32)
    for c in range(2):
        base = c * 3 * highs
        sums_ref[:, c * LANES:(c + 1) * LANES] = (
            sums[base:base + highs] + (sums[base + highs:base + 2 * highs] + sums[base + 2 * highs:base + 3 * highs])
        )


def pair_terms(bounds, pos, scores, worth, qid, inverse, leaves):
    rows = worth.shape[0]
    own = inverse.shape[0]
    docs = own * LANES
    highs = LEAVES // LANES
    row = pltpu.VMEM((rows, LANES), F32)
    mine = pltpu.VMEM((docs, LANES), F32)
    return pl.pallas_call(
        functools.partial(pairs_kernel, len(scores)),
        out_shape=(
            jax.ShapeDtypeStruct((2, docs), F32),
            jax.ShapeDtypeStruct((4 * HIGH, docs), BF16),
            jax.ShapeDtypeStruct((highs, 2 * LANES), F32),
        ),
        in_specs=[smem(), smem()] + [vmem()] * (len(scores) + 4),
        out_specs=(vmem(), vmem(), vmem()),
        scratch_shapes=[row, row, row, pltpu.VMEM((LANES, rows), F32), pltpu.VMEM((LANES, rows), jnp.int32),
                        pltpu.VMEM((rows * LANES, LANES), F32), pltpu.VMEM((rows * LANES, LANES), jnp.int32),
                        mine, mine, mine, mine, mine],
        compiler_params=pltpu.CompilerParams(vmem_limit_bytes=VMEM_LIMIT),
        cost_estimate=pl.CostEstimate(flops=40_000_000, bytes_accessed=200_000, transcendentals=2_000_000),
        name="pair_terms",
    )(bounds, pos, *scores, worth, qid, inverse, leaves)


def histogram_kernel(first, groups, tile_ref, bins_ref, *refs):
    out_ref = refs[-1]
    docs = tile_ref.shape[1]
    depth = 256
    rows = 16
    row = iota((rows, depth), 0)
    low_level = [(row + rows * k).astype(F32).astype(BF16) for k in range(LOW // rows)]
    high_level = (row % HIGH).astype(F32).astype(BF16)
    upper = row < HIGH
    zero = jnp.zeros((rows, depth), BF16)
    one = jnp.ones((rows, depth), BF16)
    lane_owner = iota((1, GROUP * LOW), 1) // LOW

    def one_group(g, carry):
        base = pl.multiple_of((first + g) * GROUP, GROUP)
        acc = None
        for k in range(docs // depth):
            span = slice(k * depth, (k + 1) * depth)
            code = bins_ref[pl.ds(base, GROUP), span]
            high = jnp.floor(code * (1.0 / LOW))
            low = code - high * LOW
            left, right, count = [], [], []
            wide = []
            for f in range(GROUP):
                high_f = jnp.broadcast_to(high[f:f + 1, :], (rows, depth))
                low_f = jnp.broadcast_to(low[f:f + 1, :], (rows, depth)).astype(BF16)
                wide.append(high_f)
                match = high_f.astype(BF16) == high_level
                for c in range(2):
                    left.append(jnp.where(match, tile_ref[c * rows:(c + 1) * rows, span], zero))
                for level in low_level:
                    right.append(jnp.where(low_f == level, one, zero))
            for f in range(0, GROUP, 2):
                both = jnp.where(upper, wide[f], wide[f + 1]).astype(BF16)
                count.append(jnp.where(both == high_level, one, zero))
            part = lax.dot_general(
                jnp.concatenate(left + count, axis=0), jnp.concatenate(right, axis=0), NT,
                preferred_element_type=F32,
            )
            acc = part if acc is None else acc + part
        stats = jnp.zeros((2 * rows, GROUP * LOW), F32)
        counts = jnp.zeros((HIGH, GROUP * LOW), F32)
        for f in range(GROUP):
            mine = lane_owner == f
            stats = jnp.where(mine, acc[f * 2 * rows:(f + 1) * 2 * rows], stats)
            at = GROUP * 2 * rows + f * HIGH
            counts = jnp.where(mine, acc[at:at + HIGH], counts)
        out_ref[pl.ds(pl.multiple_of(g * 3 * HIGH, 3 * HIGH), 3 * HIGH), :] = jnp.concatenate(
            [stats[0:HIGH] + stats[HIGH:2 * HIGH], stats[2 * HIGH:3 * HIGH] + stats[3 * HIGH:4 * HIGH], counts], axis=0)
        return carry

    if len(refs) > 1:
        out_ref[groups * 3 * HIGH:, :] = refs[0][...]
    lax.fori_loop(0, groups, one_group, 0, unroll=2)


def histogram_part(first, groups, tiles, bins_t, *tail):
    rows = groups * 3 * HIGH + sum(piece.shape[0] for piece in tail)
    return pl.pallas_call(
        functools.partial(histogram_kernel, first, groups),
        out_shape=jax.ShapeDtypeStruct((rows, GROUP * LOW), F32),
        in_specs=[vmem()] * (2 + len(tail)),
        out_specs=vmem(),
        compiler_params=pltpu.CompilerParams(vmem_limit_bytes=VMEM_LIMIT),
        cost_estimate=pl.CostEstimate(flops=groups * 330_000_000, bytes_accessed=groups * 60_000, transcendentals=0),
        name="histogram_part",
    )(tiles, bins_t, *tail)


def finish_kernel(per_dev, leaf_ref, kept_ref, sums_ref, *refs):
    arrived = refs[:-3]
    value_ref, step_ref, hist_ref = refs[-3:]
    unit = kept_ref.shape[0]
    totals = add_up([sums_ref[...]] + [ref[unit:, :] for ref in arrived])
    highs = LEAVES // LANES
    grad, curv = totals[:, :LANES], totals[:, LANES:]
    shrunk = jnp.maximum(jnp.abs(grad) - lasso_penalty, 0.0)
    values = jnp.where(grad > 0.0, -shrunk, shrunk) / (curv + ridge_penalty)
    value_ref[...] = values
    leaf = leaf_ref[...]
    top, spot = leaf // LANES, leaf % LANES
    step = jnp.zeros(leaf.shape, F32)
    for h in range(highs):
        row = jnp.broadcast_to(values[h:h + 1, :], leaf.shape)
        step = jnp.where(top == h, jnp.take_along_axis(row, spot, axis=1), step)
    step_ref[...] = shrinkage * step
    hist = add_up([kept_ref[...]] + [ref[:unit, :] for ref in arrived])
    if per_dev == GROUP:
        for c in range(3):
            for f in range(GROUP):
                line = [hist[c * HIGH + h:c * HIGH + h + 1, f * LOW:(f + 1) * LOW] for h in range(HIGH)]
                hist_ref[c:c + 1, f * BINS:(f + 1) * BINS] = jnp.concatenate(line, axis=1)
    else:
        hist_ref[...] = hist


def finish(per_dev, leaves, kept, sums, arrived):
    out = (3, per_dev * BINS) if per_dev == GROUP else kept.shape
    return pl.pallas_call(
        functools.partial(finish_kernel, per_dev),
        out_shape=(
            jax.ShapeDtypeStruct((LEAVES // LANES, LANES), F32),
            jax.ShapeDtypeStruct(leaves.shape, F32),
            jax.ShapeDtypeStruct(out, F32),
        ),
        in_specs=[vmem()] * (3 + len(arrived)),
        out_specs=(vmem(), vmem(), vmem()),
        compiler_params=pltpu.CompilerParams(vmem_limit_bytes=VMEM_LIMIT),
        name="finish",
    )(leaves, kept, sums, *arrived)


def add_up(parts):
    while len(parts) > 1:
        parts = [parts[k] + parts[k + 1] for k in range(0, len(parts), 2)]
    return parts[0]


def exchange_rounds(query_count, feat_count):
    feat_bits = [1 << b for b in range(feat_count.bit_length() - 1)]
    query_bits = [feat_count << b for b in range(query_count.bit_length() - 1)]
    rounds = [query_bits[:1]]
    for bits in (query_bits[1:], feat_bits):
        rounds += [bits[k:k + 2] for k in range(0, len(bits), 2)]
    return rounds


def local(scores, labels, leaves, bins, lengths, owner):
    query_count = lax.axis_size("query")
    feat_count = lax.axis_size("feat")
    count = query_count * feat_count
    place = lax.axis_index("query").astype(jnp.int32) * feat_count + lax.axis_index("feat").astype(jnp.int32)
    docs = scores.shape[0]
    own = docs // LANES
    features = owner.shape[0]
    per_dev = features // count
    unit = 3 * per_dev
    axes = ("query", "feat")
    rounds = exchange_rounds(query_count, feat_count)
    bit_masks = [bit for bits in reversed(rounds) for bit in bits]
    fans = [[0, bits[0]] if len(bits) == 1 else [0, bits[0], bits[1], bits[0] | bits[1]] for bits in rounds]

    def swap(value, mask):
        return lax.ppermute(value, axes, [(p, p ^ mask) for p in range(count)])

    own_scores = scores.reshape(own, LANES)
    score_parts = [own_scores] + [
        lax.ppermute(own_scores, "feat", [(p, p ^ k) for p in range(feat_count)]) for k in range(1, feat_count)]

    pos = place.reshape(1)
    bins_t, qid, worth, inverse, leaf_rows, bounds = prepare(
        feat_count, bit_masks, lengths, pos, owner.reshape(-1, LANES), bins, labels.reshape(-1, LANES),
        leaves.reshape(own, LANES))
    lambdas, tiles, sums = pair_terms(bounds, pos, score_parts, worth, qid, inverse, leaf_rows)

    def part(low, high, *tail):
        if per_dev == GROUP:
            return histogram_part(low, high - low, tiles, bins_t, *tail)
        groups = high - low
        wide = histogram_part(low, groups, tiles, bins_t)
        wide = wide.reshape(groups, 3, HIGH, GROUP // per_dev, per_dev, LOW).transpose(0, 3, 1, 4, 2, 5)
        return jnp.concatenate([wide.reshape(groups * GROUP // per_dev * unit, BINS), *tail], axis=0)

    fan = fans[1]
    half = features // GROUP // 2
    quarter = half // len(fan)
    edge = count // 2 // len(fan) * unit
    far_rest = swap(part(half + quarter, 2 * half, sums), fans[0][1])
    near_rest = part(quarter, half)
    far_first = swap(part(half, half + quarter), fans[0][1])
    near_first = part(0, quarter)

    sums = sums + far_rest[edge * (len(fan) - 1):]
    sent = [near_rest[k * edge:(k + 1) * edge] + far_rest[k * edge:(k + 1) * edge] for k in range(len(fan) - 1)]
    kept = near_first + far_first
    for k in range(1, len(rounds)):
        arrived = [swap(jnp.concatenate([block, sums], axis=0), mask) for block, mask in zip(sent, fans[k][1:])]
        if k + 1 < len(rounds):
            sums = add_up([sums] + [block[edge:] for block in arrived])
            merged = add_up([kept] + [block[:edge] for block in arrived])
            edge = edge // len(fans[k + 1])
            kept = merged[:edge]
            sent = [merged[m * edge:(m + 1) * edge] for m in range(1, len(fans[k + 1]))]

    values, step, histograms = finish(per_dev, leaf_rows, kept, sums, arrived)
    return lambdas, values.reshape(LEAVES), step.reshape(docs), histograms.reshape(3, per_dev * BINS)


def solution(mesh):
    in_specs = (
        P(("query", "feat")),
        P("query"),
        P(("query", "feat")),
        P(("query", "feat"), None),
        P("query", None),
        P(),
    )
    out_specs = (P(None, ("query", "feat")), P(), P(("query", "feat")), P(None, ("query", "feat")))
    return jax.shard_map(local, mesh=mesh, in_specs=in_specs, out_specs=out_specs, check_vma=False)
```

time: 58.9 us -> 49 us (0.83)
  starting transfers between devices: 23.6 us -> 16.1 us
  local copies, waits for them, and re-layouts: 4.72 us -> 2.61 us
  waiting for transfers between devices: 5.49 us -> 7.17 us
  Pallas kernels: 23.2 us -> 22.4 us
  other arithmetic: 0.9 us -> 0.13 us
    ppermute x14 -> x8, starting transfers between devices: 17.8 us -> 10.3 us  [swap(): return lax.ppermute(value, axes, [(p, p ^ mask) for p in range(count)])]
    pallas_call x3 -> x4, Pallas kernels: 12.5 us -> 8.84 us  [histogram_part(): pl.pallas_call(functools.partial(histogram_kernel, first, groups), out_sh...]
    pallas_call x1, Pallas kernels: 7.73 us -> 9.76 us  [pair_terms(): pl.pallas_call(functools.partial(pairs_kernel, len(scores)), out_shape=(j...]
    unnamed x16 -> x12, local copies, waits for them, and re-layouts: 4.48 us -> 2.6 us
    ppermute x14 -> x8, waiting for transfers between devices: 5.48 us -> 7.16 us  [swap(): return lax.ppermute(value, axes, [(p, p ^ mask) for p in range(count)])]
    pallas_call x2, Pallas kernels: 2.99 us -> 3.76 us  [the longest x1 2.91 us: prepare(): pl.pallas_call(functools.partial(prepare_kernel, feat_count, masks), out_...]
    reduce_sum x1 -> x0, other arithmetic: 0.64 us -> none  [local(): turned = jnp.sum(jnp.where(pick, held[None], 0), axis=1).reshape(features)]
  transfers between devices with their start and end apart: 17 -> 11, of which waited for: 3 -> 5; matrix products, arithmetic and copies ran while one was open for 2% -> 0% of each run, Pallas kernels for 14% -> 22%
where the time goes in v2:
time: 49 us; the launch traced here: 49.1 us
  Pallas kernels  22.4 us (46%)
  starting transfers between devices  16.1 us (33%)
  waiting for transfers between devices  7.17 us (15%)
  local copies, waits for them, and re-layouts  2.61 us (5%)
  between operations  0.79 us (2%)
    ppermute x8, starting transfers between devices, swap(): return lax.ppermute(value, axes, [(p, p ^ mask) for p in range(count)])  10.3 us
    pallas_call x1, Pallas kernels, pair_terms(): pl.pallas_call(functools.partial(pairs_kernel, len(scores)), out_shape=(j...  9.76 us
    pallas_call x4, Pallas kernels, histogram_part(): pl.pallas_call(functools.partial(histogram_kernel, first, groups), out_sh...  8.84 us
    ppermute x8, waiting for transfers between devices, swap(): return lax.ppermute(value, axes, [(p, p ^ mask) for p in range(count)])  7.16 us
    ppermute x3, starting transfers between devices, local(): lax.ppermute(own_scores, 'feat', [(p, p ^ k) for p in range(feat_count)])  5.76 us
    pallas_call x1, Pallas kernels, prepare(): pl.pallas_call(functools.partial(prepare_kernel, feat_count, masks), out_...  2.91 us
    unnamed x12, local copies, waits for them, and re-layouts  2.6 us
  transfers between devices with their start and end apart: 11, of which 5 were waited for; matrix products, arithmetic and copies ran while one was open for 0% of the time, Pallas kernels for 22%

profile of v2, /device:TPU:0, one launch (start us, length us, event | category | flops | bytes accessed | tf_op | source)
XLA Modules:
  0.0 49.1 jit_solution(16505607853381272247)
XLA Ops:
  0.6 5.1 %collective-permute-start.2 = (f32[8,128]{1,0:T(8,128)}, f32[8,128]{1,0:T(8,128)S(1)}, u32[]{:S(2)}, u32[]{:S(2)}) collective-permute-start(f32[8,128]{1,0:T(8,128)} %bitcast.10), channel_id=1, source_target_pairs={{0,3},{1,2},{2,1},{3,0},{4,7},{5,6},{6,5},{7,4},{8,11},{9,10},{10,... | collective-permute-start | bytes 12296 | tf_op jit(solution)/shard_map/ppermute | solution.py:463
  5.8 0.0 collective-permute-start.1
  5.8 0.6 %collective-permute-start = (f32[8,128]{1,0:T(8,128)}, f32[8,128]{1,0:T(8,128)S(1)}, u32[]{:S(2)}, u32[]{:S(2)}) collective-permute-start(f32[8,128]{1,0:T(8,128)} %bitcast.12), channel_id=1, source_target_pairs={{0,1},{1,0},{2,3},{3,2},{4,5},{5,4},{6,7},{7,6},{8,9},{9,8},{10,11... | collective-permute-start | bytes 12296 | tf_op jit(solution)/shard_map/ppermute | solution.py:463
  6.4 0.7 %copy-done.2 = s32[1024]{0:T(1024)S(1)} copy-done((s32[1024]{0:T(1024)S(1)}, s32[1024]{0:T(1024)}, u32[]{:S(2)}) %copy-start.2) | copy-done | bytes 4120
  7.1 0.0 copy-done.3
  7.1 1.2 %copy-done = s32[1024,256]{1,0:T(8,128)S(1)} copy-done((s32[1024,256]{1,0:T(8,128)S(1)}, s32[1024,256]{1,0:T(8,128)}, u32[]{:S(2)}) %copy-start) | copy-done | bytes 1048600
  8.3 2.9 %prepare.1 = (f32[256,1024]{1,0:T(8,128)S(1)}, s32[32,128]{1,0:T(8,128)S(1)}, f32[32,128]{1,0:T(8,128)S(1)}, f32[8,128]{1,0:T(8,128)S(1)}, s32[8,128]{1,0:T(8,128)S(1)}, /*index=5*/s32[2,32]{1,0:T(2,128)S(1)}) custom-call(s32[1,16]{1,0:T(1,128)S(1)} %copy-done.4, s32[1]{0:T(128)} %bitcast.pos_ref, s32[2,128]{1,0:T(2,128)S(1)} %bitcast.9, ...), custom_call_target="tpu_custom_call" | custom-call | flops 200000000 | bytes 3000000 | tf_op jit(solution)/shard_map/prepare/pallas_call | solution.py:128
  11.2 0.0 collective-permute-done.2.refs_3_
  11.2 0.0 collective-permute-done.1.refs_2_
  11.3 0.0 collective-permute-done.refs_1_
  11.3 0.0 copy-start.5
  11.3 0.7 %copy-done.5 = f32[1024]{0:T(1024)S(1)} copy-done((f32[1024]{0:T(1024)S(1)}, f32[1024]{0:T(1024)}, u32[]{:S(2)}) %copy-start.5) | copy-done | bytes 4120
  12.0 9.8 %pair_terms.1 = (f32[2,1024]{1,0:T(2,128)}, bf16[32,1024]{1,0:T(8,128)(2,1)S(1)}, f32[8,256]{1,0:T(8,128)S(1)}) custom-call(s32[2,32]{1,0:T(2,128)S(1)} %get-tuple-element.16.bounds_ref, s32[1]{0:T(128)} %bitcast.pos_ref, f32[8,128]{1,0:T(8,128)S(1)} %bitcast.13, f32[8,128]{1,0:T(8,128)S(1)} %collective-permute-done.refs_1_, ...), custom_call_target="tpu_custom_call" | custom-call | flops 40000000 | bytes 200000 | tf_op jit(solution)/shard_map/pair_terms/pallas_call | solution.py:298
  21.7 1.1 %histogram_part.5 = f32[96,256]{1,0:T(8,128)S(1)} custom-call(bf16[32,1024]{1,0:T(8,128)(2,1)S(1)} %get-tuple-element.22.tile_ref, f32[256,1024]{1,0:T(8,128)S(1)} %get-tuple-element.23.bins_ref), custom_call_target="tpu_custom_call" | custom-call | flops 1320000000 | bytes 240000 | tf_op jit(solution)/shard_map/histogram_part/pallas_call | solution.py:374
  22.8 0.1 collective-permute-start.3
  22.9 3.3 %histogram_part.7 = f32[296,256]{1,0:T(8,128)S(1)} custom-call(bf16[32,1024]{1,0:T(8,128)(2,1)S(1)} %get-tuple-element.22.tile_ref, f32[256,1024]{1,0:T(8,128)S(1)} %get-tuple-element.23.bins_ref, f32[8,256]{1,0:T(8,128)S(1)} %get-tuple-element.24.refs_0_), custom_call_target="tpu_custom_call" | custom-call | flops 3960000000 | bytes 720000 | tf_op jit(solution)/shard_map/histogram_part/pallas_call | solution.py:374
  26.2 0.6 %collective-permute-start.4 = (f32[296,256]{1,0:T(8,128)S(1)}, f32[296,256]{1,0:T(8,128)S(1)}, u32[]{:S(2)}, u32[]{:S(2)}) collective-permute-start(f32[296,256]{1,0:T(8,128)S(1)} %histogram_part.7), channel_id=1, source_target_pairs={{0,4},{1,5},{2,6},{3,7},{4,0},{5,1},{6,2},{7,3},{8,12},{9,13},{10,... | collective-permute-start | bytes 909320 | tf_op jit(solution)/shard_map/ppermute | solution.py:459
  26.8 3.3 %histogram_part.6 = f32[288,256]{1,0:T(8,128)S(1)} custom-call(bf16[32,1024]{1,0:T(8,128)(2,1)S(1)} %get-tuple-element.22.tile_ref, f32[256,1024]{1,0:T(8,128)S(1)} %get-tuple-element.23.bins_ref), custom_call_target="tpu_custom_call" | custom-call | flops 3960000000 | bytes 720000 | tf_op jit(solution)/shard_map/histogram_part/pallas_call | solution.py:374
  30.1 0.0 collective-permute-done.4
  30.2 0.4 collective-permute-start.5
  30.6 1.9 %collective-permute-start.6 = (f32[104,256]{1,0:T(8,128)S(1)}, f32[104,256]{1,0:T(8,128)S(1)}, u32[]{:S(2)}, u32[]{:S(2)}) collective-permute-start(f32[104,256]{1,0:T(8,128)S(1)} %get-tuple-element.39), channel_id=1, source_target_pairs={{0,16},{1,17},{2,18},{3,19},{4,20},{5,21},{6,22},{7,23},{8,24},{9,... | collective-permute-start | bytes 319496 | tf_op jit(solution)/shard_map/ppermute | solution.py:459
  32.5 1.3 %collective-permute-start.7 = (f32[104,256]{1,0:T(8,128)S(1)}, f32[104,256]{1,0:T(8,128)S(1)}, u32[]{:S(2)}, u32[]{:S(2)}) collective-permute-start(f32[104,256]{1,0:T(8,128)S(1)} %get-tuple-element.40), channel_id=1, source_target_pairs={{0,24},{1,25},{2,26},{3,27},{4,28},{5,29},{6,30},{7,31},{8,16},{9,... | collective-permute-start | bytes 319496 | tf_op jit(solution)/shard_map/ppermute | solution.py:459
  33.8 1.1 %histogram_part.4 = f32[96,256]{1,0:T(8,128)S(1)} custom-call(bf16[32,1024]{1,0:T(8,128)(2,1)S(1)} %get-tuple-element.22.tile_ref, f32[256,1024]{1,0:T(8,128)S(1)} %get-tuple-element.23.bins_ref), custom_call_target="tpu_custom_call" | custom-call | flops 1320000000 | bytes 240000 | tf_op jit(solution)/shard_map/histogram_part/pallas_call | solution.py:374
  34.9 1.2 %collective-permute-done.5 = f32[104,256]{1,0:T(8,128)S(1)} collective-permute-done((f32[104,256]{1,0:T(8,128)S(1)}, f32[104,256]{1,0:T(8,128)S(1)}, u32[]{:S(2)}, u32[]{:S(2)}) %collective-permute-start.5) | collective-permute-done | bytes 106528 | tf_op jit(solution)/shard_map/ppermute | solution.py:459
  36.1 0.8 %collective-permute-done.6 = f32[104,256]{1,0:T(8,128)S(1)} collective-permute-done((f32[104,256]{1,0:T(8,128)S(1)}, f32[104,256]{1,0:T(8,128)S(1)}, u32[]{:S(2)}, u32[]{:S(2)}) %collective-permute-start.6) | collective-permute-done | bytes 106528 | tf_op jit(solution)/shard_map/ppermute | solution.py:459
  36.9 1.2 %collective-permute-done.7 = f32[104,256]{1,0:T(8,128)S(1)} collective-permute-done((f32[104,256]{1,0:T(8,128)S(1)}, f32[104,256]{1,0:T(8,128)S(1)}, u32[]{:S(2)}, u32[]{:S(2)}) %collective-permute-start.7) | collective-permute-done | bytes 106528 | tf_op jit(solution)/shard_map/ppermute | solution.py:459
  38.2 3.7 %collective-permute-start.10 = (f32[32,256]{1,0:T(8,128)S(1)}, f32[32,256]{1,0:T(8,128)S(1)}, u32[]{:S(2)}, u32[]{:S(2)}) collective-permute-start(f32[32,256]{1,0:T(8,128)S(1)} %get-tuple-element.35), channel_id=1, source_target_pairs={{0,3},{1,2},{2,1},{3,0},{4,7},{5,6},{6,5},{7,4},{8,11},{9,10},{10,... | collective-permute-start | bytes 98312 | tf_op jit(solution)/shard_map/ppermute | solution.py:459
  41.9 2.5 %collective-permute-start.9 = (f32[32,256]{1,0:T(8,128)S(1)}, f32[32,256]{1,0:T(8,128)S(1)}, u32[]{:S(2)}, u32[]{:S(2)}) collective-permute-start(f32[32,256]{1,0:T(8,128)S(1)} %get-tuple-element.36), channel_id=1, source_target_pairs={{0,2},{1,3},{2,0},{3,1},{4,6},{5,7},{6,4},{7,5},{8,10},{9,11},{10,... | collective-permute-start | bytes 98312 | tf_op jit(solution)/shard_map/ppermute | solution.py:459
  44.4 0.0 collective-permute-done.10.refs_2_
  44.4 2.3 %collective-permute-done.9.refs_1_ = f32[32,256]{1,0:T(8,128)S(1)} collective-permute-done((f32[32,256]{1,0:T(8,128)S(1)}, f32[32,256]{1,0:T(8,128)S(1)}, u32[]{:S(2)}, u32[]{:S(2)}) %collective-permute-start.9) | collective-permute-done | bytes 32800 | tf_op jit(solution)/shard_map/ppermute | solution.py:459
  46.7 1.6 %collective-permute-done.8.refs_0_ = f32[32,256]{1,0:T(8,128)S(1)} collective-permute-done((f32[32,256]{1,0:T(8,128)S(1)}, f32[32,256]{1,0:T(8,128)S(1)}, u32[]{:S(2)}, u32[]{:S(2)}) %collective-permute-start.8) | collective-permute-done | bytes 32800 | tf_op jit(solution)/shard_map/ppermute | solution.py:459
  48.3 0.9 %finish.1 = (f32[8,128]{1,0:T(8,128)}, f32[8,128]{1,0:T(8,128)}, f32[3,2048]{1,0:T(4,128)}) custom-call(s32[8,128]{1,0:T(8,128)S(1)} %get-tuple-element.20.refs_7_.leaf_ref, f32[24,256]{1,0:T(8,128)S(1)} %get-tuple-element.34.kept_ref, f32[8,256]{1,0:T(8,128)S(1)} %fusion.1.sums_ref, f32[32,256]{1,0:T(8,128)S(1)} %collective-permute-done.8.refs_0_, ...), custom_call_target="tpu_custom_call" | custom-call | tf_op jit(solution)/shard_map/finish/pallas_call | solution.py:414
  (16 shorter events, 0.2 us)
Async XLA Ops:
  0.6 5.8 %copy-start.1 = (s32[4096]{0:T(1024)S(1)}, s32[4096]{0:T(1024)}, u32[]{:S(2)}) copy-start(s32[4096]{0:T(1024)} %param.7) | copy-start | bytes 49156
  0.6 10.6 %collective-permute-start.2 = (f32[8,128]{1,0:T(8,128)}, f32[8,128]{1,0:T(8,128)S(1)}, u32[]{:S(2)}, u32[]{:S(2)}) collective-permute-start(f32[8,128]{1,0:T(8,128)} %bitcast.10), channel_id=1, source_target_pairs={{0,3},{1,2},{2,1},{3,0},{4,7},{5,6},{6,5},{7,4},{8,11},{9,10},{10,... | collective-permute-start | bytes 12296 | tf_op jit(solution)/shard_map/ppermute | solution.py:463
  5.8 5.5 %collective-permute-start.1 = (f32[8,128]{1,0:T(8,128)}, f32[8,128]{1,0:T(8,128)S(1)}, u32[]{:S(2)}, u32[]{:S(2)}) collective-permute-start(f32[8,128]{1,0:T(8,128)} %bitcast.11), channel_id=1, source_target_pairs={{0,2},{1,3},{2,0},{3,1},{4,6},{5,7},{6,4},{7,5},{8,10},{9,11},{10,... | collective-permute-start | bytes 12296 | tf_op jit(solution)/shard_map/ppermute | solution.py:463
  5.8 5.5 %collective-permute-start = (f32[8,128]{1,0:T(8,128)}, f32[8,128]{1,0:T(8,128)S(1)}, u32[]{:S(2)}, u32[]{:S(2)}) collective-permute-start(f32[8,128]{1,0:T(8,128)} %bitcast.12), channel_id=1, source_target_pairs={{0,1},{1,0},{2,3},{3,2},{4,5},{5,4},{6,7},{7,6},{8,9},{9,8},{10,11... | collective-permute-start | bytes 12296 | tf_op jit(solution)/shard_map/ppermute | solution.py:463
  6.4 0.7 %copy-start.2 = (s32[1024]{0:T(1024)S(1)}, s32[1024]{0:T(1024)}, u32[]{:S(2)}) copy-start(s32[1024]{0:T(1024)} %param.8) | copy-start | bytes 12292
  6.4 0.7 %copy-start.3 = (s32[256]{0:T(256)S(1)}, s32[256]{0:T(256)}, u32[]{:S(2)}) copy-start(s32[256]{0:T(256)} %param.11) | copy-start | bytes 3076
  6.4 0.7 %copy-start.4 = (s32[1,16]{1,0:T(1,128)S(1)}, s32[1,16]{1,0:T(1,128)}, u32[]{:S(2)}) copy-start(s32[1,16]{1,0:T(1,128)} %len_ref.1) | copy-start | bytes 196
  7.1 1.2 %copy-start = (s32[1024,256]{1,0:T(8,128)S(1)}, s32[1024,256]{1,0:T(8,128)}, u32[]{:S(2)}) copy-start(s32[1024,256]{1,0:T(8,128)} %bins_hbm.1) | copy-start | bytes 3145732
  11.3 0.7 %copy-start.5 = (f32[1024]{0:T(1024)S(1)}, f32[1024]{0:T(1024)}, u32[]{:S(2)}) copy-start(f32[1024]{0:T(1024)} %param.6) | copy-start | bytes 12292
  22.8 12.1 %collective-permute-start.3 = (f32[96,256]{1,0:T(8,128)S(1)}, f32[96,256]{1,0:T(8,128)S(1)}, u32[]{:S(2)}, u32[]{:S(2)}) collective-permute-start(f32[96,256]{1,0:T(8,128)S(1)} %histogram_part.5), channel_id=1, source_target_pairs={{0,4},{1,5},{2,6},{3,7},{4,0},{5,1},{6,2},{7,3},{8,12},{9,13},{10,... | collective-permute-start | bytes 294920 | tf_op jit(solution)/shard_map/ppermute | solution.py:459
  26.2 3.9 %collective-permute-start.4 = (f32[296,256]{1,0:T(8,128)S(1)}, f32[296,256]{1,0:T(8,128)S(1)}, u32[]{:S(2)}, u32[]{:S(2)}) collective-permute-start(f32[296,256]{1,0:T(8,128)S(1)} %histogram_part.7), channel_id=1, source_target_pairs={{0,4},{1,5},{2,6},{3,7},{4,0},{5,1},{6,2},{7,3},{8,12},{9,13},{10,... | collective-permute-start | bytes 909320 | tf_op jit(solution)/shard_map/ppermute | solution.py:459
  30.2 5.9 %collective-permute-start.5 = (f32[104,256]{1,0:T(8,128)S(1)}, f32[104,256]{1,0:T(8,128)S(1)}, u32[]{:S(2)}, u32[]{:S(2)}) collective-permute-start(f32[104,256]{1,0:T(8,128)S(1)} %get-tuple-element.38), channel_id=1, source_target_pairs={{0,8},{1,9},{2,10},{3,11},{4,12},{5,13},{6,14},{7,15},{8,0},{9,1},... | collective-permute-start | bytes 319496 | tf_op jit(solution)/shard_map/ppermute | solution.py:459
  30.6 6.3 %collective-permute-start.6 = (f32[104,256]{1,0:T(8,128)S(1)}, f32[104,256]{1,0:T(8,128)S(1)}, u32[]{:S(2)}, u32[]{:S(2)}) collective-permute-start(f32[104,256]{1,0:T(8,128)S(1)} %get-tuple-element.39), channel_id=1, source_target_pairs={{0,16},{1,17},{2,18},{3,19},{4,20},{5,21},{6,22},{7,23},{8,24},{9,... | collective-permute-start | bytes 319496 | tf_op jit(solution)/shard_map/ppermute | solution.py:459
  32.5 5.7 %collective-permute-start.7 = (f32[104,256]{1,0:T(8,128)S(1)}, f32[104,256]{1,0:T(8,128)S(1)}, u32[]{:S(2)}, u32[]{:S(2)}) collective-permute-start(f32[104,256]{1,0:T(8,128)S(1)} %get-tuple-element.40), channel_id=1, source_target_pairs={{0,24},{1,25},{2,26},{3,27},{4,28},{5,29},{6,30},{7,31},{8,16},{9,... | collective-permute-start | bytes 319496 | tf_op jit(solution)/shard_map/ppermute | solution.py:459
  38.2 6.1 %collective-permute-start.10 = (f32[32,256]{1,0:T(8,128)S(1)}, f32[32,256]{1,0:T(8,128)S(1)}, u32[]{:S(2)}, u32[]{:S(2)}) collective-permute-start(f32[32,256]{1,0:T(8,128)S(1)} %get-tuple-element.35), channel_id=1, source_target_pairs={{0,3},{1,2},{2,1},{3,0},{4,7},{5,6},{6,5},{7,4},{8,11},{9,10},{10,... | collective-permute-start | bytes 98312 | tf_op jit(solution)/shard_map/ppermute | solution.py:459
  41.9 4.8 %collective-permute-start.9 = (f32[32,256]{1,0:T(8,128)S(1)}, f32[32,256]{1,0:T(8,128)S(1)}, u32[]{:S(2)}, u32[]{:S(2)}) collective-permute-start(f32[32,256]{1,0:T(8,128)S(1)} %get-tuple-element.36), channel_id=1, source_target_pairs={{0,2},{1,3},{2,0},{3,1},{4,6},{5,7},{6,4},{7,5},{8,10},{9,11},{10,... | collective-permute-start | bytes 98312 | tf_op jit(solution)/shard_map/ppermute | solution.py:459
  44.4 3.9 %collective-permute-start.8 = (f32[32,256]{1,0:T(8,128)S(1)}, f32[32,256]{1,0:T(8,128)S(1)}, u32[]{:S(2)}, u32[]{:S(2)}) collective-permute-start(f32[32,256]{1,0:T(8,128)S(1)} %get-tuple-element.37), channel_id=1, source_target_pairs={{0,1},{1,0},{2,3},{3,2},{4,5},{5,4},{6,7},{7,6},{8,9},{9,8},{10,11... | collective-permute-start | bytes 98312 | tf_op jit(solution)/shard_map/ppermute | solution.py:459

commit v3 on v2

--- a/solution.py
+++ b/solution.py
@@ -110,7 +110,7 @@
     target = jnp.zeros(square, jnp.int32)
     for b, mask in enumerate(masks):
         target = target + ((index >> b) & 1) * mask
-    target = (target ^ place) * per_dev + down % per_dev
+    target = (target ^ (place - place % feat_count)) * per_dev + down % per_dev
     pick = jnp.where(target == across, 1.0, 0.0).astype(BF16)
     holds = jnp.where(jnp.broadcast_to(owner, square) == down, 1.0, 0.0).astype(BF16)
     perm = lax.dot_general(pick, holds, NT, preferred_element_type=F32).astype(BF16)
@@ -161,16 +161,12 @@
         ref[r * LANES:(r + 1) * LANES, :] = jnp.broadcast_to(turned[:, r:r + 1], (LANES, LANES))
 
 
-def pairs_kernel(parts, bounds_ref, pos_ref, *refs):
-    score_refs = refs[:parts]
-    (worth_ref, qid_ref, inv_ref, leaf_ref, lam_ref, tile_ref, sums_ref,
-     s_row, a_row, d_row, s_turn, q_turn, s_col, q_col, a_own, w_own, d_own, push_own, bend_own) = refs[parts:]
+def pairs_kernel(parts, bounds_ref, pos_ref, s_row, worth_ref, qid_ref, inv_ref, leaf_ref, lam_ref, tile_ref, sums_ref,
+                 a_row, d_row, s_turn, q_turn, s_col, q_col, a_own, w_own, d_own, push_own, bend_own):
     rows = worth_ref.shape[0]
     own = inv_ref.shape[0]
     docs = own * LANES
     me = pos_ref[0] % parts
-    for k in range(parts):
-        s_row[pl.ds(pl.multiple_of((me ^ k) * own, own), own), :] = score_refs[k][...]
     a_row[...] = jnp.exp(s_row[...])
     d_row[...] = jnp.zeros((rows, LANES), F32)
     first = pl.multiple_of(me * own, own)
@@ -288,7 +284,7 @@
         )
 
 
-def pair_terms(bounds, pos, scores, worth, qid, inverse, leaves):
+def pair_terms(parts, bounds, pos, scores, worth, qid, inverse, leaves):
     rows = worth.shape[0]
     own = inverse.shape[0]
     docs = own * LANES
@@ -296,21 +292,21 @@
     row = pltpu.VMEM((rows, LANES), F32)
     mine = pltpu.VMEM((docs, LANES), F32)
     return pl.pallas_call(
-        functools.partial(pairs_kernel, len(scores)),
+        functools.partial(pairs_kernel, parts),
         out_shape=(
             jax.ShapeDtypeStruct((2, docs), F32),
             jax.ShapeDtypeStruct((4 * HIGH, docs), BF16),
             jax.ShapeDtypeStruct((highs, 2 * LANES), F32),
         ),
-        in_specs=[smem(), smem()] + [vmem()] * (len(scores) + 4),
+        in_specs=[smem(), smem()] + [vmem()] * 5,
         out_specs=(vmem(), vmem(), vmem()),
-        scratch_shapes=[row, row, row, pltpu.VMEM((LANES, rows), F32), pltpu.VMEM((LANES, rows), jnp.int32),
+        scratch_shapes=[row, row, pltpu.VMEM((LANES, rows), F32), pltpu.VMEM((LANES, rows), jnp.int32),
                         pltpu.VMEM((rows * LANES, LANES), F32), pltpu.VMEM((rows * LANES, LANES), jnp.int32),
                         mine, mine, mine, mine, mine],
         compiler_params=pltpu.CompilerParams(vmem_limit_bytes=VMEM_LIMIT),
         cost_estimate=pl.CostEstimate(flops=40_000_000, bytes_accessed=200_000, transcendentals=2_000_000),
         name="pair_terms",
-    )(bounds, pos, *scores, worth, qid, inverse, leaves)
+    )(bounds, pos, scores, worth, qid, inverse, leaves)
 
 
 def histogram_kernel(first, groups, tile_ref, bins_ref, *refs):
@@ -382,12 +378,11 @@
     )(tiles, bins_t, *tail)
 
 
-def finish_kernel(per_dev, leaf_ref, kept_ref, sums_ref, *refs):
-    arrived = refs[:-3]
-    value_ref, step_ref, hist_ref = refs[-3:]
-    unit = kept_ref.shape[0]
-    totals = add_up([sums_ref[...]] + [ref[unit:, :] for ref in arrived])
+def finish_kernel(per_dev, leaf_ref, arrived_ref, value_ref, step_ref, hist_ref):
     highs = LEAVES // LANES
+    unit = arrived_ref.shape[1] - highs
+    parts = range(arrived_ref.shape[0])
+    totals = add_up([arrived_ref[k, unit:, :] for k in parts])
     grad, curv = totals[:, :LANES], totals[:, LANES:]
     shrunk = jnp.maximum(jnp.abs(grad) - lasso_penalty, 0.0)
     values = jnp.where(grad > 0.0, -shrunk, shrunk) / (curv + ridge_penalty)
@@ -399,7 +394,7 @@
         row = jnp.broadcast_to(values[h:h + 1, :], leaf.shape)
         step = jnp.where(top == h, jnp.take_along_axis(row, spot, axis=1), step)
     step_ref[...] = shrinkage * step
-    hist = add_up([kept_ref[...]] + [ref[:unit, :] for ref in arrived])
+    hist = add_up([arrived_ref[k, :unit, :] for k in parts])
     if per_dev == GROUP:
         for c in range(3):
             for f in range(GROUP):
@@ -409,8 +404,8 @@
         hist_ref[...] = hist
 
 
-def finish(per_dev, leaves, kept, sums, arrived):
-    out = (3, per_dev * BINS) if per_dev == GROUP else kept.shape
+def finish(per_dev, leaves, arrived):
+    out = (3, per_dev * BINS) if per_dev == GROUP else (3 * per_dev, BINS)
     return pl.pallas_call(
         functools.partial(finish_kernel, per_dev),
         out_shape=(
@@ -418,11 +413,11 @@
             jax.ShapeDtypeStruct(leaves.shape, F32),
             jax.ShapeDtypeStruct(out, F32),
         ),
-        in_specs=[vmem()] * (3 + len(arrived)),
+        in_specs=[vmem()] * 2,
         out_specs=(vmem(), vmem(), vmem()),
         compiler_params=pltpu.CompilerParams(vmem_limit_bytes=VMEM_LIMIT),
         name="finish",
-    )(leaves, kept, sums, *arrived)
+    )(leaves, arrived)
 
 
 def add_up(parts):
@@ -435,9 +430,8 @@
     feat_bits = [1 << b for b in range(feat_count.bit_length() - 1)]
     query_bits = [feat_count << b for b in range(query_count.bit_length() - 1)]
     rounds = [query_bits[:1]]
-    for bits in (query_bits[1:], feat_bits):
-        rounds += [bits[k:k + 2] for k in range(0, len(bits), 2)]
-    return rounds
+    rounds += [query_bits[1:][k:k + 2] for k in range(0, len(query_bits) - 1, 2)]
+    return rounds, feat_bits
 
 
 def local(scores, labels, leaves, bins, lengths, owner):
@@ -451,22 +445,22 @@
     per_dev = features // count
     unit = 3 * per_dev
     axes = ("query", "feat")
-    rounds = exchange_rounds(query_count, feat_count)
-    bit_masks = [bit for bits in reversed(rounds) for bit in bits]
+    rounds, feat_bits = exchange_rounds(query_count, feat_count)
+    bit_masks = feat_bits + [bit for bits in reversed(rounds) for bit in bits]
     fans = [[0, bits[0]] if len(bits) == 1 else [0, bits[0], bits[1], bits[0] | bits[1]] for bits in rounds]
 
     def swap(value, mask):
         return lax.ppermute(value, axes, [(p, p ^ mask) for p in range(count)])
 
     own_scores = scores.reshape(own, LANES)
-    score_parts = [own_scores] + [
-        lax.ppermute(own_scores, "feat", [(p, p ^ k) for p in range(feat_count)]) for k in range(1, feat_count)]
+    own_scores = jnp.broadcast_to(own_scores[None], (feat_count, own, LANES))
+    gathered = lax.all_to_all(own_scores, "feat", 0, 0).reshape(feat_count * own, LANES)
 
     pos = place.reshape(1)
     bins_t, qid, worth, inverse, leaf_rows, bounds = prepare(
         feat_count, bit_masks, lengths, pos, owner.reshape(-1, LANES), bins, labels.reshape(-1, LANES),
         leaves.reshape(own, LANES))
-    lambdas, tiles, sums = pair_terms(bounds, pos, score_parts, worth, qid, inverse, leaf_rows)
+    lambdas, tiles, sums = pair_terms(feat_count, bounds, pos, gathered, worth, qid, inverse, leaf_rows)
 
     def part(low, high, *tail):
         if per_dev == GROUP:
@@ -490,14 +484,17 @@
     kept = near_first + far_first
     for k in range(1, len(rounds)):
         arrived = [swap(jnp.concatenate([block, sums], axis=0), mask) for block, mask in zip(sent, fans[k][1:])]
+        sums = add_up([sums] + [block[edge:] for block in arrived])
+        merged = add_up([kept] + [block[:edge] for block in arrived])
         if k + 1 < len(rounds):
-            sums = add_up([sums] + [block[edge:] for block in arrived])
-            merged = add_up([kept] + [block[:edge] for block in arrived])
             edge = edge // len(fans[k + 1])
             kept = merged[:edge]
             sent = [merged[m * edge:(m + 1) * edge] for m in range(1, len(fans[k + 1]))]
-
-    values, step, histograms = finish(per_dev, leaf_rows, kept, sums, arrived)
+    merged = merged.reshape(feat_count, unit, BINS)
+    sums = jnp.broadcast_to(sums[None], (feat_count,) + sums.shape)
+    arrived = lax.all_to_all(jnp.concatenate([merged, sums], axis=1), "feat", 0, 0)
+
+    values, step, histograms = finish(per_dev, leaf_rows, arrived)
     return lambdas, values.reshape(LEAVES), step.reshape(docs), histograms.reshape(3, per_dev * BINS)
 
 

time: 49 us -> 52.7 us (1.076)
  blocking collectives: 0 us -> 12.4 us
  starting transfers between devices: 16.1 us -> 10.5 us
  waiting for transfers between devices: 7.17 us -> 3.51 us
  local copies, waits for them, and re-layouts: 2.61 us -> 3.23 us
    all_to_all x0 -> x1, blocking collectives: none -> 12.4 us  [local(): lax.all_to_all(jnp.concatenate([merged, sums], axis=1), 'feat', 0, 0)]
    all_to_all x0 -> x1, starting transfers between devices: none -> 6.32 us  [local(): lax.all_to_all(own_scores, 'feat', 0, 0).reshape(feat_count * own, LANES)]
    ppermute x8 -> x5, starting transfers between devices: 10.3 us -> 4.18 us  [swap(): return lax.ppermute(value, axes, [(p, p ^ mask) for p in range(count)])]
    ppermute x3 -> x0, starting transfers between devices: 5.76 us -> none  [local(): lax.ppermute(own_scores, 'feat', [(p, p ^ k) for p in range(feat_count)])]
    ppermute x8 -> x5, waiting for transfers between devices: 7.16 us -> 2.75 us  [swap(): return lax.ppermute(value, axes, [(p, p ^ mask) for p in range(count)])]
    broadcast_in_dim x0 -> x2, local copies, waits for them, and re-layouts: none -> 1.3 us  [the longest x1 1.29 us: local(): own_scores = jnp.broadcast_to(own_scores[None], (feat_count, own, LANES))]
    all_to_all x0 -> x1, waiting for transfers between devices: none -> 0.76 us  [local(): lax.all_to_all(own_scores, 'feat', 0, 0).reshape(feat_count * own, LANES)]
    unnamed x12 -> x10, local copies, waits for them, and re-layouts: 2.6 us -> 1.93 us
  transfers between devices with their start and end apart: 11 -> 6, of which waited for: 5 -> 3; matrix products, arithmetic and copies ran while one was open for 0% -> 0% of each run, Pallas kernels for 22% -> 20%
where the time goes in v3:
time: 52.7 us; the launch traced here: 52.5 us
  Pallas kernels  21.9 us (42%)
  blocking collectives  12.4 us (24%)
  starting transfers between devices  10.5 us (20%)
  waiting for transfers between devices  3.51 us (7%)
  local copies, waits for them, and re-layouts  3.23 us (6%)
  between operations  0.75 us (1%)
    all_to_all x1, blocking collectives, local(): lax.all_to_all(jnp.concatenate([merged, sums], axis=1), 'feat', 0, 0)  12.4 us
    pallas_call x1, Pallas kernels, pair_terms(): pl.pallas_call(functools.partial(pairs_kernel, parts), out_shape=(jax.Sha...  9.32 us
    pallas_call x4, Pallas kernels, histogram_part(): pl.pallas_call(functools.partial(histogram_kernel, first, groups), out_sh...  8.84 us
    all_to_all x1, starting transfers between devices, local(): lax.all_to_all(own_scores, 'feat', 0, 0).reshape(feat_count * own, LANES)  6.32 us
    ppermute x5, starting transfers between devices, swap(): return lax.ppermute(value, axes, [(p, p ^ mask) for p in range(count)])  4.18 us
    pallas_call x1, Pallas kernels, prepare(): pl.pallas_call(functools.partial(prepare_kernel, feat_count, masks), out_...  2.9 us
    ppermute x5, waiting for transfers between devices, swap(): return lax.ppermute(value, axes, [(p, p ^ mask) for p in range(count)])  2.75 us
    unnamed x10, local copies, waits for them, and re-layouts  1.93 us
  transfers between devices with their start and end apart: 6, of which 3 were waited for; matrix products, arithmetic and copies ran while one was open for 0% of the time, Pallas kernels for 20%

profile of v3, /device:TPU:0, one launch (start us, length us, event | category | flops | bytes accessed | tf_op | source)
XLA Modules:
  0.0 52.5 jit_solution(2281225160099873662)
XLA Ops:
  0.6 1.3 %broadcast_in_dim.14 = f32[4,8,128]{2,1,0:T(8,128)} broadcast(f32[8,128]{1,0:T(8,128)} %bitcast.14), dimensions={1,2} | broadcast | bytes 20480 | tf_op jit(solution)/shard_map/broadcast_in_dim | solution.py:456
  1.9 6.3 %all-to-all-start = ((f32[4,8,128]{2,1,0:T(8,128)}), f32[4,8,128]{2,1,0:T(8,128)S(1)}, u32[]{:S(2)}, u32[]{:S(2)}) async-start(f32[4,8,128]{2,1,0:T(8,128)} %broadcast_in_dim.14), calls=%async_computation | async-start | bytes 32768 | tf_op jit(solution)/shard_map/all_to_all | solution.py:457
  8.2 0.0 copy-start.1
  8.2 0.0 copy-start.2
  8.2 0.0 copy-start.3
  8.3 0.0 copy-start.4
  8.3 0.7 %copy-done.1 = s32[4096]{0:T(1024)S(1)} copy-done((s32[4096]{0:T(1024)S(1)}, s32[4096]{0:T(1024)}, u32[]{:S(2)}) %copy-start.1) | copy-done | bytes 16408
  9.0 0.0 copy-done.2
  9.0 0.0 copy-done.3
  9.0 0.0 copy-done.4
  9.0 0.0 copy-start
  9.0 1.2 %copy-done = s32[1024,256]{1,0:T(8,128)S(1)} copy-done((s32[1024,256]{1,0:T(8,128)S(1)}, s32[1024,256]{1,0:T(8,128)}, u32[]{:S(2)}) %copy-start) | copy-done | bytes 1048600
  10.2 2.9 %prepare.1 = (f32[256,1024]{1,0:T(8,128)S(1)}, s32[32,128]{1,0:T(8,128)S(1)}, f32[32,128]{1,0:T(8,128)S(1)}, f32[8,128]{1,0:T(8,128)S(1)}, s32[8,128]{1,0:T(8,128)S(1)}, /*index=5*/s32[2,32]{1,0:T(2,128)S(1)}) custom-call(s32[1,16]{1,0:T(1,128)S(1)} %copy-done.4, s32[1]{0:T(128)} %bitcast.pos_ref, s32[2,128]{1,0:T(2,128)S(1)} %bitcast.12, ...), custom_call_target="tpu_custom_call" | custom-call | flops 200000000 | bytes 3000000 | tf_op jit(solution)/shard_map/prepare/pallas_call | solution.py:128
  13.1 0.8 %all-to-all-done = f32[4,8,128]{2,1,0:T(8,128)S(1)} async-done(((f32[4,8,128]{2,1,0:T(8,128)}), f32[4,8,128]{2,1,0:T(8,128)S(1)}, u32[]{:S(2)}, u32[]{:S(2)}) %all-to-all-start) | async-done | bytes 16416 | tf_op jit(solution)/shard_map/all_to_all | solution.py:457
  13.9 9.3 %pair_terms.1 = (f32[2,1024]{1,0:T(2,128)}, bf16[32,1024]{1,0:T(8,128)(2,1)S(1)}, f32[8,256]{1,0:T(8,128)S(1)}) custom-call(s32[2,32]{1,0:T(2,128)S(1)} %get-tuple-element.16.bounds_ref, s32[1]{0:T(128)} %bitcast.pos_ref, f32[32,128]{1,0:T(8,128)S(1)} %bitcast.10, f32[32,128]{1,0:T(8,128)S(1)} %get-tuple-element.17.worth_ref, ...), custom_call_target="tpu_custom_call" | custom-call | flops 40000000 | bytes 200000 | tf_op jit(solution)/shard_map/pair_terms/pallas_call | solution.py:294
  23.2 1.1 %histogram_part.5 = f32[96,256]{1,0:T(8,128)S(1)} custom-call(bf16[32,1024]{1,0:T(8,128)(2,1)S(1)} %get-tuple-element.22.tile_ref, f32[256,1024]{1,0:T(8,128)S(1)} %get-tuple-element.23.bins_ref), custom_call_target="tpu_custom_call" | custom-call | flops 1320000000 | bytes 240000 | tf_op jit(solution)/shard_map/histogram_part/pallas_call | solution.py:370
  24.3 0.1 collective-permute-start
  24.4 3.3 %histogram_part.7 = f32[296,256]{1,0:T(8,128)S(1)} custom-call(bf16[32,1024]{1,0:T(8,128)(2,1)S(1)} %get-tuple-element.22.tile_ref, f32[256,1024]{1,0:T(8,128)S(1)} %get-tuple-element.23.bins_ref, f32[8,256]{1,0:T(8,128)S(1)} %get-tuple-element.24.refs_0_), custom_call_target="tpu_custom_call" | custom-call | flops 3960000000 | bytes 720000 | tf_op jit(solution)/shard_map/histogram_part/pallas_call | solution.py:370
  27.7 0.6 %collective-permute-start.1 = (f32[296,256]{1,0:T(8,128)S(1)}, f32[296,256]{1,0:T(8,128)S(1)}, u32[]{:S(2)}, u32[]{:S(2)}) collective-permute-start(f32[296,256]{1,0:T(8,128)S(1)} %histogram_part.7), channel_id=1, source_target_pairs={{0,4},{1,5},{2,6},{3,7},{4,0},{5,1},{6,2},{7,3},{8,12},{9,13},{10,... | collective-permute-start | bytes 909320 | tf_op jit(solution)/shard_map/ppermute | solution.py:453
  28.2 3.3 %histogram_part.6 = f32[288,256]{1,0:T(8,128)S(1)} custom-call(bf16[32,1024]{1,0:T(8,128)(2,1)S(1)} %get-tuple-element.22.tile_ref, f32[256,1024]{1,0:T(8,128)S(1)} %get-tuple-element.23.bins_ref), custom_call_target="tpu_custom_call" | custom-call | flops 3960000000 | bytes 720000 | tf_op jit(solution)/shard_map/histogram_part/pallas_call | solution.py:370
  31.6 0.0 collective-permute-done.1
  31.6 0.1 slice_add_fusion.4
  31.7 0.1 collective-permute-start.2
  31.8 0.9 %collective-permute-start.3 = (f32[104,256]{1,0:T(8,128)S(1)}, f32[104,256]{1,0:T(8,128)S(1)}, u32[]{:S(2)}, u32[]{:S(2)}) collective-permute-start(f32[104,256]{1,0:T(8,128)S(1)} %get-tuple-element.32), channel_id=1, source_target_pairs={{0,16},{1,17},{2,18},{3,19},{4,20},{5,21},{6,22},{7,23},{8,24},{9,... | collective-permute-start | bytes 319496 | tf_op jit(solution)/shard_map/ppermute | solution.py:453
  32.7 2.6 %collective-permute-start.4 = (f32[104,256]{1,0:T(8,128)S(1)}, f32[104,256]{1,0:T(8,128)S(1)}, u32[]{:S(2)}, u32[]{:S(2)}) collective-permute-start(f32[104,256]{1,0:T(8,128)S(1)} %get-tuple-element.33), channel_id=1, source_target_pairs={{0,24},{1,25},{2,26},{3,27},{4,28},{5,29},{6,30},{7,31},{8,16},{9,... | collective-permute-start | bytes 319496 | tf_op jit(solution)/shard_map/ppermute | solution.py:453
  35.2 1.1 %histogram_part.4 = f32[96,256]{1,0:T(8,128)S(1)} custom-call(bf16[32,1024]{1,0:T(8,128)(2,1)S(1)} %get-tuple-element.22.tile_ref, f32[256,1024]{1,0:T(8,128)S(1)} %get-tuple-element.23.bins_ref), custom_call_target="tpu_custom_call" | custom-call | flops 1320000000 | bytes 240000 | tf_op jit(solution)/shard_map/histogram_part/pallas_call | solution.py:370
  36.3 1.2 %collective-permute-done.2 = f32[104,256]{1,0:T(8,128)S(1)} collective-permute-done((f32[104,256]{1,0:T(8,128)S(1)}, f32[104,256]{1,0:T(8,128)S(1)}, u32[]{:S(2)}, u32[]{:S(2)}) %collective-permute-start.2) | collective-permute-done | bytes 106528 | tf_op jit(solution)/shard_map/ppermute | solution.py:453
  37.6 1.5 %collective-permute-done.3 = f32[104,256]{1,0:T(8,128)S(1)} collective-permute-done((f32[104,256]{1,0:T(8,128)S(1)}, f32[104,256]{1,0:T(8,128)S(1)}, u32[]{:S(2)}, u32[]{:S(2)}) %collective-permute-start.3) | collective-permute-done | bytes 106528 | tf_op jit(solution)/shard_map/ppermute | solution.py:453
  39.1 0.0 collective-permute-done.4
  39.1 0.0 collective-permute-done
  39.2 12.4 %all_to_all.10.arrived_ref = f32[4,32,256]{2,1,0:T(8,128)S(1)} all-to-all(f32[4,32,256]{2,1,0:T(8,128)S(1)} %pad_maximum_fusion.3), channel_id=1, replica_groups=mesh['query'=8,'feat'=4] {'feat'}, dimensions={0} | all-to-all | bytes 262144 | tf_op jit(solution)/shard_map/all_to_all | solution.py:495
  51.6 0.9 %finish.1 = (f32[8,128]{1,0:T(8,128)}, f32[8,128]{1,0:T(8,128)}, f32[3,2048]{1,0:T(4,128)}) custom-call(s32[8,128]{1,0:T(8,128)S(1)} %get-tuple-element.20.leaf_ref, f32[4,32,256]{2,1,0:T(8,128)S(1)} %all_to_all.10.arrived_ref), custom_call_target="tpu_custom_call" | custom-call | tf_op jit(solution)/shard_map/finish/pallas_call | solution.py:409
  (6 shorter events, 0.1 us)
Async XLA Ops:
  1.9 11.9 %all-to-all-start = ((f32[4,8,128]{2,1,0:T(8,128)}), f32[4,8,128]{2,1,0:T(8,128)S(1)}, u32[]{:S(2)}, u32[]{:S(2)}) async-start(f32[4,8,128]{2,1,0:T(8,128)} %broadcast_in_dim.14), calls=%async_computation | async-start | bytes 32768 | tf_op jit(solution)/shard_map/all_to_all | solution.py:457
  8.2 0.7 %copy-start.1 = (s32[4096]{0:T(1024)S(1)}, s32[4096]{0:T(1024)}, u32[]{:S(2)}) copy-start(s32[4096]{0:T(1024)} %param.7) | copy-start | bytes 49156
  8.2 0.7 %copy-start.2 = (s32[1024]{0:T(1024)S(1)}, s32[1024]{0:T(1024)}, u32[]{:S(2)}) copy-start(s32[1024]{0:T(1024)} %param.8) | copy-start | bytes 12292
  8.2 0.7 %copy-start.3 = (s32[256]{0:T(256)S(1)}, s32[256]{0:T(256)}, u32[]{:S(2)}) copy-start(s32[256]{0:T(256)} %param.11) | copy-start | bytes 3076
  8.3 0.7 %copy-start.4 = (s32[1,16]{1,0:T(1,128)S(1)}, s32[1,16]{1,0:T(1,128)}, u32[]{:S(2)}) copy-start(s32[1,16]{1,0:T(1,128)} %len_ref.1) | copy-start | bytes 196
  9.0 1.2 %copy-start = (s32[1024,256]{1,0:T(8,128)S(1)}, s32[1024,256]{1,0:T(8,128)}, u32[]{:S(2)}) copy-start(s32[1024,256]{1,0:T(8,128)} %bins_hbm.1) | copy-start | bytes 3145732
  24.3 14.8 %collective-permute-start = (f32[96,256]{1,0:T(8,128)S(1)}, f32[96,256]{1,0:T(8,128)S(1)}, u32[]{:S(2)}, u32[]{:S(2)}) collective-permute-start(f32[96,256]{1,0:T(8,128)S(1)} %histogram_part.5), channel_id=1, source_target_pairs={{0,4},{1,5},{2,6},{3,7},{4,0},{5,1},{6,2},{7,3},{8,12},{9,13},{10,... | collective-permute-start | bytes 294920 | tf_op jit(solution)/shard_map/ppermute | solution.py:453
  27.7 3.9 %collective-permute-start.1 = (f32[296,256]{1,0:T(8,128)S(1)}, f32[296,256]{1,0:T(8,128)S(1)}, u32[]{:S(2)}, u32[]{:S(2)}) collective-permute-start(f32[296,256]{1,0:T(8,128)S(1)} %histogram_part.7), channel_id=1, source_target_pairs={{0,4},{1,5},{2,6},{3,7},{4,0},{5,1},{6,2},{7,3},{8,12},{9,13},{10,... | collective-permute-start | bytes 909320 | tf_op jit(solution)/shard_map/ppermute | solution.py:453
  31.7 5.9 %collective-permute-start.2 = (f32[104,256]{1,0:T(8,128)S(1)}, f32[104,256]{1,0:T(8,128)S(1)}, u32[]{:S(2)}, u32[]{:S(2)}) collective-permute-start(f32[104,256]{1,0:T(8,128)S(1)} %get-tuple-element.31), channel_id=1, source_target_pairs={{0,8},{1,9},{2,10},{3,11},{4,12},{5,13},{6,14},{7,15},{8,0},{9,1},... | collective-permute-start | bytes 319496 | tf_op jit(solution)/shard_map/ppermute | solution.py:453
  31.8 7.3 %collective-permute-start.3 = (f32[104,256]{1,0:T(8,128)S(1)}, f32[104,256]{1,0:T(8,128)S(1)}, u32[]{:S(2)}, u32[]{:S(2)}) collective-permute-start(f32[104,256]{1,0:T(8,128)S(1)} %get-tuple-element.32), channel_id=1, source_target_pairs={{0,16},{1,17},{2,18},{3,19},{4,20},{5,21},{6,22},{7,23},{8,24},{9,... | collective-permute-start | bytes 319496 | tf_op jit(solution)/shard_map/ppermute | solution.py:453
  32.7 6.4 %collective-permute-start.4 = (f32[104,256]{1,0:T(8,128)S(1)}, f32[104,256]{1,0:T(8,128)S(1)}, u32[]{:S(2)}, u32[]{:S(2)}) collective-permute-start(f32[104,256]{1,0:T(8,128)S(1)} %get-tuple-element.33), channel_id=1, source_target_pairs={{0,24},{1,25},{2,26},{3,27},{4,28},{5,29},{6,30},{7,31},{8,16},{9,... | collective-permute-start | bytes 319496 | tf_op jit(solution)/shard_map/ppermute | solution.py:453

commit v4 on v2

--- a/solution.py
+++ b/solution.py
@@ -39,18 +39,10 @@
     return pl.BlockSpec(memory_space=pltpu.SMEM)
 
 
-def prepare_kernel(feat_count, masks, len_ref, pos_ref, owner_hbm, bins_hbm, lab_hbm, leaf_hbm,
-                   bins_t_ref, qid_ref, worth_ref, inv_ref, leaf_ref, bounds_ref, bins_ref, lab_ref, owner_ref, sems):
+def label_kernel(feat_count, len_ref, pos_ref, lab_ref, qid_ref, worth_ref, inv_ref, bounds_ref):
     queries = len_ref.shape[1]
     rows = lab_ref.shape[0]
     own = inv_ref.shape[0]
-    features = bins_ref.shape[1]
-    place = pos_ref[0]
-    copies = [pltpu.make_async_copy(source, target, sems.at[k]) for k, (source, target) in enumerate(
-        ((lab_hbm, lab_ref), (owner_hbm, owner_ref), (bins_hbm, bins_ref), (leaf_hbm, leaf_ref)))]
-    for copy in copies:
-        copy.start()
-
     spot = iota((rows, LANES), 0) * LANES + iota((rows, LANES), 1)
     qid = jnp.zeros((rows, LANES), jnp.int32)
     begin = jnp.zeros((queries, LANES), jnp.int32)
@@ -75,9 +67,8 @@
         lax.fori_loop(start // LANES, end // LANES, set_high, 0)
         start = end
     qid_ref[...] = qid
-
-    copies[0].wait()
     worth_ref[...] = jnp.left_shift(1, lab_ref[...]).astype(F32)
+
     counts = [jnp.zeros((queries, LANES), F32) for _ in range(GRADES)]
     lane = iota((queries, LANES), 1)
     for r in range(rows):
@@ -95,13 +86,33 @@
     ideal = jnp.sum(gain * level, axis=1, keepdims=True)
     usable = ideal > 0.5
     inverse = jnp.where(usable, 1.0 / jnp.where(usable, ideal, 1.0), 0.0)
-    first = place % feat_count * own
+    first = pos_ref[0] % feat_count * own
     for t in range(own):
         at = lane + (first + t) * LANES
         inside = (at >= begin) & (at < finish)
         inv_ref[t:t + 1, :] = jnp.sum(jnp.where(inside, inverse, 0.0), axis=0, keepdims=True)
 
-    copies[1].wait()
+
+def label_terms(feat_count, own, lengths, pos, labels):
+    rows = labels.shape[0]
+    return pl.pallas_call(
+        functools.partial(label_kernel, feat_count),
+        out_shape=(
+            jax.ShapeDtypeStruct((rows, LANES), jnp.int32),
+            jax.ShapeDtypeStruct((rows, LANES), F32),
+            jax.ShapeDtypeStruct((own, LANES), F32),
+            jax.ShapeDtypeStruct((2, rows), jnp.int32),
+        ),
+        in_specs=[smem(), smem(), vmem()],
+        out_specs=(vmem(), vmem(), vmem(), smem()),
+        compiler_params=pltpu.CompilerParams(vmem_limit_bytes=VMEM_LIMIT),
+        cost_estimate=pl.CostEstimate(flops=10_000_000, bytes_accessed=3_000_000, transcendentals=20_000),
+        name="label_terms",
+    )(lengths, pos, labels)
+
+
+def order_kernel(masks, pos_ref, owner_ref, bins_ref, out_ref):
+    features = bins_ref.shape[1]
     per_dev = features >> len(masks)
     owner = jnp.concatenate([owner_ref[k:k + 1, :] for k in range(features // LANES)], axis=1)
     square = (features, features)
@@ -110,39 +121,25 @@
     target = jnp.zeros(square, jnp.int32)
     for b, mask in enumerate(masks):
         target = target + ((index >> b) & 1) * mask
-    target = (target ^ place) * per_dev + down % per_dev
+    target = (target ^ pos_ref[0]) * per_dev + down % per_dev
     pick = jnp.where(target == across, 1.0, 0.0).astype(BF16)
     holds = jnp.where(jnp.broadcast_to(owner, square) == down, 1.0, 0.0).astype(BF16)
     perm = lax.dot_general(pick, holds, NT, preferred_element_type=F32).astype(BF16)
-    copies[2].wait()
     bins = bins_ref[...].astype(F32).astype(BF16)
-    bins_t_ref[...] = lax.dot_general(perm, bins, NT, preferred_element_type=F32)
-    copies[3].wait()
-
-
-def prepare(feat_count, masks, lengths, pos, owner, bins, labels, leaves):
-    rows = labels.shape[0]
-    own = leaves.shape[0]
+    out_ref[...] = lax.dot_general(perm, bins, NT, preferred_element_type=F32)
+
+
+def order_bins(masks, pos, owner, bins):
     docs, features = bins.shape
-    hbm = pl.BlockSpec(memory_space=pltpu.HBM)
     return pl.pallas_call(
-        functools.partial(prepare_kernel, feat_count, masks),
-        out_shape=(
-            jax.ShapeDtypeStruct((features, docs), F32),
-            jax.ShapeDtypeStruct((rows, LANES), jnp.int32),
-            jax.ShapeDtypeStruct((rows, LANES), F32),
-            jax.ShapeDtypeStruct((own, LANES), F32),
-            jax.ShapeDtypeStruct((own, LANES), jnp.int32),
-            jax.ShapeDtypeStruct((2, rows), jnp.int32),
-        ),
-        in_specs=[smem(), smem(), hbm, hbm, hbm, hbm],
-        out_specs=(vmem(), vmem(), vmem(), vmem(), vmem(), smem()),
-        scratch_shapes=[pltpu.VMEM((docs, features), jnp.int32), pltpu.VMEM((rows, LANES), jnp.int32),
-                        pltpu.VMEM((features // LANES, LANES), jnp.int32), pltpu.SemaphoreType.DMA((4,))],
+        functools.partial(order_kernel, masks),
+        out_shape=jax.ShapeDtypeStruct((features, docs), F32),
+        in_specs=[smem(), vmem(), vmem()],
+        out_specs=vmem(),
         compiler_params=pltpu.CompilerParams(vmem_limit_bytes=VMEM_LIMIT),
-        cost_estimate=pl.CostEstimate(flops=200_000_000, bytes_accessed=3_000_000, transcendentals=20_000),
-        name="prepare",
-    )(lengths, pos, owner, bins, labels, leaves)
+        cost_estimate=pl.CostEstimate(flops=200_000_000, bytes_accessed=3_000_000, transcendentals=0),
+        name="order_bins",
+    )(pos, owner, bins)
 
 
 def split_terms(value, terms):
@@ -168,9 +165,12 @@
     rows = worth_ref.shape[0]
     own = inv_ref.shape[0]
     docs = own * LANES
-    me = pos_ref[0] % parts
-    for k in range(parts):
-        s_row[pl.ds(pl.multiple_of((me ^ k) * own, own), own), :] = score_refs[k][...]
+    me = pos_ref[0] % (rows // own)
+    k = 0
+    for ref in score_refs:
+        for piece in range(ref.shape[0] // own):
+            s_row[pl.ds(pl.multiple_of((me ^ k) * own, own), own), :] = ref[piece * own:(piece + 1) * own, :]
+            k += 1
     a_row[...] = jnp.exp(s_row[...])
     d_row[...] = jnp.zeros((rows, LANES), F32)
     first = pl.multiple_of(me * own, own)
@@ -431,15 +431,6 @@
     return parts[0]
 
 
-def exchange_rounds(query_count, feat_count):
-    feat_bits = [1 << b for b in range(feat_count.bit_length() - 1)]
-    query_bits = [feat_count << b for b in range(query_count.bit_length() - 1)]
-    rounds = [query_bits[:1]]
-    for bits in (query_bits[1:], feat_bits):
-        rounds += [bits[k:k + 2] for k in range(0, len(bits), 2)]
-    return rounds
-
-
 def local(scores, labels, leaves, bins, lengths, owner):
     query_count = lax.axis_size("query")
     feat_count = lax.axis_size("feat")
@@ -451,24 +442,27 @@
     per_dev = features // count
     unit = 3 * per_dev
     axes = ("query", "feat")
-    rounds = exchange_rounds(query_count, feat_count)
-    bit_masks = [bit for bits in reversed(rounds) for bit in bits]
-    fans = [[0, bits[0]] if len(bits) == 1 else [0, bits[0], bits[1], bits[0] | bits[1]] for bits in rounds]
+    feat_masks = [1 << b for b in range(feat_count.bit_length() - 1)]
+    masks = [feat_count << b for b in range(query_count.bit_length() - 1)] + feat_masks
 
     def swap(value, mask):
         return lax.ppermute(value, axes, [(p, p ^ mask) for p in range(count)])
 
-    own_scores = scores.reshape(own, LANES)
-    score_parts = [own_scores] + [
-        lax.ppermute(own_scores, "feat", [(p, p ^ k) for p in range(feat_count)]) for k in range(1, feat_count)]
-
     pos = place.reshape(1)
-    bins_t, qid, worth, inverse, leaf_rows, bounds = prepare(
-        feat_count, bit_masks, lengths, pos, owner.reshape(-1, LANES), bins, labels.reshape(-1, LANES),
-        leaves.reshape(own, LANES))
+    leaf_rows = leaves.reshape(own, LANES)
+    gathered = scores.reshape(own, LANES)
+    score_parts = [gathered]
+    for k, mask in enumerate(feat_masks):
+        if k == 1:
+            qid, worth, inverse, bounds = label_terms(feat_count, own, lengths, pos, labels.reshape(-1, LANES))
+            gathered, inverse = lax.optimization_barrier((gathered, inverse))
+        score_parts.append(swap(gathered, mask))
+        gathered = jnp.concatenate([gathered, score_parts[-1]], axis=0)
     lambdas, tiles, sums = pair_terms(bounds, pos, score_parts, worth, qid, inverse, leaf_rows)
-
-    def part(low, high, *tail):
+    pos, sums = lax.optimization_barrier((pos, sums))
+    bins_t = order_bins(masks[::-1], pos, owner.reshape(-1, LANES), bins)
+
+    def part(tiles, low, high, *tail):
         if per_dev == GROUP:
             return histogram_part(low, high - low, tiles, bins_t, *tail)
         groups = high - low
@@ -476,28 +470,26 @@
         wide = wide.reshape(groups, 3, HIGH, GROUP // per_dev, per_dev, LOW).transpose(0, 3, 1, 4, 2, 5)
         return jnp.concatenate([wide.reshape(groups * GROUP // per_dev * unit, BINS), *tail], axis=0)
 
-    fan = fans[1]
-    half = features // GROUP // 2
-    quarter = half // len(fan)
-    edge = count // 2 // len(fan) * unit
-    far_rest = swap(part(half + quarter, 2 * half, sums), fans[0][1])
-    near_rest = part(quarter, half)
-    far_first = swap(part(half, half + quarter), fans[0][1])
-    near_first = part(0, quarter)
-
-    sums = sums + far_rest[edge * (len(fan) - 1):]
-    sent = [near_rest[k * edge:(k + 1) * edge] + far_rest[k * edge:(k + 1) * edge] for k in range(len(fan) - 1)]
-    kept = near_first + far_first
-    for k in range(1, len(rounds)):
-        arrived = [swap(jnp.concatenate([block, sums], axis=0), mask) for block, mask in zip(sent, fans[k][1:])]
-        if k + 1 < len(rounds):
-            sums = add_up([sums] + [block[edge:] for block in arrived])
-            merged = add_up([kept] + [block[:edge] for block in arrived])
-            edge = edge // len(fans[k + 1])
-            kept = merged[:edge]
-            sent = [merged[m * edge:(m + 1) * edge] for m in range(1, len(fans[k + 1]))]
-
-    values, step, histograms = finish(per_dev, leaf_rows, kept, sums, arrived)
+    def join(block, total):
+        return jnp.concatenate([block, total], axis=0)
+
+    quarter = features // GROUP // 4
+    edge = count // 4 * unit
+    arrived = swap(part(tiles, 3 * quarter, 4 * quarter, sums), masks[0])
+    far = part(tiles, quarter, 2 * quarter) + arrived[:edge]
+    sums = sums + arrived[edge:]
+    message, tiles = lax.optimization_barrier((join(far, sums), tiles))
+    crossed = swap(message, masks[1])
+    arrived = swap(part(tiles, 2 * quarter, 3 * quarter), masks[0])
+    kept = part(tiles, 0, quarter) + arrived + crossed[:edge]
+    sums = sums + crossed[edge:]
+    for mask in masks[2:-1]:
+        edge = edge // 2
+        arrived = swap(join(kept[edge:], sums), mask)
+        kept = kept[:edge] + arrived[:edge]
+        sums = sums + arrived[edge:]
+    arrived = swap(join(kept[unit:], sums), masks[-1])
+    values, step, histograms = finish(per_dev, leaf_rows, kept[:unit], sums, [arrived])
     return lambdas, values.reshape(LEAVES), step.reshape(docs), histograms.reshape(3, per_dev * BINS)
 
 

time: 49 us -> 50.6 us (1.033); the launches traced: 49.1 us -> 50.2 us
  waiting for transfers between devices: 7.17 us -> 11.1 us
  Pallas kernels: 22.4 us -> 19.7 us
  local copies, waits for them, and re-layouts: 2.61 us -> 1.36 us
  starting transfers between devices: 16.1 us -> 17 us
    ppermute x8, starting transfers between devices: 10.3 us -> 17 us  [swap(): return lax.ppermute(value, axes, [(p, p ^ mask) for p in range(count)])]
    ppermute x3 -> x0, starting transfers between devices: 5.76 us -> none  [local(): lax.ppermute(own_scores, 'feat', [(p, p ^ k) for p in range(feat_count)])]
    ppermute x8, waiting for transfers between devices: 7.16 us -> 11.1 us  [swap(): return lax.ppermute(value, axes, [(p, p ^ mask) for p in range(count)])]
    pallas_call x1, Pallas kernels: 9.76 us -> 7.66 us  [pair_terms(): pl.pallas_call(functools.partial(pairs_kernel, len(scores)), out_shape=(j...]
    unnamed x12, local copies, waits for them, and re-layouts: 2.6 us -> 1.35 us
    pallas_call x1 -> x2, Pallas kernels: 2.91 us -> 2.3 us  [the longest x1 1.8 us: label_terms(): pl.pallas_call(functools.partial(label_kernel, feat_count), out_shape=(ja...]
  transfers between devices with their start and end apart: 11 -> 8, of which waited for: 5 -> 5; matrix products, arithmetic and copies ran while one was open for 0% -> 0% of each run, Pallas kernels for 22% -> 17%
where the time goes in v4:
time: 50.6 us; the launch traced here: 50.2 us
  Pallas kernels  19.7 us (39%)
  starting transfers between devices  17 us (34%)
  waiting for transfers between devices  11.1 us (22%)
  local copies, waits for them, and re-layouts  1.36 us (3%)
  between operations  0.83 us (2%)
    ppermute x8, starting transfers between devices, swap(): return lax.ppermute(value, axes, [(p, p ^ mask) for p in range(count)])  17 us
    ppermute x8, waiting for transfers between devices, swap(): return lax.ppermute(value, axes, [(p, p ^ mask) for p in range(count)])  11.1 us
    pallas_call x4, Pallas kernels, histogram_part(): pl.pallas_call(functools.partial(histogram_kernel, first, groups), out_sh...  8.85 us
    pallas_call x1, Pallas kernels, pair_terms(): pl.pallas_call(functools.partial(pairs_kernel, len(scores)), out_shape=(j...  7.66 us
    pallas_call x1, Pallas kernels, label_terms(): pl.pallas_call(functools.partial(label_kernel, feat_count), out_shape=(ja...  1.8 us
    unnamed x12, local copies, waits for them, and re-layouts  1.35 us
  transfers between devices with their start and end apart: 8, of which 5 were waited for; matrix products, arithmetic and copies ran while one was open for 0% of the time, Pallas kernels for 17%

profile of v4, /device:TPU:0, one launch (start us, length us, event | category | flops | bytes accessed | tf_op | source)
XLA Modules:
  0.0 50.2 jit_solution(16584136796534182636)
XLA Ops:
  0.6 0.0 copy-start.4
  0.6 3.1 %collective-permute-start = (f32[8,128]{1,0:T(8,128)}, f32[8,128]{1,0:T(8,128)S(1)}, u32[]{:S(2)}, u32[]{:S(2)}) collective-permute-start(f32[8,128]{1,0:T(8,128)} %bitcast.9), channel_id=1, source_target_pairs={{0,1},{1,0},{2,3},{3,2},{4,5},{5,4},{6,7},{7,6},{8,9},{9,8},{10,11... | collective-permute-start | bytes 12296 | tf_op jit(solution)/shard_map/ppermute | solution.py:449
  3.7 0.0 copy-done.4
  3.7 0.7 %copy-done.5 = s32[1,16]{1,0:T(1,128)S(1)} copy-done((s32[1,16]{1,0:T(1,128)S(1)}, s32[1,16]{1,0:T(1,128)}, u32[]{:S(2)}) %copy-start.5) | copy-done | bytes 88
  4.4 1.8 %label_terms.1 = (s32[32,128]{1,0:T(8,128)S(1)}, f32[32,128]{1,0:T(8,128)S(1)}, f32[8,128]{1,0:T(8,128)S(1)}, s32[2,32]{1,0:T(2,128)S(1)}) custom-call(s32[1,16]{1,0:T(1,128)S(1)} %copy-done.5, s32[1]{0:T(128)} %bitcast.pos_ref, s32[32,128]{1,0:T(8,128)S(1)} %bitcast.13), custom_call_target="tpu_custom_call" | custom-call | flops 10000000 | bytes 3000000 | tf_op jit(solution)/shard_map/label_terms/pallas_call | solution.py:98
  6.2 0.0 collective-permute-done.refs_1_
  6.2 0.0 copy-done.2
  6.2 0.0 copy-start.1
  6.2 2.7 %collective-permute-start.1 = (f32[16,128]{1,0:T(8,128)S(1)}, f32[16,128]{1,0:T(8,128)S(1)}, u32[]{:S(2)}, u32[]{:S(2)}) collective-permute-start(f32[16,128]{1,0:T(8,128)S(1)} %pad_maximum_fusion.4), channel_id=1, source_target_pairs={{0,2},{1,3},{2,0},{3,1},{4,6},{5,7},{6,4},{7,5},{8,10},{9,11},{10,... | collective-permute-start | bytes 24584 | tf_op jit(solution)/shard_map/ppermute | solution.py:449
  8.9 2.0 %collective-permute-done.1.refs_2_ = f32[16,128]{1,0:T(8,128)S(1)} collective-permute-done((f32[16,128]{1,0:T(8,128)S(1)}, f32[16,128]{1,0:T(8,128)S(1)}, u32[]{:S(2)}, u32[]{:S(2)}) %collective-permute-start.1) | collective-permute-done | bytes 8224 | tf_op jit(solution)/shard_map/ppermute | solution.py:449
  10.9 0.0 copy-done.1
  10.9 7.7 %pair_terms.1 = (f32[2,1024]{1,0:T(2,128)}, bf16[32,1024]{1,0:T(8,128)(2,1)S(1)}, f32[8,256]{1,0:T(8,128)S(1)}) custom-call(s32[2,32]{1,0:T(2,128)S(1)} %get-tuple-element.20.bounds_ref, s32[1]{0:T(128)} %bitcast.pos_ref, f32[8,128]{1,0:T(8,128)S(1)} %bitcast.11, f32[8,128]{1,0:T(8,128)S(1)} %collective-permute-done.refs_1_, ...), custom_call_target="tpu_custom_call" | custom-call | flops 40000000 | bytes 200000 | tf_op jit(solution)/shard_map/pair_terms/pallas_call | solution.py:298
  18.5 0.0 copy-done
  18.5 0.7 %copy-done.3 = s32[256]{0:T(256)S(1)} copy-done((s32[256]{0:T(256)S(1)}, s32[256]{0:T(256)}, u32[]{:S(2)}) %copy-start.3) | copy-done | bytes 1048
  19.2 0.5 %order_bins.1.bins_ref = f32[256,1024]{1,0:T(8,128)S(1)} custom-call(s32[1]{0:T(128)} %bitcast.pos_ref, s32[2,128]{1,0:T(2,128)S(1)} %bitcast.12, s32[1024,256]{1,0:T(8,128)S(1)} %copy-done), custom_call_target="tpu_custom_call" | custom-call | flops 200000000 | bytes 3000000 | tf_op jit(solution)/shard_map/order_bins/pallas_call | solution.py:134
  19.7 2.2 %histogram_part.5 = f32[200,256]{1,0:T(8,128)S(1)} custom-call(bf16[32,1024]{1,0:T(8,128)(2,1)S(1)} %get-tuple-element.31.tile_ref, f32[256,1024]{1,0:T(8,128)S(1)} %order_bins.1.bins_ref, f32[8,256]{1,0:T(8,128)S(1)} %get-tuple-element.30.refs_0_), custom_call_target="tpu_custom_call" | custom-call | flops 2640000000 | bytes 480000 | tf_op jit(solution)/shard_map/histogram_part/pallas_call | solution.py:374
  21.9 0.1 collective-permute-start.2
  22.0 2.2 %histogram_part.4 = f32[192,256]{1,0:T(8,128)S(1)} custom-call(bf16[32,1024]{1,0:T(8,128)(2,1)S(1)} %get-tuple-element.31.tile_ref, f32[256,1024]{1,0:T(8,128)S(1)} %order_bins.1.bins_ref), custom_call_target="tpu_custom_call" | custom-call | flops 2640000000 | bytes 480000 | tf_op jit(solution)/shard_map/histogram_part/pallas_call | solution.py:374
  24.2 0.0 collective-permute-done.2
  24.3 0.7 %collective-permute-start.4 = (f32[200,256]{1,0:T(8,128)S(1)}, f32[200,256]{1,0:T(8,128)S(1)}, u32[]{:S(2)}, u32[]{:S(2)}) collective-permute-start(f32[200,256]{1,0:T(8,128)S(1)} %pad_maximum_fusion), channel_id=1, source_target_pairs={{0,8},{1,9},{2,10},{3,11},{4,12},{5,13},{6,14},{7,15},{8,0},{9,1},... | collective-permute-start | bytes 614408 | tf_op jit(solution)/shard_map/ppermute | solution.py:449
  25.0 2.2 %histogram_part.7 = f32[192,256]{1,0:T(8,128)S(1)} custom-call(bf16[32,1024]{1,0:T(8,128)(2,1)S(1)} %get-tuple-element.31.tile_ref, f32[256,1024]{1,0:T(8,128)S(1)} %order_bins.1.bins_ref), custom_call_target="tpu_custom_call" | custom-call | flops 2640000000 | bytes 480000 | tf_op jit(solution)/shard_map/histogram_part/pallas_call | solution.py:374
  27.3 0.3 collective-permute-start.3
  27.5 2.2 %histogram_part.6 = f32[192,256]{1,0:T(8,128)S(1)} custom-call(bf16[32,1024]{1,0:T(8,128)(2,1)S(1)} %get-tuple-element.31.tile_ref, f32[256,1024]{1,0:T(8,128)S(1)} %order_bins.1.bins_ref), custom_call_target="tpu_custom_call" | custom-call | flops 2640000000 | bytes 480000 | tf_op jit(solution)/shard_map/histogram_part/pallas_call | solution.py:374
  29.8 0.0 collective-permute-done.3
  29.8 2.1 %collective-permute-done.4 = f32[200,256]{1,0:T(8,128)S(1)} collective-permute-done((f32[200,256]{1,0:T(8,128)S(1)}, f32[200,256]{1,0:T(8,128)S(1)}, u32[]{:S(2)}, u32[]{:S(2)}) %collective-permute-start.4) | collective-permute-done | bytes 204832 | tf_op jit(solution)/shard_map/ppermute | solution.py:449
  31.9 1.8 %collective-permute-start.5 = (f32[104,256]{1,0:T(8,128)S(1)}, f32[104,256]{1,0:T(8,128)S(1)}, u32[]{:S(2)}, u32[]{:S(2)}) collective-permute-start(f32[104,256]{1,0:T(8,128)S(1)} %pad_maximum_fusion.1), channel_id=1, source_target_pairs={{0,16},{1,17},{2,18},{3,19},{4,20},{5,21},{6,22},{7,23},{8,24},{9,... | collective-permute-start | bytes 319496 | tf_op jit(solution)/shard_map/ppermute | solution.py:449
  33.7 3.0 %collective-permute-done.5 = f32[104,256]{1,0:T(8,128)S(1)} collective-permute-done((f32[104,256]{1,0:T(8,128)S(1)}, f32[104,256]{1,0:T(8,128)S(1)}, u32[]{:S(2)}, u32[]{:S(2)}) %collective-permute-start.5) | collective-permute-done | bytes 106528 | tf_op jit(solution)/shard_map/ppermute | solution.py:449
  36.8 3.7 %collective-permute-start.6 = (f32[56,256]{1,0:T(8,128)S(1)}, f32[56,256]{1,0:T(8,128)S(1)}, u32[]{:S(2)}, u32[]{:S(2)}) collective-permute-start(f32[56,256]{1,0:T(8,128)S(1)} %pad_maximum_fusion.2), channel_id=1, source_target_pairs={{0,1},{1,0},{2,3},{3,2},{4,5},{5,4},{6,7},{7,6},{8,9},{9,8},{10,11... | collective-permute-start | bytes 172040 | tf_op jit(solution)/shard_map/ppermute | solution.py:449
  40.4 2.2 %collective-permute-done.6 = f32[56,256]{1,0:T(8,128)S(1)} collective-permute-done((f32[56,256]{1,0:T(8,128)S(1)}, f32[56,256]{1,0:T(8,128)S(1)}, u32[]{:S(2)}, u32[]{:S(2)}) %collective-permute-start.6) | collective-permute-done | bytes 57376 | tf_op jit(solution)/shard_map/ppermute | solution.py:449
  42.7 4.7 %collective-permute-start.7 = (f32[32,256]{1,0:T(8,128)S(1)}, f32[32,256]{1,0:T(8,128)S(1)}, u32[]{:S(2)}, u32[]{:S(2)}) collective-permute-start(f32[32,256]{1,0:T(8,128)S(1)} %pad_maximum_fusion.3), channel_id=1, source_target_pairs={{0,2},{1,3},{2,0},{3,1},{4,6},{5,7},{6,4},{7,5},{8,10},{9,11},{10,... | collective-permute-start | bytes 98312 | tf_op jit(solution)/shard_map/ppermute | solution.py:449
  47.4 1.9 %collective-permute-done.7.refs_0_ = f32[32,256]{1,0:T(8,128)S(1)} collective-permute-done((f32[32,256]{1,0:T(8,128)S(1)}, f32[32,256]{1,0:T(8,128)S(1)}, u32[]{:S(2)}, u32[]{:S(2)}) %collective-permute-start.7) | collective-permute-done | bytes 32800 | tf_op jit(solution)/shard_map/ppermute | solution.py:449
  49.3 0.9 %finish.1 = (f32[8,128]{1,0:T(8,128)}, f32[8,128]{1,0:T(8,128)}, f32[3,2048]{1,0:T(4,128)}) custom-call(s32[8,128]{1,0:T(8,128)S(1)} %bitcast.8, f32[24,256]{1,0:T(8,128)S(1)} %get-tuple-element.37.kept_ref, f32[8,256]{1,0:T(8,128)S(1)} %slice_add_fusion.4.sums_ref, f32[32,256]{1,0:T(8,128)S(1)} %collective-permute-done.7.refs_0_), custom_call_target="tpu_custom_call" | custom-call | tf_op jit(solution)/shard_map/finish/pallas_call | solution.py:414
  (20 shorter events, 0.2 us)
Async XLA Ops:
  0.6 3.1 %copy-start.4 = (s32[4096]{0:T(1024)S(1)}, s32[4096]{0:T(1024)}, u32[]{:S(2)}) copy-start(s32[4096]{0:T(1024)} %param.7) | copy-start | bytes 49156
  0.6 5.6 %collective-permute-start = (f32[8,128]{1,0:T(8,128)}, f32[8,128]{1,0:T(8,128)S(1)}, u32[]{:S(2)}, u32[]{:S(2)}) collective-permute-start(f32[8,128]{1,0:T(8,128)} %bitcast.9), channel_id=1, source_target_pairs={{0,1},{1,0},{2,3},{3,2},{4,5},{5,4},{6,7},{7,6},{8,9},{9,8},{10,11... | collective-permute-start | bytes 12296 | tf_op jit(solution)/shard_map/ppermute | solution.py:449
  3.7 0.7 %copy-start.5 = (s32[1,16]{1,0:T(1,128)S(1)}, s32[1,16]{1,0:T(1,128)}, u32[]{:S(2)}) copy-start(s32[1,16]{1,0:T(1,128)} %len_ref.1) | copy-start | bytes 196
  4.4 1.8 %copy-start.2 = (f32[1024]{0:T(1024)S(1)}, f32[1024]{0:T(1024)}, u32[]{:S(2)}) copy-start(f32[1024]{0:T(1024)} %param.6) | copy-start | bytes 12292
  6.2 4.6 %copy-start.1 = (s32[1024]{0:T(1024)S(1)}, s32[1024]{0:T(1024)}, u32[]{:S(2)}) copy-start(s32[1024]{0:T(1024)} %param.8) | copy-start | bytes 12292
  6.2 4.6 %collective-permute-start.1 = (f32[16,128]{1,0:T(8,128)S(1)}, f32[16,128]{1,0:T(8,128)S(1)}, u32[]{:S(2)}, u32[]{:S(2)}) collective-permute-start(f32[16,128]{1,0:T(8,128)S(1)} %pad_maximum_fusion.4), channel_id=1, source_target_pairs={{0,2},{1,3},{2,0},{3,1},{4,6},{5,7},{6,4},{7,5},{8,10},{9,11},{10,... | collective-permute-start | bytes 24584 | tf_op jit(solution)/shard_map/ppermute | solution.py:449
  10.9 7.7 %copy-start = (s32[1024,256]{1,0:T(8,128)S(1)}, s32[1024,256]{1,0:T(8,128)}, u32[]{:S(2)}) copy-start(s32[1024,256]{1,0:T(8,128)} %bins_ref.1) | copy-start | bytes 3145732
  18.5 0.7 %copy-start.3 = (s32[256]{0:T(256)S(1)}, s32[256]{0:T(256)}, u32[]{:S(2)}) copy-start(s32[256]{0:T(256)} %param.11) | copy-start | bytes 3076
  21.9 2.3 %collective-permute-start.2 = (f32[200,256]{1,0:T(8,128)S(1)}, f32[200,256]{1,0:T(8,128)S(1)}, u32[]{:S(2)}, u32[]{:S(2)}) collective-permute-start(f32[200,256]{1,0:T(8,128)S(1)} %histogram_part.5), channel_id=1, source_target_pairs={{0,4},{1,5},{2,6},{3,7},{4,0},{5,1},{6,2},{7,3},{8,12},{9,13},{10,... | collective-permute-start | bytes 614408 | tf_op jit(solution)/shard_map/ppermute | solution.py:449
  24.3 7.5 %collective-permute-start.4 = (f32[200,256]{1,0:T(8,128)S(1)}, f32[200,256]{1,0:T(8,128)S(1)}, u32[]{:S(2)}, u32[]{:S(2)}) collective-permute-start(f32[200,256]{1,0:T(8,128)S(1)} %pad_maximum_fusion), channel_id=1, source_target_pairs={{0,8},{1,9},{2,10},{3,11},{4,12},{5,13},{6,14},{7,15},{8,0},{9,1},... | collective-permute-start | bytes 614408 | tf_op jit(solution)/shard_map/ppermute | solution.py:449
  27.3 2.5 %collective-permute-start.3 = (f32[192,256]{1,0:T(8,128)S(1)}, f32[192,256]{1,0:T(8,128)S(1)}, u32[]{:S(2)}, u32[]{:S(2)}) collective-permute-start(f32[192,256]{1,0:T(8,128)S(1)} %histogram_part.7), channel_id=1, source_target_pairs={{0,4},{1,5},{2,6},{3,7},{4,0},{5,1},{6,2},{7,3},{8,12},{9,13},{10,... | collective-permute-start | bytes 589832 | tf_op jit(solution)/shard_map/ppermute | solution.py:449
  31.9 4.8 %collective-permute-start.5 = (f32[104,256]{1,0:T(8,128)S(1)}, f32[104,256]{1,0:T(8,128)S(1)}, u32[]{:S(2)}, u32[]{:S(2)}) collective-permute-start(f32[104,256]{1,0:T(8,128)S(1)} %pad_maximum_fusion.1), channel_id=1, source_target_pairs={{0,16},{1,17},{2,18},{3,19},{4,20},{5,21},{6,22},{7,23},{8,24},{9,... | collective-permute-start | bytes 319496 | tf_op jit(solution)/shard_map/ppermute | solution.py:449
  36.8 5.8 %collective-permute-start.6 = (f32[56,256]{1,0:T(8,128)S(1)}, f32[56,256]{1,0:T(8,128)S(1)}, u32[]{:S(2)}, u32[]{:S(2)}) collective-permute-start(f32[56,256]{1,0:T(8,128)S(1)} %pad_maximum_fusion.2), channel_id=1, source_target_pairs={{0,1},{1,0},{2,3},{3,2},{4,5},{5,4},{6,7},{7,6},{8,9},{9,8},{10,11... | collective-permute-start | bytes 172040 | tf_op jit(solution)/shard_map/ppermute | solution.py:449
  42.7 6.7 %collective-permute-start.7 = (f32[32,256]{1,0:T(8,128)S(1)}, f32[32,256]{1,0:T(8,128)S(1)}, u32[]{:S(2)}, u32[]{:S(2)}) collective-permute-start(f32[32,256]{1,0:T(8,128)S(1)} %pad_maximum_fusion.3), channel_id=1, source_target_pairs={{0,2},{1,3},{2,0},{3,1},{4,6},{5,7},{6,4},{7,5},{8,10},{9,11},{10,... | collective-permute-start | bytes 98312 | tf_op jit(solution)/shard_map/ppermute | solution.py:449

commit v5 on v4

--- a/solution.py
+++ b/solution.py
@@ -39,10 +39,13 @@
     return pl.BlockSpec(memory_space=pltpu.SMEM)
 
 
-def label_kernel(feat_count, len_ref, pos_ref, lab_ref, qid_ref, worth_ref, inv_ref, bounds_ref):
+def prepare_kernel(feat_count, masks, len_ref, pos_ref, lab_ref, owner_ref, leaf_ref, score_ref,
+                   kept_ref, qid_ref, worth_ref, inv_ref, perm_ref, spot_ref, top_ref, bounds_ref):
     queries = len_ref.shape[1]
     rows = lab_ref.shape[0]
-    own = inv_ref.shape[0]
+    own = leaf_ref.shape[0]
+    docs = own * LANES
+    kept_ref[...] = score_ref[...]
     spot = iota((rows, LANES), 0) * LANES + iota((rows, LANES), 1)
     qid = jnp.zeros((rows, LANES), jnp.int32)
     begin = jnp.zeros((queries, LANES), jnp.int32)
@@ -55,8 +58,9 @@
         begin = jnp.where(which == q, start, begin)
         finish = jnp.where(which == q, end, finish)
 
-        def set_low(r, carry, start=start):
+        def set_low(r, carry, start=start, end=end):
             bounds_ref[0, r] = start
+            bounds_ref[2, r] = end
             return carry
 
         def set_high(r, carry, end=end):
@@ -90,56 +94,69 @@
     for t in range(own):
         at = lane + (first + t) * LANES
         inside = (at >= begin) & (at < finish)
-        inv_ref[t:t + 1, :] = jnp.sum(jnp.where(inside, inverse, 0.0), axis=0, keepdims=True)
-
-
-def label_terms(feat_count, own, lengths, pos, labels):
-    rows = labels.shape[0]
-    return pl.pallas_call(
-        functools.partial(label_kernel, feat_count),
-        out_shape=(
-            jax.ShapeDtypeStruct((rows, LANES), jnp.int32),
-            jax.ShapeDtypeStruct((rows, LANES), F32),
-            jax.ShapeDtypeStruct((own, LANES), F32),
-            jax.ShapeDtypeStruct((2, rows), jnp.int32),
-        ),
-        in_specs=[smem(), smem(), vmem()],
-        out_specs=(vmem(), vmem(), vmem(), smem()),
-        compiler_params=pltpu.CompilerParams(vmem_limit_bytes=VMEM_LIMIT),
-        cost_estimate=pl.CostEstimate(flops=10_000_000, bytes_accessed=3_000_000, transcendentals=20_000),
-        name="label_terms",
-    )(lengths, pos, labels)
-
-
-def order_kernel(masks, pos_ref, owner_ref, bins_ref, out_ref):
-    features = bins_ref.shape[1]
+        inv_ref[0:1, t * LANES:(t + 1) * LANES] = jnp.sum(jnp.where(inside, inverse, 0.0), axis=0, keepdims=True)
+
+    features = perm_ref.shape[0]
     per_dev = features >> len(masks)
     owner = jnp.concatenate([owner_ref[k:k + 1, :] for k in range(features // LANES)], axis=1)
     square = (features, features)
     down, across = iota(square, 0), iota(square, 1)
-    index = down // per_dev
-    target = jnp.zeros(square, jnp.int32)
+    index = iota((features, 1), 0) // per_dev
+    target = jnp.zeros((features, 1), jnp.int32)
     for b, mask in enumerate(masks):
         target = target + ((index >> b) & 1) * mask
-    target = (target ^ pos_ref[0]) * per_dev + down % per_dev
+    target = (target ^ pos_ref[0]) * per_dev + iota((features, 1), 0) % per_dev
     pick = jnp.where(target == across, 1.0, 0.0).astype(BF16)
     holds = jnp.where(jnp.broadcast_to(owner, square) == down, 1.0, 0.0).astype(BF16)
-    perm = lax.dot_general(pick, holds, NT, preferred_element_type=F32).astype(BF16)
+    perm_ref[...] = lax.dot_general(pick, holds, NT, preferred_element_type=F32).astype(BF16)
+
+    leaf = jnp.concatenate([leaf_ref[t:t + 1, :] for t in range(own)], axis=1)
+    highs = LEAVES // LANES
+    top_ref[...] = jnp.where(jnp.broadcast_to(leaf // LANES, (highs, docs)) == iota((highs, docs), 0), 1.0, 0.0)
+    spot_ref[...] = jnp.where(
+        jnp.broadcast_to(leaf % LANES, (LANES, docs)) == iota((LANES, docs), 0), 1.0, 0.0).astype(BF16)
+
+
+def prepare(feat_count, masks, lengths, pos, labels, owner, leaves, scores):
+    rows = labels.shape[0]
+    docs = leaves.shape[0] * LANES
+    features = owner.shape[0] * LANES
+    return pl.pallas_call(
+        functools.partial(prepare_kernel, feat_count, masks),
+        out_shape=(
+            jax.ShapeDtypeStruct(scores.shape, F32),
+            jax.ShapeDtypeStruct((rows, LANES), jnp.int32),
+            jax.ShapeDtypeStruct((rows, LANES), F32),
+            jax.ShapeDtypeStruct((1, docs), F32),
+            jax.ShapeDtypeStruct((features, features), BF16),
+            jax.ShapeDtypeStruct((LANES, docs), BF16),
+            jax.ShapeDtypeStruct((LEAVES // LANES, docs), F32),
+            jax.ShapeDtypeStruct((3, rows), jnp.int32),
+        ),
+        in_specs=[smem(), smem()] + [vmem()] * 4,
+        out_specs=(vmem(),) * 7 + (smem(),),
+        compiler_params=pltpu.CompilerParams(vmem_limit_bytes=VMEM_LIMIT),
+        cost_estimate=pl.CostEstimate(flops=50_000_000, bytes_accessed=3_000_000, transcendentals=20_000),
+        name="prepare",
+    )(lengths, pos, labels, owner, leaves, scores)
+
+
+def order_kernel(perm_ref, bins_ref, out_ref):
     bins = bins_ref[...].astype(F32).astype(BF16)
-    out_ref[...] = lax.dot_general(perm, bins, NT, preferred_element_type=F32)
-
-
-def order_bins(masks, pos, owner, bins):
+    out_ref[...] = lax.dot_general(perm_ref[...], bins, NT, preferred_element_type=F32)
+
+
+def order_bins(perm, bins):
     docs, features = bins.shape
     return pl.pallas_call(
-        functools.partial(order_kernel, masks),
+        order_kernel,
         out_shape=jax.ShapeDtypeStruct((features, docs), F32),
-        in_specs=[smem(), vmem(), vmem()],
+        in_specs=[vmem(), vmem()],
         out_specs=vmem(),
         compiler_params=pltpu.CompilerParams(vmem_limit_bytes=VMEM_LIMIT),
         cost_estimate=pl.CostEstimate(flops=200_000_000, bytes_accessed=3_000_000, transcendentals=0),
         name="order_bins",
-    )(pos, owner, bins)
+    )(perm, bins)
 
 
 def split_terms(value, terms):
@@ -158,25 +175,37 @@
         ref[r * LANES:(r + 1) * LANES, :] = jnp.broadcast_to(turned[:, r:r + 1], (LANES, LANES))
 
 
-def pairs_kernel(parts, bounds_ref, pos_ref, *refs):
-    score_refs = refs[:parts]
-    (worth_ref, qid_ref, inv_ref, leaf_ref, lam_ref, tile_ref, sums_ref,
-     s_row, a_row, d_row, s_turn, q_turn, s_col, q_col, a_own, w_own, d_own, push_own, bend_own) = refs[parts:]
+def lane_sums(source):
+    parts = split_terms(source, 3)
+    ones = jnp.ones((8, 2 * LANES), BF16)
+    wide = lax.dot_general(ones, jnp.concatenate(parts[:2], axis=1), NT, preferred_element_type=F32)
+    return (wide + lax.dot_general(ones[:, :LANES], parts[2], NT, preferred_element_type=F32))[0:1, :]
+
+
+def pairs_kernel(feat_count, bounds_ref, pos_ref, *refs):
+    scores = refs[:-21]
+    (worth_ref, qid_ref, inv_ref, spot_ref, top_ref, lam_ref, tile_ref, sums_ref,
+     s_row, a_row, d_row, w_row, q_row, s_turn, q_turn, s_col, q_col, a_own, w_own, d_own, sums_own) = refs[-21:]
     rows = worth_ref.shape[0]
-    own = inv_ref.shape[0]
+    own = rows // feat_count
     docs = own * LANES
-    me = pos_ref[0] % (rows // own)
-    k = 0
-    for ref in score_refs:
-        for piece in range(ref.shape[0] // own):
-            s_row[pl.ds(pl.multiple_of((me ^ k) * own, own), own), :] = ref[piece * own:(piece + 1) * own, :]
-            k += 1
+    me = pos_ref[0] % feat_count
+    s_row[...] = jnp.zeros(s_row.shape, F32)
+    near = [me, me ^ 1, ((me + 1) ^ 1) - 1]
+    for where, ref in zip(near, scores):
+        @pl.when((where >= 0) & (where < feat_count))
+        def _(where=where, ref=ref):
+            s_row[pl.ds(pl.multiple_of(where * own, own), own), :] = ref[...]
     a_row[...] = jnp.exp(s_row[...])
-    d_row[...] = jnp.zeros((rows, LANES), F32)
+    d_row[...] = jnp.zeros(d_row.shape, F32)
+    w_row[0:rows, :] = worth_ref[...]
+    w_row[rows:, :] = jnp.zeros((8, LANES), F32)
+    q_row[0:rows, :] = qid_ref[...]
+    q_row[rows:, :] = jnp.full((8, LANES), -1, jnp.int32)
     first = pl.multiple_of(me * own, own)
     window_low = bounds_ref[0, first] // LANES
     window_high = (bounds_ref[1, first + own - 1] + LANES - 1) // LANES
-    s_turn[...] = jnp.transpose(s_row[...])
+    s_turn[...] = jnp.transpose(s_row[0:rows, :])
     q_turn[...] = jnp.transpose(qid_ref[...])
     for r in range(rows):
         @pl.when((r >= window_low) & (r < window_high))
@@ -185,33 +214,39 @@
             s_col[at, :] = jnp.broadcast_to(s_turn[:, r:r + 1], (LANES, LANES))
             q_col[at, :] = jnp.broadcast_to(q_turn[:, r:r + 1], (LANES, LANES))
     widen(a_own, a_row[pl.ds(first, own), :])
-    widen(w_own, worth_ref[pl.ds(first, own), :])
+    widen(w_own, w_row[pl.ds(first, own), :])
 
     def row_of(ref, r):
         return jnp.broadcast_to(ref[pl.ds(r, 1), :], (8, LANES))
 
     def rank_group(r, carry):
         score = row_of(s_row, r)
-        query = row_of(qid_ref, r)
-
-        def sweep(ahead):
+        query = row_of(q_row, r)
+
+        def sweep(ahead, masked):
             def step(c, acc):
-                base = pl.multiple_of(c * CHUNK, CHUNK)
+                base = pl.multiple_of(c * LANES, LANES)
                 acc = list(acc)
-                for u in range(CHUNK // 8):
+                for u in range(LANES // 8):
                     other = s_col[pl.ds(base + 8 * u, 8), :]
-                    above = (other >= score) if ahead else (other > score)
-                    hit = above & (q_col[pl.ds(base + 8 * u, 8), :] == query)
+                    hit = (other >= score) if ahead else (other > score)
+                    if masked:
+                        hit = hit & (q_col[pl.ds(base + 8 * u, 8), :] == query)
                     acc[u % 4] = acc[u % 4] + jnp.where(hit, 1.0, 0.0)
                 return tuple(acc)
             return step
 
         acc = tuple(jnp.zeros((8, LANES), F32) for _ in range(4))
-        per = LANES // CHUNK
-        low = jnp.maximum(bounds_ref[0, r] // CHUNK, window_low * per)
-        high = jnp.minimum((bounds_ref[1, r] + CHUNK - 1) // CHUNK, window_high * per)
-        acc = lax.fori_loop(low, r * per, sweep(True), acc)
-        acc = list(lax.fori_loop((r + 1) * per, high, sweep(False), acc))
+        start, end = bounds_ref[0, r], bounds_ref[1, r]
+        low = jnp.maximum(start // LANES, window_low)
+        high = jnp.minimum((end + LANES - 1) // LANES, window_high)
+        single = bounds_ref[2, r] >= (r + 1) * LANES
+        inner_low = jnp.where(single, jnp.maximum((start + LANES - 1) // LANES, window_low), r)
+        inner_high = jnp.where(single, jnp.minimum(end // LANES, window_high), r + 1)
+        acc = lax.fori_loop(low, inner_low, sweep(True, True), acc)
+        acc = lax.fori_loop(inner_low, r, sweep(True, False), acc)
+        acc = lax.fori_loop(r + 1, inner_high, sweep(False, False), acc)
+        acc = list(lax.fori_loop(inner_high, high, sweep(False, True), acc))
         base = pl.multiple_of(r * LANES, LANES)
         for u in range(LANES // 8):
             other = s_col[pl.ds(base + 8 * u, 8), :]
@@ -233,54 +268,56 @@
         count = CHUNK // 8
         queries = pl.multiple_of(first * LANES + base, CHUNK)
 
-        def step(c, acc):
-            acc = list(acc)
-            a_j = row_of(a_row, c)
-            w_j = row_of(worth_ref, c)
-            d_j = row_of(d_row, c)
-            query = row_of(qid_ref, c)
-            for u in range(count):
-                at = pl.ds(base + 8 * u, 8)
-                a_i = a_own[at, :]
-                total = a_i + a_j
-                rough = pl.reciprocal(total, approx=True)
-                recip = rough * (2.0 - total * rough)
-                gap = jnp.abs(d_own[at, :] - d_j)
-                lift = w_own[at, :] - w_j
-                weight = jnp.where(q_col[pl.ds(queries + 8 * u, 8), :] == query, gap * recip, 0.0) * lift
-                acc[u] = acc[u] + weight * jnp.where(lift > 0.0, a_j, a_i)
-                acc[count + u] = acc[count + u] + jnp.abs(weight) * (recip * a_j)
-            return tuple(acc)
+        def columns(width):
+            def step(c, acc):
+                acc = list(acc)
+                other = []
+                for k in range(width):
+                    at = (r_low + width * c + k) if width > 1 else c
+                    other.append([row_of(ref, at) for ref in (a_row, w_row, d_row, q_row)])
+                for u in range(count):
+                    at = pl.ds(base + 8 * u, 8)
+                    a_i, w_i, d_i = a_own[at, :], w_own[at, :], d_own[at, :]
+                    q_i = q_col[pl.ds(queries + 8 * u, 8), :]
+                    for a_j, w_j, d_j, q_j in other:
+                        recip = pl.reciprocal(a_i + a_j, approx=True)
+                        lift = w_i - w_j
+                        weight = jnp.where(q_i == q_j, jnp.abs(d_i - d_j) * recip, 0.0) * lift
+                        acc[u] = acc[u] + weight * jnp.where(lift > 0.0, a_j, a_i)
+                        acc[count + u] = acc[count + u] + jnp.abs(weight) * (recip * a_j)
+                return tuple(acc)
+            return step
 
         acc = tuple(jnp.zeros((8, LANES), F32) for _ in range(2 * count))
-        acc = lax.fori_loop(bounds_ref[0, r] // LANES, (bounds_ref[1, r] + LANES - 1) // LANES, step, acc)
+        r_low = bounds_ref[0, r] // LANES
+        r_high = (bounds_ref[1, r] + LANES - 1) // LANES
+        twos = (r_high - r_low) // 2
+        acc = lax.fori_loop(0, twos, columns(2), acc)
+        acc = lax.fori_loop(r_low + 2 * twos, r_high, columns(1), acc)
         for u in range(count):
-            push_own[pl.ds(base + 8 * u, 8), :] = acc[u]
-            bend_own[pl.ds(base + 8 * u, 8), :] = acc[count + u]
+            sums_own[pl.ds(base + 8 * u, 8), :] = acc[u]
+            sums_own[pl.ds(docs + base + 8 * u, 8), :] = acc[count + u]
         return carry
 
     lax.fori_loop(0, docs // CHUNK, pair_block, 0)
-    for t in range(own):
-        at = slice(t * LANES, (t + 1) * LANES)
-        inverse = inv_ref[t:t + 1, :]
-        lam_ref[0:1, at] = -inverse * jnp.sum(jnp.transpose(push_own[at, :]), axis=0, keepdims=True)
-        lam_ref[1:2, at] = (inverse * a_row[pl.ds(first + t, 1), :]
-                            * jnp.sum(jnp.transpose(bend_own[at, :]), axis=0, keepdims=True))
-
-    leaf = jnp.concatenate([leaf_ref[t:t + 1, :] for t in range(own)], axis=1)
+    totals = lane_sums(sums_own[...])
+    inverse = inv_ref[...]
+    a_line = jnp.concatenate([a_row[pl.ds(first + t, 1), :] for t in range(own)], axis=1)
+    terms = [-inverse * totals[:, :docs], inverse * a_line * totals[:, docs:]]
+
     highs = LEAVES // LANES
-    top = jnp.broadcast_to(leaf // LANES, (highs, docs)) == iota((highs, docs), 0)
-    spots = jnp.where(jnp.broadcast_to(leaf % LANES, (LANES, docs)) == iota((LANES, docs), 0), 1.0, 0.0).astype(BF16)
+    top = top_ref[...] > 0.0
     pieces, tiles = [], []
     for c in range(2):
-        for k, part in enumerate(split_terms(lam_ref[c:c + 1, :], 3)):
+        lam_ref[c:c + 1, :] = terms[c]
+        for k, part in enumerate(split_terms(terms[c], 3)):
             wide = jnp.broadcast_to(part.astype(F32), (highs, docs))
             pieces.append(jnp.where(top, wide, 0.0))
             if k < 2:
                 tiles.append(wide)
     tile_ref[...] = jnp.concatenate(tiles, axis=0).astype(BF16)
     stacked = jnp.concatenate(pieces, axis=0).astype(BF16)
-    sums = lax.dot_general(stacked, spots, NT, preferred_element_type=F32)
+    sums = lax.dot_general(stacked, spot_ref[...], NT, preferred_element_type=F32)
     for c in range(2):
         base = c * 3 * highs
         sums_ref[:, c * LANES:(c + 1) * LANES] = (
@@ -288,29 +325,29 @@
         )
 
 
-def pair_terms(bounds, pos, scores, worth, qid, inverse, leaves):
+def pair_terms(feat_count, bounds, pos, scores, worth, qid, inverse, spots, top):
     rows = worth.shape[0]
-    own = inverse.shape[0]
-    docs = own * LANES
+    docs = inverse.shape[1]
     highs = LEAVES // LANES
-    row = pltpu.VMEM((rows, LANES), F32)
+    row = pltpu.VMEM((rows + 8, LANES), F32)
     mine = pltpu.VMEM((docs, LANES), F32)
     return pl.pallas_call(
-        functools.partial(pairs_kernel, len(scores)),
+        functools.partial(pairs_kernel, feat_count),
         out_shape=(
             jax.ShapeDtypeStruct((2, docs), F32),
             jax.ShapeDtypeStruct((4 * HIGH, docs), BF16),
             jax.ShapeDtypeStruct((highs, 2 * LANES), F32),
         ),
-        in_specs=[smem(), smem()] + [vmem()] * (len(scores) + 4),
+        in_specs=[smem(), smem()] + [vmem()] * (len(scores) + 5),
         out_specs=(vmem(), vmem(), vmem()),
-        scratch_shapes=[row, row, row, pltpu.VMEM((LANES, rows), F32), pltpu.VMEM((LANES, rows), jnp.int32),
+        scratch_shapes=[row, row, row, row, pltpu.VMEM((rows + 8, LANES), jnp.int32),
+                        pltpu.VMEM((LANES, rows), F32), pltpu.VMEM((LANES, rows), jnp.int32),
                         pltpu.VMEM((rows * LANES, LANES), F32), pltpu.VMEM((rows * LANES, LANES), jnp.int32),
-                        mine, mine, mine, mine, mine],
+                        mine, mine, mine, pltpu.VMEM((2 * docs, LANES), F32)],
         compiler_params=pltpu.CompilerParams(vmem_limit_bytes=VMEM_LIMIT),
         cost_estimate=pl.CostEstimate(flops=40_000_000, bytes_accessed=200_000, transcendentals=2_000_000),
         name="pair_terms",
-    )(bounds, pos, *scores, worth, qid, inverse, leaves)
+    )(bounds, pos, *scores, worth, qid, inverse, spots, top)
 
 
 def histogram_kernel(first, groups, tile_ref, bins_ref, *refs):
@@ -443,24 +480,24 @@
     unit = 3 * per_dev
     axes = ("query", "feat")
     feat_masks = [1 << b for b in range(feat_count.bit_length() - 1)]
-    masks = [feat_count << b for b in range(query_count.bit_length() - 1)] + feat_masks
+    query_masks = [feat_count << b for b in range(query_count.bit_length() - 1)]
 
     def swap(value, mask):
         return lax.ppermute(value, axes, [(p, p ^ mask) for p in range(count)])
 
     pos = place.reshape(1)
     leaf_rows = leaves.reshape(own, LANES)
-    gathered = scores.reshape(own, LANES)
-    score_parts = [gathered]
-    for k, mask in enumerate(feat_masks):
-        if k == 1:
-            qid, worth, inverse, bounds = label_terms(feat_count, own, lengths, pos, labels.reshape(-1, LANES))
-            gathered, inverse = lax.optimization_barrier((gathered, inverse))
-        score_parts.append(swap(gathered, mask))
-        gathered = jnp.concatenate([gathered, score_parts[-1]], axis=0)
-    lambdas, tiles, sums = pair_terms(bounds, pos, score_parts, worth, qid, inverse, leaf_rows)
-    pos, sums = lax.optimization_barrier((pos, sums))
-    bins_t = order_bins(masks[::-1], pos, owner.reshape(-1, LANES), bins)
+    own_scores = scores.reshape(own, LANES)
+    score_parts = [own_scores]
+    for begin in range(2):
+        links = [(z, z + 1) for z in range(begin, feat_count - 1, 2)]
+        score_parts.append(lax.ppermute(own_scores, "feat", links + [(b, a) for a, b in links]))
+    score_parts[0], qid, worth, inverse, perm, spots, top, bounds = prepare(
+        feat_count, feat_masks + query_masks[:0:-1] + query_masks[:1], lengths, pos, labels.reshape(-1, LANES),
+        owner.reshape(-1, LANES), leaf_rows, own_scores)
+    lambdas, tiles, sums = pair_terms(feat_count, bounds, pos, score_parts, worth, qid, inverse, spots, top)
+    perm, sums = lax.optimization_barrier((perm, sums))
+    bins_t = order_bins(perm, bins)
 
     def part(tiles, low, high, *tail):
         if per_dev == GROUP:
@@ -475,21 +512,21 @@
 
     quarter = features // GROUP // 4
     edge = count // 4 * unit
-    arrived = swap(part(tiles, 3 * quarter, 4 * quarter, sums), masks[0])
+    arrived = swap(part(tiles, 3 * quarter, 4 * quarter, sums), query_masks[0])
     far = part(tiles, quarter, 2 * quarter) + arrived[:edge]
     sums = sums + arrived[edge:]
     message, tiles = lax.optimization_barrier((join(far, sums), tiles))
-    crossed = swap(message, masks[1])
-    arrived = swap(part(tiles, 2 * quarter, 3 * quarter), masks[0])
+    crossed = swap(message, query_masks[1])
+    arrived = swap(part(tiles, 2 * quarter, 3 * quarter), query_masks[0])
     kept = part(tiles, 0, quarter) + arrived + crossed[:edge]
     sums = sums + crossed[edge:]
-    for mask in masks[2:-1]:
+    for mask in query_masks[2:]:
         edge = edge // 2
         arrived = swap(join(kept[edge:], sums), mask)
         kept = kept[:edge] + arrived[:edge]
         sums = sums + arrived[edge:]
-    arrived = swap(join(kept[unit:], sums), masks[-1])
-    values, step, histograms = finish(per_dev, leaf_rows, kept[:unit], sums, [arrived])
+    arrived = [swap(join(kept[m * unit:(m + 1) * unit], sums), m) for m in range(1, feat_count)]
+    values, step, histograms = finish(per_dev, leaf_rows, kept[:unit], sums, arrived)
     return lambdas, values.reshape(LEAVES), step.reshape(docs), histograms.reshape(3, per_dev * BINS)
 
 

time: 50.6 us -> 47.6 us (0.941)
  waiting for transfers between devices: 11.1 us -> 8.11 us
  Pallas kernels: 19.7 us -> 21 us
  starting transfers between devices: 17 us -> 15.7 us
    ppermute x8 -> x7, starting transfers between devices: 17 us -> 12 us  [swap(): return lax.ppermute(value, axes, [(p, p ^ mask) for p in range(count)])]
    ppermute x0 -> x2, starting transfers between devices: none -> 3.74 us  [local(): lax.ppermute(own_scores, 'feat', links + [(b, a) for a, b in links])]
    ppermute x8 -> x7, waiting for transfers between devices: 11.1 us -> 8.1 us  [swap(): return lax.ppermute(value, axes, [(p, p ^ mask) for p in range(count)])]
    pallas_call x3, Pallas kernels: 9.97 us -> 11.3 us  [the longest x1 8.84 us: pair_terms(): pl.pallas_call(functools.partial(pairs_kernel, feat_count), out_shape=(ja...]
  transfers between devices with their start and end apart: 8 -> 9, of which waited for: 5 -> 4; matrix products, arithmetic and copies ran while one was open for 0% -> 0% of each run, Pallas kernels for 17% -> 19%
where the time goes in v5:
time: 47.6 us; the launch traced here: 47.2 us
  Pallas kernels  21 us (44%)
  starting transfers between devices  15.7 us (33%)
  waiting for transfers between devices  8.11 us (17%)
  local copies, waits for them, and re-layouts  1.38 us (3%)
  between operations  0.84 us (2%)
    ppermute x7, starting transfers between devices, swap(): return lax.ppermute(value, axes, [(p, p ^ mask) for p in range(count)])  12 us
    pallas_call x4, Pallas kernels, histogram_part(): pl.pallas_call(functools.partial(histogram_kernel, first, groups), out_sh...  8.88 us
    pallas_call x1, Pallas kernels, pair_terms(): pl.pallas_call(functools.partial(pairs_kernel, feat_count), out_shape=(ja...  8.84 us
    ppermute x7, waiting for transfers between devices, swap(): return lax.ppermute(value, axes, [(p, p ^ mask) for p in range(count)])  8.1 us
    ppermute x2, starting transfers between devices, local(): lax.ppermute(own_scores, 'feat', links + [(b, a) for a, b in links])  3.74 us
    pallas_call x1, Pallas kernels, prepare(): pl.pallas_call(functools.partial(prepare_kernel, feat_count, masks), out_...  2.09 us
    unnamed x12, local copies, waits for them, and re-layouts  1.36 us
  transfers between devices with their start and end apart: 9, of which 4 were waited for; matrix products, arithmetic and copies ran while one was open for 0% of the time, Pallas kernels for 19%

profile of v5, /device:TPU:0, one launch (start us, length us, event | category | flops | bytes accessed | tf_op | source)
XLA Modules:
  0.0 47.2 jit_solution(2012852226142486976)
XLA Ops:
  0.6 0.0 copy-start.2
  0.6 3.1 %collective-permute-start = (f32[8,128]{1,0:T(8,128)}, f32[8,128]{1,0:T(8,128)S(1)}, u32[]{:S(2)}, u32[]{:S(2)}) collective-permute-start(f32[8,128]{1,0:T(8,128)} %bitcast.10), channel_id=1, source_target_pairs={{0,1},{2,3},{1,0},{3,2},{4,5},{6,7},{5,4},{7,6},{8,9},{10,11},{9,8... | collective-permute-start | bytes 12296 | tf_op jit(solution)/shard_map/ppermute | solution.py:494
  3.7 0.6 %collective-permute-start.1 = (f32[8,128]{1,0:T(8,128)}, f32[8,128]{1,0:T(8,128)S(1)}, u32[]{:S(2)}, u32[]{:S(2)}) collective-permute-start(f32[8,128]{1,0:T(8,128)} %bitcast.11), channel_id=1, source_target_pairs={{1,2},{2,1},{5,6},{6,5},{9,10},{10,9},{13,14},{14,13},{17,18},{18,... | collective-permute-start | bytes 12296 | tf_op jit(solution)/shard_map/ppermute | solution.py:494
  4.4 0.0 copy-start.3
  4.4 0.6 %copy-done.3 = f32[1024]{0:T(1024)S(1)} copy-done((f32[1024]{0:T(1024)S(1)}, f32[1024]{0:T(1024)}, u32[]{:S(2)}) %copy-start.3) | copy-done | bytes 4120
  5.1 0.0 copy-done.1
  5.1 0.7 %copy-done.4 = s32[256]{0:T(256)S(1)} copy-done((s32[256]{0:T(256)S(1)}, s32[256]{0:T(256)}, u32[]{:S(2)}) %copy-start.4) | copy-done | bytes 1048
  5.8 2.1 %prepare.1 = (f32[8,128]{1,0:T(8,128)S(1)}, s32[32,128]{1,0:T(8,128)S(1)}, f32[32,128]{1,0:T(8,128)S(1)}, f32[1,1024]{1,0:T(1,128)S(1)}, bf16[256,256]{1,0:T(8,1...) custom-call(s32[1,16]{1,0:T(1,128)S(1)} %copy-done.5, s32[1]{0:T(128)} %bitcast.pos_ref, ...), custom_call_target="tpu_custom_call" | custom-call | flops 50000000 | bytes 3000000 | tf_op jit(solution)/shard_map/prepare/pallas_call | solution.py:124
  7.9 0.0 collective-permute-done.refs_1_
  7.9 0.0 collective-permute-done.1.refs_2_
  7.9 0.0 copy-start
  7.9 8.8 %pair_terms.1 = (f32[2,1024]{1,0:T(2,128)}, bf16[32,1024]{1,0:T(8,128)(2,1)S(1)}, f32[8,256]{1,0:T(8,128)S(1)}) custom-call(s32[3,32]{1,0:T(4,128)S(1)} %get-tuple-element.22.bounds_ref, s32[1]{0:T(128)} %bitcast.pos_ref, f32[8,128]{1,0:T(8,128)S(1)} %get-tuple-element.23.refs_0_, f32[8,128]{1,0:T(8,128)S(1)} %collective-permute-done.refs_1_, ...), custom_call_target="tpu_custom_call" | custom-call | flops 40000000 | bytes 200000 | tf_op jit(solution)/shard_map/pair_terms/pallas_call | solution.py:334
  16.8 0.3 order_bins.1.bins_ref
  17.1 2.2 %histogram_part.5 = f32[200,256]{1,0:T(8,128)S(1)} custom-call(bf16[32,1024]{1,0:T(8,128)(2,1)S(1)} %get-tuple-element.35.tile_ref, f32[256,1024]{1,0:T(8,128)S(1)} %order_bins.1.bins_ref, f32[8,256]{1,0:T(8,128)S(1)} %get-tuple-element.34.refs_0_), custom_call_target="tpu_custom_call" | custom-call | flops 2640000000 | bytes 480000 | tf_op jit(solution)/shard_map/histogram_part/pallas_call | solution.py:411
  19.3 0.1 collective-permute-start.2
  19.4 2.2 %histogram_part.4 = f32[192,256]{1,0:T(8,128)S(1)} custom-call(bf16[32,1024]{1,0:T(8,128)(2,1)S(1)} %get-tuple-element.35.tile_ref, f32[256,1024]{1,0:T(8,128)S(1)} %order_bins.1.bins_ref), custom_call_target="tpu_custom_call" | custom-call | flops 2640000000 | bytes 480000 | tf_op jit(solution)/shard_map/histogram_part/pallas_call | solution.py:411
  21.6 0.0 collective-permute-done.2
  21.7 1.7 %collective-permute-start.4 = (f32[200,256]{1,0:T(8,128)S(1)}, f32[200,256]{1,0:T(8,128)S(1)}, u32[]{:S(2)}, u32[]{:S(2)}) collective-permute-start(f32[200,256]{1,0:T(8,128)S(1)} %pad_maximum_fusion), channel_id=1, source_target_pairs={{0,8},{1,9},{2,10},{3,11},{4,12},{5,13},{6,14},{7,15},{8,0},{9,1},... | collective-permute-start | bytes 614408 | tf_op jit(solution)/shard_map/ppermute | solution.py:486
  23.4 2.2 %histogram_part.7 = f32[192,256]{1,0:T(8,128)S(1)} custom-call(bf16[32,1024]{1,0:T(8,128)(2,1)S(1)} %get-tuple-element.35.tile_ref, f32[256,1024]{1,0:T(8,128)S(1)} %order_bins.1.bins_ref), custom_call_target="tpu_custom_call" | custom-call | flops 2640000000 | bytes 480000 | tf_op jit(solution)/shard_map/histogram_part/pallas_call | solution.py:411
  25.6 0.3 collective-permute-start.3
  25.9 2.2 %histogram_part.6 = f32[192,256]{1,0:T(8,128)S(1)} custom-call(bf16[32,1024]{1,0:T(8,128)(2,1)S(1)} %get-tuple-element.35.tile_ref, f32[256,1024]{1,0:T(8,128)S(1)} %order_bins.1.bins_ref), custom_call_target="tpu_custom_call" | custom-call | flops 2640000000 | bytes 480000 | tf_op jit(solution)/shard_map/histogram_part/pallas_call | solution.py:411
  28.1 0.0 collective-permute-done.3
  28.1 1.1 %collective-permute-done.4 = f32[200,256]{1,0:T(8,128)S(1)} collective-permute-done((f32[200,256]{1,0:T(8,128)S(1)}, f32[200,256]{1,0:T(8,128)S(1)}, u32[]{:S(2)}, u32[]{:S(2)}) %collective-permute-start.4) | collective-permute-done | bytes 204832 | tf_op jit(solution)/shard_map/ppermute | solution.py:486
  29.3 1.1 %collective-permute-start.5 = (f32[104,256]{1,0:T(8,128)S(1)}, f32[104,256]{1,0:T(8,128)S(1)}, u32[]{:S(2)}, u32[]{:S(2)}) collective-permute-start(f32[104,256]{1,0:T(8,128)S(1)} %pad_maximum_fusion.1), channel_id=1, source_target_pairs={{0,16},{1,17},{2,18},{3,19},{4,20},{5,21},{6,22},{7,23},{8,24},{9,... | collective-permute-start | bytes 319496 | tf_op jit(solution)/shard_map/ppermute | solution.py:486
  30.4 3.7 %collective-permute-done.5 = f32[104,256]{1,0:T(8,128)S(1)} collective-permute-done((f32[104,256]{1,0:T(8,128)S(1)}, f32[104,256]{1,0:T(8,128)S(1)}, u32[]{:S(2)}, u32[]{:S(2)}) %collective-permute-start.5) | collective-permute-done | bytes 106528 | tf_op jit(solution)/shard_map/ppermute | solution.py:486
  34.2 6.4 %collective-permute-start.6 = (f32[32,256]{1,0:T(8,128)S(1)}, f32[32,256]{1,0:T(8,128)S(1)}, u32[]{:S(2)}, u32[]{:S(2)}) collective-permute-start(f32[32,256]{1,0:T(8,128)S(1)} %get-tuple-element.46), channel_id=1, source_target_pairs={{0,1},{1,0},{2,3},{3,2},{4,5},{5,4},{6,7},{7,6},{8,9},{9,8},{10,11... | collective-permute-start | bytes 98312 | tf_op jit(solution)/shard_map/ppermute | solution.py:486
  40.6 0.0 collective-permute-start.7
  40.6 2.4 %collective-permute-start.8 = (f32[32,256]{1,0:T(8,128)S(1)}, f32[32,256]{1,0:T(8,128)S(1)}, u32[]{:S(2)}, u32[]{:S(2)}) collective-permute-start(f32[32,256]{1,0:T(8,128)S(1)} %get-tuple-element.44), channel_id=1, source_target_pairs={{0,3},{1,2},{2,1},{3,0},{4,7},{5,6},{6,5},{7,4},{8,11},{9,10},{10,... | collective-permute-start | bytes 98312 | tf_op jit(solution)/shard_map/ppermute | solution.py:486
  43.0 0.0 collective-permute-done.6.refs_0_
  43.0 2.4 %collective-permute-done.7.refs_1_ = f32[32,256]{1,0:T(8,128)S(1)} collective-permute-done((f32[32,256]{1,0:T(8,128)S(1)}, f32[32,256]{1,0:T(8,128)S(1)}, u32[]{:S(2)}, u32[]{:S(2)}) %collective-permute-start.7) | collective-permute-done | bytes 32800 | tf_op jit(solution)/shard_map/ppermute | solution.py:486
  45.4 0.9 %collective-permute-done.8.refs_2_ = f32[32,256]{1,0:T(8,128)S(1)} collective-permute-done((f32[32,256]{1,0:T(8,128)S(1)}, f32[32,256]{1,0:T(8,128)S(1)}, u32[]{:S(2)}, u32[]{:S(2)}) %collective-permute-start.8) | collective-permute-done | bytes 32800 | tf_op jit(solution)/shard_map/ppermute | solution.py:486
  46.3 0.9 %finish.1 = (f32[8,128]{1,0:T(8,128)}, f32[8,128]{1,0:T(8,128)}, f32[3,2048]{1,0:T(4,128)}) custom-call(s32[8,128]{1,0:T(8,128)S(1)} %bitcast.8, f32[24,256]{1,0:T(8,128)S(1)} %get-tuple-element.43.kept_ref, f32[8,256]{1,0:T(8,128)S(1)} %slice_add_fusion.3.sums_ref, f32[32,256]{1,0:T(8,128)S(1)} %collective-permute-done.6.refs_0_, ...), custom_call_target="tpu_custom_call" | custom-call | tf_op jit(solution)/shard_map/finish/pallas_call | solution.py:451
  (17 shorter events, 0.2 us)
Async XLA Ops:
  0.6 3.8 %copy-start.2 = (s32[4096]{0:T(1024)S(1)}, s32[4096]{0:T(1024)}, u32[]{:S(2)}) copy-start(s32[4096]{0:T(1024)} %param.7) | copy-start | bytes 49156
  0.6 7.2 %collective-permute-start = (f32[8,128]{1,0:T(8,128)}, f32[8,128]{1,0:T(8,128)S(1)}, u32[]{:S(2)}, u32[]{:S(2)}) collective-permute-start(f32[8,128]{1,0:T(8,128)} %bitcast.10), channel_id=1, source_target_pairs={{0,1},{2,3},{1,0},{3,2},{4,5},{6,7},{5,4},{7,6},{8,9},{10,11},{9,8... | collective-permute-start | bytes 12296 | tf_op jit(solution)/shard_map/ppermute | solution.py:494
  3.7 4.2 %collective-permute-start.1 = (f32[8,128]{1,0:T(8,128)}, f32[8,128]{1,0:T(8,128)S(1)}, u32[]{:S(2)}, u32[]{:S(2)}) collective-permute-start(f32[8,128]{1,0:T(8,128)} %bitcast.11), channel_id=1, source_target_pairs={{1,2},{2,1},{5,6},{6,5},{9,10},{10,9},{13,14},{14,13},{17,18},{18,... | collective-permute-start | bytes 12296 | tf_op jit(solution)/shard_map/ppermute | solution.py:494
  4.4 0.7 %copy-start.3 = (f32[1024]{0:T(1024)S(1)}, f32[1024]{0:T(1024)}, u32[]{:S(2)}) copy-start(f32[1024]{0:T(1024)} %param.6) | copy-start | bytes 12292
  4.4 0.7 %copy-start.1 = (s32[1024]{0:T(1024)S(1)}, s32[1024]{0:T(1024)}, u32[]{:S(2)}) copy-start(s32[1024]{0:T(1024)} %param.8) | copy-start | bytes 12292
  4.4 0.7 %copy-start.5 = (s32[1,16]{1,0:T(1,128)S(1)}, s32[1,16]{1,0:T(1,128)}, u32[]{:S(2)}) copy-start(s32[1,16]{1,0:T(1,128)} %len_ref.1) | copy-start | bytes 196
  5.1 0.7 %copy-start.4 = (s32[256]{0:T(256)S(1)}, s32[256]{0:T(256)}, u32[]{:S(2)}) copy-start(s32[256]{0:T(256)} %param.11) | copy-start | bytes 3076
  7.9 8.9 %copy-start = (s32[1024,256]{1,0:T(8,128)S(1)}, s32[1024,256]{1,0:T(8,128)}, u32[]{:S(2)}) copy-start(s32[1024,256]{1,0:T(8,128)} %bins_ref.1) | copy-start | bytes 3145732
  19.3 2.3 %collective-permute-start.2 = (f32[200,256]{1,0:T(8,128)S(1)}, f32[200,256]{1,0:T(8,128)S(1)}, u32[]{:S(2)}, u32[]{:S(2)}) collective-permute-start(f32[200,256]{1,0:T(8,128)S(1)} %histogram_part.5), channel_id=1, source_target_pairs={{0,4},{1,5},{2,6},{3,7},{4,0},{5,1},{6,2},{7,3},{8,12},{9,13},{10,... | collective-permute-start | bytes 614408 | tf_op jit(solution)/shard_map/ppermute | solution.py:486
  21.7 7.5 %collective-permute-start.4 = (f32[200,256]{1,0:T(8,128)S(1)}, f32[200,256]{1,0:T(8,128)S(1)}, u32[]{:S(2)}, u32[]{:S(2)}) collective-permute-start(f32[200,256]{1,0:T(8,128)S(1)} %pad_maximum_fusion), channel_id=1, source_target_pairs={{0,8},{1,9},{2,10},{3,11},{4,12},{5,13},{6,14},{7,15},{8,0},{9,1},... | collective-permute-start | bytes 614408 | tf_op jit(solution)/shard_map/ppermute | solution.py:486
  25.6 2.5 %collective-permute-start.3 = (f32[192,256]{1,0:T(8,128)S(1)}, f32[192,256]{1,0:T(8,128)S(1)}, u32[]{:S(2)}, u32[]{:S(2)}) collective-permute-start(f32[192,256]{1,0:T(8,128)S(1)} %histogram_part.7), channel_id=1, source_target_pairs={{0,4},{1,5},{2,6},{3,7},{4,0},{5,1},{6,2},{7,3},{8,12},{9,13},{10,... | collective-permute-start | bytes 589832 | tf_op jit(solution)/shard_map/ppermute | solution.py:486
  29.3 4.8 %collective-permute-start.5 = (f32[104,256]{1,0:T(8,128)S(1)}, f32[104,256]{1,0:T(8,128)S(1)}, u32[]{:S(2)}, u32[]{:S(2)}) collective-permute-start(f32[104,256]{1,0:T(8,128)S(1)} %pad_maximum_fusion.1), channel_id=1, source_target_pairs={{0,16},{1,17},{2,18},{3,19},{4,20},{5,21},{6,22},{7,23},{8,24},{9,... | collective-permute-start | bytes 319496 | tf_op jit(solution)/shard_map/ppermute | solution.py:486
  34.2 8.9 %collective-permute-start.6 = (f32[32,256]{1,0:T(8,128)S(1)}, f32[32,256]{1,0:T(8,128)S(1)}, u32[]{:S(2)}, u32[]{:S(2)}) collective-permute-start(f32[32,256]{1,0:T(8,128)S(1)} %get-tuple-element.46), channel_id=1, source_target_pairs={{0,1},{1,0},{2,3},{3,2},{4,5},{5,4},{6,7},{7,6},{8,9},{9,8},{10,11... | collective-permute-start | bytes 98312 | tf_op jit(solution)/shard_map/ppermute | solution.py:486
  40.6 4.8 %collective-permute-start.7 = (f32[32,256]{1,0:T(8,128)S(1)}, f32[32,256]{1,0:T(8,128)S(1)}, u32[]{:S(2)}, u32[]{:S(2)}) collective-permute-start(f32[32,256]{1,0:T(8,128)S(1)} %get-tuple-element.45), channel_id=1, source_target_pairs={{0,2},{1,3},{2,0},{3,1},{4,6},{5,7},{6,4},{7,5},{8,10},{9,11},{10,... | collective-permute-start | bytes 98312 | tf_op jit(solution)/shard_map/ppermute | solution.py:486
  40.6 5.7 %collective-permute-start.8 = (f32[32,256]{1,0:T(8,128)S(1)}, f32[32,256]{1,0:T(8,128)S(1)}, u32[]{:S(2)}, u32[]{:S(2)}) collective-permute-start(f32[32,256]{1,0:T(8,128)S(1)} %get-tuple-element.44), channel_id=1, source_target_pairs={{0,3},{1,2},{2,1},{3,0},{4,7},{5,6},{6,5},{7,4},{8,11},{9,10},{10,... | collective-permute-start | bytes 98312 | tf_op jit(solution)/shard_map/ppermute | solution.py:486

commit v6 on v5

--- a/solution.py
+++ b/solution.py
@@ -39,13 +39,12 @@
     return pl.BlockSpec(memory_space=pltpu.SMEM)
 
 
-def prepare_kernel(feat_count, masks, len_ref, pos_ref, lab_ref, owner_ref, leaf_ref, score_ref,
-                   kept_ref, qid_ref, worth_ref, inv_ref, perm_ref, spot_ref, top_ref, bounds_ref):
+def prepare_kernel(feat_count, masks, len_ref, pos_ref, lab_ref, owner_ref, score_ref,
+                   kept_ref, qid_ref, worth_ref, inv_ref, perm_ref, bounds_ref):
+    kept_ref[...] = score_ref[...]
     queries = len_ref.shape[1]
     rows = lab_ref.shape[0]
-    own = leaf_ref.shape[0]
-    docs = own * LANES
-    kept_ref[...] = score_ref[...]
+    own = rows // feat_count
     spot = iota((rows, LANES), 0) * LANES + iota((rows, LANES), 1)
     qid = jnp.zeros((rows, LANES), jnp.int32)
     begin = jnp.zeros((queries, LANES), jnp.int32)
@@ -110,16 +109,9 @@
     holds = jnp.where(jnp.broadcast_to(owner, square) == down, 1.0, 0.0).astype(BF16)
     perm_ref[...] = lax.dot_general(pick, holds, NT, preferred_element_type=F32).astype(BF16)
 
-    leaf = jnp.concatenate([leaf_ref[t:t + 1, :] for t in range(own)], axis=1)
-    highs = LEAVES // LANES
-    top_ref[...] = jnp.where(jnp.broadcast_to(leaf // LANES, (highs, docs)) == iota((highs, docs), 0), 1.0, 0.0)
-    spot_ref[...] = jnp.where(
-        jnp.broadcast_to(leaf % LANES, (LANES, docs)) == iota((LANES, docs), 0), 1.0, 0.0).astype(BF16)
-
-
-def prepare(feat_count, masks, lengths, pos, labels, owner, leaves, scores):
+
+def prepare(feat_count, masks, lengths, pos, labels, owner, scores):
     rows = labels.shape[0]
-    docs = leaves.shape[0] * LANES
     features = owner.shape[0] * LANES
     return pl.pallas_call(
         functools.partial(prepare_kernel, feat_count, masks),
@@ -127,36 +119,16 @@
             jax.ShapeDtypeStruct(scores.shape, F32),
             jax.ShapeDtypeStruct((rows, LANES), jnp.int32),
             jax.ShapeDtypeStruct((rows, LANES), F32),
-            jax.ShapeDtypeStruct((1, docs), F32),
+            jax.ShapeDtypeStruct((1, rows // feat_count * LANES), F32),
             jax.ShapeDtypeStruct((features, features), BF16),
-            jax.ShapeDtypeStruct((LANES, docs), BF16),
-            jax.ShapeDtypeStruct((LEAVES // LANES, docs), F32),
             jax.ShapeDtypeStruct((3, rows), jnp.int32),
         ),
-        in_specs=[smem(), smem()] + [vmem()] * 4,
-        out_specs=(vmem(),) * 7 + (smem(),),
+        in_specs=[smem(), smem(), vmem(), vmem(), vmem()],
+        out_specs=(vmem(),) * 5 + (smem(),),
         compiler_params=pltpu.CompilerParams(vmem_limit_bytes=VMEM_LIMIT),
-        cost_estimate=pl.CostEstimate(flops=50_000_000, bytes_accessed=3_000_000, transcendentals=20_000),
+        cost_estimate=pl.CostEstimate(flops=2_000_000_000, bytes_accessed=300_000, transcendentals=20_000),
         name="prepare",
-    )(lengths, pos, labels, owner, leaves, scores)
-
-
-def order_kernel(perm_ref, bins_ref, out_ref):
-    bins = bins_ref[...].astype(F32).astype(BF16)
-    out_ref[...] = lax.dot_general(perm_ref[...], bins, NT, preferred_element_type=F32)
-
-
-def order_bins(perm, bins):
-    docs, features = bins.shape
-    return pl.pallas_call(
-        order_kernel,
-        out_shape=jax.ShapeDtypeStruct((features, docs), F32),
-        in_specs=[vmem(), vmem()],
-        out_specs=vmem(),
-        compiler_params=pltpu.CompilerParams(vmem_limit_bytes=VMEM_LIMIT),
-        cost_estimate=pl.CostEstimate(flops=200_000_000, bytes_accessed=3_000_000, transcendentals=0),
-        name="order_bins",
-    )(perm, bins)
+    )(lengths, pos, labels, owner, scores)
 
 
 def split_terms(value, terms):
@@ -169,23 +141,10 @@
     return parts
 
 
-def widen(ref, source):
-    turned = jnp.transpose(source)
-    for r in range(source.shape[0]):
-        ref[r * LANES:(r + 1) * LANES, :] = jnp.broadcast_to(turned[:, r:r + 1], (LANES, LANES))
-
-
-def lane_sums(source):
-    parts = split_terms(source, 3)
-    ones = jnp.ones((8, 2 * LANES), BF16)
-    wide = lax.dot_general(ones, jnp.concatenate(parts[:2], axis=1), NT, preferred_element_type=F32)
-    return (wide + lax.dot_general(ones[:, :LANES], parts[2], NT, preferred_element_type=F32))[0:1, :]
-
-
 def pairs_kernel(feat_count, bounds_ref, pos_ref, *refs):
-    scores = refs[:-21]
-    (worth_ref, qid_ref, inv_ref, spot_ref, top_ref, lam_ref, tile_ref, sums_ref,
-     s_row, a_row, d_row, w_row, q_row, s_turn, q_turn, s_col, q_col, a_own, w_own, d_own, sums_own) = refs[-21:]
+    scores = refs[:-20]
+    (worth_ref, qid_ref, inv_ref, lam_ref, near_ref,
+     s_row, a_row, d_row, s_turn, a_turn, w_turn, q_turn, d_turn, s_col, a_col, w_col, q_col, d_col, grad, curv) = refs[-20:]
     rows = worth_ref.shape[0]
     own = rows // feat_count
     docs = own * LANES
@@ -198,30 +157,36 @@
             s_row[pl.ds(pl.multiple_of(where * own, own), own), :] = ref[...]
     a_row[...] = jnp.exp(s_row[...])
     d_row[...] = jnp.zeros(d_row.shape, F32)
-    w_row[0:rows, :] = worth_ref[...]
-    w_row[rows:, :] = jnp.zeros((8, LANES), F32)
-    q_row[0:rows, :] = qid_ref[...]
-    q_row[rows:, :] = jnp.full((8, LANES), -1, jnp.int32)
-    first = pl.multiple_of(me * own, own)
+    first = me * own
     window_low = bounds_ref[0, first] // LANES
     window_high = (bounds_ref[1, first + own - 1] + LANES - 1) // LANES
-    s_turn[...] = jnp.transpose(s_row[0:rows, :])
-    q_turn[...] = jnp.transpose(qid_ref[...])
-    for r in range(rows):
-        @pl.when((r >= window_low) & (r < window_high))
-        def _(r=r):
-            at = slice(r * LANES, (r + 1) * LANES)
-            s_col[at, :] = jnp.broadcast_to(s_turn[:, r:r + 1], (LANES, LANES))
-            q_col[at, :] = jnp.broadcast_to(q_turn[:, r:r + 1], (LANES, LANES))
-    widen(a_own, a_row[pl.ds(first, own), :])
-    widen(w_own, w_row[pl.ds(first, own), :])
+
+    def widen(pairs):
+        for turn, source, _ in pairs:
+            turn[...] = jnp.transpose(source[...])
+        for r in range(rows):
+            @pl.when((r >= window_low) & (r < window_high))
+            def _(r=r):
+                for turn, _, col in pairs:
+                    col[r * LANES:(r + 1) * LANES, :] = jnp.broadcast_to(turn[:, r:r + 1], (LANES, LANES))
+
+    widen([(s_turn, s_row, s_col), (q_turn, qid_ref, q_col), (a_turn, a_row, a_col), (w_turn, worth_ref, w_col)])
 
     def row_of(ref, r):
         return jnp.broadcast_to(ref[pl.ds(r, 1), :], (8, LANES))
 
+    def spans(r):
+        start, end = bounds_ref[0, r], bounds_ref[1, r]
+        low = jnp.maximum(start // LANES, window_low)
+        high = jnp.minimum((end + LANES - 1) // LANES, window_high)
+        single = bounds_ref[2, r] >= (r + 1) * LANES
+        inner_low = jnp.where(single, jnp.maximum((start + LANES - 1) // LANES, window_low), r)
+        inner_high = jnp.where(single, jnp.minimum(end // LANES, window_high), r)
+        return low, inner_low, inner_high, high
+
     def rank_group(r, carry):
         score = row_of(s_row, r)
-        query = row_of(q_row, r)
+        query = row_of(qid_ref, r)
 
         def sweep(ahead, masked):
             def step(c, acc):
@@ -237,16 +202,12 @@
             return step
 
         acc = tuple(jnp.zeros((8, LANES), F32) for _ in range(4))
-        start, end = bounds_ref[0, r], bounds_ref[1, r]
-        low = jnp.maximum(start // LANES, window_low)
-        high = jnp.minimum((end + LANES - 1) // LANES, window_high)
-        single = bounds_ref[2, r] >= (r + 1) * LANES
-        inner_low = jnp.where(single, jnp.maximum((start + LANES - 1) // LANES, window_low), r)
-        inner_high = jnp.where(single, jnp.minimum(end // LANES, window_high), r + 1)
+        low, inner_low, inner_high, high = spans(r)
+        after = jnp.maximum(inner_high, r + 1)
         acc = lax.fori_loop(low, inner_low, sweep(True, True), acc)
         acc = lax.fori_loop(inner_low, r, sweep(True, False), acc)
-        acc = lax.fori_loop(r + 1, inner_high, sweep(False, False), acc)
-        acc = list(lax.fori_loop(inner_high, high, sweep(False, True), acc))
+        acc = lax.fori_loop(r + 1, after, sweep(False, False), acc)
+        acc = list(lax.fori_loop(after, high, sweep(False, True), acc))
         base = pl.multiple_of(r * LANES, LANES)
         for u in range(LANES // 8):
             other = s_col[pl.ds(base + 8 * u, 8), :]
@@ -260,64 +221,87 @@
 
     lax.fori_loop(window_low, window_high, rank_group, 0)
     d_row[...] = 1.0 / jnp.log2(2.0 + d_row[...])
-    widen(d_own, d_row[pl.ds(first, own), :])
-
-    def pair_block(b, carry):
-        base = pl.multiple_of(b * CHUNK, CHUNK)
-        r = first + b // (LANES // CHUNK)
-        count = CHUNK // 8
-        queries = pl.multiple_of(first * LANES + base, CHUNK)
-
-        def columns(width):
+    widen([(d_turn, d_row, d_col)])
+
+    def pair_group(t, carry):
+        r = first + t
+        a_i, w_i, d_i = row_of(a_row, r), row_of(worth_ref, r), row_of(d_row, r)
+        query = row_of(qid_ref, r)
+
+        def columns(masked):
             def step(c, acc):
+                base = pl.multiple_of(c * LANES, LANES)
                 acc = list(acc)
-                other = []
-                for k in range(width):
-                    at = (r_low + width * c + k) if width > 1 else c
-                    other.append([row_of(ref, at) for ref in (a_row, w_row, d_row, q_row)])
-                for u in range(count):
+                for u in range(LANES // 8):
                     at = pl.ds(base + 8 * u, 8)
-                    a_i, w_i, d_i = a_own[at, :], w_own[at, :], d_own[at, :]
-                    q_i = q_col[pl.ds(queries + 8 * u, 8), :]
-                    for a_j, w_j, d_j, q_j in other:
-                        recip = pl.reciprocal(a_i + a_j, approx=True)
-                        lift = w_i - w_j
-                        weight = jnp.where(q_i == q_j, jnp.abs(d_i - d_j) * recip, 0.0) * lift
-                        acc[u] = acc[u] + weight * jnp.where(lift > 0.0, a_j, a_i)
-                        acc[count + u] = acc[count + u] + jnp.abs(weight) * (recip * a_j)
+                    a_j = a_col[at, :]
+                    recip = pl.reciprocal(a_i + a_j, approx=True)
+                    lift = w_i - w_col[at, :]
+                    weight = jnp.abs(d_i - d_col[at, :]) * recip
+                    if masked:
+                        weight = jnp.where(q_col[at, :] == query, weight, 0.0)
+                    weight = weight * lift
+                    acc[u % 2] = acc[u % 2] + weight * jnp.where(lift > 0.0, a_j, a_i)
+                    acc[2 + u % 2] = acc[2 + u % 2] + jnp.abs(weight) * (recip * a_j)
                 return tuple(acc)
             return step
 
-        acc = tuple(jnp.zeros((8, LANES), F32) for _ in range(2 * count))
-        r_low = bounds_ref[0, r] // LANES
-        r_high = (bounds_ref[1, r] + LANES - 1) // LANES
-        twos = (r_high - r_low) // 2
-        acc = lax.fori_loop(0, twos, columns(2), acc)
-        acc = lax.fori_loop(r_low + 2 * twos, r_high, columns(1), acc)
-        for u in range(count):
-            sums_own[pl.ds(base + 8 * u, 8), :] = acc[u]
-            sums_own[pl.ds(docs + base + 8 * u, 8), :] = acc[count + u]
+        acc = tuple(jnp.zeros((8, LANES), F32) for _ in range(4))
+        low, inner_low, inner_high, high = spans(r)
+        acc = lax.fori_loop(low, inner_low, columns(True), acc)
+        acc = lax.fori_loop(inner_low, inner_high, columns(False), acc)
+        acc = lax.fori_loop(inner_high, high, columns(True), acc)
+        grad[pl.ds(t, 1), :] = -jnp.sum(acc[0] + acc[1], axis=0, keepdims=True)
+        curv[pl.ds(t, 1), :] = a_row[pl.ds(r, 1), :] * jnp.sum(acc[2] + acc[3], axis=0, keepdims=True)
         return carry
 
-    lax.fori_loop(0, docs // CHUNK, pair_block, 0)
-    totals = lane_sums(sums_own[...])
+    lax.fori_loop(0, own, pair_group, 0)
     inverse = inv_ref[...]
-    a_line = jnp.concatenate([a_row[pl.ds(first + t, 1), :] for t in range(own)], axis=1)
-    terms = [-inverse * totals[:, :docs], inverse * a_line * totals[:, docs:]]
-
+    terms = [inverse * jnp.concatenate([ref[t:t + 1, :] for t in range(own)], axis=1) for ref in (grad, curv)]
+    for c in range(2):
+        lam_ref[c:c + 1, :] = terms[c]
+        near_ref[c:c + 1, :] = terms[c]
+
+
+def pair_terms(feat_count, bounds, pos, scores, worth, qid, inverse):
+    rows = worth.shape[0]
+    docs = inverse.shape[1]
+    row = pltpu.VMEM((rows, LANES), F32)
+    turn = pltpu.VMEM((LANES, rows), F32)
+    col = pltpu.VMEM((rows * LANES, LANES), F32)
+    mine = pltpu.VMEM((docs // LANES, LANES), F32)
+    return pl.pallas_call(
+        functools.partial(pairs_kernel, feat_count),
+        out_shape=(jax.ShapeDtypeStruct((2, docs), F32), jax.ShapeDtypeStruct((2, docs), F32)),
+        in_specs=[smem(), smem()] + [vmem()] * (len(scores) + 3),
+        out_specs=(vmem(), vmem()),
+        scratch_shapes=[row, row, row, turn, turn, turn, pltpu.VMEM((LANES, rows), jnp.int32), turn,
+                        col, col, col, pltpu.VMEM((rows * LANES, LANES), jnp.int32), col, mine, mine],
+        compiler_params=pltpu.CompilerParams(vmem_limit_bytes=VMEM_LIMIT),
+        cost_estimate=pl.CostEstimate(flops=9_000_000_000, bytes_accessed=200_000, transcendentals=2_000_000),
+        name="pair_terms",
+    )(bounds, pos, *scores, worth, qid, inverse)
+
+
+def leaf_kernel(perm_ref, bins_ref, leaf_ref, lam_ref, bins_t_ref, tile_ref, sums_ref):
+    bins = bins_ref[...].astype(F32).astype(BF16)
+    bins_t_ref[...] = lax.dot_general(perm_ref[...], bins, NT, preferred_element_type=F32)
+    own = leaf_ref.shape[0]
+    docs = own * LANES
+    leaf = jnp.concatenate([leaf_ref[t:t + 1, :] for t in range(own)], axis=1)
     highs = LEAVES // LANES
-    top = top_ref[...] > 0.0
+    top = jnp.broadcast_to(leaf // LANES, (highs, docs)) == iota((highs, docs), 0)
+    spots = jnp.where(jnp.broadcast_to(leaf % LANES, (LANES, docs)) == iota((LANES, docs), 0), 1.0, 0.0).astype(BF16)
     pieces, tiles = [], []
     for c in range(2):
-        lam_ref[c:c + 1, :] = terms[c]
-        for k, part in enumerate(split_terms(terms[c], 3)):
+        for k, part in enumerate(split_terms(lam_ref[c:c + 1, :], 3)):
             wide = jnp.broadcast_to(part.astype(F32), (highs, docs))
             pieces.append(jnp.where(top, wide, 0.0))
             if k < 2:
                 tiles.append(wide)
     tile_ref[...] = jnp.concatenate(tiles, axis=0).astype(BF16)
     stacked = jnp.concatenate(pieces, axis=0).astype(BF16)
-    sums = lax.dot_general(stacked, spot_ref[...], NT, preferred_element_type=F32)
+    sums = lax.dot_general(stacked, spots, NT, preferred_element_type=F32)
     for c in range(2):
         base = c * 3 * highs
         sums_ref[:, c * LANES:(c + 1) * LANES] = (
@@ -325,29 +309,21 @@
         )
 
 
-def pair_terms(feat_count, bounds, pos, scores, worth, qid, inverse, spots, top):
-    rows = worth.shape[0]
-    docs = inverse.shape[1]
-    highs = LEAVES // LANES
-    row = pltpu.VMEM((rows + 8, LANES), F32)
-    mine = pltpu.VMEM((docs, LANES), F32)
+def leaf_terms(perm, bins, leaves, lambdas):
+    docs, features = bins.shape
     return pl.pallas_call(
-        functools.partial(pairs_kernel, feat_count),
+        leaf_kernel,
         out_shape=(
-            jax.ShapeDtypeStruct((2, docs), F32),
+            jax.ShapeDtypeStruct((features, docs), F32),
             jax.ShapeDtypeStruct((4 * HIGH, docs), BF16),
-            jax.ShapeDtypeStruct((highs, 2 * LANES), F32),
+            jax.ShapeDtypeStruct((LEAVES // LANES, 2 * LANES), F32),
         ),
-        in_specs=[smem(), smem()] + [vmem()] * (len(scores) + 5),
+        in_specs=[vmem()] * 4,
         out_specs=(vmem(), vmem(), vmem()),
-        scratch_shapes=[row, row, row, row, pltpu.VMEM((rows + 8, LANES), jnp.int32),
-                        pltpu.VMEM((LANES, rows), F32), pltpu.VMEM((LANES, rows), jnp.int32),
-                        pltpu.VMEM((rows * LANES, LANES), F32), pltpu.VMEM((rows * LANES, LANES), jnp.int32),
-                        mine, mine, mine, pltpu.VMEM((2 * docs, LANES), F32)],
         compiler_params=pltpu.CompilerParams(vmem_limit_bytes=VMEM_LIMIT),
-        cost_estimate=pl.CostEstimate(flops=40_000_000, bytes_accessed=200_000, transcendentals=2_000_000),
-        name="pair_terms",
-    )(bounds, pos, *scores, worth, qid, inverse, spots, top)
+        cost_estimate=pl.CostEstimate(flops=200_000_000, bytes_accessed=3_000_000, transcendentals=0),
+        name="leaf_terms",
+    )(perm, bins, leaves, lambdas)
 
 
 def histogram_kernel(first, groups, tile_ref, bins_ref, *refs):
@@ -492,12 +468,11 @@
     for begin in range(2):
         links = [(z, z + 1) for z in range(begin, feat_count - 1, 2)]
         score_parts.append(lax.ppermute(own_scores, "feat", links + [(b, a) for a, b in links]))
-    score_parts[0], qid, worth, inverse, perm, spots, top, bounds = prepare(
-        feat_count, feat_masks + query_masks[:0:-1] + query_masks[:1], lengths, pos, labels.reshape(-1, LANES),
-        owner.reshape(-1, LANES), leaf_rows, own_scores)
-    lambdas, tiles, sums = pair_terms(feat_count, bounds, pos, score_parts, worth, qid, inverse, spots, top)
-    perm, sums = lax.optimization_barrier((perm, sums))
-    bins_t = order_bins(perm, bins)
+    masks = feat_masks + query_masks[:0:-1] + query_masks[:1]
+    score_parts[0], qid, worth, inverse, perm, bounds = prepare(
+        feat_count, masks, lengths, pos, labels.reshape(-1, LANES), owner.reshape(-1, LANES), own_scores)
+    lambdas, near_lambdas = pair_terms(feat_count, bounds, pos, score_parts, worth, qid, inverse)
+    bins_t, tiles, sums = leaf_terms(perm, bins, leaf_rows, near_lambdas)
 
     def part(tiles, low, high, *tail):
         if per_dev == GROUP:

time: 47.6 us -> 46.9 us (0.985)
  Pallas kernels: 21 us -> 18.4 us
  starting transfers between devices: 15.7 us -> 18 us
    pallas_call x1, Pallas kernels: 8.84 us -> 6.4 us  [pair_terms(): pl.pallas_call(functools.partial(pairs_kernel, feat_count), out_shape=(ja...]
    ppermute x7, starting transfers between devices: 12 us -> 14.2 us  [swap(): return lax.ppermute(value, axes, [(p, p ^ mask) for p in range(count)])]
  transfers between devices with their start and end apart: 9 -> 9, of which waited for: 4 -> 4; matrix products, arithmetic and copies ran while one was open for 0% -> 0% of each run, Pallas kernels for 19% -> 18%
where the time goes in v6:
time: 46.9 us; the launch traced here: 46.7 us
  Pallas kernels  18.4 us (39%)
  starting transfers between devices  18 us (38%)
  waiting for transfers between devices  8.04 us (17%)
  local copies, waits for them, and re-layouts  1.37 us (3%)
  between operations  0.84 us (2%)
    ppermute x7, starting transfers between devices, swap(): return lax.ppermute(value, axes, [(p, p ^ mask) for p in range(count)])  14.2 us
    pallas_call x4, Pallas kernels, histogram_part(): pl.pallas_call(functools.partial(histogram_kernel, first, groups), out_sh...  8.86 us
    ppermute x7, waiting for transfers between devices, swap(): return lax.ppermute(value, axes, [(p, p ^ mask) for p in range(count)])  8.04 us
    pallas_call x1, Pallas kernels, pair_terms(): pl.pallas_call(functools.partial(pairs_kernel, feat_count), out_shape=(ja...  6.4 us
    ppermute x2, starting transfers between devices, local(): lax.ppermute(own_scores, 'feat', links + [(b, a) for a, b in links])  3.74 us
    pallas_call x1, Pallas kernels, prepare(): pl.pallas_call(functools.partial(prepare_kernel, feat_count, masks), out_...  1.84 us
    unnamed x12, local copies, waits for them, and re-layouts  1.36 us
  transfers between devices with their start and end apart: 9, of which 4 were waited for; matrix products, arithmetic and copies ran while one was open for 0% of the time, Pallas kernels for 18%

profile of v6, /device:TPU:0, one launch (start us, length us, event | category | flops | bytes accessed | tf_op | source)
XLA Modules:
  0.0 46.7 jit_solution(16982597598188798568)
XLA Ops:
  0.6 0.0 copy-start.2
  0.6 3.1 %collective-permute-start = (f32[8,128]{1,0:T(8,128)}, f32[8,128]{1,0:T(8,128)S(1)}, u32[]{:S(2)}, u32[]{:S(2)}) collective-permute-start(f32[8,128]{1,0:T(8,128)} %bitcast.10), channel_id=1, source_target_pairs={{0,1},{2,3},{1,0},{3,2},{4,5},{6,7},{5,4},{7,6},{8,9},{10,11},{9,8... | collective-permute-start | bytes 12296 | tf_op jit(solution)/shard_map/ppermute | solution.py:470
  3.7 0.6 %collective-permute-start.1 = (f32[8,128]{1,0:T(8,128)}, f32[8,128]{1,0:T(8,128)S(1)}, u32[]{:S(2)}, u32[]{:S(2)}) collective-permute-start(f32[8,128]{1,0:T(8,128)} %bitcast.11), channel_id=1, source_target_pairs={{1,2},{2,1},{5,6},{6,5},{9,10},{10,9},{13,14},{14,13},{17,18},{18,... | collective-permute-start | bytes 12296 | tf_op jit(solution)/shard_map/ppermute | solution.py:470
  4.4 0.0 copy-start.3
  4.4 0.6 %copy-done.3 = f32[1024]{0:T(1024)S(1)} copy-done((f32[1024]{0:T(1024)S(1)}, f32[1024]{0:T(1024)}, u32[]{:S(2)}) %copy-start.3) | copy-done | bytes 4120
  5.1 0.0 copy-done.4
  5.1 1.8 %prepare.1 = (f32[8,128]{1,0:T(8,128)S(1)}, s32[32,128]{1,0:T(8,128)S(1)}, f32[32,128]{1,0:T(8,128)S(1)}, f32[1,1024]{1,0:T(1,128)S(1)}, bf16[256,256]{1,0:T(8,128)(2,1)S(1)}, /*index=5*/s32[3,32]{1,0:T(4,128)S(1)}) custom-call(s32[1,16]{1,0:T(1,128)S(1)} %copy-done.5, s32[1]{0:T(128)} %bitcast.pos_ref, s32[32,128]{1,0:T(8,128)S(1)} %bitcast.9, ...), custom_call_target="tpu_custom_call" | custom-call | flops 2000000000 | bytes 300000 | tf_op jit(solution)/shard_map/prepare/pallas_call | solution.py:116
  6.9 0.0 collective-permute-done.refs_1_
  7.0 0.0 collective-permute-done.1.refs_2_
  7.0 0.0 copy-start
  7.0 6.4 %pair_terms.1 = (f32[2,1024]{1,0:T(2,128)}, f32[2,1024]{1,0:T(2,128)S(1)}) custom-call(s32[3,32]{1,0:T(4,128)S(1)} %get-tuple-element.20.bounds_ref, s32[1]{0:T(128)} %bitcast.pos_ref, f32[8,128]{1,0:T(8,128)S(1)} %get-tuple-element.21.refs_0_, f32[8,128]{1,0:T(8,128)S(1)} %collective-permute-done.refs_1_, f32[8,128]{1,0:T(8,128)S(1)} %collective-permute-done.1.refs_2_, ...), custom_call_target="tpu_custom_call" | custom-call | flops 8999999488 | bytes 200000 | tf_op jit(solution)/shard_map/pair_terms/pallas_call | solution.py:273
  13.4 0.7 %copy-done.1 = s32[1024]{0:T(1024)S(1)} copy-done((s32[1024]{0:T(1024)S(1)}, s32[1024]{0:T(1024)}, u32[]{:S(2)}) %copy-start.1) | copy-done | bytes 4120
  14.1 0.4 leaf_terms.1
  14.5 2.2 %histogram_part.5 = f32[200,256]{1,0:T(8,128)S(1)} custom-call(bf16[32,1024]{1,0:T(8,128)(2,1)S(1)} %get-tuple-element.31.tile_ref, f32[256,1024]{1,0:T(8,128)S(1)} %get-tuple-element.29.bins_ref, f32[8,256]{1,0:T(8,128)S(1)} %get-tuple-element.30.refs_0_), custom_call_target="tpu_custom_call" | custom-call | flops 2640000000 | bytes 480000 | tf_op jit(solution)/shard_map/histogram_part/pallas_call | solution.py:387
  16.7 0.1 collective-permute-start.2
  16.8 2.2 %histogram_part.4 = f32[192,256]{1,0:T(8,128)S(1)} custom-call(bf16[32,1024]{1,0:T(8,128)(2,1)S(1)} %get-tuple-element.31.tile_ref, f32[256,1024]{1,0:T(8,128)S(1)} %get-tuple-element.29.bins_ref), custom_call_target="tpu_custom_call" | custom-call | flops 2640000000 | bytes 480000 | tf_op jit(solution)/shard_map/histogram_part/pallas_call | solution.py:387
  19.0 0.0 collective-permute-done.2
  19.1 3.3 %collective-permute-start.4 = (f32[200,256]{1,0:T(8,128)S(1)}, f32[200,256]{1,0:T(8,128)S(1)}, u32[]{:S(2)}, u32[]{:S(2)}) collective-permute-start(f32[200,256]{1,0:T(8,128)S(1)} %pad_maximum_fusion), channel_id=1, source_target_pairs={{0,8},{1,9},{2,10},{3,11},{4,12},{5,13},{6,14},{7,15},{8,0},{9,1},... | collective-permute-start | bytes 614408 | tf_op jit(solution)/shard_map/ppermute | solution.py:462
  22.4 2.2 %histogram_part.7 = f32[192,256]{1,0:T(8,128)S(1)} custom-call(bf16[32,1024]{1,0:T(8,128)(2,1)S(1)} %get-tuple-element.31.tile_ref, f32[256,1024]{1,0:T(8,128)S(1)} %get-tuple-element.29.bins_ref), custom_call_target="tpu_custom_call" | custom-call | flops 2640000000 | bytes 480000 | tf_op jit(solution)/shard_map/histogram_part/pallas_call | solution.py:387
  24.7 0.3 collective-permute-start.3
  24.9 2.2 %histogram_part.6 = f32[192,256]{1,0:T(8,128)S(1)} custom-call(bf16[32,1024]{1,0:T(8,128)(2,1)S(1)} %get-tuple-element.31.tile_ref, f32[256,1024]{1,0:T(8,128)S(1)} %get-tuple-element.29.bins_ref), custom_call_target="tpu_custom_call" | custom-call | flops 2640000000 | bytes 480000 | tf_op jit(solution)/shard_map/histogram_part/pallas_call | solution.py:387
  27.1 0.0 collective-permute-done.3
  27.2 1.0 %collective-permute-done.4 = f32[200,256]{1,0:T(8,128)S(1)} collective-permute-done((f32[200,256]{1,0:T(8,128)S(1)}, f32[200,256]{1,0:T(8,128)S(1)}, u32[]{:S(2)}, u32[]{:S(2)}) %collective-permute-start.4) | collective-permute-done | bytes 204832 | tf_op jit(solution)/shard_map/ppermute | solution.py:462
  28.3 1.9 %collective-permute-start.5 = (f32[104,256]{1,0:T(8,128)S(1)}, f32[104,256]{1,0:T(8,128)S(1)}, u32[]{:S(2)}, u32[]{:S(2)}) collective-permute-start(f32[104,256]{1,0:T(8,128)S(1)} %pad_maximum_fusion.1), channel_id=1, source_target_pairs={{0,16},{1,17},{2,18},{3,19},{4,20},{5,21},{6,22},{7,23},{8,24},{9,... | collective-permute-start | bytes 319496 | tf_op jit(solution)/shard_map/ppermute | solution.py:462
  30.1 3.0 %collective-permute-done.5 = f32[104,256]{1,0:T(8,128)S(1)} collective-permute-done((f32[104,256]{1,0:T(8,128)S(1)}, f32[104,256]{1,0:T(8,128)S(1)}, u32[]{:S(2)}, u32[]{:S(2)}) %collective-permute-start.5) | collective-permute-done | bytes 106528 | tf_op jit(solution)/shard_map/ppermute | solution.py:462
  33.2 6.2 %collective-permute-start.6 = (f32[32,256]{1,0:T(8,128)S(1)}, f32[32,256]{1,0:T(8,128)S(1)}, u32[]{:S(2)}, u32[]{:S(2)}) collective-permute-start(f32[32,256]{1,0:T(8,128)S(1)} %get-tuple-element.42), channel_id=1, source_target_pairs={{0,1},{1,0},{2,3},{3,2},{4,5},{5,4},{6,7},{7,6},{8,9},{9,8},{10,11... | collective-permute-start | bytes 98312 | tf_op jit(solution)/shard_map/ppermute | solution.py:462
  39.4 0.7 %collective-permute-start.7 = (f32[32,256]{1,0:T(8,128)S(1)}, f32[32,256]{1,0:T(8,128)S(1)}, u32[]{:S(2)}, u32[]{:S(2)}) collective-permute-start(f32[32,256]{1,0:T(8,128)S(1)} %get-tuple-element.41), channel_id=1, source_target_pairs={{0,2},{1,3},{2,0},{3,1},{4,6},{5,7},{6,4},{7,5},{8,10},{9,11},{10,... | collective-permute-start | bytes 98312 | tf_op jit(solution)/shard_map/ppermute | solution.py:462
  40.2 1.7 %collective-permute-start.8 = (f32[32,256]{1,0:T(8,128)S(1)}, f32[32,256]{1,0:T(8,128)S(1)}, u32[]{:S(2)}, u32[]{:S(2)}) collective-permute-start(f32[32,256]{1,0:T(8,128)S(1)} %get-tuple-element.40), channel_id=1, source_target_pairs={{0,3},{1,2},{2,1},{3,0},{4,7},{5,6},{6,5},{7,4},{8,11},{9,10},{10,... | collective-permute-start | bytes 98312 | tf_op jit(solution)/shard_map/ppermute | solution.py:462
  41.9 0.0 collective-permute-done.6.refs_0_
  41.9 2.4 %collective-permute-done.7.refs_1_ = f32[32,256]{1,0:T(8,128)S(1)} collective-permute-done((f32[32,256]{1,0:T(8,128)S(1)}, f32[32,256]{1,0:T(8,128)S(1)}, u32[]{:S(2)}, u32[]{:S(2)}) %collective-permute-start.7) | collective-permute-done | bytes 32800 | tf_op jit(solution)/shard_map/ppermute | solution.py:462
  44.2 1.6 %collective-permute-done.8.refs_2_ = f32[32,256]{1,0:T(8,128)S(1)} collective-permute-done((f32[32,256]{1,0:T(8,128)S(1)}, f32[32,256]{1,0:T(8,128)S(1)}, u32[]{:S(2)}, u32[]{:S(2)}) %collective-permute-start.8) | collective-permute-done | bytes 32800 | tf_op jit(solution)/shard_map/ppermute | solution.py:462
  45.9 0.9 %finish.1 = (f32[8,128]{1,0:T(8,128)}, f32[8,128]{1,0:T(8,128)}, f32[3,2048]{1,0:T(4,128)}) custom-call(s32[8,128]{1,0:T(8,128)S(1)} %bitcast.8, f32[24,256]{1,0:T(8,128)S(1)} %get-tuple-element.39.kept_ref, f32[8,256]{1,0:T(8,128)S(1)} %slice_add_fusion.3.sums_ref, f32[32,256]{1,0:T(8,128)S(1)} %collective-permute-done.6.refs_0_, ...), custom_call_target="tpu_custom_call" | custom-call | tf_op jit(solution)/shard_map/finish/pallas_call | solution.py:427
  (17 shorter events, 0.2 us)
Async XLA Ops:
  0.6 3.8 %copy-start.2 = (s32[4096]{0:T(1024)S(1)}, s32[4096]{0:T(1024)}, u32[]{:S(2)}) copy-start(s32[4096]{0:T(1024)} %param.7) | copy-start | bytes 49156
  0.6 6.3 %collective-permute-start = (f32[8,128]{1,0:T(8,128)}, f32[8,128]{1,0:T(8,128)S(1)}, u32[]{:S(2)}, u32[]{:S(2)}) collective-permute-start(f32[8,128]{1,0:T(8,128)} %bitcast.10), channel_id=1, source_target_pairs={{0,1},{2,3},{1,0},{3,2},{4,5},{6,7},{5,4},{7,6},{8,9},{10,11},{9,8... | collective-permute-start | bytes 12296 | tf_op jit(solution)/shard_map/ppermute | solution.py:470
  3.7 3.2 %collective-permute-start.1 = (f32[8,128]{1,0:T(8,128)}, f32[8,128]{1,0:T(8,128)S(1)}, u32[]{:S(2)}, u32[]{:S(2)}) collective-permute-start(f32[8,128]{1,0:T(8,128)} %bitcast.11), channel_id=1, source_target_pairs={{1,2},{2,1},{5,6},{6,5},{9,10},{10,9},{13,14},{14,13},{17,18},{18,... | collective-permute-start | bytes 12296 | tf_op jit(solution)/shard_map/ppermute | solution.py:470
  4.4 0.7 %copy-start.3 = (f32[1024]{0:T(1024)S(1)}, f32[1024]{0:T(1024)}, u32[]{:S(2)}) copy-start(f32[1024]{0:T(1024)} %param.6) | copy-start | bytes 12292
  4.4 0.7 %copy-start.4 = (s32[256]{0:T(256)S(1)}, s32[256]{0:T(256)}, u32[]{:S(2)}) copy-start(s32[256]{0:T(256)} %param.11) | copy-start | bytes 3076
  4.4 0.7 %copy-start.5 = (s32[1,16]{1,0:T(1,128)S(1)}, s32[1,16]{1,0:T(1,128)}, u32[]{:S(2)}) copy-start(s32[1,16]{1,0:T(1,128)} %len_ref.1) | copy-start | bytes 196
  7.0 6.4 %copy-start = (s32[1024,256]{1,0:T(8,128)S(1)}, s32[1024,256]{1,0:T(8,128)}, u32[]{:S(2)}) copy-start(s32[1024,256]{1,0:T(8,128)} %bins_ref.1) | copy-start | bytes 3145732
  13.4 0.7 %copy-start.1 = (s32[1024]{0:T(1024)S(1)}, s32[1024]{0:T(1024)}, u32[]{:S(2)}) copy-start(s32[1024]{0:T(1024)} %param.8) | copy-start | bytes 12292
  16.7 2.3 %collective-permute-start.2 = (f32[200,256]{1,0:T(8,128)S(1)}, f32[200,256]{1,0:T(8,128)S(1)}, u32[]{:S(2)}, u32[]{:S(2)}) collective-permute-start(f32[200,256]{1,0:T(8,128)S(1)} %histogram_part.5), channel_id=1, source_target_pairs={{0,4},{1,5},{2,6},{3,7},{4,0},{5,1},{6,2},{7,3},{8,12},{9,13},{10,... | collective-permute-start | bytes 614408 | tf_op jit(solution)/shard_map/ppermute | solution.py:462
  19.1 9.1 %collective-permute-start.4 = (f32[200,256]{1,0:T(8,128)S(1)}, f32[200,256]{1,0:T(8,128)S(1)}, u32[]{:S(2)}, u32[]{:S(2)}) collective-permute-start(f32[200,256]{1,0:T(8,128)S(1)} %pad_maximum_fusion), channel_id=1, source_target_pairs={{0,8},{1,9},{2,10},{3,11},{4,12},{5,13},{6,14},{7,15},{8,0},{9,1},... | collective-permute-start | bytes 614408 | tf_op jit(solution)/shard_map/ppermute | solution.py:462
  24.7 2.5 %collective-permute-start.3 = (f32[192,256]{1,0:T(8,128)S(1)}, f32[192,256]{1,0:T(8,128)S(1)}, u32[]{:S(2)}, u32[]{:S(2)}) collective-permute-start(f32[192,256]{1,0:T(8,128)S(1)} %histogram_part.7), channel_id=1, source_target_pairs={{0,4},{1,5},{2,6},{3,7},{4,0},{5,1},{6,2},{7,3},{8,12},{9,13},{10,... | collective-permute-start | bytes 589832 | tf_op jit(solution)/shard_map/ppermute | solution.py:462
  28.3 4.9 %collective-permute-start.5 = (f32[104,256]{1,0:T(8,128)S(1)}, f32[104,256]{1,0:T(8,128)S(1)}, u32[]{:S(2)}, u32[]{:S(2)}) collective-permute-start(f32[104,256]{1,0:T(8,128)S(1)} %pad_maximum_fusion.1), channel_id=1, source_target_pairs={{0,16},{1,17},{2,18},{3,19},{4,20},{5,21},{6,22},{7,23},{8,24},{9,... | collective-permute-start | bytes 319496 | tf_op jit(solution)/shard_map/ppermute | solution.py:462
  33.2 8.7 %collective-permute-start.6 = (f32[32,256]{1,0:T(8,128)S(1)}, f32[32,256]{1,0:T(8,128)S(1)}, u32[]{:S(2)}, u32[]{:S(2)}) collective-permute-start(f32[32,256]{1,0:T(8,128)S(1)} %get-tuple-element.42), channel_id=1, source_target_pairs={{0,1},{1,0},{2,3},{3,2},{4,5},{5,4},{6,7},{7,6},{8,9},{9,8},{10,11... | collective-permute-start | bytes 98312 | tf_op jit(solution)/shard_map/ppermute | solution.py:462
  39.4 4.8 %collective-permute-start.7 = (f32[32,256]{1,0:T(8,128)S(1)}, f32[32,256]{1,0:T(8,128)S(1)}, u32[]{:S(2)}, u32[]{:S(2)}) collective-permute-start(f32[32,256]{1,0:T(8,128)S(1)} %get-tuple-element.41), channel_id=1, source_target_pairs={{0,2},{1,3},{2,0},{3,1},{4,6},{5,7},{6,4},{7,5},{8,10},{9,11},{10,... | collective-permute-start | bytes 98312 | tf_op jit(solution)/shard_map/ppermute | solution.py:462
  40.2 5.7 %collective-permute-start.8 = (f32[32,256]{1,0:T(8,128)S(1)}, f32[32,256]{1,0:T(8,128)S(1)}, u32[]{:S(2)}, u32[]{:S(2)}) collective-permute-start(f32[32,256]{1,0:T(8,128)S(1)} %get-tuple-element.40), channel_id=1, source_target_pairs={{0,3},{1,2},{2,1},{3,0},{4,7},{5,6},{6,5},{7,4},{8,11},{9,10},{10,... | collective-permute-start | bytes 98312 | tf_op jit(solution)/shard_map/ppermute | solution.py:462

commit v7 on v6

--- a/solution.py
+++ b/solution.py
@@ -158,75 +158,85 @@
     a_row[...] = jnp.exp(s_row[...])
     d_row[...] = jnp.zeros(d_row.shape, F32)
     first = me * own
-    window_low = bounds_ref[0, first] // LANES
-    window_high = (bounds_ref[1, first + own - 1] + LANES - 1) // LANES
+    window_low = bounds_ref[0, first] // (2 * LANES) * 2
+    window_high = (bounds_ref[1, first + own - 1] + 2 * LANES - 1) // (2 * LANES) * 2
+    stride = 4
 
     def widen(pairs):
         for turn, source, _ in pairs:
             turn[...] = jnp.transpose(source[...])
-        for r in range(rows):
-            @pl.when((r >= window_low) & (r < window_high))
+        for r in range(0, rows, stride):
+            @pl.when((r + stride > window_low) & (r < window_high))
             def _(r=r):
                 for turn, _, col in pairs:
-                    col[r * LANES:(r + 1) * LANES, :] = jnp.broadcast_to(turn[:, r:r + 1], (LANES, LANES))
+                    for k in range(r, r + stride):
+                        col[k * LANES:(k + 1) * LANES, :] = jnp.broadcast_to(turn[:, k:k + 1], (LANES, LANES))
 
     widen([(s_turn, s_row, s_col), (q_turn, qid_ref, q_col), (a_turn, a_row, a_col), (w_turn, worth_ref, w_col)])
 
-    def row_of(ref, r):
-        return jnp.broadcast_to(ref[pl.ds(r, 1), :], (8, LANES))
+    def rows_of(ref, r):
+        return [jnp.broadcast_to(ref[pl.ds(r + g, 1), :], (8, LANES)) for g in range(2)]
 
     def spans(r):
-        start, end = bounds_ref[0, r], bounds_ref[1, r]
+        start, end = bounds_ref[0, r], bounds_ref[1, r + 1]
         low = jnp.maximum(start // LANES, window_low)
         high = jnp.minimum((end + LANES - 1) // LANES, window_high)
-        single = bounds_ref[2, r] >= (r + 1) * LANES
+        single = bounds_ref[2, r] >= (r + 2) * LANES
         inner_low = jnp.where(single, jnp.maximum((start + LANES - 1) // LANES, window_low), r)
         inner_high = jnp.where(single, jnp.minimum(end // LANES, window_high), r)
         return low, inner_low, inner_high, high
 
-    def rank_group(r, carry):
-        score = row_of(s_row, r)
-        query = row_of(qid_ref, r)
-
-        def sweep(ahead, masked):
-            def step(c, acc):
-                base = pl.multiple_of(c * LANES, LANES)
-                acc = list(acc)
-                for u in range(LANES // 8):
-                    other = s_col[pl.ds(base + 8 * u, 8), :]
-                    hit = (other >= score) if ahead else (other > score)
+    def rank_groups(k, carry):
+        r = window_low + 2 * k
+        score = rows_of(s_row, r)
+        query = rows_of(qid_ref, r)
+
+        def gather(c, acc, masked, test):
+            base = pl.multiple_of(c * LANES, LANES)
+            acc = list(acc)
+            for u in range(LANES // 8):
+                other = s_col[pl.ds(base + 8 * u, 8), :]
+                for g in range(2):
+                    hit = test(other, g, u)
                     if masked:
-                        hit = hit & (q_col[pl.ds(base + 8 * u, 8), :] == query)
-                    acc[u % 4] = acc[u % 4] + jnp.where(hit, 1.0, 0.0)
-                return tuple(acc)
-            return step
+                        hit = hit & (q_col[pl.ds(base + 8 * u, 8), :] == query[g])
+                    acc[2 * g + u % 2] = acc[2 * g + u % 2] + jnp.where(hit, 1.0, 0.0)
+            return tuple(acc)
+
+        def ahead(other, g, u):
+            return other >= score[g]
+
+        def behind(other, g, u):
+            return other > score[g]
+
+        def within(mine):
+            def test(other, g, u):
+                if g != mine:
+                    return ahead(other, g, u) if mine < g else behind(other, g, u)
+                earlier = iota((8, LANES), 0) + 8 * u < iota((8, LANES), 1)
+                return (other > score[g]) | ((other == score[g]) & earlier)
+            return test
 
         acc = tuple(jnp.zeros((8, LANES), F32) for _ in range(4))
         low, inner_low, inner_high, high = spans(r)
-        after = jnp.maximum(inner_high, r + 1)
-        acc = lax.fori_loop(low, inner_low, sweep(True, True), acc)
-        acc = lax.fori_loop(inner_low, r, sweep(True, False), acc)
-        acc = lax.fori_loop(r + 1, after, sweep(False, False), acc)
-        acc = list(lax.fori_loop(after, high, sweep(False, True), acc))
-        base = pl.multiple_of(r * LANES, LANES)
-        for u in range(LANES // 8):
-            other = s_col[pl.ds(base + 8 * u, 8), :]
-            earlier = iota((8, LANES), 0) + 8 * u < iota((8, LANES), 1)
-            above = (other > score) | ((other == score) & earlier)
-            hit = above & (q_col[pl.ds(base + 8 * u, 8), :] == query)
-            acc[u % 4] = acc[u % 4] + jnp.where(hit, 1.0, 0.0)
-        total = (acc[0] + acc[1]) + (acc[2] + acc[3])
-        d_row[pl.ds(r, 1), :] = jnp.sum(total, axis=0, keepdims=True)
+        after = jnp.maximum(inner_high, r + 2)
+        acc = lax.fori_loop(low, inner_low, lambda c, acc: gather(c, acc, True, ahead), acc)
+        acc = lax.fori_loop(inner_low, r, lambda c, acc: gather(c, acc, False, ahead), acc)
+        acc = lax.fori_loop(r + 2, after, lambda c, acc: gather(c, acc, False, behind), acc)
+        acc = lax.fori_loop(after, high, lambda c, acc: gather(c, acc, True, behind), acc)
+        for mine in range(2):
+            acc = gather(r + mine, acc, True, within(mine))
+        for g in range(2):
+            d_row[pl.ds(r + g, 1), :] = jnp.sum(acc[2 * g] + acc[2 * g + 1], axis=0, keepdims=True)
         return carry
 
-    lax.fori_loop(window_low, window_high, rank_group, 0)
+    lax.fori_loop(0, (window_high - window_low) // 2, rank_groups, 0)
     d_row[...] = 1.0 / jnp.log2(2.0 + d_row[...])
     widen([(d_turn, d_row, d_col)])
 
-    def pair_group(t, carry):
-        r = first + t
-        a_i, w_i, d_i = row_of(a_row, r), row_of(worth_ref, r), row_of(d_row, r)
-        query = row_of(qid_ref, r)
+    def pair_groups(t, carry):
+        r = first + 2 * t
+        a_i, w_i, d_i, query = [rows_of(ref, r) for ref in (a_row, worth_ref, d_row, qid_ref)]
 
         def columns(masked):
             def step(c, acc):
@@ -234,28 +244,32 @@
                 acc = list(acc)
                 for u in range(LANES // 8):
                     at = pl.ds(base + 8 * u, 8)
-                    a_j = a_col[at, :]
-                    recip = pl.reciprocal(a_i + a_j, approx=True)
-                    lift = w_i - w_col[at, :]
-                    weight = jnp.abs(d_i - d_col[at, :]) * recip
-                    if masked:
-                        weight = jnp.where(q_col[at, :] == query, weight, 0.0)
-                    weight = weight * lift
-                    acc[u % 2] = acc[u % 2] + weight * jnp.where(lift > 0.0, a_j, a_i)
-                    acc[2 + u % 2] = acc[2 + u % 2] + jnp.abs(weight) * (recip * a_j)
+                    a_j, w_j, d_j = a_col[at, :], w_col[at, :], d_col[at, :]
+                    for g in range(2):
+                        recip = pl.reciprocal(a_i[g] + a_j, approx=True)
+                        lift = w_i[g] - w_j
+                        weight = jnp.abs(d_i[g] - d_j) * recip
+                        if masked:
+                            weight = jnp.where(q_col[at, :] == query[g], weight, 0.0)
+                        weight = weight * lift
+                        k = 4 * g + u % 2
+                        acc[k] = acc[k] + weight * jnp.where(lift > 0.0, a_j, a_i[g])
+                        acc[k + 2] = acc[k + 2] + jnp.abs(weight) * (recip * a_j)
                 return tuple(acc)
             return step
 
-        acc = tuple(jnp.zeros((8, LANES), F32) for _ in range(4))
+        acc = tuple(jnp.zeros((8, LANES), F32) for _ in range(8))
         low, inner_low, inner_high, high = spans(r)
         acc = lax.fori_loop(low, inner_low, columns(True), acc)
         acc = lax.fori_loop(inner_low, inner_high, columns(False), acc)
         acc = lax.fori_loop(inner_high, high, columns(True), acc)
-        grad[pl.ds(t, 1), :] = -jnp.sum(acc[0] + acc[1], axis=0, keepdims=True)
-        curv[pl.ds(t, 1), :] = a_row[pl.ds(r, 1), :] * jnp.sum(acc[2] + acc[3], axis=0, keepdims=True)
+        for g in range(2):
+            at = pl.ds(2 * t + g, 1)
+            grad[at, :] = -jnp.sum(acc[4 * g] + acc[4 * g + 1], axis=0, keepdims=True)
+            curv[at, :] = a_i[g][0:1, :] * jnp.sum(acc[4 * g + 2] + acc[4 * g + 3], axis=0, keepdims=True)
         return carry
 
-    lax.fori_loop(0, own, pair_group, 0)
+    lax.fori_loop(0, own // 2, pair_groups, 0)
     inverse = inv_ref[...]
     terms = [inverse * jnp.concatenate([ref[t:t + 1, :] for t in range(own)], axis=1) for ref in (grad, curv)]
     for c in range(2):

time: 46.9 us -> 45.7 us (0.974)
  starting transfers between devices: 18 us -> 16.3 us
  waiting for transfers between devices: 8.04 us -> 9.03 us
  Pallas kernels: 18.4 us -> 17.7 us
    ppermute x7, starting transfers between devices: 14.2 us -> 12.6 us  [swap(): return lax.ppermute(value, axes, [(p, p ^ mask) for p in range(count)])]
    ppermute x7, waiting for transfers between devices: 8.04 us -> 9.02 us  [swap(): return lax.ppermute(value, axes, [(p, p ^ mask) for p in range(count)])]
    pallas_call x1, Pallas kernels: 6.4 us -> 5.73 us  [pair_terms(): pl.pallas_call(functools.partial(pairs_kernel, feat_count), out_shape=(ja...]
  transfers between devices with their start and end apart: 9 -> 9, of which waited for: 4 -> 4; matrix products, arithmetic and copies ran while one was open for 0% -> 0% of each run, Pallas kernels for 18% -> 19%
where the time goes in v7:
time: 45.7 us; the launch traced here: 45.4 us
  Pallas kernels  17.7 us (39%)
  starting transfers between devices  16.3 us (36%)
  waiting for transfers between devices  9.03 us (20%)
  local copies, waits for them, and re-layouts  1.37 us (3%)
  between operations  0.83 us (2%)
    ppermute x7, starting transfers between devices, swap(): return lax.ppermute(value, axes, [(p, p ^ mask) for p in range(count)])  12.6 us
    ppermute x7, waiting for transfers between devices, swap(): return lax.ppermute(value, axes, [(p, p ^ mask) for p in range(count)])  9.02 us
    pallas_call x4, Pallas kernels, histogram_part(): pl.pallas_call(functools.partial(histogram_kernel, first, groups), out_sh...  8.85 us
    pallas_call x1, Pallas kernels, pair_terms(): pl.pallas_call(functools.partial(pairs_kernel, feat_count), out_shape=(ja...  5.73 us
    ppermute x2, starting transfers between devices, local(): lax.ppermute(own_scores, 'feat', links + [(b, a) for a, b in links])  3.74 us
    pallas_call x1, Pallas kernels, prepare(): pl.pallas_call(functools.partial(prepare_kernel, feat_count, masks), out_...  1.84 us
    unnamed x12, local copies, waits for them, and re-layouts  1.36 us
  transfers between devices with their start and end apart: 9, of which 4 were waited for; matrix products, arithmetic and copies ran while one was open for 0% of the time, Pallas kernels for 19%

profile of v7, /device:TPU:0, one launch (start us, length us, event | category | flops | bytes accessed | tf_op | source)
XLA Modules:
  0.0 45.4 jit_solution(3130468792993323978)
XLA Ops:
  0.6 0.0 copy-start.2
  0.6 3.1 %collective-permute-start = (f32[8,128]{1,0:T(8,128)}, f32[8,128]{1,0:T(8,128)S(1)}, u32[]{:S(2)}, u32[]{:S(2)}) collective-permute-start(f32[8,128]{1,0:T(8,128)} %bitcast.10), channel_id=1, source_target_pairs={{0,1},{2,3},{1,0},{3,2},{4,5},{6,7},{5,4},{7,6},{8,9},{10,11},{9,8... | collective-permute-start | bytes 12296 | tf_op jit(solution)/shard_map/ppermute | solution.py:484
  3.7 0.6 %collective-permute-start.1 = (f32[8,128]{1,0:T(8,128)}, f32[8,128]{1,0:T(8,128)S(1)}, u32[]{:S(2)}, u32[]{:S(2)}) collective-permute-start(f32[8,128]{1,0:T(8,128)} %bitcast.11), channel_id=1, source_target_pairs={{1,2},{2,1},{5,6},{6,5},{9,10},{10,9},{13,14},{14,13},{17,18},{18,... | collective-permute-start | bytes 12296 | tf_op jit(solution)/shard_map/ppermute | solution.py:484
  4.4 0.0 copy-start.3
  4.4 0.6 %copy-done.3 = f32[1024]{0:T(1024)S(1)} copy-done((f32[1024]{0:T(1024)S(1)}, f32[1024]{0:T(1024)}, u32[]{:S(2)}) %copy-start.3) | copy-done | bytes 4120
  5.1 0.0 copy-done.4
  5.1 1.8 %prepare.1 = (f32[8,128]{1,0:T(8,128)S(1)}, s32[32,128]{1,0:T(8,128)S(1)}, f32[32,128]{1,0:T(8,128)S(1)}, f32[1,1024]{1,0:T(1,128)S(1)}, bf16[256,256]{1,0:T(8,128)(2,1)S(1)}, /*index=5*/s32[3,32]{1,0:T(4,128)S(1)}) custom-call(s32[1,16]{1,0:T(1,128)S(1)} %copy-done.5, s32[1]{0:T(128)} %bitcast.pos_ref, s32[32,128]{1,0:T(8,128)S(1)} %bitcast.9, ...), custom_call_target="tpu_custom_call" | custom-call | flops 2000000000 | bytes 300000 | tf_op jit(solution)/shard_map/prepare/pallas_call | solution.py:116
  6.9 0.0 collective-permute-done.refs_1_
  7.0 0.0 collective-permute-done.1.refs_2_
  7.0 0.0 copy-start
  7.0 5.7 %pair_terms.1 = (f32[2,1024]{1,0:T(2,128)}, f32[2,1024]{1,0:T(2,128)S(1)}) custom-call(s32[3,32]{1,0:T(4,128)S(1)} %get-tuple-element.20.bounds_ref, s32[1]{0:T(128)} %bitcast.pos_ref, f32[8,128]{1,0:T(8,128)S(1)} %get-tuple-element.21.refs_0_, f32[8,128]{1,0:T(8,128)S(1)} %collective-permute-done.refs_1_, f32[8,128]{1,0:T(8,128)S(1)} %collective-permute-done.1.refs_2_, ...), custom_call_target="tpu_custom_call" | custom-call | flops 8999999488 | bytes 200000 | tf_op jit(solution)/shard_map/pair_terms/pallas_call | solution.py:287
  12.7 0.7 %copy-done.1 = s32[1024]{0:T(1024)S(1)} copy-done((s32[1024]{0:T(1024)S(1)}, s32[1024]{0:T(1024)}, u32[]{:S(2)}) %copy-start.1) | copy-done | bytes 4120
  13.4 0.4 leaf_terms.1
  13.8 2.2 %histogram_part.5 = f32[200,256]{1,0:T(8,128)S(1)} custom-call(bf16[32,1024]{1,0:T(8,128)(2,1)S(1)} %get-tuple-element.31.tile_ref, f32[256,1024]{1,0:T(8,128)S(1)} %get-tuple-element.29.bins_ref, f32[8,256]{1,0:T(8,128)S(1)} %get-tuple-element.30.refs_0_), custom_call_target="tpu_custom_call" | custom-call | flops 2640000000 | bytes 480000 | tf_op jit(solution)/shard_map/histogram_part/pallas_call | solution.py:401
  16.0 0.9 %collective-permute-start.2 = (f32[200,256]{1,0:T(8,128)S(1)}, f32[200,256]{1,0:T(8,128)S(1)}, u32[]{:S(2)}, u32[]{:S(2)}) collective-permute-start(f32[200,256]{1,0:T(8,128)S(1)} %histogram_part.5), channel_id=1, source_target_pairs={{0,4},{1,5},{2,6},{3,7},{4,0},{5,1},{6,2},{7,3},{8,12},{9,13},{10,... | collective-permute-start | bytes 614408 | tf_op jit(solution)/shard_map/ppermute | solution.py:476
  16.9 2.2 %histogram_part.4 = f32[192,256]{1,0:T(8,128)S(1)} custom-call(bf16[32,1024]{1,0:T(8,128)(2,1)S(1)} %get-tuple-element.31.tile_ref, f32[256,1024]{1,0:T(8,128)S(1)} %get-tuple-element.29.bins_ref), custom_call_target="tpu_custom_call" | custom-call | flops 2640000000 | bytes 480000 | tf_op jit(solution)/shard_map/histogram_part/pallas_call | solution.py:401
  19.2 0.0 collective-permute-done.2
  19.2 0.7 %collective-permute-start.4 = (f32[200,256]{1,0:T(8,128)S(1)}, f32[200,256]{1,0:T(8,128)S(1)}, u32[]{:S(2)}, u32[]{:S(2)}) collective-permute-start(f32[200,256]{1,0:T(8,128)S(1)} %pad_maximum_fusion), channel_id=1, source_target_pairs={{0,8},{1,9},{2,10},{3,11},{4,12},{5,13},{6,14},{7,15},{8,0},{9,1},... | collective-permute-start | bytes 614408 | tf_op jit(solution)/shard_map/ppermute | solution.py:476
  19.9 2.2 %histogram_part.7 = f32[192,256]{1,0:T(8,128)S(1)} custom-call(bf16[32,1024]{1,0:T(8,128)(2,1)S(1)} %get-tuple-element.31.tile_ref, f32[256,1024]{1,0:T(8,128)S(1)} %get-tuple-element.29.bins_ref), custom_call_target="tpu_custom_call" | custom-call | flops 2640000000 | bytes 480000 | tf_op jit(solution)/shard_map/histogram_part/pallas_call | solution.py:401
  22.1 0.3 collective-permute-start.3
  22.4 2.2 %histogram_part.6 = f32[192,256]{1,0:T(8,128)S(1)} custom-call(bf16[32,1024]{1,0:T(8,128)(2,1)S(1)} %get-tuple-element.31.tile_ref, f32[256,1024]{1,0:T(8,128)S(1)} %get-tuple-element.29.bins_ref), custom_call_target="tpu_custom_call" | custom-call | flops 2640000000 | bytes 480000 | tf_op jit(solution)/shard_map/histogram_part/pallas_call | solution.py:401
  24.6 0.0 collective-permute-done.3
  24.6 1.7 %collective-permute-done.4 = f32[200,256]{1,0:T(8,128)S(1)} collective-permute-done((f32[200,256]{1,0:T(8,128)S(1)}, f32[200,256]{1,0:T(8,128)S(1)}, u32[]{:S(2)}, u32[]{:S(2)}) %collective-permute-start.4) | collective-permute-done | bytes 204832 | tf_op jit(solution)/shard_map/ppermute | solution.py:476
  26.4 2.8 %collective-permute-start.5 = (f32[104,256]{1,0:T(8,128)S(1)}, f32[104,256]{1,0:T(8,128)S(1)}, u32[]{:S(2)}, u32[]{:S(2)}) collective-permute-start(f32[104,256]{1,0:T(8,128)S(1)} %pad_maximum_fusion.1), channel_id=1, source_target_pairs={{0,16},{1,17},{2,18},{3,19},{4,20},{5,21},{6,22},{7,23},{8,24},{9,... | collective-permute-start | bytes 319496 | tf_op jit(solution)/shard_map/ppermute | solution.py:476
  29.2 3.0 %collective-permute-done.5 = f32[104,256]{1,0:T(8,128)S(1)} collective-permute-done((f32[104,256]{1,0:T(8,128)S(1)}, f32[104,256]{1,0:T(8,128)S(1)}, u32[]{:S(2)}, u32[]{:S(2)}) %collective-permute-start.5) | collective-permute-done | bytes 106528 | tf_op jit(solution)/shard_map/ppermute | solution.py:476
  32.4 5.5 %collective-permute-start.6 = (f32[32,256]{1,0:T(8,128)S(1)}, f32[32,256]{1,0:T(8,128)S(1)}, u32[]{:S(2)}, u32[]{:S(2)}) collective-permute-start(f32[32,256]{1,0:T(8,128)S(1)} %get-tuple-element.42), channel_id=1, source_target_pairs={{0,1},{1,0},{2,3},{3,2},{4,5},{5,4},{6,7},{7,6},{8,9},{9,8},{10,11... | collective-permute-start | bytes 98312 | tf_op jit(solution)/shard_map/ppermute | solution.py:476
  37.8 1.0 %collective-permute-start.7 = (f32[32,256]{1,0:T(8,128)S(1)}, f32[32,256]{1,0:T(8,128)S(1)}, u32[]{:S(2)}, u32[]{:S(2)}) collective-permute-start(f32[32,256]{1,0:T(8,128)S(1)} %get-tuple-element.41), channel_id=1, source_target_pairs={{0,2},{1,3},{2,0},{3,1},{4,6},{5,7},{6,4},{7,5},{8,10},{9,11},{10,... | collective-permute-start | bytes 98312 | tf_op jit(solution)/shard_map/ppermute | solution.py:476
  38.8 1.4 %collective-permute-start.8 = (f32[32,256]{1,0:T(8,128)S(1)}, f32[32,256]{1,0:T(8,128)S(1)}, u32[]{:S(2)}, u32[]{:S(2)}) collective-permute-start(f32[32,256]{1,0:T(8,128)S(1)} %get-tuple-element.40), channel_id=1, source_target_pairs={{0,3},{1,2},{2,1},{3,0},{4,7},{5,6},{6,5},{7,4},{8,11},{9,10},{10,... | collective-permute-start | bytes 98312 | tf_op jit(solution)/shard_map/ppermute | solution.py:476
  40.3 0.0 collective-permute-done.6.refs_0_
  40.3 2.9 %collective-permute-done.7.refs_1_ = f32[32,256]{1,0:T(8,128)S(1)} collective-permute-done((f32[32,256]{1,0:T(8,128)S(1)}, f32[32,256]{1,0:T(8,128)S(1)}, u32[]{:S(2)}, u32[]{:S(2)}) %collective-permute-start.7) | collective-permute-done | bytes 32800 | tf_op jit(solution)/shard_map/ppermute | solution.py:476
  43.2 1.4 %collective-permute-done.8.refs_2_ = f32[32,256]{1,0:T(8,128)S(1)} collective-permute-done((f32[32,256]{1,0:T(8,128)S(1)}, f32[32,256]{1,0:T(8,128)S(1)}, u32[]{:S(2)}, u32[]{:S(2)}) %collective-permute-start.8) | collective-permute-done | bytes 32800 | tf_op jit(solution)/shard_map/ppermute | solution.py:476
  44.6 0.9 %finish.1 = (f32[8,128]{1,0:T(8,128)}, f32[8,128]{1,0:T(8,128)}, f32[3,2048]{1,0:T(4,128)}) custom-call(s32[8,128]{1,0:T(8,128)S(1)} %bitcast.8, f32[24,256]{1,0:T(8,128)S(1)} %get-tuple-element.39.kept_ref, f32[8,256]{1,0:T(8,128)S(1)} %slice_add_fusion.3.sums_ref, f32[32,256]{1,0:T(8,128)S(1)} %collective-permute-done.6.refs_0_, ...), custom_call_target="tpu_custom_call" | custom-call | tf_op jit(solution)/shard_map/finish/pallas_call | solution.py:441
  (17 shorter events, 0.2 us)
Async XLA Ops:
  0.6 3.8 %copy-start.2 = (s32[4096]{0:T(1024)S(1)}, s32[4096]{0:T(1024)}, u32[]{:S(2)}) copy-start(s32[4096]{0:T(1024)} %param.7) | copy-start | bytes 49156
  0.6 6.3 %collective-permute-start = (f32[8,128]{1,0:T(8,128)}, f32[8,128]{1,0:T(8,128)S(1)}, u32[]{:S(2)}, u32[]{:S(2)}) collective-permute-start(f32[8,128]{1,0:T(8,128)} %bitcast.10), channel_id=1, source_target_pairs={{0,1},{2,3},{1,0},{3,2},{4,5},{6,7},{5,4},{7,6},{8,9},{10,11},{9,8... | collective-permute-start | bytes 12296 | tf_op jit(solution)/shard_map/ppermute | solution.py:484
  3.7 3.2 %collective-permute-start.1 = (f32[8,128]{1,0:T(8,128)}, f32[8,128]{1,0:T(8,128)S(1)}, u32[]{:S(2)}, u32[]{:S(2)}) collective-permute-start(f32[8,128]{1,0:T(8,128)} %bitcast.11), channel_id=1, source_target_pairs={{1,2},{2,1},{5,6},{6,5},{9,10},{10,9},{13,14},{14,13},{17,18},{18,... | collective-permute-start | bytes 12296 | tf_op jit(solution)/shard_map/ppermute | solution.py:484
  4.4 0.7 %copy-start.3 = (f32[1024]{0:T(1024)S(1)}, f32[1024]{0:T(1024)}, u32[]{:S(2)}) copy-start(f32[1024]{0:T(1024)} %param.6) | copy-start | bytes 12292
  4.4 0.7 %copy-start.4 = (s32[256]{0:T(256)S(1)}, s32[256]{0:T(256)}, u32[]{:S(2)}) copy-start(s32[256]{0:T(256)} %param.11) | copy-start | bytes 3076
  4.4 0.7 %copy-start.5 = (s32[1,16]{1,0:T(1,128)S(1)}, s32[1,16]{1,0:T(1,128)}, u32[]{:S(2)}) copy-start(s32[1,16]{1,0:T(1,128)} %len_ref.1) | copy-start | bytes 196
  7.0 5.7 %copy-start = (s32[1024,256]{1,0:T(8,128)S(1)}, s32[1024,256]{1,0:T(8,128)}, u32[]{:S(2)}) copy-start(s32[1024,256]{1,0:T(8,128)} %bins_ref.1) | copy-start | bytes 3145732
  12.7 0.7 %copy-start.1 = (s32[1024]{0:T(1024)S(1)}, s32[1024]{0:T(1024)}, u32[]{:S(2)}) copy-start(s32[1024]{0:T(1024)} %param.8) | copy-start | bytes 12292
  16.0 3.1 %collective-permute-start.2 = (f32[200,256]{1,0:T(8,128)S(1)}, f32[200,256]{1,0:T(8,128)S(1)}, u32[]{:S(2)}, u32[]{:S(2)}) collective-permute-start(f32[200,256]{1,0:T(8,128)S(1)} %histogram_part.5), channel_id=1, source_target_pairs={{0,4},{1,5},{2,6},{3,7},{4,0},{5,1},{6,2},{7,3},{8,12},{9,13},{10,... | collective-permute-start | bytes 614408 | tf_op jit(solution)/shard_map/ppermute | solution.py:476
  19.2 7.1 %collective-permute-start.4 = (f32[200,256]{1,0:T(8,128)S(1)}, f32[200,256]{1,0:T(8,128)S(1)}, u32[]{:S(2)}, u32[]{:S(2)}) collective-permute-start(f32[200,256]{1,0:T(8,128)S(1)} %pad_maximum_fusion), channel_id=1, source_target_pairs={{0,8},{1,9},{2,10},{3,11},{4,12},{5,13},{6,14},{7,15},{8,0},{9,1},... | collective-permute-start | bytes 614408 | tf_op jit(solution)/shard_map/ppermute | solution.py:476
  22.1 2.5 %collective-permute-start.3 = (f32[192,256]{1,0:T(8,128)S(1)}, f32[192,256]{1,0:T(8,128)S(1)}, u32[]{:S(2)}, u32[]{:S(2)}) collective-permute-start(f32[192,256]{1,0:T(8,128)S(1)} %histogram_part.7), channel_id=1, source_target_pairs={{0,4},{1,5},{2,6},{3,7},{4,0},{5,1},{6,2},{7,3},{8,12},{9,13},{10,... | collective-permute-start | bytes 589832 | tf_op jit(solution)/shard_map/ppermute | solution.py:476
  26.4 5.9 %collective-permute-start.5 = (f32[104,256]{1,0:T(8,128)S(1)}, f32[104,256]{1,0:T(8,128)S(1)}, u32[]{:S(2)}, u32[]{:S(2)}) collective-permute-start(f32[104,256]{1,0:T(8,128)S(1)} %pad_maximum_fusion.1), channel_id=1, source_target_pairs={{0,16},{1,17},{2,18},{3,19},{4,20},{5,21},{6,22},{7,23},{8,24},{9,... | collective-permute-start | bytes 319496 | tf_op jit(solution)/shard_map/ppermute | solution.py:476
  32.4 7.9 %collective-permute-start.6 = (f32[32,256]{1,0:T(8,128)S(1)}, f32[32,256]{1,0:T(8,128)S(1)}, u32[]{:S(2)}, u32[]{:S(2)}) collective-permute-start(f32[32,256]{1,0:T(8,128)S(1)} %get-tuple-element.42), channel_id=1, source_target_pairs={{0,1},{1,0},{2,3},{3,2},{4,5},{5,4},{6,7},{7,6},{8,9},{9,8},{10,11... | collective-permute-start | bytes 98312 | tf_op jit(solution)/shard_map/ppermute | solution.py:476
  37.8 5.4 %collective-permute-start.7 = (f32[32,256]{1,0:T(8,128)S(1)}, f32[32,256]{1,0:T(8,128)S(1)}, u32[]{:S(2)}, u32[]{:S(2)}) collective-permute-start(f32[32,256]{1,0:T(8,128)S(1)} %get-tuple-element.41), channel_id=1, source_target_pairs={{0,2},{1,3},{2,0},{3,1},{4,6},{5,7},{6,4},{7,5},{8,10},{9,11},{10,... | collective-permute-start | bytes 98312 | tf_op jit(solution)/shard_map/ppermute | solution.py:476
  38.8 5.7 %collective-permute-start.8 = (f32[32,256]{1,0:T(8,128)S(1)}, f32[32,256]{1,0:T(8,128)S(1)}, u32[]{:S(2)}, u32[]{:S(2)}) collective-permute-start(f32[32,256]{1,0:T(8,128)S(1)} %get-tuple-element.40), channel_id=1, source_target_pairs={{0,3},{1,2},{2,1},{3,0},{4,7},{5,6},{6,5},{7,4},{8,11},{9,10},{10,... | collective-permute-start | bytes 98312 | tf_op jit(solution)/shard_map/ppermute | solution.py:476

commit v8 on v7

--- a/solution.py
+++ b/solution.py
@@ -410,7 +410,7 @@
 
 
 def finish_kernel(per_dev, leaf_ref, kept_ref, sums_ref, *refs):
-    arrived = refs[:-3]
+    arrived = refs[:-3][::-1]
     value_ref, step_ref, hist_ref = refs[-3:]
     unit = kept_ref.shape[0]
     totals = add_up([sums_ref[...]] + [ref[unit:, :] for ref in arrived])
@@ -481,7 +481,8 @@
     score_parts = [own_scores]
     for begin in range(2):
         links = [(z, z + 1) for z in range(begin, feat_count - 1, 2)]
-        score_parts.append(lax.ppermute(own_scores, "feat", links + [(b, a) for a, b in links]))
+        ends = [(z, z) for z in (0, feat_count - 1)] if begin else []
+        score_parts.append(lax.ppermute(own_scores, "feat", links + [(b, a) for a, b in links] + ends))
     masks = feat_masks + query_masks[:0:-1] + query_masks[:1]
     score_parts[0], qid, worth, inverse, perm, bounds = prepare(
         feat_count, masks, lengths, pos, labels.reshape(-1, LANES), owner.reshape(-1, LANES), own_scores)
@@ -515,7 +516,7 @@
         kept = kept[:edge] + arrived[:edge]
         sums = sums + arrived[edge:]
     arrived = [swap(join(kept[m * unit:(m + 1) * unit], sums), m) for m in range(1, feat_count)]
-    values, step, histograms = finish(per_dev, leaf_rows, kept[:unit], sums, arrived)
+    values, step, histograms = finish(per_dev, leaf_rows, kept[:unit], sums, arrived[::-1])
     return lambdas, values.reshape(LEAVES), step.reshape(docs), histograms.reshape(3, per_dev * BINS)
 
 

time: 45.7 us -> 45.3 us (level)
  Pallas kernels: 17.7 us -> 19.1 us
  waiting for transfers between devices: 9.03 us -> 8.03 us
  starting transfers between devices: 16.3 us -> 15.8 us
    pallas_call x1, Pallas kernels: 5.73 us -> 7.12 us  [pair_terms(): pl.pallas_call(functools.partial(pairs_kernel, feat_count), out_shape=(ja...]
    ppermute x7, starting transfers between devices: 12.6 us -> 11.4 us  [swap(): return lax.ppermute(value, axes, [(p, p ^ mask) for p in range(count)])]
    ppermute x7, waiting for transfers between devices: 9.02 us -> 8.02 us  [swap(): return lax.ppermute(value, axes, [(p, p ^ mask) for p in range(count)])]
    ppermute x2, starting transfers between devices: 3.74 us -> 4.42 us  [local(): lax.ppermute(own_scores, 'feat', links + [(b, a) for a, b in links] + ends)]
where the time goes in v8:
time: 45.3 us
  Pallas kernels  19.1 us (42%)
  starting transfers between devices  15.8 us (35%)
  waiting for transfers between devices  8.03 us (18%)
  local copies, waits for them, and re-layouts  1.4 us (3%)
  between operations  0.8 us (2%)
    ppermute x7, starting transfers between devices, swap(): return lax.ppermute(value, axes, [(p, p ^ mask) for p in range(count)])  11.4 us
    pallas_call x4, Pallas kernels, histogram_part(): pl.pallas_call(functools.partial(histogram_kernel, first, groups), out_sh...  8.86 us
    ppermute x7, waiting for transfers between devices, swap(): return lax.ppermute(value, axes, [(p, p ^ mask) for p in range(count)])  8.02 us
    pallas_call x1, Pallas kernels, pair_terms(): pl.pallas_call(functools.partial(pairs_kernel, feat_count), out_shape=(ja...  7.12 us
    ppermute x2, starting transfers between devices, local(): lax.ppermute(own_scores, 'feat', links + [(b, a) for a, b in links] + ends)  4.42 us
    pallas_call x1, Pallas kernels, prepare(): pl.pallas_call(functools.partial(prepare_kernel, feat_count, masks), out_...  1.86 us
    unnamed x12, local copies, waits for them, and re-layouts  1.38 us
  transfers between devices with their start and end apart: 9, of which 4 were waited for; matrix products, arithmetic and copies ran while one was open for 0% of the time, Pallas kernels for 19%

profile of v8, /device:TPU:0, one launch (start us, length us, event | category | flops | bytes accessed | tf_op | source)
XLA Modules:
  0.0 45.3 jit_solution(2121376559991440709)
XLA Ops:
  0.6 3.1 %collective-permute-start = (f32[8,128]{1,0:T(8,128)}, f32[8,128]{1,0:T(8,128)S(1)}, u32[]{:S(2)}, u32[]{:S(2)}) collective-permute-start(f32[8,128]{1,0:T(8,128)} %bitcast.10), channel_id=1, source_target_pairs={{0,1},{2,3},{1,0},{3,2},{4,5},{6,7},{5,4},{7,6},{8,9},{10,11},{9,8... | collective-permute-start | bytes 12296 | tf_op jit(solution)/shard_map/ppermute | solution.py:485
  3.7 1.3 %collective-permute-start.1 = (f32[8,128]{1,0:T(8,128)}, f32[8,128]{1,0:T(8,128)S(1)}, u32[]{:S(2)}, u32[]{:S(2)}) collective-permute-start(f32[8,128]{1,0:T(8,128)} %bitcast.11), channel_id=1, source_target_pairs={{1,2},{2,1},{0,0},{3,3},{5,6},{6,5},{4,4},{7,7},{9,10},{10,9},{8,8... | collective-permute-start | bytes 12296 | tf_op jit(solution)/shard_map/ppermute | solution.py:485
  5.1 0.7 %copy-done.3 = f32[1024]{0:T(1024)S(1)} copy-done((f32[1024]{0:T(1024)S(1)}, f32[1024]{0:T(1024)}, u32[]{:S(2)}) %copy-start.3) | copy-done | bytes 4120
  5.8 0.0 copy-done.4
  5.8 0.0 copy-done.5
  5.8 1.9 %prepare.1 = (f32[8,128]{1,0:T(8,128)S(1)}, s32[32,128]{1,0:T(8,128)S(1)}, f32[32,128]{1,0:T(8,128)S(1)}, f32[1,1024]{1,0:T(1,128)S(1)}, bf16[256,256]{1,0:T(8,128)(2,1)S(1)}, /*index=5*/s32[3,32]{1,0:T(4,128)S(1)}) custom-call(s32[1,16]{1,0:T(1,128)S(1)} %copy-done.5, s32[1]{0:T(128)} %bitcast.pos_ref, s32[32,128]{1,0:T(8,128)S(1)} %bitcast.9, ...), custom_call_target="tpu_custom_call" | custom-call | flops 2000000000 | bytes 300000 | tf_op jit(solution)/shard_map/prepare/pallas_call | solution.py:116
  7.6 0.0 collective-permute-done.refs_1_
  7.6 0.0 collective-permute-done.1.refs_2_
  7.6 0.0 copy-start
  7.7 7.1 %pair_terms.1 = (f32[2,1024]{1,0:T(2,128)}, f32[2,1024]{1,0:T(2,128)S(1)}) custom-call(s32[3,32]{1,0:T(4,128)S(1)} %get-tuple-element.20.bounds_ref, s32[1]{0:T(128)} %bitcast.pos_ref, f32[8,128]{1,0:T(8,128)S(1)} %get-tuple-element.21.refs_0_, f32[8,128]{1,0:T(8,128)S(1)} %collective-permute-done.refs_1_, f32[8,128]{1,0:T(8,128)S(1)} %collective-permute-done.1.refs_2_, ...), custom_call_target="tpu_custom_call" | custom-call | flops 8999999488 | bytes 200000 | tf_op jit(solution)/shard_map/pair_terms/pallas_call | solution.py:287
  14.8 0.0 copy-done
  14.8 0.7 %copy-done.1 = s32[1024]{0:T(1024)S(1)} copy-done((s32[1024]{0:T(1024)S(1)}, s32[1024]{0:T(1024)}, u32[]{:S(2)}) %copy-start.1) | copy-done | bytes 4120
  15.5 0.4 leaf_terms.1
  15.9 2.2 %histogram_part.5 = f32[200,256]{1,0:T(8,128)S(1)} custom-call(bf16[32,1024]{1,0:T(8,128)(2,1)S(1)} %get-tuple-element.31.tile_ref, f32[256,1024]{1,0:T(8,128)S(1)} %get-tuple-element.29.bins_ref, f32[8,256]{1,0:T(8,128)S(1)} %get-tuple-element.30.refs_0_), custom_call_target="tpu_custom_call" | custom-call | flops 2640000000 | bytes 480000 | tf_op jit(solution)/shard_map/histogram_part/pallas_call | solution.py:401
  18.1 0.1 collective-permute-start.2
  18.2 2.2 %histogram_part.4 = f32[192,256]{1,0:T(8,128)S(1)} custom-call(bf16[32,1024]{1,0:T(8,128)(2,1)S(1)} %get-tuple-element.31.tile_ref, f32[256,1024]{1,0:T(8,128)S(1)} %get-tuple-element.29.bins_ref), custom_call_target="tpu_custom_call" | custom-call | flops 2640000000 | bytes 480000 | tf_op jit(solution)/shard_map/histogram_part/pallas_call | solution.py:401
  20.4 0.0 collective-permute-done.2
  20.5 1.7 %collective-permute-start.4 = (f32[200,256]{1,0:T(8,128)S(1)}, f32[200,256]{1,0:T(8,128)S(1)}, u32[]{:S(2)}, u32[]{:S(2)}) collective-permute-start(f32[200,256]{1,0:T(8,128)S(1)} %pad_maximum_fusion), channel_id=1, source_target_pairs={{0,8},{1,9},{2,10},{3,11},{4,12},{5,13},{6,14},{7,15},{8,0},{9,1},... | collective-permute-start | bytes 614408 | tf_op jit(solution)/shard_map/ppermute | solution.py:476
  22.2 2.2 %histogram_part.7 = f32[192,256]{1,0:T(8,128)S(1)} custom-call(bf16[32,1024]{1,0:T(8,128)(2,1)S(1)} %get-tuple-element.31.tile_ref, f32[256,1024]{1,0:T(8,128)S(1)} %get-tuple-element.29.bins_ref), custom_call_target="tpu_custom_call" | custom-call | flops 2640000000 | bytes 480000 | tf_op jit(solution)/shard_map/histogram_part/pallas_call | solution.py:401
  24.4 0.3 collective-permute-start.3
  24.7 2.2 %histogram_part.6 = f32[192,256]{1,0:T(8,128)S(1)} custom-call(bf16[32,1024]{1,0:T(8,128)(2,1)S(1)} %get-tuple-element.31.tile_ref, f32[256,1024]{1,0:T(8,128)S(1)} %get-tuple-element.29.bins_ref), custom_call_target="tpu_custom_call" | custom-call | flops 2640000000 | bytes 480000 | tf_op jit(solution)/shard_map/histogram_part/pallas_call | solution.py:401
  26.9 0.0 collective-permute-done.3
  27.0 1.1 %collective-permute-done.4 = f32[200,256]{1,0:T(8,128)S(1)} collective-permute-done((f32[200,256]{1,0:T(8,128)S(1)}, f32[200,256]{1,0:T(8,128)S(1)}, u32[]{:S(2)}, u32[]{:S(2)}) %collective-permute-start.4) | collective-permute-done | bytes 204832 | tf_op jit(solution)/shard_map/ppermute | solution.py:476
  28.1 1.7 %collective-permute-start.5 = (f32[104,256]{1,0:T(8,128)S(1)}, f32[104,256]{1,0:T(8,128)S(1)}, u32[]{:S(2)}, u32[]{:S(2)}) collective-permute-start(f32[104,256]{1,0:T(8,128)S(1)} %pad_maximum_fusion.1), channel_id=1, source_target_pairs={{0,16},{1,17},{2,18},{3,19},{4,20},{5,21},{6,22},{7,23},{8,24},{9,... | collective-permute-start | bytes 319496 | tf_op jit(solution)/shard_map/ppermute | solution.py:476
  29.9 3.0 %collective-permute-done.5 = f32[104,256]{1,0:T(8,128)S(1)} collective-permute-done((f32[104,256]{1,0:T(8,128)S(1)}, f32[104,256]{1,0:T(8,128)S(1)}, u32[]{:S(2)}, u32[]{:S(2)}) %collective-permute-start.5) | collective-permute-done | bytes 106528 | tf_op jit(solution)/shard_map/ppermute | solution.py:476
  33.0 2.8 %collective-permute-start.6 = (f32[32,256]{1,0:T(8,128)S(1)}, f32[32,256]{1,0:T(8,128)S(1)}, u32[]{:S(2)}, u32[]{:S(2)}) collective-permute-start(f32[32,256]{1,0:T(8,128)S(1)} %get-tuple-element.42), channel_id=1, source_target_pairs={{0,3},{1,2},{2,1},{3,0},{4,7},{5,6},{6,5},{7,4},{8,11},{9,10},{10,... | collective-permute-start | bytes 98312 | tf_op jit(solution)/shard_map/ppermute | solution.py:476
  35.8 4.8 %collective-permute-start.7 = (f32[32,256]{1,0:T(8,128)S(1)}, f32[32,256]{1,0:T(8,128)S(1)}, u32[]{:S(2)}, u32[]{:S(2)}) collective-permute-start(f32[32,256]{1,0:T(8,128)S(1)} %get-tuple-element.41), channel_id=1, source_target_pairs={{0,2},{1,3},{2,0},{3,1},{4,6},{5,7},{6,4},{7,5},{8,10},{9,11},{10,... | collective-permute-start | bytes 98312 | tf_op jit(solution)/shard_map/ppermute | solution.py:476
  40.6 0.0 collective-permute-start.8
  40.6 0.0 collective-permute-done.6.refs_0_
  40.6 2.6 %collective-permute-done.7.refs_1_ = f32[32,256]{1,0:T(8,128)S(1)} collective-permute-done((f32[32,256]{1,0:T(8,128)S(1)}, f32[32,256]{1,0:T(8,128)S(1)}, u32[]{:S(2)}, u32[]{:S(2)}) %collective-permute-start.7) | collective-permute-done | bytes 32800 | tf_op jit(solution)/shard_map/ppermute | solution.py:476
  43.2 1.3 %collective-permute-done.8.refs_2_ = f32[32,256]{1,0:T(8,128)S(1)} collective-permute-done((f32[32,256]{1,0:T(8,128)S(1)}, f32[32,256]{1,0:T(8,128)S(1)}, u32[]{:S(2)}, u32[]{:S(2)}) %collective-permute-start.8) | collective-permute-done | bytes 32800 | tf_op jit(solution)/shard_map/ppermute | solution.py:476
  44.5 0.9 %finish.1 = (f32[8,128]{1,0:T(8,128)}, f32[8,128]{1,0:T(8,128)}, f32[3,2048]{1,0:T(4,128)}) custom-call(s32[8,128]{1,0:T(8,128)S(1)} %bitcast.8, f32[24,256]{1,0:T(8,128)S(1)} %get-tuple-element.39.kept_ref, f32[8,256]{1,0:T(8,128)S(1)} %slice_add_fusion.3.sums_ref, f32[32,256]{1,0:T(8,128)S(1)} %collective-permute-done.6.refs_0_, ...), custom_call_target="tpu_custom_call" | custom-call | tf_op jit(solution)/shard_map/finish/pallas_call | solution.py:441
  (17 shorter events, 0.2 us)
Async XLA Ops:
  0.6 4.4 %copy-start.2 = (s32[4096]{0:T(1024)S(1)}, s32[4096]{0:T(1024)}, u32[]{:S(2)}) copy-start(s32[4096]{0:T(1024)} %param.7) | copy-start | bytes 49156
  0.6 7.0 %collective-permute-start = (f32[8,128]{1,0:T(8,128)}, f32[8,128]{1,0:T(8,128)S(1)}, u32[]{:S(2)}, u32[]{:S(2)}) collective-permute-start(f32[8,128]{1,0:T(8,128)} %bitcast.10), channel_id=1, source_target_pairs={{0,1},{2,3},{1,0},{3,2},{4,5},{6,7},{5,4},{7,6},{8,9},{10,11},{9,8... | collective-permute-start | bytes 12296 | tf_op jit(solution)/shard_map/ppermute | solution.py:485
  3.7 3.9 %collective-permute-start.1 = (f32[8,128]{1,0:T(8,128)}, f32[8,128]{1,0:T(8,128)S(1)}, u32[]{:S(2)}, u32[]{:S(2)}) collective-permute-start(f32[8,128]{1,0:T(8,128)} %bitcast.11), channel_id=1, source_target_pairs={{1,2},{2,1},{0,0},{3,3},{5,6},{6,5},{4,4},{7,7},{9,10},{10,9},{8,8... | collective-permute-start | bytes 12296 | tf_op jit(solution)/shard_map/ppermute | solution.py:485
  5.1 0.7 %copy-start.3 = (f32[1024]{0:T(1024)S(1)}, f32[1024]{0:T(1024)}, u32[]{:S(2)}) copy-start(f32[1024]{0:T(1024)} %param.6) | copy-start | bytes 12292
  5.1 0.7 %copy-start.4 = (s32[256]{0:T(256)S(1)}, s32[256]{0:T(256)}, u32[]{:S(2)}) copy-start(s32[256]{0:T(256)} %param.11) | copy-start | bytes 3076
  5.1 0.7 %copy-start.5 = (s32[1,16]{1,0:T(1,128)S(1)}, s32[1,16]{1,0:T(1,128)}, u32[]{:S(2)}) copy-start(s32[1,16]{1,0:T(1,128)} %len_ref.1) | copy-start | bytes 196
  7.6 7.1 %copy-start = (s32[1024,256]{1,0:T(8,128)S(1)}, s32[1024,256]{1,0:T(8,128)}, u32[]{:S(2)}) copy-start(s32[1024,256]{1,0:T(8,128)} %bins_ref.1) | copy-start | bytes 3145732
  14.8 0.7 %copy-start.1 = (s32[1024]{0:T(1024)S(1)}, s32[1024]{0:T(1024)}, u32[]{:S(2)}) copy-start(s32[1024]{0:T(1024)} %param.8) | copy-start | bytes 12292
  18.1 2.3 %collective-permute-start.2 = (f32[200,256]{1,0:T(8,128)S(1)}, f32[200,256]{1,0:T(8,128)S(1)}, u32[]{:S(2)}, u32[]{:S(2)}) collective-permute-start(f32[200,256]{1,0:T(8,128)S(1)} %histogram_part.5), channel_id=1, source_target_pairs={{0,4},{1,5},{2,6},{3,7},{4,0},{5,1},{6,2},{7,3},{8,12},{9,13},{10,... | collective-permute-start | bytes 614408 | tf_op jit(solution)/shard_map/ppermute | solution.py:476
  20.5 7.5 %collective-permute-start.4 = (f32[200,256]{1,0:T(8,128)S(1)}, f32[200,256]{1,0:T(8,128)S(1)}, u32[]{:S(2)}, u32[]{:S(2)}) collective-permute-start(f32[200,256]{1,0:T(8,128)S(1)} %pad_maximum_fusion), channel_id=1, source_target_pairs={{0,8},{1,9},{2,10},{3,11},{4,12},{5,13},{6,14},{7,15},{8,0},{9,1},... | collective-permute-start | bytes 614408 | tf_op jit(solution)/shard_map/ppermute | solution.py:476
  24.4 2.5 %collective-permute-start.3 = (f32[192,256]{1,0:T(8,128)S(1)}, f32[192,256]{1,0:T(8,128)S(1)}, u32[]{:S(2)}, u32[]{:S(2)}) collective-permute-start(f32[192,256]{1,0:T(8,128)S(1)} %histogram_part.7), channel_id=1, source_target_pairs={{0,4},{1,5},{2,6},{3,7},{4,0},{5,1},{6,2},{7,3},{8,12},{9,13},{10,... | collective-permute-start | bytes 589832 | tf_op jit(solution)/shard_map/ppermute | solution.py:476
  28.1 4.8 %collective-permute-start.5 = (f32[104,256]{1,0:T(8,128)S(1)}, f32[104,256]{1,0:T(8,128)S(1)}, u32[]{:S(2)}, u32[]{:S(2)}) collective-permute-start(f32[104,256]{1,0:T(8,128)S(1)} %pad_maximum_fusion.1), channel_id=1, source_target_pairs={{0,16},{1,17},{2,18},{3,19},{4,20},{5,21},{6,22},{7,23},{8,24},{9,... | collective-permute-start | bytes 319496 | tf_op jit(solution)/shard_map/ppermute | solution.py:476
  33.0 7.6 %collective-permute-start.6 = (f32[32,256]{1,0:T(8,128)S(1)}, f32[32,256]{1,0:T(8,128)S(1)}, u32[]{:S(2)}, u32[]{:S(2)}) collective-permute-start(f32[32,256]{1,0:T(8,128)S(1)} %get-tuple-element.42), channel_id=1, source_target_pairs={{0,3},{1,2},{2,1},{3,0},{4,7},{5,6},{6,5},{7,4},{8,11},{9,10},{10,... | collective-permute-start | bytes 98312 | tf_op jit(solution)/shard_map/ppermute | solution.py:476
  35.8 7.4 %collective-permute-start.7 = (f32[32,256]{1,0:T(8,128)S(1)}, f32[32,256]{1,0:T(8,128)S(1)}, u32[]{:S(2)}, u32[]{:S(2)}) collective-permute-start(f32[32,256]{1,0:T(8,128)S(1)} %get-tuple-element.41), channel_id=1, source_target_pairs={{0,2},{1,3},{2,0},{3,1},{4,6},{5,7},{6,4},{7,5},{8,10},{9,11},{10,... | collective-permute-start | bytes 98312 | tf_op jit(solution)/shard_map/ppermute | solution.py:476
  40.6 3.9 %collective-permute-start.8 = (f32[32,256]{1,0:T(8,128)S(1)}, f32[32,256]{1,0:T(8,128)S(1)}, u32[]{:S(2)}, u32[]{:S(2)}) collective-permute-start(f32[32,256]{1,0:T(8,128)S(1)} %get-tuple-element.40), channel_id=1, source_target_pairs={{0,1},{1,0},{2,3},{3,2},{4,5},{5,4},{6,7},{7,6},{8,9},{9,8},{10,11... | collective-permute-start | bytes 98312 | tf_op jit(solution)/shard_map/ppermute | solution.py:476

commit v9 on v8

--- a/solution.py
+++ b/solution.py
@@ -39,9 +39,24 @@
     return pl.BlockSpec(memory_space=pltpu.SMEM)
 
 
-def prepare_kernel(feat_count, masks, len_ref, pos_ref, lab_ref, owner_ref, score_ref,
-                   kept_ref, qid_ref, worth_ref, inv_ref, perm_ref, bounds_ref):
-    kept_ref[...] = score_ref[...]
+def stage_kernel(score_ref, first_ref, second_ref):
+    first_ref[...] = score_ref[...]
+    second_ref[...] = score_ref[...]
+
+
+def stage(scores):
+    return pl.pallas_call(
+        stage_kernel,
+        out_shape=(jax.ShapeDtypeStruct(scores.shape, F32),) * 2,
+        in_specs=[vmem()],
+        out_specs=(vmem(), vmem()),
+        cost_estimate=pl.CostEstimate(flops=10_000_000_000, bytes_accessed=10_000, transcendentals=0),
+        name="stage",
+    )(scores)
+
+
+def prepare_kernel(feat_count, masks, len_ref, pos_ref, lab_ref, owner_ref,
+                   qid_ref, worth_ref, inv_ref, perm_ref, bounds_ref):
     queries = len_ref.shape[1]
     rows = lab_ref.shape[0]
     own = rows // feat_count
@@ -110,25 +125,24 @@
     perm_ref[...] = lax.dot_general(pick, holds, NT, preferred_element_type=F32).astype(BF16)
 
 
-def prepare(feat_count, masks, lengths, pos, labels, owner, scores):
+def prepare(feat_count, masks, lengths, pos, labels, owner):
     rows = labels.shape[0]
     features = owner.shape[0] * LANES
     return pl.pallas_call(
         functools.partial(prepare_kernel, feat_count, masks),
         out_shape=(
-            jax.ShapeDtypeStruct(scores.shape, F32),
             jax.ShapeDtypeStruct((rows, LANES), jnp.int32),
             jax.ShapeDtypeStruct((rows, LANES), F32),
             jax.ShapeDtypeStruct((1, rows // feat_count * LANES), F32),
             jax.ShapeDtypeStruct((features, features), BF16),
             jax.ShapeDtypeStruct((3, rows), jnp.int32),
         ),
-        in_specs=[smem(), smem(), vmem(), vmem(), vmem()],
-        out_specs=(vmem(),) * 5 + (smem(),),
+        in_specs=[smem(), smem(), vmem(), vmem()],
+        out_specs=(vmem(),) * 4 + (smem(),),
         compiler_params=pltpu.CompilerParams(vmem_limit_bytes=VMEM_LIMIT),
         cost_estimate=pl.CostEstimate(flops=2_000_000_000, bytes_accessed=300_000, transcendentals=20_000),
         name="prepare",
-    )(lengths, pos, labels, owner, scores)
+    )(lengths, pos, labels, owner)
 
 
 def split_terms(value, terms):
@@ -477,15 +491,15 @@
 
     pos = place.reshape(1)
     leaf_rows = leaves.reshape(own, LANES)
-    own_scores = scores.reshape(own, LANES)
-    score_parts = [own_scores]
-    for begin in range(2):
+    first_scores, second_scores = stage(scores.reshape(own, LANES))
+    score_parts = [first_scores]
+    for begin, own_scores in enumerate((first_scores, second_scores)):
         links = [(z, z + 1) for z in range(begin, feat_count - 1, 2)]
         ends = [(z, z) for z in (0, feat_count - 1)] if begin else []
         score_parts.append(lax.ppermute(own_scores, "feat", links + [(b, a) for a, b in links] + ends))
     masks = feat_masks + query_masks[:0:-1] + query_masks[:1]
-    score_parts[0], qid, worth, inverse, perm, bounds = prepare(
-        feat_count, masks, lengths, pos, labels.reshape(-1, LANES), owner.reshape(-1, LANES), own_scores)
+    qid, worth, inverse, perm, bounds = prepare(
+        feat_count, masks, lengths, pos, labels.reshape(-1, LANES), owner.reshape(-1, LANES))
     lambdas, near_lambdas = pair_terms(feat_count, bounds, pos, score_parts, worth, qid, inverse)
     bins_t, tiles, sums = leaf_terms(perm, bins, leaf_rows, near_lambdas)
 

time: 45.3 us -> 45.8 us (1.011)
  local copies, waits for them, and re-layouts: 1.4 us -> 2.05 us
    pallas_call x0 -> x1, Pallas kernels: none -> 1.28 us  [stage(): pl.pallas_call(stage_kernel, out_shape=(jax.ShapeDtypeStruct(scores.shape...]
    pallas_call x1, Pallas kernels: 7.12 us -> 6.18 us  [pair_terms(): pl.pallas_call(functools.partial(pairs_kernel, feat_count), out_shape=(ja...]
    unnamed x12, local copies, waits for them, and re-layouts: 1.38 us -> 2.03 us
where the time goes in v9:
time: 45.8 us
  Pallas kernels  19.5 us (43%)
  starting transfers between devices  15.7 us (34%)
  waiting for transfers between devices  7.69 us (17%)
  local copies, waits for them, and re-layouts  2.05 us (4%)
  between operations  0.79 us (2%)
    ppermute x7, starting transfers between devices, swap(): return lax.ppermute(value, axes, [(p, p ^ mask) for p in range(count)])  11.4 us
    pallas_call x4, Pallas kernels, histogram_part(): pl.pallas_call(functools.partial(histogram_kernel, first, groups), out_sh...  8.86 us
    ppermute x7, waiting for transfers between devices, swap(): return lax.ppermute(value, axes, [(p, p ^ mask) for p in range(count)])  7.69 us
    pallas_call x1, Pallas kernels, pair_terms(): pl.pallas_call(functools.partial(pairs_kernel, feat_count), out_shape=(ja...  6.18 us
    ppermute x2, starting transfers between devices, local(): lax.ppermute(own_scores, 'feat', links + [(b, a) for a, b in links] + ends)  4.36 us
    unnamed x12, local copies, waits for them, and re-layouts  2.03 us
    pallas_call x1, Pallas kernels, prepare(): pl.pallas_call(functools.partial(prepare_kernel, feat_count, masks), out_...  1.86 us
    pallas_call x1, Pallas kernels, stage(): pl.pallas_call(stage_kernel, out_shape=(jax.ShapeDtypeStruct(scores.shape...  1.28 us
  transfers between devices with their start and end apart: 9, of which 4 were waited for; matrix products, arithmetic and copies ran while one was open for 0% of the time, Pallas kernels for 19%

profile of v9, /device:TPU:0, one launch (start us, length us, event | category | flops | bytes accessed | tf_op | source)
XLA Modules:
  0.0 45.8 jit_solution(16626328011439039983)
XLA Ops:
  0.6 1.3 %stage.1 = (f32[8,128]{1,0:T(8,128)}, f32[8,128]{1,0:T(8,128)}) custom-call(f32[8,128]{1,0:T(8,128)} %bitcast.11), custom_call_target="tpu_custom_call" | custom-call | flops 10000000000 | bytes 10000 | tf_op jit(solution)/shard_map/stage/pallas_call | solution.py:48
  1.9 3.0 %collective-permute-start = (f32[8,128]{1,0:T(8,128)}, f32[8,128]{1,0:T(8,128)S(1)}, u32[]{:S(2)}, u32[]{:S(2)}) collective-permute-start(f32[8,128]{1,0:T(8,128)} %get-tuple-element.22.refs_0_), channel_id=1, source_target_pairs={{0,1},{2,3},{1,0},{3,2},{4,5},{6,7},{5,4},{7,6},{8,9},{10,11},{9,8... | collective-permute-start | bytes 12296 | tf_op jit(solution)/shard_map/ppermute | solution.py:499
  4.9 1.3 %collective-permute-start.1 = (f32[8,128]{1,0:T(8,128)}, f32[8,128]{1,0:T(8,128)S(1)}, u32[]{:S(2)}, u32[]{:S(2)}) collective-permute-start(f32[8,128]{1,0:T(8,128)} %get-tuple-element.23), channel_id=1, source_target_pairs={{1,2},{2,1},{0,0},{3,3},{5,6},{6,5},{4,4},{7,7},{9,10},{10,9},{8,8... | collective-permute-start | bytes 12296 | tf_op jit(solution)/shard_map/ppermute | solution.py:499
  6.3 0.7 %copy-done.4 = s32[256]{0:T(256)S(1)} copy-done((s32[256]{0:T(256)S(1)}, s32[256]{0:T(256)}, u32[]{:S(2)}) %copy-start.4) | copy-done | bytes 1048
  7.0 0.0 copy-done.5
  7.0 1.9 %prepare.1 = (s32[32,128]{1,0:T(8,128)S(1)}, f32[32,128]{1,0:T(8,128)S(1)}, f32[1,1024]{1,0:T(1,128)S(1)}, bf16[256,256]{1,0:T(8,128)(2,1)S(1)}, s32[3,32]{1,0:T(4,128)S(1)}) custom-call(s32[1,16]{1,0:T(1,128)S(1)} %copy-done.5, s32[1]{0:T(128)} %bitcast.pos_ref, s32[32,128]{1,0:T(8,128)S(1)} %bitcast.9, s32[2,128]{1,0:T(2,128)S(1)} %bitcast.10), custom_call_target="tpu_custom_call" | custom-call | flops 2000000000 | bytes 300000 | tf_op jit(solution)/shard_map/prepare/pallas_call | solution.py:131
  8.8 0.0 copy-start.3
  8.8 0.0 collective-permute-done.refs_1_
  8.8 0.0 collective-permute-done.1.refs_2_
  8.9 0.7 %copy-done.3 = f32[8,128]{1,0:T(8,128)S(1)} copy-done((f32[8,128]{1,0:T(8,128)S(1)}, f32[8,128]{1,0:T(8,128)}, u32[]{:S(2)}) %copy-start.3) | copy-done | bytes 4120
  9.5 6.2 %pair_terms.1 = (f32[2,1024]{1,0:T(2,128)}, f32[2,1024]{1,0:T(2,128)S(1)}) custom-call(s32[3,32]{1,0:T(4,128)S(1)} %get-tuple-element.21.bounds_ref, s32[1]{0:T(128)} %bitcast.pos_ref, f32[8,128]{1,0:T(8,128)S(1)} %copy-done.3, f32[8,128]{1,0:T(8,128)S(1)} %collective-permute-done.refs_1_, f32[8,128]{1,0:T(8,128)S(1)} %collective-permute-done.1.refs_2_, ...), custom_call_target="tpu_custom_call" | custom-call | flops 8999999488 | bytes 200000 | tf_op jit(solution)/shard_map/pair_terms/pallas_call | solution.py:301
  15.7 0.7 %copy-done.1 = s32[1024]{0:T(1024)S(1)} copy-done((s32[1024]{0:T(1024)S(1)}, s32[1024]{0:T(1024)}, u32[]{:S(2)}) %copy-start.1) | copy-done | bytes 4120
  16.4 0.4 leaf_terms.1
  16.8 2.2 %histogram_part.5 = f32[200,256]{1,0:T(8,128)S(1)} custom-call(bf16[32,1024]{1,0:T(8,128)(2,1)S(1)} %get-tuple-element.33.tile_ref, f32[256,1024]{1,0:T(8,128)S(1)} %get-tuple-element.31.bins_ref, f32[8,256]{1,0:T(8,128)S(1)} %get-tuple-element.32.refs_0_), custom_call_target="tpu_custom_call" | custom-call | flops 2640000000 | bytes 480000 | tf_op jit(solution)/shard_map/histogram_part/pallas_call | solution.py:415
  19.0 0.1 collective-permute-start.2
  19.1 2.2 %histogram_part.4 = f32[192,256]{1,0:T(8,128)S(1)} custom-call(bf16[32,1024]{1,0:T(8,128)(2,1)S(1)} %get-tuple-element.33.tile_ref, f32[256,1024]{1,0:T(8,128)S(1)} %get-tuple-element.31.bins_ref), custom_call_target="tpu_custom_call" | custom-call | flops 2640000000 | bytes 480000 | tf_op jit(solution)/shard_map/histogram_part/pallas_call | solution.py:415
  21.3 0.0 collective-permute-done.2
  21.4 2.7 %collective-permute-start.4 = (f32[200,256]{1,0:T(8,128)S(1)}, f32[200,256]{1,0:T(8,128)S(1)}, u32[]{:S(2)}, u32[]{:S(2)}) collective-permute-start(f32[200,256]{1,0:T(8,128)S(1)} %pad_maximum_fusion), channel_id=1, source_target_pairs={{0,8},{1,9},{2,10},{3,11},{4,12},{5,13},{6,14},{7,15},{8,0},{9,1},... | collective-permute-start | bytes 614408 | tf_op jit(solution)/shard_map/ppermute | solution.py:490
  24.1 2.2 %histogram_part.7 = f32[192,256]{1,0:T(8,128)S(1)} custom-call(bf16[32,1024]{1,0:T(8,128)(2,1)S(1)} %get-tuple-element.33.tile_ref, f32[256,1024]{1,0:T(8,128)S(1)} %get-tuple-element.31.bins_ref), custom_call_target="tpu_custom_call" | custom-call | flops 2640000000 | bytes 480000 | tf_op jit(solution)/shard_map/histogram_part/pallas_call | solution.py:415
  26.3 0.3 collective-permute-start.3
  26.6 2.2 %histogram_part.6 = f32[192,256]{1,0:T(8,128)S(1)} custom-call(bf16[32,1024]{1,0:T(8,128)(2,1)S(1)} %get-tuple-element.33.tile_ref, f32[256,1024]{1,0:T(8,128)S(1)} %get-tuple-element.31.bins_ref), custom_call_target="tpu_custom_call" | custom-call | flops 2640000000 | bytes 480000 | tf_op jit(solution)/shard_map/histogram_part/pallas_call | solution.py:415
  28.8 0.0 collective-permute-done.3
  28.8 1.0 %collective-permute-done.4 = f32[200,256]{1,0:T(8,128)S(1)} collective-permute-done((f32[200,256]{1,0:T(8,128)S(1)}, f32[200,256]{1,0:T(8,128)S(1)}, u32[]{:S(2)}, u32[]{:S(2)}) %collective-permute-start.4) | collective-permute-done | bytes 204832 | tf_op jit(solution)/shard_map/ppermute | solution.py:490
  29.9 1.6 %collective-permute-start.5 = (f32[104,256]{1,0:T(8,128)S(1)}, f32[104,256]{1,0:T(8,128)S(1)}, u32[]{:S(2)}, u32[]{:S(2)}) collective-permute-start(f32[104,256]{1,0:T(8,128)S(1)} %pad_maximum_fusion.1), channel_id=1, source_target_pairs={{0,16},{1,17},{2,18},{3,19},{4,20},{5,21},{6,22},{7,23},{8,24},{9,... | collective-permute-start | bytes 319496 | tf_op jit(solution)/shard_map/ppermute | solution.py:490
  31.5 3.3 %collective-permute-done.5 = f32[104,256]{1,0:T(8,128)S(1)} collective-permute-done((f32[104,256]{1,0:T(8,128)S(1)}, f32[104,256]{1,0:T(8,128)S(1)}, u32[]{:S(2)}, u32[]{:S(2)}) %collective-permute-start.5) | collective-permute-done | bytes 106528 | tf_op jit(solution)/shard_map/ppermute | solution.py:490
  34.8 2.3 %collective-permute-start.6 = (f32[32,256]{1,0:T(8,128)S(1)}, f32[32,256]{1,0:T(8,128)S(1)}, u32[]{:S(2)}, u32[]{:S(2)}) collective-permute-start(f32[32,256]{1,0:T(8,128)S(1)} %get-tuple-element.44), channel_id=1, source_target_pairs={{0,3},{1,2},{2,1},{3,0},{4,7},{5,6},{6,5},{7,4},{8,11},{9,10},{10,... | collective-permute-start | bytes 98312 | tf_op jit(solution)/shard_map/ppermute | solution.py:490
  37.1 3.9 %collective-permute-start.7 = (f32[32,256]{1,0:T(8,128)S(1)}, f32[32,256]{1,0:T(8,128)S(1)}, u32[]{:S(2)}, u32[]{:S(2)}) collective-permute-start(f32[32,256]{1,0:T(8,128)S(1)} %get-tuple-element.43), channel_id=1, source_target_pairs={{0,2},{1,3},{2,0},{3,1},{4,6},{5,7},{6,4},{7,5},{8,10},{9,11},{10,... | collective-permute-start | bytes 98312 | tf_op jit(solution)/shard_map/ppermute | solution.py:490
  41.1 0.5 %collective-permute-start.8 = (f32[32,256]{1,0:T(8,128)S(1)}, f32[32,256]{1,0:T(8,128)S(1)}, u32[]{:S(2)}, u32[]{:S(2)}) collective-permute-start(f32[32,256]{1,0:T(8,128)S(1)} %get-tuple-element.42), channel_id=1, source_target_pairs={{0,1},{1,0},{2,3},{3,2},{4,5},{5,4},{6,7},{7,6},{8,9},{9,8},{10,11... | collective-permute-start | bytes 98312 | tf_op jit(solution)/shard_map/ppermute | solution.py:490
  41.6 0.0 collective-permute-done.6.refs_0_
  41.6 1.7 %collective-permute-done.7.refs_1_ = f32[32,256]{1,0:T(8,128)S(1)} collective-permute-done((f32[32,256]{1,0:T(8,128)S(1)}, f32[32,256]{1,0:T(8,128)S(1)}, u32[]{:S(2)}, u32[]{:S(2)}) %collective-permute-start.7) | collective-permute-done | bytes 32800 | tf_op jit(solution)/shard_map/ppermute | solution.py:490
  43.2 1.7 %collective-permute-done.8.refs_2_ = f32[32,256]{1,0:T(8,128)S(1)} collective-permute-done((f32[32,256]{1,0:T(8,128)S(1)}, f32[32,256]{1,0:T(8,128)S(1)}, u32[]{:S(2)}, u32[]{:S(2)}) %collective-permute-start.8) | collective-permute-done | bytes 32800 | tf_op jit(solution)/shard_map/ppermute | solution.py:490
  45.0 0.9 %finish.1 = (f32[8,128]{1,0:T(8,128)}, f32[8,128]{1,0:T(8,128)}, f32[3,2048]{1,0:T(4,128)}) custom-call(s32[8,128]{1,0:T(8,128)S(1)} %bitcast.8, f32[24,256]{1,0:T(8,128)S(1)} %get-tuple-element.41.kept_ref, f32[8,256]{1,0:T(8,128)S(1)} %slice_add_fusion.3.sums_ref, f32[32,256]{1,0:T(8,128)S(1)} %collective-permute-done.6.refs_0_, ...), custom_call_target="tpu_custom_call" | custom-call | tf_op jit(solution)/shard_map/finish/pallas_call | solution.py:455
  (18 shorter events, 0.2 us)
Async XLA Ops:
  1.9 4.4 %copy-start.2 = (s32[4096]{0:T(1024)S(1)}, s32[4096]{0:T(1024)}, u32[]{:S(2)}) copy-start(s32[4096]{0:T(1024)} %param.7) | copy-start | bytes 49156
  1.9 6.9 %collective-permute-start = (f32[8,128]{1,0:T(8,128)}, f32[8,128]{1,0:T(8,128)S(1)}, u32[]{:S(2)}, u32[]{:S(2)}) collective-permute-start(f32[8,128]{1,0:T(8,128)} %get-tuple-element.22.refs_0_), channel_id=1, source_target_pairs={{0,1},{2,3},{1,0},{3,2},{4,5},{6,7},{5,4},{7,6},{8,9},{10,11},{9,8... | collective-permute-start | bytes 12296 | tf_op jit(solution)/shard_map/ppermute | solution.py:499
  4.9 3.9 %collective-permute-start.1 = (f32[8,128]{1,0:T(8,128)}, f32[8,128]{1,0:T(8,128)S(1)}, u32[]{:S(2)}, u32[]{:S(2)}) collective-permute-start(f32[8,128]{1,0:T(8,128)} %get-tuple-element.23), channel_id=1, source_target_pairs={{1,2},{2,1},{0,0},{3,3},{5,6},{6,5},{4,4},{7,7},{9,10},{10,9},{8,8... | collective-permute-start | bytes 12296 | tf_op jit(solution)/shard_map/ppermute | solution.py:499
  6.3 0.7 %copy-start.4 = (s32[256]{0:T(256)S(1)}, s32[256]{0:T(256)}, u32[]{:S(2)}) copy-start(s32[256]{0:T(256)} %param.11) | copy-start | bytes 3076
  6.3 0.7 %copy-start.5 = (s32[1,16]{1,0:T(1,128)S(1)}, s32[1,16]{1,0:T(1,128)}, u32[]{:S(2)}) copy-start(s32[1,16]{1,0:T(1,128)} %len_ref.1) | copy-start | bytes 196
  8.8 0.7 %copy-start.3 = (f32[8,128]{1,0:T(8,128)S(1)}, f32[8,128]{1,0:T(8,128)}, u32[]{:S(2)}) copy-start(f32[8,128]{1,0:T(8,128)} %get-tuple-element.22.refs_0_) | copy-start | bytes 12292
  9.5 6.2 %copy-start = (s32[1024,256]{1,0:T(8,128)S(1)}, s32[1024,256]{1,0:T(8,128)}, u32[]{:S(2)}) copy-start(s32[1024,256]{1,0:T(8,128)} %bins_ref.1) | copy-start | bytes 3145732
  15.7 0.7 %copy-start.1 = (s32[1024]{0:T(1024)S(1)}, s32[1024]{0:T(1024)}, u32[]{:S(2)}) copy-start(s32[1024]{0:T(1024)} %param.8) | copy-start | bytes 12292
  19.0 2.3 %collective-permute-start.2 = (f32[200,256]{1,0:T(8,128)S(1)}, f32[200,256]{1,0:T(8,128)S(1)}, u32[]{:S(2)}, u32[]{:S(2)}) collective-permute-start(f32[200,256]{1,0:T(8,128)S(1)} %histogram_part.5), channel_id=1, source_target_pairs={{0,4},{1,5},{2,6},{3,7},{4,0},{5,1},{6,2},{7,3},{8,12},{9,13},{10,... | collective-permute-start | bytes 614408 | tf_op jit(solution)/shard_map/ppermute | solution.py:490
  21.4 8.4 %collective-permute-start.4 = (f32[200,256]{1,0:T(8,128)S(1)}, f32[200,256]{1,0:T(8,128)S(1)}, u32[]{:S(2)}, u32[]{:S(2)}) collective-permute-start(f32[200,256]{1,0:T(8,128)S(1)} %pad_maximum_fusion), channel_id=1, source_target_pairs={{0,8},{1,9},{2,10},{3,11},{4,12},{5,13},{6,14},{7,15},{8,0},{9,1},... | collective-permute-start | bytes 614408 | tf_op jit(solution)/shard_map/ppermute | solution.py:490
  26.3 2.5 %collective-permute-start.3 = (f32[192,256]{1,0:T(8,128)S(1)}, f32[192,256]{1,0:T(8,128)S(1)}, u32[]{:S(2)}, u32[]{:S(2)}) collective-permute-start(f32[192,256]{1,0:T(8,128)S(1)} %histogram_part.7), channel_id=1, source_target_pairs={{0,4},{1,5},{2,6},{3,7},{4,0},{5,1},{6,2},{7,3},{8,12},{9,13},{10,... | collective-permute-start | bytes 589832 | tf_op jit(solution)/shard_map/ppermute | solution.py:490
  29.9 4.9 %collective-permute-start.5 = (f32[104,256]{1,0:T(8,128)S(1)}, f32[104,256]{1,0:T(8,128)S(1)}, u32[]{:S(2)}, u32[]{:S(2)}) collective-permute-start(f32[104,256]{1,0:T(8,128)S(1)} %pad_maximum_fusion.1), channel_id=1, source_target_pairs={{0,16},{1,17},{2,18},{3,19},{4,20},{5,21},{6,22},{7,23},{8,24},{9,... | collective-permute-start | bytes 319496 | tf_op jit(solution)/shard_map/ppermute | solution.py:490
  34.8 6.8 %collective-permute-start.6 = (f32[32,256]{1,0:T(8,128)S(1)}, f32[32,256]{1,0:T(8,128)S(1)}, u32[]{:S(2)}, u32[]{:S(2)}) collective-permute-start(f32[32,256]{1,0:T(8,128)S(1)} %get-tuple-element.44), channel_id=1, source_target_pairs={{0,3},{1,2},{2,1},{3,0},{4,7},{5,6},{6,5},{7,4},{8,11},{9,10},{10,... | collective-permute-start | bytes 98312 | tf_op jit(solution)/shard_map/ppermute | solution.py:490
  37.1 6.1 %collective-permute-start.7 = (f32[32,256]{1,0:T(8,128)S(1)}, f32[32,256]{1,0:T(8,128)S(1)}, u32[]{:S(2)}, u32[]{:S(2)}) collective-permute-start(f32[32,256]{1,0:T(8,128)S(1)} %get-tuple-element.43), channel_id=1, source_target_pairs={{0,2},{1,3},{2,0},{3,1},{4,6},{5,7},{6,4},{7,5},{8,10},{9,11},{10,... | collective-permute-start | bytes 98312 | tf_op jit(solution)/shard_map/ppermute | solution.py:490
  41.1 3.9 %collective-permute-start.8 = (f32[32,256]{1,0:T(8,128)S(1)}, f32[32,256]{1,0:T(8,128)S(1)}, u32[]{:S(2)}, u32[]{:S(2)}) collective-permute-start(f32[32,256]{1,0:T(8,128)S(1)} %get-tuple-element.42), channel_id=1, source_target_pairs={{0,1},{1,0},{2,3},{3,2},{4,5},{5,4},{6,7},{7,6},{8,9},{9,8},{10,11... | collective-permute-start | bytes 98312 | tf_op jit(solution)/shard_map/ppermute | solution.py:490

commit v10 on v8

--- a/solution.py
+++ b/solution.py
@@ -481,8 +481,8 @@
     score_parts = [own_scores]
     for begin in range(2):
         links = [(z, z + 1) for z in range(begin, feat_count - 1, 2)]
-        ends = [(z, z) for z in (0, feat_count - 1)] if begin else []
-        score_parts.append(lax.ppermute(own_scores, "feat", links + [(b, a) for a, b in links] + ends))
+        links += [(0, feat_count - 1)] if begin else []
+        score_parts.append(lax.ppermute(own_scores, "feat", links + [(b, a) for a, b in links]))
     masks = feat_masks + query_masks[:0:-1] + query_masks[:1]
     score_parts[0], qid, worth, inverse, perm, bounds = prepare(
         feat_count, masks, lengths, pos, labels.reshape(-1, LANES), owner.reshape(-1, LANES), own_scores)

time: 45.3 us -> 43.6 us (0.962)
  Pallas kernels: 19.1 us -> 17.2 us
    pallas_call x1, Pallas kernels: 7.12 us -> 5.18 us  [pair_terms(): pl.pallas_call(functools.partial(pairs_kernel, feat_count), out_shape=(ja...]
    ppermute x7, starting transfers between devices: 11.4 us -> 9.81 us  [swap(): return lax.ppermute(value, axes, [(p, p ^ mask) for p in range(count)])]
    ppermute x2, starting transfers between devices: 4.42 us -> 5.56 us  [local(): lax.ppermute(own_scores, 'feat', links + [(b, a) for a, b in links])]
    ppermute x2, waiting for transfers between devices: 0.01 us -> 0.56 us  [local(): lax.ppermute(own_scores, 'feat', links + [(b, a) for a, b in links])]
  transfers between devices with their start and end apart: 9 -> 9, of which waited for: 4 -> 5; matrix products, arithmetic and copies ran while one was open for 0% -> 0% of each run, Pallas kernels for 19% -> 20%
where the time goes in v10:
time: 43.6 us; the launch traced here: 43.3 us
  Pallas kernels  17.2 us (39%)
  starting transfers between devices  15.4 us (35%)
  waiting for transfers between devices  8.46 us (19%)
  local copies, waits for them, and re-layouts  1.43 us (3%)
  between operations  0.79 us (2%)
    ppermute x7, starting transfers between devices, swap(): return lax.ppermute(value, axes, [(p, p ^ mask) for p in range(count)])  9.81 us
    pallas_call x4, Pallas kernels, histogram_part(): pl.pallas_call(functools.partial(histogram_kernel, first, groups), out_sh...  8.85 us
    ppermute x7, waiting for transfers between devices, swap(): return lax.ppermute(value, axes, [(p, p ^ mask) for p in range(count)])  7.9 us
    ppermute x2, starting transfers between devices, local(): lax.ppermute(own_scores, 'feat', links + [(b, a) for a, b in links])  5.56 us
    pallas_call x1, Pallas kernels, pair_terms(): pl.pallas_call(functools.partial(pairs_kernel, feat_count), out_shape=(ja...  5.18 us
    pallas_call x1, Pallas kernels, prepare(): pl.pallas_call(functools.partial(prepare_kernel, feat_count, masks), out_...  1.84 us
    unnamed x12, local copies, waits for them, and re-layouts  1.41 us
  transfers between devices with their start and end apart: 9, of which 5 were waited for; matrix products, arithmetic and copies ran while one was open for 0% of the time, Pallas kernels for 20%

profile of v10, /device:TPU:0, one launch (start us, length us, event | category | flops | bytes accessed | tf_op | source)
XLA Modules:
  0.0 43.3 jit_solution(9322295166634754833)
XLA Ops:
  0.6 0.0 copy-start.2
  0.6 3.1 %collective-permute-start = (f32[8,128]{1,0:T(8,128)}, f32[8,128]{1,0:T(8,128)S(1)}, u32[]{:S(2)}, u32[]{:S(2)}) collective-permute-start(f32[8,128]{1,0:T(8,128)} %bitcast.10), channel_id=1, source_target_pairs={{0,1},{2,3},{1,0},{3,2},{4,5},{6,7},{5,4},{7,6},{8,9},{10,11},{9,8... | collective-permute-start | bytes 12296 | tf_op jit(solution)/shard_map/ppermute | solution.py:485
  3.7 2.5 %collective-permute-start.1 = (f32[8,128]{1,0:T(8,128)}, f32[8,128]{1,0:T(8,128)S(1)}, u32[]{:S(2)}, u32[]{:S(2)}) collective-permute-start(f32[8,128]{1,0:T(8,128)} %bitcast.11), channel_id=1, source_target_pairs={{1,2},{0,3},{2,1},{3,0},{5,6},{4,7},{6,5},{7,4},{9,10},{8,11},{10,... | collective-permute-start | bytes 12296 | tf_op jit(solution)/shard_map/ppermute | solution.py:485
  6.2 0.0 copy-done.2
  6.2 0.7 %copy-done.3 = f32[1024]{0:T(1024)S(1)} copy-done((f32[1024]{0:T(1024)S(1)}, f32[1024]{0:T(1024)}, u32[]{:S(2)}) %copy-start.3) | copy-done | bytes 4120
  6.9 0.0 copy-done.5
  6.9 1.8 %prepare.1 = (f32[8,128]{1,0:T(8,128)S(1)}, s32[32,128]{1,0:T(8,128)S(1)}, f32[32,128]{1,0:T(8,128)S(1)}, f32[1,1024]{1,0:T(1,128)S(1)}, bf16[256,256]{1,0:T(8,128)(2,1)S(1)}, /*index=5*/s32[3,32]{1,0:T(4,128)S(1)}) custom-call(s32[1,16]{1,0:T(1,128)S(1)} %copy-done.5, s32[1]{0:T(128)} %bitcast.pos_ref, s32[32,128]{1,0:T(8,128)S(1)} %bitcast.9, ...), custom_call_target="tpu_custom_call" | custom-call | flops 2000000000 | bytes 300000 | tf_op jit(solution)/shard_map/prepare/pallas_call | solution.py:116
  8.8 0.0 collective-permute-done.refs_1_
  8.8 0.6 %collective-permute-done.1.refs_2_ = f32[8,128]{1,0:T(8,128)S(1)} collective-permute-done((f32[8,128]{1,0:T(8,128)}, f32[8,128]{1,0:T(8,128)S(1)}, u32[]{:S(2)}, u32[]{:S(2)}) %collective-permute-start.1) | collective-permute-done | bytes 4128 | tf_op jit(solution)/shard_map/ppermute | solution.py:485
  9.3 5.2 %pair_terms.1 = (f32[2,1024]{1,0:T(2,128)}, f32[2,1024]{1,0:T(2,128)S(1)}) custom-call(s32[3,32]{1,0:T(4,128)S(1)} %get-tuple-element.20.bounds_ref, s32[1]{0:T(128)} %bitcast.pos_ref, f32[8,128]{1,0:T(8,128)S(1)} %get-tuple-element.21.refs_0_, f32[8,128]{1,0:T(8,128)S(1)} %collective-permute-done.refs_1_, f32[8,128]{1,0:T(8,128)S(1)} %collective-permute-done.1.refs_2_, ...), custom_call_target="tpu_custom_call" | custom-call | flops 8999999488 | bytes 200000 | tf_op jit(solution)/shard_map/pair_terms/pallas_call | solution.py:287
  14.5 0.0 copy-done
  14.5 0.7 %copy-done.1 = s32[1024]{0:T(1024)S(1)} copy-done((s32[1024]{0:T(1024)S(1)}, s32[1024]{0:T(1024)}, u32[]{:S(2)}) %copy-start.1) | copy-done | bytes 4120
  15.2 0.4 leaf_terms.1
  15.6 2.2 %histogram_part.5 = f32[200,256]{1,0:T(8,128)S(1)} custom-call(bf16[32,1024]{1,0:T(8,128)(2,1)S(1)} %get-tuple-element.31.tile_ref, f32[256,1024]{1,0:T(8,128)S(1)} %get-tuple-element.29.bins_ref, f32[8,256]{1,0:T(8,128)S(1)} %get-tuple-element.30.refs_0_), custom_call_target="tpu_custom_call" | custom-call | flops 2640000000 | bytes 480000 | tf_op jit(solution)/shard_map/histogram_part/pallas_call | solution.py:401
  17.9 0.1 collective-permute-start.2
  17.9 2.2 %histogram_part.4 = f32[192,256]{1,0:T(8,128)S(1)} custom-call(bf16[32,1024]{1,0:T(8,128)(2,1)S(1)} %get-tuple-element.31.tile_ref, f32[256,1024]{1,0:T(8,128)S(1)} %get-tuple-element.29.bins_ref), custom_call_target="tpu_custom_call" | custom-call | flops 2640000000 | bytes 480000 | tf_op jit(solution)/shard_map/histogram_part/pallas_call | solution.py:401
  20.2 0.0 collective-permute-done.2
  20.2 3.8 %collective-permute-start.4 = (f32[200,256]{1,0:T(8,128)S(1)}, f32[200,256]{1,0:T(8,128)S(1)}, u32[]{:S(2)}, u32[]{:S(2)}) collective-permute-start(f32[200,256]{1,0:T(8,128)S(1)} %pad_maximum_fusion), channel_id=1, source_target_pairs={{0,8},{1,9},{2,10},{3,11},{4,12},{5,13},{6,14},{7,15},{8,0},{9,1},... | collective-permute-start | bytes 614408 | tf_op jit(solution)/shard_map/ppermute | solution.py:476
  24.1 2.2 %histogram_part.7 = f32[192,256]{1,0:T(8,128)S(1)} custom-call(bf16[32,1024]{1,0:T(8,128)(2,1)S(1)} %get-tuple-element.31.tile_ref, f32[256,1024]{1,0:T(8,128)S(1)} %get-tuple-element.29.bins_ref), custom_call_target="tpu_custom_call" | custom-call | flops 2640000000 | bytes 480000 | tf_op jit(solution)/shard_map/histogram_part/pallas_call | solution.py:401
  26.3 0.3 collective-permute-start.3
  26.6 2.2 %histogram_part.6 = f32[192,256]{1,0:T(8,128)S(1)} custom-call(bf16[32,1024]{1,0:T(8,128)(2,1)S(1)} %get-tuple-element.31.tile_ref, f32[256,1024]{1,0:T(8,128)S(1)} %get-tuple-element.29.bins_ref), custom_call_target="tpu_custom_call" | custom-call | flops 2640000000 | bytes 480000 | tf_op jit(solution)/shard_map/histogram_part/pallas_call | solution.py:401
  28.8 0.0 collective-permute-done.3
  28.8 1.0 %collective-permute-done.4 = f32[200,256]{1,0:T(8,128)S(1)} collective-permute-done((f32[200,256]{1,0:T(8,128)S(1)}, f32[200,256]{1,0:T(8,128)S(1)}, u32[]{:S(2)}, u32[]{:S(2)}) %collective-permute-start.4) | collective-permute-done | bytes 204832 | tf_op jit(solution)/shard_map/ppermute | solution.py:476
  29.9 1.2 %collective-permute-start.5 = (f32[104,256]{1,0:T(8,128)S(1)}, f32[104,256]{1,0:T(8,128)S(1)}, u32[]{:S(2)}, u32[]{:S(2)}) collective-permute-start(f32[104,256]{1,0:T(8,128)S(1)} %pad_maximum_fusion.1), channel_id=1, source_target_pairs={{0,16},{1,17},{2,18},{3,19},{4,20},{5,21},{6,22},{7,23},{8,24},{9,... | collective-permute-start | bytes 319496 | tf_op jit(solution)/shard_map/ppermute | solution.py:476
  31.1 3.7 %collective-permute-done.5 = f32[104,256]{1,0:T(8,128)S(1)} collective-permute-done((f32[104,256]{1,0:T(8,128)S(1)}, f32[104,256]{1,0:T(8,128)S(1)}, u32[]{:S(2)}, u32[]{:S(2)}) %collective-permute-start.5) | collective-permute-done | bytes 106528 | tf_op jit(solution)/shard_map/ppermute | solution.py:476
  34.8 2.8 %collective-permute-start.6 = (f32[32,256]{1,0:T(8,128)S(1)}, f32[32,256]{1,0:T(8,128)S(1)}, u32[]{:S(2)}, u32[]{:S(2)}) collective-permute-start(f32[32,256]{1,0:T(8,128)S(1)} %get-tuple-element.42), channel_id=1, source_target_pairs={{0,3},{1,2},{2,1},{3,0},{4,7},{5,6},{6,5},{7,4},{8,11},{9,10},{10,... | collective-permute-start | bytes 98312 | tf_op jit(solution)/shard_map/ppermute | solution.py:476
  37.7 0.0 collective-permute-start.7
  37.7 1.6 %collective-permute-start.8 = (f32[32,256]{1,0:T(8,128)S(1)}, f32[32,256]{1,0:T(8,128)S(1)}, u32[]{:S(2)}, u32[]{:S(2)}) collective-permute-start(f32[32,256]{1,0:T(8,128)S(1)} %get-tuple-element.40), channel_id=1, source_target_pairs={{0,1},{1,0},{2,3},{3,2},{4,5},{5,4},{6,7},{7,6},{8,9},{9,8},{10,11... | collective-permute-start | bytes 98312 | tf_op jit(solution)/shard_map/ppermute | solution.py:476
  39.3 1.4 %collective-permute-done.6.refs_0_ = f32[32,256]{1,0:T(8,128)S(1)} collective-permute-done((f32[32,256]{1,0:T(8,128)S(1)}, f32[32,256]{1,0:T(8,128)S(1)}, u32[]{:S(2)}, u32[]{:S(2)}) %collective-permute-start.6) | collective-permute-done | bytes 32800 | tf_op jit(solution)/shard_map/ppermute | solution.py:476
  40.7 1.8 %collective-permute-done.7.refs_1_ = f32[32,256]{1,0:T(8,128)S(1)} collective-permute-done((f32[32,256]{1,0:T(8,128)S(1)}, f32[32,256]{1,0:T(8,128)S(1)}, u32[]{:S(2)}, u32[]{:S(2)}) %collective-permute-start.7) | collective-permute-done | bytes 32800 | tf_op jit(solution)/shard_map/ppermute | solution.py:476
  42.5 0.0 collective-permute-done.8.refs_2_
  42.5 0.9 %finish.1 = (f32[8,128]{1,0:T(8,128)}, f32[8,128]{1,0:T(8,128)}, f32[3,2048]{1,0:T(4,128)}) custom-call(s32[8,128]{1,0:T(8,128)S(1)} %bitcast.8, f32[24,256]{1,0:T(8,128)S(1)} %get-tuple-element.39.kept_ref, f32[8,256]{1,0:T(8,128)S(1)} %slice_add_fusion.3.sums_ref, f32[32,256]{1,0:T(8,128)S(1)} %collective-permute-done.6.refs_0_, ...), custom_call_target="tpu_custom_call" | custom-call | tf_op jit(solution)/shard_map/finish/pallas_call | solution.py:441
  (17 shorter events, 0.2 us)
Async XLA Ops:
  0.6 5.6 %copy-start.2 = (s32[4096]{0:T(1024)S(1)}, s32[4096]{0:T(1024)}, u32[]{:S(2)}) copy-start(s32[4096]{0:T(1024)} %param.7) | copy-start | bytes 49156
  0.6 8.1 %collective-permute-start = (f32[8,128]{1,0:T(8,128)}, f32[8,128]{1,0:T(8,128)S(1)}, u32[]{:S(2)}, u32[]{:S(2)}) collective-permute-start(f32[8,128]{1,0:T(8,128)} %bitcast.10), channel_id=1, source_target_pairs={{0,1},{2,3},{1,0},{3,2},{4,5},{6,7},{5,4},{7,6},{8,9},{10,11},{9,8... | collective-permute-start | bytes 12296 | tf_op jit(solution)/shard_map/ppermute | solution.py:485
  3.7 5.6 %collective-permute-start.1 = (f32[8,128]{1,0:T(8,128)}, f32[8,128]{1,0:T(8,128)S(1)}, u32[]{:S(2)}, u32[]{:S(2)}) collective-permute-start(f32[8,128]{1,0:T(8,128)} %bitcast.11), channel_id=1, source_target_pairs={{1,2},{0,3},{2,1},{3,0},{5,6},{4,7},{6,5},{7,4},{9,10},{8,11},{10,... | collective-permute-start | bytes 12296 | tf_op jit(solution)/shard_map/ppermute | solution.py:485
  6.2 0.7 %copy-start.3 = (f32[1024]{0:T(1024)S(1)}, f32[1024]{0:T(1024)}, u32[]{:S(2)}) copy-start(f32[1024]{0:T(1024)} %param.6) | copy-start | bytes 12292
  6.2 0.7 %copy-start.4 = (s32[256]{0:T(256)S(1)}, s32[256]{0:T(256)}, u32[]{:S(2)}) copy-start(s32[256]{0:T(256)} %param.11) | copy-start | bytes 3076
  6.2 0.7 %copy-start.5 = (s32[1,16]{1,0:T(1,128)S(1)}, s32[1,16]{1,0:T(1,128)}, u32[]{:S(2)}) copy-start(s32[1,16]{1,0:T(1,128)} %len_ref.1) | copy-start | bytes 196
  9.3 5.2 %copy-start = (s32[1024,256]{1,0:T(8,128)S(1)}, s32[1024,256]{1,0:T(8,128)}, u32[]{:S(2)}) copy-start(s32[1024,256]{1,0:T(8,128)} %bins_ref.1) | copy-start | bytes 3145732
  14.5 0.7 %copy-start.1 = (s32[1024]{0:T(1024)S(1)}, s32[1024]{0:T(1024)}, u32[]{:S(2)}) copy-start(s32[1024]{0:T(1024)} %param.8) | copy-start | bytes 12292
  17.9 2.3 %collective-permute-start.2 = (f32[200,256]{1,0:T(8,128)S(1)}, f32[200,256]{1,0:T(8,128)S(1)}, u32[]{:S(2)}, u32[]{:S(2)}) collective-permute-start(f32[200,256]{1,0:T(8,128)S(1)} %histogram_part.5), channel_id=1, source_target_pairs={{0,4},{1,5},{2,6},{3,7},{4,0},{5,1},{6,2},{7,3},{8,12},{9,13},{10,... | collective-permute-start | bytes 614408 | tf_op jit(solution)/shard_map/ppermute | solution.py:476
  20.2 9.6 %collective-permute-start.4 = (f32[200,256]{1,0:T(8,128)S(1)}, f32[200,256]{1,0:T(8,128)S(1)}, u32[]{:S(2)}, u32[]{:S(2)}) collective-permute-start(f32[200,256]{1,0:T(8,128)S(1)} %pad_maximum_fusion), channel_id=1, source_target_pairs={{0,8},{1,9},{2,10},{3,11},{4,12},{5,13},{6,14},{7,15},{8,0},{9,1},... | collective-permute-start | bytes 614408 | tf_op jit(solution)/shard_map/ppermute | solution.py:476
  26.3 2.5 %collective-permute-start.3 = (f32[192,256]{1,0:T(8,128)S(1)}, f32[192,256]{1,0:T(8,128)S(1)}, u32[]{:S(2)}, u32[]{:S(2)}) collective-permute-start(f32[192,256]{1,0:T(8,128)S(1)} %histogram_part.7), channel_id=1, source_target_pairs={{0,4},{1,5},{2,6},{3,7},{4,0},{5,1},{6,2},{7,3},{8,12},{9,13},{10,... | collective-permute-start | bytes 589832 | tf_op jit(solution)/shard_map/ppermute | solution.py:476
  29.9 4.9 %collective-permute-start.5 = (f32[104,256]{1,0:T(8,128)S(1)}, f32[104,256]{1,0:T(8,128)S(1)}, u32[]{:S(2)}, u32[]{:S(2)}) collective-permute-start(f32[104,256]{1,0:T(8,128)S(1)} %pad_maximum_fusion.1), channel_id=1, source_target_pairs={{0,16},{1,17},{2,18},{3,19},{4,20},{5,21},{6,22},{7,23},{8,24},{9,... | collective-permute-start | bytes 319496 | tf_op jit(solution)/shard_map/ppermute | solution.py:476
  34.8 5.9 %collective-permute-start.6 = (f32[32,256]{1,0:T(8,128)S(1)}, f32[32,256]{1,0:T(8,128)S(1)}, u32[]{:S(2)}, u32[]{:S(2)}) collective-permute-start(f32[32,256]{1,0:T(8,128)S(1)} %get-tuple-element.42), channel_id=1, source_target_pairs={{0,3},{1,2},{2,1},{3,0},{4,7},{5,6},{6,5},{7,4},{8,11},{9,10},{10,... | collective-permute-start | bytes 98312 | tf_op jit(solution)/shard_map/ppermute | solution.py:476
  37.7 4.8 %collective-permute-start.7 = (f32[32,256]{1,0:T(8,128)S(1)}, f32[32,256]{1,0:T(8,128)S(1)}, u32[]{:S(2)}, u32[]{:S(2)}) collective-permute-start(f32[32,256]{1,0:T(8,128)S(1)} %get-tuple-element.41), channel_id=1, source_target_pairs={{0,2},{1,3},{2,0},{3,1},{4,6},{5,7},{6,4},{7,5},{8,10},{9,11},{10,... | collective-permute-start | bytes 98312 | tf_op jit(solution)/shard_map/ppermute | solution.py:476
  37.7 4.8 %collective-permute-start.8 = (f32[32,256]{1,0:T(8,128)S(1)}, f32[32,256]{1,0:T(8,128)S(1)}, u32[]{:S(2)}, u32[]{:S(2)}) collective-permute-start(f32[32,256]{1,0:T(8,128)S(1)} %get-tuple-element.40), channel_id=1, source_target_pairs={{0,1},{1,0},{2,3},{3,2},{4,5},{5,4},{6,7},{7,6},{8,9},{9,8},{10,11... | collective-permute-start | bytes 98312 | tf_op jit(solution)/shard_map/ppermute | solution.py:476

commit v11 on v10

--- a/solution.py
+++ b/solution.py
@@ -50,6 +50,9 @@
     begin = jnp.zeros((queries, LANES), jnp.int32)
     finish = jnp.zeros((queries, LANES), jnp.int32)
     which = iota((queries, LANES), 0)
+    group = iota((1, LANES), 1) * LANES
+    low = jnp.zeros((1, LANES), jnp.int32)
+    high = first_end = jnp.full((1, LANES), rows * LANES, jnp.int32)
     start = jnp.int32(0)
     for q in range(queries):
         end = start + len_ref[0, q]
@@ -57,18 +60,11 @@
         begin = jnp.where(which == q, start, begin)
         finish = jnp.where(which == q, end, finish)
 
-        def set_low(r, carry, start=start, end=end):
-            bounds_ref[0, r] = start
-            bounds_ref[2, r] = end
-            return carry
-
-        def set_high(r, carry, end=end):
-            bounds_ref[1, r] = end
-            return carry
-
-        lax.fori_loop((start + LANES - 1) // LANES, (end + LANES - 1) // LANES, set_low, 0)
-        lax.fori_loop(start // LANES, end // LANES, set_high, 0)
+        low = low + jnp.where(end <= group, len_ref[0, q], 0)
+        high = jnp.minimum(high, jnp.where(end >= group + LANES, end, rows * LANES))
+        first_end = jnp.minimum(first_end, jnp.where(end > group, end, rows * LANES))
         start = end
+    bounds_ref[...] = jnp.concatenate([low, high, first_end, low, low, low, low, low], axis=0)
     qid_ref[...] = qid
     worth_ref[...] = jnp.left_shift(1, lab_ref[...]).astype(F32)
 
@@ -121,10 +117,10 @@
             jax.ShapeDtypeStruct((rows, LANES), F32),
             jax.ShapeDtypeStruct((1, rows // feat_count * LANES), F32),
             jax.ShapeDtypeStruct((features, features), BF16),
-            jax.ShapeDtypeStruct((3, rows), jnp.int32),
+            jax.ShapeDtypeStruct((8, LANES), jnp.int32),
         ),
         in_specs=[smem(), smem(), vmem(), vmem(), vmem()],
-        out_specs=(vmem(),) * 5 + (smem(),),
+        out_specs=(vmem(),) * 6,
         compiler_params=pltpu.CompilerParams(vmem_limit_bytes=VMEM_LIMIT),
         cost_estimate=pl.CostEstimate(flops=2_000_000_000, bytes_accessed=300_000, transcendentals=20_000),
         name="prepare",
@@ -150,7 +146,7 @@
     docs = own * LANES
     me = pos_ref[0] % feat_count
     s_row[...] = jnp.zeros(s_row.shape, F32)
-    near = [me, me ^ 1, ((me + 1) ^ 1) - 1]
+    near = [me, ((me + 1) ^ 1) - 1, me ^ 1]
     for where, ref in zip(near, scores):
         @pl.when((where >= 0) & (where < feat_count))
         def _(where=where, ref=ref):
@@ -404,7 +400,7 @@
         in_specs=[vmem()] * (2 + len(tail)),
         out_specs=vmem(),
         compiler_params=pltpu.CompilerParams(vmem_limit_bytes=VMEM_LIMIT),
-        cost_estimate=pl.CostEstimate(flops=groups * 330_000_000, bytes_accessed=groups * 60_000, transcendentals=0),
+        cost_estimate=pl.CostEstimate(flops=groups * 1_000_000, bytes_accessed=groups * 1_000, transcendentals=0),
         name="histogram_part",
     )(tiles, bins_t, *tail)
 
@@ -479,7 +475,7 @@
     leaf_rows = leaves.reshape(own, LANES)
     own_scores = scores.reshape(own, LANES)
     score_parts = [own_scores]
-    for begin in range(2):
+    for begin in (1, 0):
         links = [(z, z + 1) for z in range(begin, feat_count - 1, 2)]
         links += [(0, feat_count - 1)] if begin else []
         score_parts.append(lax.ppermute(own_scores, "feat", links + [(b, a) for a, b in links]))
@@ -500,17 +496,24 @@
     def join(block, total):
         return jnp.concatenate([block, total], axis=0)
 
-    quarter = features // GROUP // 4
-    edge = count // 4 * unit
-    arrived = swap(part(tiles, 3 * quarter, 4 * quarter, sums), query_masks[0])
-    far = part(tiles, quarter, 2 * quarter) + arrived[:edge]
-    sums = sums + arrived[edge:]
-    message, tiles = lax.optimization_barrier((join(far, sums), tiles))
-    crossed = swap(message, query_masks[1])
-    arrived = swap(part(tiles, 2 * quarter, 3 * quarter), query_masks[0])
-    kept = part(tiles, 0, quarter) + arrived + crossed[:edge]
-    sums = sums + crossed[edge:]
-    for mask in query_masks[2:]:
+    eighth = features // GROUP // 8
+    edge = count // 8 * unit
+    arrived = swap(part(tiles, 6 * eighth, 8 * eighth, sums), query_masks[0])
+    block = part(tiles, 3 * eighth, 4 * eighth) + arrived[edge:2 * edge]
+    sums = sums + arrived[2 * edge:]
+    message, tiles = lax.optimization_barrier((join(block, sums), tiles))
+    crossed_far = swap(message, query_masks[1])
+    block = part(tiles, 2 * eighth, 3 * eighth) + arrived[:edge]
+    message, tiles = lax.optimization_barrier((block, tiles))
+    crossed_near = swap(message, query_masks[1])
+    arrived = swap(part(tiles, 4 * eighth, 6 * eighth), query_masks[0])
+    block = part(tiles, eighth, 2 * eighth) + arrived[edge:] + crossed_far[:edge]
+    sums = sums + crossed_far[edge:]
+    message, tiles = lax.optimization_barrier((join(block, sums), tiles))
+    turned = swap(message, query_masks[2])
+    kept = part(tiles, 0, eighth) + arrived[:edge] + crossed_near + turned[:edge]
+    sums = sums + turned[edge:]
+    for mask in query_masks[3:]:
         edge = edge // 2
         arrived = swap(join(kept[edge:], sums), mask)
         kept = kept[:edge] + arrived[:edge]

time: 43.6 us -> 42.3 us (0.970)
  starting transfers between devices: 15.4 us -> 13.5 us
    ppermute x2, waiting for transfers between devices: 0.56 us -> 2.04 us  [local(): lax.ppermute(own_scores, 'feat', links + [(b, a) for a, b in links])]
    ppermute x7 -> x8, starting transfers between devices: 9.81 us -> 8.39 us  [swap(): return lax.ppermute(value, axes, [(p, p ^ mask) for p in range(count)])]
    ppermute x7 -> x8, waiting for transfers between devices: 7.9 us -> 6.68 us  [swap(): return lax.ppermute(value, axes, [(p, p ^ mask) for p in range(count)])]
    pallas_call x1, Pallas kernels: 5.18 us -> 6.36 us  [pair_terms(): pl.pallas_call(functools.partial(pairs_kernel, feat_count), out_shape=(ja...]
    pallas_call x1, Pallas kernels: 1.84 us -> 1.01 us  [prepare(): pl.pallas_call(functools.partial(prepare_kernel, feat_count, masks), out_...]
    ppermute x2, starting transfers between devices: 5.56 us -> 5.12 us  [local(): lax.ppermute(own_scores, 'feat', links + [(b, a) for a, b in links])]
    pallas_call x4 -> x6, Pallas kernels: 8.85 us -> 8.86 us  [histogram_part(): pl.pallas_call(functools.partial(histogram_kernel, first, groups), out_sh...]
  transfers between devices with their start and end apart: 9 -> 10, of which waited for: 5 -> 7; matrix products, arithmetic and copies ran while one was open for 0% -> 0% of each run, Pallas kernels for 20% -> 16%
where the time goes in v11:
time: 42.3 us; the launch traced here: 42.1 us
  Pallas kernels  17.5 us (41%)
  starting transfers between devices  13.5 us (32%)
  waiting for transfers between devices  8.72 us (21%)
  local copies, waits for them, and re-layouts  1.44 us (3%)
  between operations  0.77 us (2%)
    pallas_call x6, Pallas kernels, histogram_part(): pl.pallas_call(functools.partial(histogram_kernel, first, groups), out_sh...  8.86 us
    ppermute x8, starting transfers between devices, swap(): return lax.ppermute(value, axes, [(p, p ^ mask) for p in range(count)])  8.39 us
    ppermute x8, waiting for transfers between devices, swap(): return lax.ppermute(value, axes, [(p, p ^ mask) for p in range(count)])  6.68 us
    pallas_call x1, Pallas kernels, pair_terms(): pl.pallas_call(functools.partial(pairs_kernel, feat_count), out_shape=(ja...  6.36 us
    ppermute x2, starting transfers between devices, local(): lax.ppermute(own_scores, 'feat', links + [(b, a) for a, b in links])  5.12 us
    ppermute x2, waiting for transfers between devices, local(): lax.ppermute(own_scores, 'feat', links + [(b, a) for a, b in links])  2.04 us
    unnamed x12, local copies, waits for them, and re-layouts  1.43 us
    pallas_call x1, Pallas kernels, prepare(): pl.pallas_call(functools.partial(prepare_kernel, feat_count, masks), out_...  1.01 us
  transfers between devices with their start and end apart: 10, of which 7 were waited for; matrix products, arithmetic and copies ran while one was open for 0% of the time, Pallas kernels for 16%

profile of v11, /device:TPU:0, one launch (start us, length us, event | category | flops | bytes accessed | tf_op | source)
XLA Modules:
  0.0 42.1 jit_solution(5111164631331623561)
XLA Ops:
  0.6 5.1 %collective-permute-start = (f32[8,128]{1,0:T(8,128)}, f32[8,128]{1,0:T(8,128)S(1)}, u32[]{:S(2)}, u32[]{:S(2)}) collective-permute-start(f32[8,128]{1,0:T(8,128)} %bitcast.10), channel_id=1, source_target_pairs={{1,2},{0,3},{2,1},{3,0},{5,6},{4,7},{6,5},{7,4},{9,10},{8,11},{10,... | collective-permute-start | bytes 12296 | tf_op jit(solution)/shard_map/ppermute | solution.py:481
  5.8 0.0 collective-permute-start.1
  5.8 0.7 %copy-done.3 = f32[1024]{0:T(1024)S(1)} copy-done((f32[1024]{0:T(1024)S(1)}, f32[1024]{0:T(1024)}, u32[]{:S(2)}) %copy-start.3) | copy-done | bytes 4120
  6.5 1.0 %prepare.1 = (f32[8,128]{1,0:T(8,128)S(1)}, s32[32,128]{1,0:T(8,128)S(1)}, f32[32,128]{1,0:T(8,128)S(1)}, f32[1,1024]{1,0:T(1,128)S(1)}, bf16[256,256]{1,0:T(8,128)(2,1)S(1)}, /*index=5*/s32[8,128]{1,0:T(8,128)S(1)}) custom-call(s32[1,16]{1,0:T(1,128)S(1)} %copy-done.5, s32[1]{0:T(128)} %bitcast.pos_ref, s32[32,128]{1,0:T(8,128)S(1)} %bitcast.9, ...), custom_call_target="tpu_custom_call" | custom-call | flops 2000000000 | bytes 300000 | tf_op jit(solution)/shard_map/prepare/pallas_call | solution.py:112
  7.5 0.0 collective-permute-done.refs_1_
  7.6 2.0 %collective-permute-done.1.refs_2_ = f32[8,128]{1,0:T(8,128)S(1)} collective-permute-done((f32[8,128]{1,0:T(8,128)}, f32[8,128]{1,0:T(8,128)S(1)}, u32[]{:S(2)}, u32[]{:S(2)}) %collective-permute-start.1) | collective-permute-done | bytes 4128 | tf_op jit(solution)/shard_map/ppermute | solution.py:481
  9.6 6.4 %pair_terms.1 = (f32[2,1024]{1,0:T(2,128)}, f32[2,1024]{1,0:T(2,128)S(1)}) custom-call(s32[8,128]{1,0:T(8,128)S(1)} %get-tuple-element.24.bounds_ref, s32[1]{0:T(128)} %bitcast.pos_ref, f32[8,128]{1,0:T(8,128)S(1)} %get-tuple-element.25.refs_0_, f32[8,128]{1,0:T(8,128)S(1)} %collective-permute-done.refs_1_, f32[8,128]{1,0:T(8,128)S(1)} %collective-permute-done.1.refs_2_, ...), custom_call_target="tpu_custom_call" | custom-call | flops 8999999488 | bytes 200000 | tf_op jit(solution)/shard_map/pair_terms/pallas_call | solution.py:283
  15.9 0.7 %copy-done.1 = s32[1024]{0:T(1024)S(1)} copy-done((s32[1024]{0:T(1024)S(1)}, s32[1024]{0:T(1024)}, u32[]{:S(2)}) %copy-start.1) | copy-done | bytes 4120
  16.6 0.4 %leaf_terms.1 = (f32[256,1024]{1,0:T(8,128)S(1)}, bf16[32,1024]{1,0:T(8,128)(2,1)S(1)}, f32[8,256]{1,0:T(8,128)S(1)}) custom-call(bf16[256,256]{1,0:T(8,128)(2,1)S(1)} %get-tuple-element.30.perm_ref, s32[1024,256]{1,0:T(8,128)S(1)} %copy-done, s32[8,128]{1,0:T(8,128)S(1)} %bitcast.7, f32[2,1024]{1,0:T(2,128)S(1)} %get-tuple-element.31.lam_ref), custom_call_target="tpu_custom_call" | custom-call | flops 200000000 | bytes 3000000 | tf_op jit(solution)/shard_map/leaf_terms/pallas_call | solution.py:324
  17.1 2.2 %histogram_part.7 = f32[200,256]{1,0:T(8,128)S(1)} custom-call(bf16[32,1024]{1,0:T(8,128)(2,1)S(1)} %get-tuple-element.38.tile_ref, f32[256,1024]{1,0:T(8,128)S(1)} %get-tuple-element.33.bins_ref, f32[8,256]{1,0:T(8,128)S(1)} %get-tuple-element.34.refs_0_), custom_call_target="tpu_custom_call" | custom-call | flops 8000000 | bytes 8000 | tf_op jit(solution)/shard_map/histogram_part/pallas_call | solution.py:397
  19.3 0.1 collective-permute-start.2
  19.4 1.1 %histogram_part.6 = f32[96,256]{1,0:T(8,128)S(1)} custom-call(bf16[32,1024]{1,0:T(8,128)(2,1)S(1)} %get-tuple-element.38.tile_ref, f32[256,1024]{1,0:T(8,128)S(1)} %get-tuple-element.33.bins_ref), custom_call_target="tpu_custom_call" | custom-call | flops 4000000 | bytes 4000 | tf_op jit(solution)/shard_map/histogram_part/pallas_call | solution.py:397
  20.5 0.3 collective-permute-done.2
  20.8 1.1 %histogram_part.8 = f32[96,256]{1,0:T(8,128)S(1)} custom-call(bf16[32,1024]{1,0:T(8,128)(2,1)S(1)} %get-tuple-element.38.tile_ref, f32[256,1024]{1,0:T(8,128)S(1)} %get-tuple-element.33.bins_ref), custom_call_target="tpu_custom_call" | custom-call | flops 4000000 | bytes 4000 | tf_op jit(solution)/shard_map/histogram_part/pallas_call | solution.py:397
  21.9 0.8 %collective-permute-start.4 = (f32[104,256]{1,0:T(8,128)S(1)}, f32[104,256]{1,0:T(8,128)S(1)}, u32[]{:S(2)}, u32[]{:S(2)}) collective-permute-start(f32[104,256]{1,0:T(8,128)S(1)} %pad_maximum_fusion), channel_id=1, source_target_pairs={{0,8},{1,9},{2,10},{3,11},{4,12},{5,13},{6,14},{7,15},{8,0},{9,1},... | collective-permute-start | bytes 319496 | tf_op jit(solution)/shard_map/ppermute | solution.py:472
  22.8 2.2 %histogram_part.10 = f32[192,256]{1,0:T(8,128)S(1)} custom-call(bf16[32,1024]{1,0:T(8,128)(2,1)S(1)} %get-tuple-element.38.tile_ref, f32[256,1024]{1,0:T(8,128)S(1)} %get-tuple-element.33.bins_ref), custom_call_target="tpu_custom_call" | custom-call | flops 8000000 | bytes 8000 | tf_op jit(solution)/shard_map/histogram_part/pallas_call | solution.py:397
  25.0 0.1 collective-permute-start.3
  25.1 1.1 %histogram_part.9 = f32[96,256]{1,0:T(8,128)S(1)} custom-call(bf16[32,1024]{1,0:T(8,128)(2,1)S(1)} %get-tuple-element.38.tile_ref, f32[256,1024]{1,0:T(8,128)S(1)} %get-tuple-element.33.bins_ref), custom_call_target="tpu_custom_call" | custom-call | flops 4000000 | bytes 4000 | tf_op jit(solution)/shard_map/histogram_part/pallas_call | solution.py:397
  26.2 0.9 %collective-permute-done.4 = f32[104,256]{1,0:T(8,128)S(1)} collective-permute-done((f32[104,256]{1,0:T(8,128)S(1)}, f32[104,256]{1,0:T(8,128)S(1)}, u32[]{:S(2)}, u32[]{:S(2)}) %collective-permute-start.4) | collective-permute-done | bytes 106528 | tf_op jit(solution)/shard_map/ppermute | solution.py:472
  27.1 0.0 collective-permute-done.3
  27.1 2.3 %collective-permute-start.6 = (f32[104,256]{1,0:T(8,128)S(1)}, f32[104,256]{1,0:T(8,128)S(1)}, u32[]{:S(2)}, u32[]{:S(2)}) collective-permute-start(f32[104,256]{1,0:T(8,128)S(1)} %pad_maximum_fusion.1), channel_id=1, source_target_pairs={{0,16},{1,17},{2,18},{3,19},{4,20},{5,21},{6,22},{7,23},{8,24},{9,... | collective-permute-start | bytes 319496 | tf_op jit(solution)/shard_map/ppermute | solution.py:472
  29.4 0.7 %collective-permute-start.5 = (f32[96,256]{1,0:T(8,128)S(1)}, f32[96,256]{1,0:T(8,128)S(1)}, u32[]{:S(2)}, u32[]{:S(2)}) collective-permute-start(f32[96,256]{1,0:T(8,128)S(1)} %slice_add_fusion.4), channel_id=1, source_target_pairs={{0,8},{1,9},{2,10},{3,11},{4,12},{5,13},{6,14},{7,15},{8,0},{9,1},... | collective-permute-start | bytes 294920 | tf_op jit(solution)/shard_map/ppermute | solution.py:472
  30.1 1.1 %histogram_part.11 = f32[96,256]{1,0:T(8,128)S(1)} custom-call(bf16[32,1024]{1,0:T(8,128)(2,1)S(1)} %get-tuple-element.38.tile_ref, f32[256,1024]{1,0:T(8,128)S(1)} %get-tuple-element.33.bins_ref), custom_call_target="tpu_custom_call" | custom-call | flops 4000000 | bytes 4000 | tf_op jit(solution)/shard_map/histogram_part/pallas_call | solution.py:397
  31.2 2.8 %collective-permute-done.5 = f32[96,256]{1,0:T(8,128)S(1)} collective-permute-done((f32[96,256]{1,0:T(8,128)S(1)}, f32[96,256]{1,0:T(8,128)S(1)}, u32[]{:S(2)}, u32[]{:S(2)}) %collective-permute-start.5) | collective-permute-done | bytes 98336 | tf_op jit(solution)/shard_map/ppermute | solution.py:472
  34.0 0.0 collective-permute-done.6
  34.1 2.1 %collective-permute-start.7 = (f32[32,256]{1,0:T(8,128)S(1)}, f32[32,256]{1,0:T(8,128)S(1)}, u32[]{:S(2)}, u32[]{:S(2)}) collective-permute-start(f32[32,256]{1,0:T(8,128)S(1)} %get-tuple-element.50), channel_id=1, source_target_pairs={{0,3},{1,2},{2,1},{3,0},{4,7},{5,6},{6,5},{7,4},{8,11},{9,10},{10,... | collective-permute-start | bytes 98312 | tf_op jit(solution)/shard_map/ppermute | solution.py:472
  36.2 0.8 %collective-permute-start.8 = (f32[32,256]{1,0:T(8,128)S(1)}, f32[32,256]{1,0:T(8,128)S(1)}, u32[]{:S(2)}, u32[]{:S(2)}) collective-permute-start(f32[32,256]{1,0:T(8,128)S(1)} %get-tuple-element.49), channel_id=1, source_target_pairs={{0,2},{1,3},{2,0},{3,1},{4,6},{5,7},{6,4},{7,5},{8,10},{9,11},{10,... | collective-permute-start | bytes 98312 | tf_op jit(solution)/shard_map/ppermute | solution.py:472
  36.9 1.6 %collective-permute-start.9 = (f32[32,256]{1,0:T(8,128)S(1)}, f32[32,256]{1,0:T(8,128)S(1)}, u32[]{:S(2)}, u32[]{:S(2)}) collective-permute-start(f32[32,256]{1,0:T(8,128)S(1)} %get-tuple-element.48), channel_id=1, source_target_pairs={{0,1},{1,0},{2,3},{3,2},{4,5},{5,4},{6,7},{7,6},{8,9},{9,8},{10,11... | collective-permute-start | bytes 98312 | tf_op jit(solution)/shard_map/ppermute | solution.py:472
  38.6 1.3 %collective-permute-done.7.refs_0_ = f32[32,256]{1,0:T(8,128)S(1)} collective-permute-done((f32[32,256]{1,0:T(8,128)S(1)}, f32[32,256]{1,0:T(8,128)S(1)}, u32[]{:S(2)}, u32[]{:S(2)}) %collective-permute-start.7) | collective-permute-done | bytes 32800 | tf_op jit(solution)/shard_map/ppermute | solution.py:472
  39.9 1.2 %collective-permute-done.8.refs_1_ = f32[32,256]{1,0:T(8,128)S(1)} collective-permute-done((f32[32,256]{1,0:T(8,128)S(1)}, f32[32,256]{1,0:T(8,128)S(1)}, u32[]{:S(2)}, u32[]{:S(2)}) %collective-permute-start.8) | collective-permute-done | bytes 32800 | tf_op jit(solution)/shard_map/ppermute | solution.py:472
  41.1 0.1 collective-permute-done.9.refs_2_
  41.2 0.9 %finish.1 = (f32[8,128]{1,0:T(8,128)}, f32[8,128]{1,0:T(8,128)}, f32[3,2048]{1,0:T(4,128)}) custom-call(s32[8,128]{1,0:T(8,128)S(1)} %bitcast.8, f32[24,256]{1,0:T(8,128)S(1)} %get-tuple-element.47.kept_ref, f32[8,256]{1,0:T(8,128)S(1)} %slice_add_fusion.6.sums_ref, f32[32,256]{1,0:T(8,128)S(1)} %collective-permute-done.7.refs_0_, ...), custom_call_target="tpu_custom_call" | custom-call | tf_op jit(solution)/shard_map/finish/pallas_call | solution.py:437
  (21 shorter events, 0.1 us)
Async XLA Ops:
  0.6 5.1 %copy-start.2 = (s32[4096]{0:T(1024)S(1)}, s32[4096]{0:T(1024)}, u32[]{:S(2)}) copy-start(s32[4096]{0:T(1024)} %param.7) | copy-start | bytes 49156
  0.6 6.9 %collective-permute-start = (f32[8,128]{1,0:T(8,128)}, f32[8,128]{1,0:T(8,128)S(1)}, u32[]{:S(2)}, u32[]{:S(2)}) collective-permute-start(f32[8,128]{1,0:T(8,128)} %bitcast.10), channel_id=1, source_target_pairs={{1,2},{0,3},{2,1},{3,0},{5,6},{4,7},{6,5},{7,4},{9,10},{8,11},{10,... | collective-permute-start | bytes 12296 | tf_op jit(solution)/shard_map/ppermute | solution.py:481
  5.8 3.8 %collective-permute-start.1 = (f32[8,128]{1,0:T(8,128)}, f32[8,128]{1,0:T(8,128)S(1)}, u32[]{:S(2)}, u32[]{:S(2)}) collective-permute-start(f32[8,128]{1,0:T(8,128)} %bitcast.11), channel_id=1, source_target_pairs={{0,1},{2,3},{1,0},{3,2},{4,5},{6,7},{5,4},{7,6},{8,9},{10,11},{9,8... | collective-permute-start | bytes 12296 | tf_op jit(solution)/shard_map/ppermute | solution.py:481
  5.8 0.8 %copy-start.3 = (f32[1024]{0:T(1024)S(1)}, f32[1024]{0:T(1024)}, u32[]{:S(2)}) copy-start(f32[1024]{0:T(1024)} %param.6) | copy-start | bytes 12292
  5.8 0.8 %copy-start.4 = (s32[256]{0:T(256)S(1)}, s32[256]{0:T(256)}, u32[]{:S(2)}) copy-start(s32[256]{0:T(256)} %param.11) | copy-start | bytes 3076
  5.8 0.8 %copy-start.5 = (s32[1,16]{1,0:T(1,128)S(1)}, s32[1,16]{1,0:T(1,128)}, u32[]{:S(2)}) copy-start(s32[1,16]{1,0:T(1,128)} %len_ref.1) | copy-start | bytes 196
  9.6 6.4 %copy-start = (s32[1024,256]{1,0:T(8,128)S(1)}, s32[1024,256]{1,0:T(8,128)}, u32[]{:S(2)}) copy-start(s32[1024,256]{1,0:T(8,128)} %bins_ref.1) | copy-start | bytes 3145732
  15.9 0.7 %copy-start.1 = (s32[1024]{0:T(1024)S(1)}, s32[1024]{0:T(1024)}, u32[]{:S(2)}) copy-start(s32[1024]{0:T(1024)} %param.8) | copy-start | bytes 12292
  19.3 1.5 %collective-permute-start.2 = (f32[200,256]{1,0:T(8,128)S(1)}, f32[200,256]{1,0:T(8,128)S(1)}, u32[]{:S(2)}, u32[]{:S(2)}) collective-permute-start(f32[200,256]{1,0:T(8,128)S(1)} %histogram_part.7), channel_id=1, source_target_pairs={{0,4},{1,5},{2,6},{3,7},{4,0},{5,1},{6,2},{7,3},{8,12},{9,13},{10,... | collective-permute-start | bytes 614408 | tf_op jit(solution)/shard_map/ppermute | solution.py:472
  21.9 5.1 %collective-permute-start.4 = (f32[104,256]{1,0:T(8,128)S(1)}, f32[104,256]{1,0:T(8,128)S(1)}, u32[]{:S(2)}, u32[]{:S(2)}) collective-permute-start(f32[104,256]{1,0:T(8,128)S(1)} %pad_maximum_fusion), channel_id=1, source_target_pairs={{0,8},{1,9},{2,10},{3,11},{4,12},{5,13},{6,14},{7,15},{8,0},{9,1},... | collective-permute-start | bytes 319496 | tf_op jit(solution)/shard_map/ppermute | solution.py:472
  25.0 2.1 %collective-permute-start.3 = (f32[192,256]{1,0:T(8,128)S(1)}, f32[192,256]{1,0:T(8,128)S(1)}, u32[]{:S(2)}, u32[]{:S(2)}) collective-permute-start(f32[192,256]{1,0:T(8,128)S(1)} %histogram_part.10), channel_id=1, source_target_pairs={{0,4},{1,5},{2,6},{3,7},{4,0},{5,1},{6,2},{7,3},{8,12},{9,13},{10,... | collective-permute-start | bytes 589832 | tf_op jit(solution)/shard_map/ppermute | solution.py:472
  27.1 6.9 %collective-permute-start.6 = (f32[104,256]{1,0:T(8,128)S(1)}, f32[104,256]{1,0:T(8,128)S(1)}, u32[]{:S(2)}, u32[]{:S(2)}) collective-permute-start(f32[104,256]{1,0:T(8,128)S(1)} %pad_maximum_fusion.1), channel_id=1, source_target_pairs={{0,16},{1,17},{2,18},{3,19},{4,20},{5,21},{6,22},{7,23},{8,24},{9,... | collective-permute-start | bytes 319496 | tf_op jit(solution)/shard_map/ppermute | solution.py:472
  29.4 4.6 %collective-permute-start.5 = (f32[96,256]{1,0:T(8,128)S(1)}, f32[96,256]{1,0:T(8,128)S(1)}, u32[]{:S(2)}, u32[]{:S(2)}) collective-permute-start(f32[96,256]{1,0:T(8,128)S(1)} %slice_add_fusion.4), channel_id=1, source_target_pairs={{0,8},{1,9},{2,10},{3,11},{4,12},{5,13},{6,14},{7,15},{8,0},{9,1},... | collective-permute-start | bytes 294920 | tf_op jit(solution)/shard_map/ppermute | solution.py:472
  34.1 5.8 %collective-permute-start.7 = (f32[32,256]{1,0:T(8,128)S(1)}, f32[32,256]{1,0:T(8,128)S(1)}, u32[]{:S(2)}, u32[]{:S(2)}) collective-permute-start(f32[32,256]{1,0:T(8,128)S(1)} %get-tuple-element.50), channel_id=1, source_target_pairs={{0,3},{1,2},{2,1},{3,0},{4,7},{5,6},{6,5},{7,4},{8,11},{9,10},{10,... | collective-permute-start | bytes 98312 | tf_op jit(solution)/shard_map/ppermute | solution.py:472
  36.2 4.9 %collective-permute-start.8 = (f32[32,256]{1,0:T(8,128)S(1)}, f32[32,256]{1,0:T(8,128)S(1)}, u32[]{:S(2)}, u32[]{:S(2)}) collective-permute-start(f32[32,256]{1,0:T(8,128)S(1)} %get-tuple-element.49), channel_id=1, source_target_pairs={{0,2},{1,3},{2,0},{3,1},{4,6},{5,7},{6,4},{7,5},{8,10},{9,11},{10,... | collective-permute-start | bytes 98312 | tf_op jit(solution)/shard_map/ppermute | solution.py:472
  36.9 4.3 %collective-permute-start.9 = (f32[32,256]{1,0:T(8,128)S(1)}, f32[32,256]{1,0:T(8,128)S(1)}, u32[]{:S(2)}, u32[]{:S(2)}) collective-permute-start(f32[32,256]{1,0:T(8,128)S(1)} %get-tuple-element.48), channel_id=1, source_target_pairs={{0,1},{1,0},{2,3},{3,2},{4,5},{5,4},{6,7},{7,6},{8,9},{9,8},{10,11... | collective-permute-start | bytes 98312 | tf_op jit(solution)/shard_map/ppermute | solution.py:472

commit v12 on v11

--- a/solution.py
+++ b/solution.py
@@ -11,9 +11,10 @@
 LEAVES = 1024
 LANES = 128
 GRADES = 4
-LOW = 32
+LOW = 64
 HIGH = BINS // LOW
 GROUP = 8
+FEW = 4
 CHUNK = 64
 MAX_LEN = 1024
 
@@ -305,10 +306,10 @@
     pieces, tiles = [], []
     for c in range(2):
         for k, part in enumerate(split_terms(lam_ref[c:c + 1, :], 3)):
-            wide = jnp.broadcast_to(part.astype(F32), (highs, docs))
-            pieces.append(jnp.where(top, wide, 0.0))
+            line = part.astype(F32)
+            pieces.append(jnp.where(top, jnp.broadcast_to(line, (highs, docs)), 0.0))
             if k < 2:
-                tiles.append(wide)
+                tiles.append(jnp.broadcast_to(line, (HIGH, docs)))
     tile_ref[...] = jnp.concatenate(tiles, axis=0).astype(BF16)
     stacked = jnp.concatenate(pieces, axis=0).astype(BF16)
     sums = lax.dot_general(stacked, spots, NT, preferred_element_type=F32)
@@ -339,64 +340,60 @@
 def histogram_kernel(first, groups, tile_ref, bins_ref, *refs):
     out_ref = refs[-1]
     docs = tile_ref.shape[1]
-    depth = 256
-    rows = 16
-    row = iota((rows, depth), 0)
+    rows = 4 * HIGH
+    width = FEW * LOW
+    row = iota((rows, docs), 0)
     low_level = [(row + rows * k).astype(F32).astype(BF16) for k in range(LOW // rows)]
     high_level = (row % HIGH).astype(F32).astype(BF16)
-    upper = row < HIGH
-    zero = jnp.zeros((rows, depth), BF16)
-    one = jnp.ones((rows, depth), BF16)
-    lane_owner = iota((1, GROUP * LOW), 1) // LOW
+    whose = [row // HIGH == f for f in range(FEW)]
+    zero = jnp.zeros((rows, docs), BF16)
+    one = jnp.ones((rows, docs), BF16)
+    lane_owner = iota((1, width), 1) // LOW
+    own_count = iota((rows, width), 0) // HIGH == iota((rows, width), 1) // LOW
+    upper = iota((2 * HIGH, width), 0) < HIGH
+
+    def fold(part):
+        return part + pltpu.roll(part, HIGH, 0)
 
     def one_group(g, carry):
         base = pl.multiple_of((first + g) * GROUP, GROUP)
-        acc = None
-        for k in range(docs // depth):
-            span = slice(k * depth, (k + 1) * depth)
-            code = bins_ref[pl.ds(base, GROUP), span]
-            high = jnp.floor(code * (1.0 / LOW))
-            low = code - high * LOW
-            left, right, count = [], [], []
-            wide = []
-            for f in range(GROUP):
-                high_f = jnp.broadcast_to(high[f:f + 1, :], (rows, depth))
-                low_f = jnp.broadcast_to(low[f:f + 1, :], (rows, depth)).astype(BF16)
-                wide.append(high_f)
-                match = high_f.astype(BF16) == high_level
-                for c in range(2):
-                    left.append(jnp.where(match, tile_ref[c * rows:(c + 1) * rows, span], zero))
+        code = bins_ref[pl.ds(base, GROUP), :]
+        high = jnp.floor(code * (1.0 / LOW))
+        low = code - high * LOW
+        halves = []
+        for half in range(GROUP // FEW):
+            left, right = [], []
+            both = None
+            for f in range(FEW):
+                at = slice(half * FEW + f, half * FEW + f + 1)
+                high_f = jnp.broadcast_to(high[at, :], (rows, docs))
+                low_f = jnp.broadcast_to(low[at, :], (rows, docs)).astype(BF16)
+                both = high_f if both is None else jnp.where(whose[f], high_f, both)
+                left.append(jnp.where(high_f.astype(BF16) == high_level, tile_ref[...], zero))
                 for level in low_level:
                     right.append(jnp.where(low_f == level, one, zero))
-            for f in range(0, GROUP, 2):
-                both = jnp.where(upper, wide[f], wide[f + 1]).astype(BF16)
-                count.append(jnp.where(both == high_level, one, zero))
-            part = lax.dot_general(
-                jnp.concatenate(left + count, axis=0), jnp.concatenate(right, axis=0), NT,
-                preferred_element_type=F32,
-            )
-            acc = part if acc is None else acc + part
-        stats = jnp.zeros((2 * rows, GROUP * LOW), F32)
-        counts = jnp.zeros((HIGH, GROUP * LOW), F32)
-        for f in range(GROUP):
-            mine = lane_owner == f
-            stats = jnp.where(mine, acc[f * 2 * rows:(f + 1) * 2 * rows], stats)
-            at = GROUP * 2 * rows + f * HIGH
-            counts = jnp.where(mine, acc[at:at + HIGH], counts)
-        out_ref[pl.ds(pl.multiple_of(g * 3 * HIGH, 3 * HIGH), 3 * HIGH), :] = jnp.concatenate(
-            [stats[0:HIGH] + stats[HIGH:2 * HIGH], stats[2 * HIGH:3 * HIGH] + stats[3 * HIGH:4 * HIGH], counts], axis=0)
+            left.append(jnp.where(both.astype(BF16) == high_level, one, zero))
+            acc = lax.dot_general(
+                jnp.concatenate(left, axis=0), jnp.concatenate(right, axis=0), NT, preferred_element_type=F32)
+            stats = acc[0:rows]
+            for f in range(1, FEW):
+                stats = jnp.where(lane_owner == f, acc[f * rows:(f + 1) * rows], stats)
+            counts = jnp.where(own_count, acc[FEW * rows:], 0.0)
+            halves.append([fold(stats[:2 * HIGH]), fold(stats[2 * HIGH:]), fold(counts[:2 * HIGH] + counts[2 * HIGH:])])
+        out_ref[pl.ds(pl.multiple_of(g * 6 * HIGH, 6 * HIGH), 6 * HIGH), :] = jnp.concatenate(
+            [jnp.where(upper, a, b) for a, b in zip(*halves)], axis=0)
         return carry
 
     if len(refs) > 1:
-        out_ref[groups * 3 * HIGH:, :] = refs[0][...]
+        out_ref[groups * 6 * HIGH:, :] = refs[0][...]
     lax.fori_loop(0, groups, one_group, 0, unroll=2)
 
 
 def histogram_part(first, groups, tiles, bins_t, *tail):
-    rows = groups * 3 * HIGH + sum(piece.shape[0] for piece in tail)
+    rows = groups * 6 * HIGH + sum(piece.shape[0] for piece in tail)
     return pl.pallas_call(
         functools.partial(histogram_kernel, first, groups),
-        out_shape=jax.ShapeDtypeStruct((rows, GROUP * LOW), F32),
+        out_shape=jax.ShapeDtypeStruct((rows, FEW * LOW), F32),
         in_specs=[vmem()] * (2 + len(tail)),
         out_specs=vmem(),
         compiler_params=pltpu.CompilerParams(vmem_limit_bytes=VMEM_LIMIT),
@@ -426,7 +423,9 @@
     if per_dev == GROUP:
         for c in range(3):
             for f in range(GROUP):
-                line = [hist[c * HIGH + h:c * HIGH + h + 1, f * LOW:(f + 1) * LOW] for h in range(HIGH)]
+                at = c * 2 * HIGH + f // FEW * HIGH
+                span = slice(f % FEW * LOW, (f % FEW + 1) * LOW)
+                line = [hist[at + h:at + h + 1, span] for h in range(HIGH)]
                 hist_ref[c:c + 1, f * BINS:(f + 1) * BINS] = jnp.concatenate(line, axis=1)
     else:
         hist_ref[...] = hist
@@ -490,7 +489,8 @@
             return histogram_part(low, high - low, tiles, bins_t, *tail)
         groups = high - low
         wide = histogram_part(low, groups, tiles, bins_t)
-        wide = wide.reshape(groups, 3, HIGH, GROUP // per_dev, per_dev, LOW).transpose(0, 3, 1, 4, 2, 5)
+        wide = wide.reshape(groups, 3, GROUP // FEW, HIGH, FEW, LOW).transpose(0, 2, 4, 1, 3, 5)
+        wide = wide.reshape(groups, GROUP // per_dev, per_dev, 3, BINS).transpose(0, 1, 3, 2, 4)
         return jnp.concatenate([wide.reshape(groups * GROUP // per_dev * unit, BINS), *tail], axis=0)
 
     def join(block, total):

time: 42.3 us -> 45.3 us (1.071)
  Pallas kernels: 17.5 us -> 20.3 us
  starting transfers between devices: 13.5 us -> 15.4 us
  waiting for transfers between devices: 8.72 us -> 7.08 us
    pallas_call x6, Pallas kernels: 8.86 us -> 12.5 us  [histogram_part(): pl.pallas_call(functools.partial(histogram_kernel, first, groups), out_sh...]
    ppermute x8, starting transfers between devices: 8.39 us -> 10.3 us  [swap(): return lax.ppermute(value, axes, [(p, p ^ mask) for p in range(count)])]
    ppermute x8, waiting for transfers between devices: 6.68 us -> 5.04 us  [swap(): return lax.ppermute(value, axes, [(p, p ^ mask) for p in range(count)])]
    pallas_call x1, Pallas kernels: 6.36 us -> 5.61 us  [pair_terms(): pl.pallas_call(functools.partial(pairs_kernel, feat_count), out_shape=(ja...]
  transfers between devices with their start and end apart: 10 -> 10, of which waited for: 7 -> 5; matrix products, arithmetic and copies ran while one was open for 0% -> 0% of each run, Pallas kernels for 16% -> 20%
where the time goes in v12:
time: 45.3 us; the launch traced here: 45.1 us
  Pallas kernels  20.3 us (45%)
  starting transfers between devices  15.4 us (34%)
  waiting for transfers between devices  7.08 us (16%)
  local copies, waits for them, and re-layouts  1.44 us (3%)
  between operations  0.83 us (2%)
    pallas_call x6, Pallas kernels, histogram_part(): pl.pallas_call(functools.partial(histogram_kernel, first, groups), out_sh...  12.5 us
    ppermute x8, starting transfers between devices, swap(): return lax.ppermute(value, axes, [(p, p ^ mask) for p in range(count)])  10.3 us
    pallas_call x1, Pallas kernels, pair_terms(): pl.pallas_call(functools.partial(pairs_kernel, feat_count), out_shape=(ja...  5.61 us
    ppermute x2, starting transfers between devices, local(): lax.ppermute(own_scores, 'feat', links + [(b, a) for a, b in links])  5.12 us
    ppermute x8, waiting for transfers between devices, swap(): return lax.ppermute(value, axes, [(p, p ^ mask) for p in range(count)])  5.04 us
    ppermute x2, waiting for transfers between devices, local(): lax.ppermute(own_scores, 'feat', links + [(b, a) for a, b in links])  2.04 us
    unnamed x12, local copies, waits for them, and re-layouts  1.43 us
    pallas_call x1, Pallas kernels, prepare(): pl.pallas_call(functools.partial(prepare_kernel, feat_count, masks), out_...  1.01 us
  transfers between devices with their start and end apart: 10, of which 5 were waited for; matrix products, arithmetic and copies ran while one was open for 0% of the time, Pallas kernels for 20%

profile of v12, /device:TPU:0, one launch (start us, length us, event | category | flops | bytes accessed | tf_op | source)
XLA Modules:
  0.0 45.1 jit_solution(12378352611382450806)
XLA Ops:
  0.6 5.1 %collective-permute-start = (f32[8,128]{1,0:T(8,128)}, f32[8,128]{1,0:T(8,128)S(1)}, u32[]{:S(2)}, u32[]{:S(2)}) collective-permute-start(f32[8,128]{1,0:T(8,128)} %bitcast.10), channel_id=1, source_target_pairs={{1,2},{0,3},{2,1},{3,0},{5,6},{4,7},{6,5},{7,4},{9,10},{8,11},{10,... | collective-permute-start | bytes 12296 | tf_op jit(solution)/shard_map/ppermute | solution.py:480
  5.8 0.0 collective-permute-start.1
  5.8 0.7 %copy-done.3 = f32[1024]{0:T(1024)S(1)} copy-done((f32[1024]{0:T(1024)S(1)}, f32[1024]{0:T(1024)}, u32[]{:S(2)}) %copy-start.3) | copy-done | bytes 4120
  6.5 1.0 %prepare.1 = (f32[8,128]{1,0:T(8,128)S(1)}, s32[32,128]{1,0:T(8,128)S(1)}, f32[32,128]{1,0:T(8,128)S(1)}, f32[1,1024]{1,0:T(1,128)S(1)}, bf16[256,256]{1,0:T(8,128)(2,1)S(1)}, /*index=5*/s32[8,128]{1,0:T(8,128)S(1)}) custom-call(s32[1,16]{1,0:T(1,128)S(1)} %copy-done.5, s32[1]{0:T(128)} %bitcast.pos_ref, s32[32,128]{1,0:T(8,128)S(1)} %bitcast.9, ...), custom_call_target="tpu_custom_call" | custom-call | flops 2000000000 | bytes 300000 | tf_op jit(solution)/shard_map/prepare/pallas_call | solution.py:113
  7.5 0.0 collective-permute-done.refs_1_
  7.6 2.0 %collective-permute-done.1.refs_2_ = f32[8,128]{1,0:T(8,128)S(1)} collective-permute-done((f32[8,128]{1,0:T(8,128)}, f32[8,128]{1,0:T(8,128)S(1)}, u32[]{:S(2)}, u32[]{:S(2)}) %collective-permute-start.1) | collective-permute-done | bytes 4128 | tf_op jit(solution)/shard_map/ppermute | solution.py:480
  9.6 5.6 %pair_terms.1 = (f32[2,1024]{1,0:T(2,128)}, f32[2,1024]{1,0:T(2,128)S(1)}) custom-call(s32[8,128]{1,0:T(8,128)S(1)} %get-tuple-element.24.bounds_ref, s32[1]{0:T(128)} %bitcast.pos_ref, f32[8,128]{1,0:T(8,128)S(1)} %get-tuple-element.25.refs_0_, f32[8,128]{1,0:T(8,128)S(1)} %collective-permute-done.refs_1_, f32[8,128]{1,0:T(8,128)S(1)} %collective-permute-done.1.refs_2_, ...), custom_call_target="tpu_custom_call" | custom-call | flops 8999999488 | bytes 200000 | tf_op jit(solution)/shard_map/pair_terms/pallas_call | solution.py:284
  15.2 0.7 %copy-done.1 = s32[1024]{0:T(1024)S(1)} copy-done((s32[1024]{0:T(1024)S(1)}, s32[1024]{0:T(1024)}, u32[]{:S(2)}) %copy-start.1) | copy-done | bytes 4120
  15.9 0.4 leaf_terms.1
  16.3 3.1 %histogram_part.7 = f32[200,256]{1,0:T(8,128)S(1)} custom-call(bf16[16,1024]{1,0:T(8,128)(2,1)S(1)} %get-tuple-element.38.tile_ref, f32[256,1024]{1,0:T(8,128)S(1)} %get-tuple-element.33.bins_ref, f32[8,256]{1,0:T(8,128)S(1)} %get-tuple-element.34.refs_0_), custom_call_target="tpu_custom_call" | custom-call | flops 8000000 | bytes 8000 | tf_op jit(solution)/shard_map/histogram_part/pallas_call | solution.py:394
  19.4 0.1 collective-permute-start.2
  19.5 1.6 %histogram_part.6 = f32[96,256]{1,0:T(8,128)S(1)} custom-call(bf16[16,1024]{1,0:T(8,128)(2,1)S(1)} %get-tuple-element.38.tile_ref, f32[256,1024]{1,0:T(8,128)S(1)} %get-tuple-element.33.bins_ref), custom_call_target="tpu_custom_call" | custom-call | flops 4000000 | bytes 4000 | tf_op jit(solution)/shard_map/histogram_part/pallas_call | solution.py:394
  21.1 0.0 collective-permute-done.2
  21.1 1.6 %histogram_part.8 = f32[96,256]{1,0:T(8,128)S(1)} custom-call(bf16[16,1024]{1,0:T(8,128)(2,1)S(1)} %get-tuple-element.38.tile_ref, f32[256,1024]{1,0:T(8,128)S(1)} %get-tuple-element.33.bins_ref), custom_call_target="tpu_custom_call" | custom-call | flops 4000000 | bytes 4000 | tf_op jit(solution)/shard_map/histogram_part/pallas_call | solution.py:394
  22.7 1.6 %collective-permute-start.4 = (f32[104,256]{1,0:T(8,128)S(1)}, f32[104,256]{1,0:T(8,128)S(1)}, u32[]{:S(2)}, u32[]{:S(2)}) collective-permute-start(f32[104,256]{1,0:T(8,128)S(1)} %pad_maximum_fusion), channel_id=1, source_target_pairs={{0,8},{1,9},{2,10},{3,11},{4,12},{5,13},{6,14},{7,15},{8,0},{9,1},... | collective-permute-start | bytes 319496 | tf_op jit(solution)/shard_map/ppermute | solution.py:471
  24.4 3.1 %histogram_part.10 = f32[192,256]{1,0:T(8,128)S(1)} custom-call(bf16[16,1024]{1,0:T(8,128)(2,1)S(1)} %get-tuple-element.38.tile_ref, f32[256,1024]{1,0:T(8,128)S(1)} %get-tuple-element.33.bins_ref), custom_call_target="tpu_custom_call" | custom-call | flops 8000000 | bytes 8000 | tf_op jit(solution)/shard_map/histogram_part/pallas_call | solution.py:394
  27.5 0.3 collective-permute-start.3
  27.8 1.6 %histogram_part.9 = f32[96,256]{1,0:T(8,128)S(1)} custom-call(bf16[16,1024]{1,0:T(8,128)(2,1)S(1)} %get-tuple-element.38.tile_ref, f32[256,1024]{1,0:T(8,128)S(1)} %get-tuple-element.33.bins_ref), custom_call_target="tpu_custom_call" | custom-call | flops 4000000 | bytes 4000 | tf_op jit(solution)/shard_map/histogram_part/pallas_call | solution.py:394
  29.4 0.0 collective-permute-done.4
  29.4 0.0 collective-permute-done.3
  29.4 3.5 %collective-permute-start.6 = (f32[104,256]{1,0:T(8,128)S(1)}, f32[104,256]{1,0:T(8,128)S(1)}, u32[]{:S(2)}, u32[]{:S(2)}) collective-permute-start(f32[104,256]{1,0:T(8,128)S(1)} %pad_maximum_fusion.1), channel_id=1, source_target_pairs={{0,16},{1,17},{2,18},{3,19},{4,20},{5,21},{6,22},{7,23},{8,24},{9,... | collective-permute-start | bytes 319496 | tf_op jit(solution)/shard_map/ppermute | solution.py:471
  32.9 0.3 collective-permute-start.5
  33.3 1.6 %histogram_part.11 = f32[96,256]{1,0:T(8,128)S(1)} custom-call(bf16[16,1024]{1,0:T(8,128)(2,1)S(1)} %get-tuple-element.38.tile_ref, f32[256,1024]{1,0:T(8,128)S(1)} %get-tuple-element.33.bins_ref), custom_call_target="tpu_custom_call" | custom-call | flops 4000000 | bytes 4000 | tf_op jit(solution)/shard_map/histogram_part/pallas_call | solution.py:394
  34.8 2.8 %collective-permute-done.5 = f32[96,256]{1,0:T(8,128)S(1)} collective-permute-done((f32[96,256]{1,0:T(8,128)S(1)}, f32[96,256]{1,0:T(8,128)S(1)}, u32[]{:S(2)}, u32[]{:S(2)}) %collective-permute-start.5) | collective-permute-done | bytes 98336 | tf_op jit(solution)/shard_map/ppermute | solution.py:471
  37.6 0.0 collective-permute-done.6
  37.7 1.4 %collective-permute-start.7 = (f32[32,256]{1,0:T(8,128)S(1)}, f32[32,256]{1,0:T(8,128)S(1)}, u32[]{:S(2)}, u32[]{:S(2)}) collective-permute-start(f32[32,256]{1,0:T(8,128)S(1)} %get-tuple-element.50), channel_id=1, source_target_pairs={{0,3},{1,2},{2,1},{3,0},{4,7},{5,6},{6,5},{7,4},{8,11},{9,10},{10,... | collective-permute-start | bytes 98312 | tf_op jit(solution)/shard_map/ppermute | solution.py:471
  39.1 0.3 collective-permute-start.8
  39.4 2.8 %collective-permute-start.9 = (f32[32,256]{1,0:T(8,128)S(1)}, f32[32,256]{1,0:T(8,128)S(1)}, u32[]{:S(2)}, u32[]{:S(2)}) collective-permute-start(f32[32,256]{1,0:T(8,128)S(1)} %get-tuple-element.48), channel_id=1, source_target_pairs={{0,1},{1,0},{2,3},{3,2},{4,5},{5,4},{6,7},{7,6},{8,9},{9,8},{10,11... | collective-permute-start | bytes 98312 | tf_op jit(solution)/shard_map/ppermute | solution.py:471
  42.2 1.3 %collective-permute-done.7.refs_0_ = f32[32,256]{1,0:T(8,128)S(1)} collective-permute-done((f32[32,256]{1,0:T(8,128)S(1)}, f32[32,256]{1,0:T(8,128)S(1)}, u32[]{:S(2)}, u32[]{:S(2)}) %collective-permute-start.7) | collective-permute-done | bytes 32800 | tf_op jit(solution)/shard_map/ppermute | solution.py:471
  43.5 0.8 %collective-permute-done.8.refs_1_ = f32[32,256]{1,0:T(8,128)S(1)} collective-permute-done((f32[32,256]{1,0:T(8,128)S(1)}, f32[32,256]{1,0:T(8,128)S(1)}, u32[]{:S(2)}, u32[]{:S(2)}) %collective-permute-start.8) | collective-permute-done | bytes 32800 | tf_op jit(solution)/shard_map/ppermute | solution.py:471
  44.3 0.1 collective-permute-done.9.refs_2_
  44.4 0.7 %finish.1 = (f32[8,128]{1,0:T(8,128)}, f32[8,128]{1,0:T(8,128)}, f32[3,2048]{1,0:T(4,128)}) custom-call(s32[8,128]{1,0:T(8,128)S(1)} %bitcast.8, f32[24,256]{1,0:T(8,128)S(1)} %get-tuple-element.47.kept_ref, f32[8,256]{1,0:T(8,128)S(1)} %slice_add_fusion.6.sums_ref, f32[32,256]{1,0:T(8,128)S(1)} %collective-permute-done.7.refs_0_, ...), custom_call_target="tpu_custom_call" | custom-call | tf_op jit(solution)/shard_map/finish/pallas_call | solution.py:436
  (21 shorter events, 0.1 us)
Async XLA Ops:
  0.6 5.1 %copy-start.2 = (s32[4096]{0:T(1024)S(1)}, s32[4096]{0:T(1024)}, u32[]{:S(2)}) copy-start(s32[4096]{0:T(1024)} %param.7) | copy-start | bytes 49156
  0.6 6.9 %collective-permute-start = (f32[8,128]{1,0:T(8,128)}, f32[8,128]{1,0:T(8,128)S(1)}, u32[]{:S(2)}, u32[]{:S(2)}) collective-permute-start(f32[8,128]{1,0:T(8,128)} %bitcast.10), channel_id=1, source_target_pairs={{1,2},{0,3},{2,1},{3,0},{5,6},{4,7},{6,5},{7,4},{9,10},{8,11},{10,... | collective-permute-start | bytes 12296 | tf_op jit(solution)/shard_map/ppermute | solution.py:480
  5.8 3.8 %collective-permute-start.1 = (f32[8,128]{1,0:T(8,128)}, f32[8,128]{1,0:T(8,128)S(1)}, u32[]{:S(2)}, u32[]{:S(2)}) collective-permute-start(f32[8,128]{1,0:T(8,128)} %bitcast.11), channel_id=1, source_target_pairs={{0,1},{2,3},{1,0},{3,2},{4,5},{6,7},{5,4},{7,6},{8,9},{10,11},{9,8... | collective-permute-start | bytes 12296 | tf_op jit(solution)/shard_map/ppermute | solution.py:480
  5.8 0.8 %copy-start.3 = (f32[1024]{0:T(1024)S(1)}, f32[1024]{0:T(1024)}, u32[]{:S(2)}) copy-start(f32[1024]{0:T(1024)} %param.6) | copy-start | bytes 12292
  5.8 0.8 %copy-start.4 = (s32[256]{0:T(256)S(1)}, s32[256]{0:T(256)}, u32[]{:S(2)}) copy-start(s32[256]{0:T(256)} %param.11) | copy-start | bytes 3076
  5.8 0.8 %copy-start.5 = (s32[1,16]{1,0:T(1,128)S(1)}, s32[1,16]{1,0:T(1,128)}, u32[]{:S(2)}) copy-start(s32[1,16]{1,0:T(1,128)} %len_ref.1) | copy-start | bytes 196
  9.6 5.6 %copy-start = (s32[1024,256]{1,0:T(8,128)S(1)}, s32[1024,256]{1,0:T(8,128)}, u32[]{:S(2)}) copy-start(s32[1024,256]{1,0:T(8,128)} %bins_ref.1) | copy-start | bytes 3145732
  15.2 0.7 %copy-start.1 = (s32[1024]{0:T(1024)S(1)}, s32[1024]{0:T(1024)}, u32[]{:S(2)}) copy-start(s32[1024]{0:T(1024)} %param.8) | copy-start | bytes 12292
  19.4 1.7 %collective-permute-start.2 = (f32[200,256]{1,0:T(8,128)S(1)}, f32[200,256]{1,0:T(8,128)S(1)}, u32[]{:S(2)}, u32[]{:S(2)}) collective-permute-start(f32[200,256]{1,0:T(8,128)S(1)} %histogram_part.7), channel_id=1, source_target_pairs={{0,4},{1,5},{2,6},{3,7},{4,0},{5,1},{6,2},{7,3},{8,12},{9,13},{10,... | collective-permute-start | bytes 614408 | tf_op jit(solution)/shard_map/ppermute | solution.py:471
  22.7 6.6 %collective-permute-start.4 = (f32[104,256]{1,0:T(8,128)S(1)}, f32[104,256]{1,0:T(8,128)S(1)}, u32[]{:S(2)}, u32[]{:S(2)}) collective-permute-start(f32[104,256]{1,0:T(8,128)S(1)} %pad_maximum_fusion), channel_id=1, source_target_pairs={{0,8},{1,9},{2,10},{3,11},{4,12},{5,13},{6,14},{7,15},{8,0},{9,1},... | collective-permute-start | bytes 319496 | tf_op jit(solution)/shard_map/ppermute | solution.py:471
  27.5 1.9 %collective-permute-start.3 = (f32[192,256]{1,0:T(8,128)S(1)}, f32[192,256]{1,0:T(8,128)S(1)}, u32[]{:S(2)}, u32[]{:S(2)}) collective-permute-start(f32[192,256]{1,0:T(8,128)S(1)} %histogram_part.10), channel_id=1, source_target_pairs={{0,4},{1,5},{2,6},{3,7},{4,0},{5,1},{6,2},{7,3},{8,12},{9,13},{10,... | collective-permute-start | bytes 589832 | tf_op jit(solution)/shard_map/ppermute | solution.py:471
  29.4 8.2 %collective-permute-start.6 = (f32[104,256]{1,0:T(8,128)S(1)}, f32[104,256]{1,0:T(8,128)S(1)}, u32[]{:S(2)}, u32[]{:S(2)}) collective-permute-start(f32[104,256]{1,0:T(8,128)S(1)} %pad_maximum_fusion.1), channel_id=1, source_target_pairs={{0,16},{1,17},{2,18},{3,19},{4,20},{5,21},{6,22},{7,23},{8,24},{9,... | collective-permute-start | bytes 319496 | tf_op jit(solution)/shard_map/ppermute | solution.py:471
  32.9 4.7 %collective-permute-start.5 = (f32[96,256]{1,0:T(8,128)S(1)}, f32[96,256]{1,0:T(8,128)S(1)}, u32[]{:S(2)}, u32[]{:S(2)}) collective-permute-start(f32[96,256]{1,0:T(8,128)S(1)} %slice_add_fusion.4), channel_id=1, source_target_pairs={{0,8},{1,9},{2,10},{3,11},{4,12},{5,13},{6,14},{7,15},{8,0},{9,1},... | collective-permute-start | bytes 294920 | tf_op jit(solution)/shard_map/ppermute | solution.py:471
  37.7 5.8 %collective-permute-start.7 = (f32[32,256]{1,0:T(8,128)S(1)}, f32[32,256]{1,0:T(8,128)S(1)}, u32[]{:S(2)}, u32[]{:S(2)}) collective-permute-start(f32[32,256]{1,0:T(8,128)S(1)} %get-tuple-element.50), channel_id=1, source_target_pairs={{0,3},{1,2},{2,1},{3,0},{4,7},{5,6},{6,5},{7,4},{8,11},{9,10},{10,... | collective-permute-start | bytes 98312 | tf_op jit(solution)/shard_map/ppermute | solution.py:471
  39.1 5.2 %collective-permute-start.8 = (f32[32,256]{1,0:T(8,128)S(1)}, f32[32,256]{1,0:T(8,128)S(1)}, u32[]{:S(2)}, u32[]{:S(2)}) collective-permute-start(f32[32,256]{1,0:T(8,128)S(1)} %get-tuple-element.49), channel_id=1, source_target_pairs={{0,2},{1,3},{2,0},{3,1},{4,6},{5,7},{6,4},{7,5},{8,10},{9,11},{10,... | collective-permute-start | bytes 98312 | tf_op jit(solution)/shard_map/ppermute | solution.py:471
  39.4 5.0 %collective-permute-start.9 = (f32[32,256]{1,0:T(8,128)S(1)}, f32[32,256]{1,0:T(8,128)S(1)}, u32[]{:S(2)}, u32[]{:S(2)}) collective-permute-start(f32[32,256]{1,0:T(8,128)S(1)} %get-tuple-element.48), channel_id=1, source_target_pairs={{0,1},{1,0},{2,3},{3,2},{4,5},{5,4},{6,7},{7,6},{8,9},{9,8},{10,11... | collective-permute-start | bytes 98312 | tf_op jit(solution)/shard_map/ppermute | solution.py:471

commit v13 on v11

--- a/solution.py
+++ b/solution.py
@@ -339,12 +339,12 @@
 def histogram_kernel(first, groups, tile_ref, bins_ref, *refs):
     out_ref = refs[-1]
     docs = tile_ref.shape[1]
-    depth = 256
+    depth = docs
     rows = 16
     row = iota((rows, depth), 0)
     low_level = [(row + rows * k).astype(F32).astype(BF16) for k in range(LOW // rows)]
     high_level = (row % HIGH).astype(F32).astype(BF16)
-    upper = row < HIGH
+    upper = jnp.where(row < HIGH, 1.0, 0.0).astype(BF16) > 0
     zero = jnp.zeros((rows, depth), BF16)
     one = jnp.ones((rows, depth), BF16)
     lane_owner = iota((1, GROUP * LOW), 1) // LOW
@@ -362,14 +362,15 @@
             for f in range(GROUP):
                 high_f = jnp.broadcast_to(high[f:f + 1, :], (rows, depth))
                 low_f = jnp.broadcast_to(low[f:f + 1, :], (rows, depth)).astype(BF16)
+                high_f = high_f.astype(BF16)
                 wide.append(high_f)
-                match = high_f.astype(BF16) == high_level
+                match = high_f == high_level
                 for c in range(2):
                     left.append(jnp.where(match, tile_ref[c * rows:(c + 1) * rows, span], zero))
                 for level in low_level:
                     right.append(jnp.where(low_f == level, one, zero))
             for f in range(0, GROUP, 2):
-                both = jnp.where(upper, wide[f], wide[f + 1]).astype(BF16)
+                both = jnp.where(upper, wide[f], wide[f + 1])
                 count.append(jnp.where(both == high_level, one, zero))
             part = lax.dot_general(
                 jnp.concatenate(left + count, axis=0), jnp.concatenate(right, axis=0), NT,

time: 42.3 us -> 42.1 us (level)
  starting transfers between devices: 13.5 us -> 15 us
  waiting for transfers between devices: 8.72 us -> 7.84 us
  Pallas kernels: 17.5 us -> 16.7 us
    ppermute x8, starting transfers between devices: 8.39 us -> 9.92 us  [swap(): return lax.ppermute(value, axes, [(p, p ^ mask) for p in range(count)])]
    ppermute x8, waiting for transfers between devices: 6.68 us -> 5.8 us  [swap(): return lax.ppermute(value, axes, [(p, p ^ mask) for p in range(count)])]
    pallas_call x1, Pallas kernels: 6.36 us -> 5.58 us  [pair_terms(): pl.pallas_call(functools.partial(pairs_kernel, feat_count), out_shape=(ja...]
where the time goes in v13:
time: 42.1 us; the launch traced here: 41.9 us
  Pallas kernels  16.7 us (40%)
  starting transfers between devices  15 us (36%)
  waiting for transfers between devices  7.84 us (19%)
  local copies, waits for them, and re-layouts  1.44 us (3%)
  between operations  0.77 us (2%)
    ppermute x8, starting transfers between devices, swap(): return lax.ppermute(value, axes, [(p, p ^ mask) for p in range(count)])  9.92 us
    pallas_call x6, Pallas kernels, histogram_part(): pl.pallas_call(functools.partial(histogram_kernel, first, groups), out_sh...  8.82 us
    ppermute x8, waiting for transfers between devices, swap(): return lax.ppermute(value, axes, [(p, p ^ mask) for p in range(count)])  5.8 us
    pallas_call x1, Pallas kernels, pair_terms(): pl.pallas_call(functools.partial(pairs_kernel, feat_count), out_shape=(ja...  5.58 us
    ppermute x2, starting transfers between devices, local(): lax.ppermute(own_scores, 'feat', links + [(b, a) for a, b in links])  5.12 us
    ppermute x2, waiting for transfers between devices, local(): lax.ppermute(own_scores, 'feat', links + [(b, a) for a, b in links])  2.04 us
    unnamed x12, local copies, waits for them, and re-layouts  1.43 us
    pallas_call x1, Pallas kernels, prepare(): pl.pallas_call(functools.partial(prepare_kernel, feat_count, masks), out_...  1.01 us
  transfers between devices with their start and end apart: 10, of which 7 were waited for; matrix products, arithmetic and copies ran while one was open for 0% of the time, Pallas kernels for 16%

profile of v13, /device:TPU:0, one launch (start us, length us, event | category | flops | bytes accessed | tf_op | source)
XLA Modules:
  0.0 41.9 jit_solution(4094903138713315363)
XLA Ops:
  0.6 5.1 %collective-permute-start = (f32[8,128]{1,0:T(8,128)}, f32[8,128]{1,0:T(8,128)S(1)}, u32[]{:S(2)}, u32[]{:S(2)}) collective-permute-start(f32[8,128]{1,0:T(8,128)} %bitcast.10), channel_id=1, source_target_pairs={{1,2},{0,3},{2,1},{3,0},{5,6},{4,7},{6,5},{7,4},{9,10},{8,11},{10,... | collective-permute-start | bytes 12296 | tf_op jit(solution)/shard_map/ppermute | solution.py:482
  5.8 0.0 collective-permute-start.1
  5.8 0.7 %copy-done.3 = f32[1024]{0:T(1024)S(1)} copy-done((f32[1024]{0:T(1024)S(1)}, f32[1024]{0:T(1024)}, u32[]{:S(2)}) %copy-start.3) | copy-done | bytes 4120
  6.5 1.0 %prepare.1 = (f32[8,128]{1,0:T(8,128)S(1)}, s32[32,128]{1,0:T(8,128)S(1)}, f32[32,128]{1,0:T(8,128)S(1)}, f32[1,1024]{1,0:T(1,128)S(1)}, bf16[256,256]{1,0:T(8,128)(2,1)S(1)}, /*index=5*/s32[8,128]{1,0:T(8,128)S(1)}) custom-call(s32[1,16]{1,0:T(1,128)S(1)} %copy-done.5, s32[1]{0:T(128)} %bitcast.pos_ref, s32[32,128]{1,0:T(8,128)S(1)} %bitcast.9, ...), custom_call_target="tpu_custom_call" | custom-call | flops 2000000000 | bytes 300000 | tf_op jit(solution)/shard_map/prepare/pallas_call | solution.py:112
  7.5 0.0 collective-permute-done.refs_1_
  7.6 2.0 %collective-permute-done.1.refs_2_ = f32[8,128]{1,0:T(8,128)S(1)} collective-permute-done((f32[8,128]{1,0:T(8,128)}, f32[8,128]{1,0:T(8,128)S(1)}, u32[]{:S(2)}, u32[]{:S(2)}) %collective-permute-start.1) | collective-permute-done | bytes 4128 | tf_op jit(solution)/shard_map/ppermute | solution.py:482
  9.6 5.6 %pair_terms.1 = (f32[2,1024]{1,0:T(2,128)}, f32[2,1024]{1,0:T(2,128)S(1)}) custom-call(s32[8,128]{1,0:T(8,128)S(1)} %get-tuple-element.24.bounds_ref, s32[1]{0:T(128)} %bitcast.pos_ref, f32[8,128]{1,0:T(8,128)S(1)} %get-tuple-element.25.refs_0_, f32[8,128]{1,0:T(8,128)S(1)} %collective-permute-done.refs_1_, f32[8,128]{1,0:T(8,128)S(1)} %collective-permute-done.1.refs_2_, ...), custom_call_target="tpu_custom_call" | custom-call | flops 8999999488 | bytes 200000 | tf_op jit(solution)/shard_map/pair_terms/pallas_call | solution.py:283
  15.2 0.7 %copy-done.1 = s32[1024]{0:T(1024)S(1)} copy-done((s32[1024]{0:T(1024)S(1)}, s32[1024]{0:T(1024)}, u32[]{:S(2)}) %copy-start.1) | copy-done | bytes 4120
  15.8 0.4 %leaf_terms.1 = (f32[256,1024]{1,0:T(8,128)S(1)}, bf16[32,1024]{1,0:T(8,128)(2,1)S(1)}, f32[8,256]{1,0:T(8,128)S(1)}) custom-call(bf16[256,256]{1,0:T(8,128)(2,1)S(1)} %get-tuple-element.30.perm_ref, s32[1024,256]{1,0:T(8,128)S(1)} %copy-done, s32[8,128]{1,0:T(8,128)S(1)} %bitcast.7, f32[2,1024]{1,0:T(2,128)S(1)} %get-tuple-element.31.lam_ref), custom_call_target="tpu_custom_call" | custom-call | flops 200000000 | bytes 3000000 | tf_op jit(solution)/shard_map/leaf_terms/pallas_call | solution.py:324
  16.3 2.2 %histogram_part.7 = f32[200,256]{1,0:T(8,128)S(1)} custom-call(bf16[32,1024]{1,0:T(8,128)(2,1)S(1)} %get-tuple-element.38.tile_ref, f32[256,1024]{1,0:T(8,128)S(1)} %get-tuple-element.33.bins_ref, f32[8,256]{1,0:T(8,128)S(1)} %get-tuple-element.34.refs_0_), custom_call_target="tpu_custom_call" | custom-call | flops 8000000 | bytes 8000 | tf_op jit(solution)/shard_map/histogram_part/pallas_call | solution.py:398
  18.5 0.1 collective-permute-start.2
  18.6 1.1 %histogram_part.6 = f32[96,256]{1,0:T(8,128)S(1)} custom-call(bf16[32,1024]{1,0:T(8,128)(2,1)S(1)} %get-tuple-element.38.tile_ref, f32[256,1024]{1,0:T(8,128)S(1)} %get-tuple-element.33.bins_ref), custom_call_target="tpu_custom_call" | custom-call | flops 4000000 | bytes 4000 | tf_op jit(solution)/shard_map/histogram_part/pallas_call | solution.py:398
  19.7 0.3 collective-permute-done.2
  20.1 1.1 %histogram_part.8 = f32[96,256]{1,0:T(8,128)S(1)} custom-call(bf16[32,1024]{1,0:T(8,128)(2,1)S(1)} %get-tuple-element.38.tile_ref, f32[256,1024]{1,0:T(8,128)S(1)} %get-tuple-element.33.bins_ref), custom_call_target="tpu_custom_call" | custom-call | flops 4000000 | bytes 4000 | tf_op jit(solution)/shard_map/histogram_part/pallas_call | solution.py:398
  21.2 1.4 %collective-permute-start.4 = (f32[104,256]{1,0:T(8,128)S(1)}, f32[104,256]{1,0:T(8,128)S(1)}, u32[]{:S(2)}, u32[]{:S(2)}) collective-permute-start(f32[104,256]{1,0:T(8,128)S(1)} %pad_maximum_fusion), channel_id=1, source_target_pairs={{0,8},{1,9},{2,10},{3,11},{4,12},{5,13},{6,14},{7,15},{8,0},{9,1},... | collective-permute-start | bytes 319496 | tf_op jit(solution)/shard_map/ppermute | solution.py:473
  22.5 2.2 %histogram_part.10 = f32[192,256]{1,0:T(8,128)S(1)} custom-call(bf16[32,1024]{1,0:T(8,128)(2,1)S(1)} %get-tuple-element.38.tile_ref, f32[256,1024]{1,0:T(8,128)S(1)} %get-tuple-element.33.bins_ref), custom_call_target="tpu_custom_call" | custom-call | flops 8000000 | bytes 8000 | tf_op jit(solution)/shard_map/histogram_part/pallas_call | solution.py:398
  24.7 0.1 collective-permute-start.3
  24.8 1.1 %histogram_part.9 = f32[96,256]{1,0:T(8,128)S(1)} custom-call(bf16[32,1024]{1,0:T(8,128)(2,1)S(1)} %get-tuple-element.38.tile_ref, f32[256,1024]{1,0:T(8,128)S(1)} %get-tuple-element.33.bins_ref), custom_call_target="tpu_custom_call" | custom-call | flops 4000000 | bytes 4000 | tf_op jit(solution)/shard_map/histogram_part/pallas_call | solution.py:398
  25.9 0.4 collective-permute-done.4
  26.3 0.0 collective-permute-done.3
  26.4 3.2 %collective-permute-start.6 = (f32[104,256]{1,0:T(8,128)S(1)}, f32[104,256]{1,0:T(8,128)S(1)}, u32[]{:S(2)}, u32[]{:S(2)}) collective-permute-start(f32[104,256]{1,0:T(8,128)S(1)} %pad_maximum_fusion.1), channel_id=1, source_target_pairs={{0,16},{1,17},{2,18},{3,19},{4,20},{5,21},{6,22},{7,23},{8,24},{9,... | collective-permute-start | bytes 319496 | tf_op jit(solution)/shard_map/ppermute | solution.py:473
  29.6 0.7 %collective-permute-start.5 = (f32[96,256]{1,0:T(8,128)S(1)}, f32[96,256]{1,0:T(8,128)S(1)}, u32[]{:S(2)}, u32[]{:S(2)}) collective-permute-start(f32[96,256]{1,0:T(8,128)S(1)} %slice_add_fusion.4), channel_id=1, source_target_pairs={{0,8},{1,9},{2,10},{3,11},{4,12},{5,13},{6,14},{7,15},{8,0},{9,1},... | collective-permute-start | bytes 294920 | tf_op jit(solution)/shard_map/ppermute | solution.py:473
  30.3 1.1 %histogram_part.11 = f32[96,256]{1,0:T(8,128)S(1)} custom-call(bf16[32,1024]{1,0:T(8,128)(2,1)S(1)} %get-tuple-element.38.tile_ref, f32[256,1024]{1,0:T(8,128)S(1)} %get-tuple-element.33.bins_ref), custom_call_target="tpu_custom_call" | custom-call | flops 4000000 | bytes 4000 | tf_op jit(solution)/shard_map/histogram_part/pallas_call | solution.py:398
  31.4 2.8 %collective-permute-done.5 = f32[96,256]{1,0:T(8,128)S(1)} collective-permute-done((f32[96,256]{1,0:T(8,128)S(1)}, f32[96,256]{1,0:T(8,128)S(1)}, u32[]{:S(2)}, u32[]{:S(2)}) %collective-permute-start.5) | collective-permute-done | bytes 98336 | tf_op jit(solution)/shard_map/ppermute | solution.py:473
  34.2 0.0 collective-permute-done.6
  34.3 1.7 %collective-permute-start.7 = (f32[32,256]{1,0:T(8,128)S(1)}, f32[32,256]{1,0:T(8,128)S(1)}, u32[]{:S(2)}, u32[]{:S(2)}) collective-permute-start(f32[32,256]{1,0:T(8,128)S(1)} %get-tuple-element.50), channel_id=1, source_target_pairs={{0,3},{1,2},{2,1},{3,0},{4,7},{5,6},{6,5},{7,4},{8,11},{9,10},{10,... | collective-permute-start | bytes 98312 | tf_op jit(solution)/shard_map/ppermute | solution.py:473
  36.0 0.8 %collective-permute-start.8 = (f32[32,256]{1,0:T(8,128)S(1)}, f32[32,256]{1,0:T(8,128)S(1)}, u32[]{:S(2)}, u32[]{:S(2)}) collective-permute-start(f32[32,256]{1,0:T(8,128)S(1)} %get-tuple-element.49), channel_id=1, source_target_pairs={{0,2},{1,3},{2,0},{3,1},{4,6},{5,7},{6,4},{7,5},{8,10},{9,11},{10,... | collective-permute-start | bytes 98312 | tf_op jit(solution)/shard_map/ppermute | solution.py:473
  36.8 1.9 %collective-permute-start.9 = (f32[32,256]{1,0:T(8,128)S(1)}, f32[32,256]{1,0:T(8,128)S(1)}, u32[]{:S(2)}, u32[]{:S(2)}) collective-permute-start(f32[32,256]{1,0:T(8,128)S(1)} %get-tuple-element.48), channel_id=1, source_target_pairs={{0,1},{1,0},{2,3},{3,2},{4,5},{5,4},{6,7},{7,6},{8,9},{9,8},{10,11... | collective-permute-start | bytes 98312 | tf_op jit(solution)/shard_map/ppermute | solution.py:473
  38.7 1.4 %collective-permute-done.7.refs_0_ = f32[32,256]{1,0:T(8,128)S(1)} collective-permute-done((f32[32,256]{1,0:T(8,128)S(1)}, f32[32,256]{1,0:T(8,128)S(1)}, u32[]{:S(2)}, u32[]{:S(2)}) %collective-permute-start.7) | collective-permute-done | bytes 32800 | tf_op jit(solution)/shard_map/ppermute | solution.py:473
  40.2 0.8 %collective-permute-done.8.refs_1_ = f32[32,256]{1,0:T(8,128)S(1)} collective-permute-done((f32[32,256]{1,0:T(8,128)S(1)}, f32[32,256]{1,0:T(8,128)S(1)}, u32[]{:S(2)}, u32[]{:S(2)}) %collective-permute-start.8) | collective-permute-done | bytes 32800 | tf_op jit(solution)/shard_map/ppermute | solution.py:473
  41.0 0.1 collective-permute-done.9.refs_2_
  41.1 0.9 %finish.1 = (f32[8,128]{1,0:T(8,128)}, f32[8,128]{1,0:T(8,128)}, f32[3,2048]{1,0:T(4,128)}) custom-call(s32[8,128]{1,0:T(8,128)S(1)} %bitcast.8, f32[24,256]{1,0:T(8,128)S(1)} %get-tuple-element.47.kept_ref, f32[8,256]{1,0:T(8,128)S(1)} %slice_add_fusion.6.sums_ref, f32[32,256]{1,0:T(8,128)S(1)} %collective-permute-done.7.refs_0_, ...), custom_call_target="tpu_custom_call" | custom-call | tf_op jit(solution)/shard_map/finish/pallas_call | solution.py:438
  (21 shorter events, 0.1 us)
Async XLA Ops:
  0.6 5.1 %copy-start.2 = (s32[4096]{0:T(1024)S(1)}, s32[4096]{0:T(1024)}, u32[]{:S(2)}) copy-start(s32[4096]{0:T(1024)} %param.7) | copy-start | bytes 49156
  0.6 6.9 %collective-permute-start = (f32[8,128]{1,0:T(8,128)}, f32[8,128]{1,0:T(8,128)S(1)}, u32[]{:S(2)}, u32[]{:S(2)}) collective-permute-start(f32[8,128]{1,0:T(8,128)} %bitcast.10), channel_id=1, source_target_pairs={{1,2},{0,3},{2,1},{3,0},{5,6},{4,7},{6,5},{7,4},{9,10},{8,11},{10,... | collective-permute-start | bytes 12296 | tf_op jit(solution)/shard_map/ppermute | solution.py:482
  5.8 3.8 %collective-permute-start.1 = (f32[8,128]{1,0:T(8,128)}, f32[8,128]{1,0:T(8,128)S(1)}, u32[]{:S(2)}, u32[]{:S(2)}) collective-permute-start(f32[8,128]{1,0:T(8,128)} %bitcast.11), channel_id=1, source_target_pairs={{0,1},{2,3},{1,0},{3,2},{4,5},{6,7},{5,4},{7,6},{8,9},{10,11},{9,8... | collective-permute-start | bytes 12296 | tf_op jit(solution)/shard_map/ppermute | solution.py:482
  5.8 0.8 %copy-start.3 = (f32[1024]{0:T(1024)S(1)}, f32[1024]{0:T(1024)}, u32[]{:S(2)}) copy-start(f32[1024]{0:T(1024)} %param.6) | copy-start | bytes 12292
  5.8 0.8 %copy-start.4 = (s32[256]{0:T(256)S(1)}, s32[256]{0:T(256)}, u32[]{:S(2)}) copy-start(s32[256]{0:T(256)} %param.11) | copy-start | bytes 3076
  5.8 0.8 %copy-start.5 = (s32[1,16]{1,0:T(1,128)S(1)}, s32[1,16]{1,0:T(1,128)}, u32[]{:S(2)}) copy-start(s32[1,16]{1,0:T(1,128)} %len_ref.1) | copy-start | bytes 196
  9.6 5.6 %copy-start = (s32[1024,256]{1,0:T(8,128)S(1)}, s32[1024,256]{1,0:T(8,128)}, u32[]{:S(2)}) copy-start(s32[1024,256]{1,0:T(8,128)} %bins_ref.1) | copy-start | bytes 3145732
  15.2 0.7 %copy-start.1 = (s32[1024]{0:T(1024)S(1)}, s32[1024]{0:T(1024)}, u32[]{:S(2)}) copy-start(s32[1024]{0:T(1024)} %param.8) | copy-start | bytes 12292
  18.5 1.5 %collective-permute-start.2 = (f32[200,256]{1,0:T(8,128)S(1)}, f32[200,256]{1,0:T(8,128)S(1)}, u32[]{:S(2)}, u32[]{:S(2)}) collective-permute-start(f32[200,256]{1,0:T(8,128)S(1)} %histogram_part.7), channel_id=1, source_target_pairs={{0,4},{1,5},{2,6},{3,7},{4,0},{5,1},{6,2},{7,3},{8,12},{9,13},{10,... | collective-permute-start | bytes 614408 | tf_op jit(solution)/shard_map/ppermute | solution.py:473
  21.2 5.1 %collective-permute-start.4 = (f32[104,256]{1,0:T(8,128)S(1)}, f32[104,256]{1,0:T(8,128)S(1)}, u32[]{:S(2)}, u32[]{:S(2)}) collective-permute-start(f32[104,256]{1,0:T(8,128)S(1)} %pad_maximum_fusion), channel_id=1, source_target_pairs={{0,8},{1,9},{2,10},{3,11},{4,12},{5,13},{6,14},{7,15},{8,0},{9,1},... | collective-permute-start | bytes 319496 | tf_op jit(solution)/shard_map/ppermute | solution.py:473
  24.7 1.6 %collective-permute-start.3 = (f32[192,256]{1,0:T(8,128)S(1)}, f32[192,256]{1,0:T(8,128)S(1)}, u32[]{:S(2)}, u32[]{:S(2)}) collective-permute-start(f32[192,256]{1,0:T(8,128)S(1)} %histogram_part.10), channel_id=1, source_target_pairs={{0,4},{1,5},{2,6},{3,7},{4,0},{5,1},{6,2},{7,3},{8,12},{9,13},{10,... | collective-permute-start | bytes 589832 | tf_op jit(solution)/shard_map/ppermute | solution.py:473
  26.4 7.9 %collective-permute-start.6 = (f32[104,256]{1,0:T(8,128)S(1)}, f32[104,256]{1,0:T(8,128)S(1)}, u32[]{:S(2)}, u32[]{:S(2)}) collective-permute-start(f32[104,256]{1,0:T(8,128)S(1)} %pad_maximum_fusion.1), channel_id=1, source_target_pairs={{0,16},{1,17},{2,18},{3,19},{4,20},{5,21},{6,22},{7,23},{8,24},{9,... | collective-permute-start | bytes 319496 | tf_op jit(solution)/shard_map/ppermute | solution.py:473
  29.6 4.6 %collective-permute-start.5 = (f32[96,256]{1,0:T(8,128)S(1)}, f32[96,256]{1,0:T(8,128)S(1)}, u32[]{:S(2)}, u32[]{:S(2)}) collective-permute-start(f32[96,256]{1,0:T(8,128)S(1)} %slice_add_fusion.4), channel_id=1, source_target_pairs={{0,8},{1,9},{2,10},{3,11},{4,12},{5,13},{6,14},{7,15},{8,0},{9,1},... | collective-permute-start | bytes 294920 | tf_op jit(solution)/shard_map/ppermute | solution.py:473
  34.3 5.9 %collective-permute-start.7 = (f32[32,256]{1,0:T(8,128)S(1)}, f32[32,256]{1,0:T(8,128)S(1)}, u32[]{:S(2)}, u32[]{:S(2)}) collective-permute-start(f32[32,256]{1,0:T(8,128)S(1)} %get-tuple-element.50), channel_id=1, source_target_pairs={{0,3},{1,2},{2,1},{3,0},{4,7},{5,6},{6,5},{7,4},{8,11},{9,10},{10,... | collective-permute-start | bytes 98312 | tf_op jit(solution)/shard_map/ppermute | solution.py:473
  36.0 5.0 %collective-permute-start.8 = (f32[32,256]{1,0:T(8,128)S(1)}, f32[32,256]{1,0:T(8,128)S(1)}, u32[]{:S(2)}, u32[]{:S(2)}) collective-permute-start(f32[32,256]{1,0:T(8,128)S(1)} %get-tuple-element.49), channel_id=1, source_target_pairs={{0,2},{1,3},{2,0},{3,1},{4,6},{5,7},{6,4},{7,5},{8,10},{9,11},{10,... | collective-permute-start | bytes 98312 | tf_op jit(solution)/shard_map/ppermute | solution.py:473
  36.8 4.3 %collective-permute-start.9 = (f32[32,256]{1,0:T(8,128)S(1)}, f32[32,256]{1,0:T(8,128)S(1)}, u32[]{:S(2)}, u32[]{:S(2)}) collective-permute-start(f32[32,256]{1,0:T(8,128)S(1)} %get-tuple-element.48), channel_id=1, source_target_pairs={{0,1},{1,0},{2,3},{3,2},{4,5},{5,4},{6,7},{7,6},{8,9},{9,8},{10,11... | collective-permute-start | bytes 98312 | tf_op jit(solution)/shard_map/ppermute | solution.py:473

commit v14 on v13

--- a/solution.py
+++ b/solution.py
@@ -476,10 +476,14 @@
     leaf_rows = leaves.reshape(own, LANES)
     own_scores = scores.reshape(own, LANES)
     score_parts = [own_scores]
-    for begin in (1, 0):
-        links = [(z, z + 1) for z in range(begin, feat_count - 1, 2)]
-        links += [(0, feat_count - 1)] if begin else []
-        score_parts.append(lax.ppermute(own_scores, "feat", links + [(b, a) for a, b in links]))
+    def inner_partner(p):
+        z = p % feat_count
+        if z in (0, feat_count - 1):
+            return p ^ query_masks[0]
+        return p + 1 if z % 2 else p - 1
+
+    score_parts.append(lax.ppermute(own_scores, axes, [(p, inner_partner(p)) for p in range(count)]))
+    score_parts.append(swap(own_scores, 1))
     masks = feat_masks + query_masks[:0:-1] + query_masks[:1]
     score_parts[0], qid, worth, inverse, perm, bounds = prepare(
         feat_count, masks, lengths, pos, labels.reshape(-1, LANES), owner.reshape(-1, LANES), own_scores)

time: 42.1 us -> 41.6 us (0.988)
  waiting for transfers between devices: 7.84 us -> 6.97 us
  starting transfers between devices: 15 us -> 15.6 us
    ppermute x8 -> x9, starting transfers between devices: 9.92 us -> 15.1 us  [swap(): return lax.ppermute(value, axes, [(p, p ^ mask) for p in range(count)])]
    ppermute x2 -> x1, starting transfers between devices: 5.12 us -> 0.52 us  [local(): lax.ppermute(own_scores, axes, [(p, inner_partner(p)) for p in range(coun...]
    ppermute x2 -> x1, waiting for transfers between devices: 2.04 us -> 0.01 us  [local(): lax.ppermute(own_scores, axes, [(p, inner_partner(p)) for p in range(coun...]
    ppermute x8 -> x9, waiting for transfers between devices: 5.8 us -> 6.96 us  [swap(): return lax.ppermute(value, axes, [(p, p ^ mask) for p in range(count)])]
  transfers between devices with their start and end apart: 10 -> 10, of which waited for: 7 -> 6; matrix products, arithmetic and copies ran while one was open for 0% -> 0% of each run, Pallas kernels for 16% -> 16%
where the time goes in v14:
time: 41.6 us; the launch traced here: 41.2 us
  Pallas kernels  16.3 us (39%)
  starting transfers between devices  15.6 us (38%)
  waiting for transfers between devices  6.97 us (17%)
  local copies, waits for them, and re-layouts  1.42 us (3%)
  between operations  0.79 us (2%)
    ppermute x9, starting transfers between devices, swap(): return lax.ppermute(value, axes, [(p, p ^ mask) for p in range(count)])  15.1 us
    pallas_call x6, Pallas kernels, histogram_part(): pl.pallas_call(functools.partial(histogram_kernel, first, groups), out_sh...  8.81 us
    ppermute x9, waiting for transfers between devices, swap(): return lax.ppermute(value, axes, [(p, p ^ mask) for p in range(count)])  6.96 us
    pallas_call x1, Pallas kernels, pair_terms(): pl.pallas_call(functools.partial(pairs_kernel, feat_count), out_shape=(ja...  5.19 us
    unnamed x12, local copies, waits for them, and re-layouts  1.41 us
    pallas_call x1, Pallas kernels, prepare(): pl.pallas_call(functools.partial(prepare_kernel, feat_count, masks), out_...  1.01 us
    pallas_call x1, Pallas kernels, finish(): pl.pallas_call(functools.partial(finish_kernel, per_dev), out_shape=(jax....  0.86 us
  transfers between devices with their start and end apart: 10, of which 6 were waited for; matrix products, arithmetic and copies ran while one was open for 0% of the time, Pallas kernels for 16%

profile of v14, /device:TPU:0, one launch (start us, length us, event | category | flops | bytes accessed | tf_op | source)
XLA Modules:
  0.0 41.2 jit_solution(12904670894866703131)
XLA Ops:
  0.6 0.5 %collective-permute-start = (f32[8,128]{1,0:T(8,128)}, f32[8,128]{1,0:T(8,128)S(1)}, u32[]{:S(2)}, u32[]{:S(2)}) collective-permute-start(f32[8,128]{1,0:T(8,128)} %bitcast.10), channel_id=1, source_target_pairs={{0,4},{1,2},{2,1},{3,7},{4,0},{5,6},{6,5},{7,3},{8,12},{9,10},{10,... | collective-permute-start | bytes 12296 | tf_op jit(solution)/shard_map/ppermute | solution.py:485
  1.2 4.1 %collective-permute-start.1 = (f32[8,128]{1,0:T(8,128)}, f32[8,128]{1,0:T(8,128)S(1)}, u32[]{:S(2)}, u32[]{:S(2)}) collective-permute-start(f32[8,128]{1,0:T(8,128)} %bitcast.11), channel_id=1, source_target_pairs={{0,1},{1,0},{2,3},{3,2},{4,5},{5,4},{6,7},{7,6},{8,9},{9,8},{10,11... | collective-permute-start | bytes 12296 | tf_op jit(solution)/shard_map/ppermute | solution.py:473
  5.3 0.7 %copy-done.3 = f32[1024]{0:T(1024)S(1)} copy-done((f32[1024]{0:T(1024)S(1)}, f32[1024]{0:T(1024)}, u32[]{:S(2)}) %copy-start.3) | copy-done | bytes 4120
  6.0 1.0 %prepare.1 = (f32[8,128]{1,0:T(8,128)S(1)}, s32[32,128]{1,0:T(8,128)S(1)}, f32[32,128]{1,0:T(8,128)S(1)}, f32[1,1024]{1,0:T(1,128)S(1)}, bf16[256,256]{1,0:T(8,128)(2,1)S(1)}, /*index=5*/s32[8,128]{1,0:T(8,128)S(1)}) custom-call(s32[1,16]{1,0:T(1,128)S(1)} %copy-done.5, s32[1]{0:T(128)} %bitcast.pos_ref, s32[32,128]{1,0:T(8,128)S(1)} %bitcast.9, ...), custom_call_target="tpu_custom_call" | custom-call | flops 2000000000 | bytes 300000 | tf_op jit(solution)/shard_map/prepare/pallas_call | solution.py:112
  7.1 0.0 collective-permute-done.refs_1_
  7.1 0.1 collective-permute-done.1.refs_2_
  7.1 5.2 %pair_terms.1 = (f32[2,1024]{1,0:T(2,128)}, f32[2,1024]{1,0:T(2,128)S(1)}) custom-call(s32[8,128]{1,0:T(8,128)S(1)} %get-tuple-element.24.bounds_ref, s32[1]{0:T(128)} %bitcast.pos_ref, f32[8,128]{1,0:T(8,128)S(1)} %get-tuple-element.25.refs_0_, f32[8,128]{1,0:T(8,128)S(1)} %collective-permute-done.refs_1_, f32[8,128]{1,0:T(8,128)S(1)} %collective-permute-done.1.refs_2_, ...), custom_call_target="tpu_custom_call" | custom-call | flops 8999999488 | bytes 200000 | tf_op jit(solution)/shard_map/pair_terms/pallas_call | solution.py:283
  12.3 0.7 %copy-done.1 = s32[1024]{0:T(1024)S(1)} copy-done((s32[1024]{0:T(1024)S(1)}, s32[1024]{0:T(1024)}, u32[]{:S(2)}) %copy-start.1) | copy-done | bytes 4120
  13.0 0.4 %leaf_terms.1 = (f32[256,1024]{1,0:T(8,128)S(1)}, bf16[32,1024]{1,0:T(8,128)(2,1)S(1)}, f32[8,256]{1,0:T(8,128)S(1)}) custom-call(bf16[256,256]{1,0:T(8,128)(2,1)S(1)} %get-tuple-element.30.perm_ref, s32[1024,256]{1,0:T(8,128)S(1)} %copy-done, s32[8,128]{1,0:T(8,128)S(1)} %bitcast.7, f32[2,1024]{1,0:T(2,128)S(1)} %get-tuple-element.31.lam_ref), custom_call_target="tpu_custom_call" | custom-call | flops 200000000 | bytes 3000000 | tf_op jit(solution)/shard_map/leaf_terms/pallas_call | solution.py:324
  13.5 2.2 %histogram_part.7 = f32[200,256]{1,0:T(8,128)S(1)} custom-call(bf16[32,1024]{1,0:T(8,128)(2,1)S(1)} %get-tuple-element.38.tile_ref, f32[256,1024]{1,0:T(8,128)S(1)} %get-tuple-element.33.bins_ref, f32[8,256]{1,0:T(8,128)S(1)} %get-tuple-element.34.refs_0_), custom_call_target="tpu_custom_call" | custom-call | flops 8000000 | bytes 8000 | tf_op jit(solution)/shard_map/histogram_part/pallas_call | solution.py:398
  15.7 1.2 %collective-permute-start.2 = (f32[200,256]{1,0:T(8,128)S(1)}, f32[200,256]{1,0:T(8,128)S(1)}, u32[]{:S(2)}, u32[]{:S(2)}) collective-permute-start(f32[200,256]{1,0:T(8,128)S(1)} %histogram_part.7), channel_id=1, source_target_pairs={{0,4},{1,5},{2,6},{3,7},{4,0},{5,1},{6,2},{7,3},{8,12},{9,13},{10,... | collective-permute-start | bytes 614408 | tf_op jit(solution)/shard_map/ppermute | solution.py:473
  16.8 1.1 %histogram_part.6 = f32[96,256]{1,0:T(8,128)S(1)} custom-call(bf16[32,1024]{1,0:T(8,128)(2,1)S(1)} %get-tuple-element.38.tile_ref, f32[256,1024]{1,0:T(8,128)S(1)} %get-tuple-element.33.bins_ref), custom_call_target="tpu_custom_call" | custom-call | flops 4000000 | bytes 4000 | tf_op jit(solution)/shard_map/histogram_part/pallas_call | solution.py:398
  17.9 0.0 collective-permute-done.2
  18.0 1.1 %histogram_part.8 = f32[96,256]{1,0:T(8,128)S(1)} custom-call(bf16[32,1024]{1,0:T(8,128)(2,1)S(1)} %get-tuple-element.38.tile_ref, f32[256,1024]{1,0:T(8,128)S(1)} %get-tuple-element.33.bins_ref), custom_call_target="tpu_custom_call" | custom-call | flops 4000000 | bytes 4000 | tf_op jit(solution)/shard_map/histogram_part/pallas_call | solution.py:398
  19.1 1.1 %collective-permute-start.4 = (f32[104,256]{1,0:T(8,128)S(1)}, f32[104,256]{1,0:T(8,128)S(1)}, u32[]{:S(2)}, u32[]{:S(2)}) collective-permute-start(f32[104,256]{1,0:T(8,128)S(1)} %pad_maximum_fusion), channel_id=1, source_target_pairs={{0,8},{1,9},{2,10},{3,11},{4,12},{5,13},{6,14},{7,15},{8,0},{9,1},... | collective-permute-start | bytes 319496 | tf_op jit(solution)/shard_map/ppermute | solution.py:473
  20.2 2.2 %histogram_part.10 = f32[192,256]{1,0:T(8,128)S(1)} custom-call(bf16[32,1024]{1,0:T(8,128)(2,1)S(1)} %get-tuple-element.38.tile_ref, f32[256,1024]{1,0:T(8,128)S(1)} %get-tuple-element.33.bins_ref), custom_call_target="tpu_custom_call" | custom-call | flops 8000000 | bytes 8000 | tf_op jit(solution)/shard_map/histogram_part/pallas_call | solution.py:398
  22.4 0.1 collective-permute-start.3
  22.5 1.1 %histogram_part.9 = f32[96,256]{1,0:T(8,128)S(1)} custom-call(bf16[32,1024]{1,0:T(8,128)(2,1)S(1)} %get-tuple-element.38.tile_ref, f32[256,1024]{1,0:T(8,128)S(1)} %get-tuple-element.33.bins_ref), custom_call_target="tpu_custom_call" | custom-call | flops 4000000 | bytes 4000 | tf_op jit(solution)/shard_map/histogram_part/pallas_call | solution.py:398
  23.6 0.8 %collective-permute-done.4 = f32[104,256]{1,0:T(8,128)S(1)} collective-permute-done((f32[104,256]{1,0:T(8,128)S(1)}, f32[104,256]{1,0:T(8,128)S(1)}, u32[]{:S(2)}, u32[]{:S(2)}) %collective-permute-start.4) | collective-permute-done | bytes 106528 | tf_op jit(solution)/shard_map/ppermute | solution.py:473
  24.4 0.0 collective-permute-done.3
  24.4 2.6 %collective-permute-start.6 = (f32[104,256]{1,0:T(8,128)S(1)}, f32[104,256]{1,0:T(8,128)S(1)}, u32[]{:S(2)}, u32[]{:S(2)}) collective-permute-start(f32[104,256]{1,0:T(8,128)S(1)} %pad_maximum_fusion.1), channel_id=1, source_target_pairs={{0,16},{1,17},{2,18},{3,19},{4,20},{5,21},{6,22},{7,23},{8,24},{9,... | collective-permute-start | bytes 319496 | tf_op jit(solution)/shard_map/ppermute | solution.py:473
  27.1 0.9 %collective-permute-start.5 = (f32[96,256]{1,0:T(8,128)S(1)}, f32[96,256]{1,0:T(8,128)S(1)}, u32[]{:S(2)}, u32[]{:S(2)}) collective-permute-start(f32[96,256]{1,0:T(8,128)S(1)} %slice_add_fusion.4), channel_id=1, source_target_pairs={{0,8},{1,9},{2,10},{3,11},{4,12},{5,13},{6,14},{7,15},{8,0},{9,1},... | collective-permute-start | bytes 294920 | tf_op jit(solution)/shard_map/ppermute | solution.py:473
  27.9 1.1 %histogram_part.11 = f32[96,256]{1,0:T(8,128)S(1)} custom-call(bf16[32,1024]{1,0:T(8,128)(2,1)S(1)} %get-tuple-element.38.tile_ref, f32[256,1024]{1,0:T(8,128)S(1)} %get-tuple-element.33.bins_ref), custom_call_target="tpu_custom_call" | custom-call | flops 4000000 | bytes 4000 | tf_op jit(solution)/shard_map/histogram_part/pallas_call | solution.py:398
  29.0 2.7 %collective-permute-done.5 = f32[96,256]{1,0:T(8,128)S(1)} collective-permute-done((f32[96,256]{1,0:T(8,128)S(1)}, f32[96,256]{1,0:T(8,128)S(1)}, u32[]{:S(2)}, u32[]{:S(2)}) %collective-permute-start.5) | collective-permute-done | bytes 98336 | tf_op jit(solution)/shard_map/ppermute | solution.py:473
  31.7 0.0 collective-permute-done.6
  31.8 2.7 %collective-permute-start.7 = (f32[32,256]{1,0:T(8,128)S(1)}, f32[32,256]{1,0:T(8,128)S(1)}, u32[]{:S(2)}, u32[]{:S(2)}) collective-permute-start(f32[32,256]{1,0:T(8,128)S(1)} %get-tuple-element.50), channel_id=1, source_target_pairs={{0,3},{1,2},{2,1},{3,0},{4,7},{5,6},{6,5},{7,4},{8,11},{9,10},{10,... | collective-permute-start | bytes 98312 | tf_op jit(solution)/shard_map/ppermute | solution.py:473
  34.4 2.0 %collective-permute-start.8 = (f32[32,256]{1,0:T(8,128)S(1)}, f32[32,256]{1,0:T(8,128)S(1)}, u32[]{:S(2)}, u32[]{:S(2)}) collective-permute-start(f32[32,256]{1,0:T(8,128)S(1)} %get-tuple-element.49), channel_id=1, source_target_pairs={{0,2},{1,3},{2,0},{3,1},{4,6},{5,7},{6,4},{7,5},{8,10},{9,11},{10,... | collective-permute-start | bytes 98312 | tf_op jit(solution)/shard_map/ppermute | solution.py:473
  36.4 0.5 %collective-permute-start.9 = (f32[32,256]{1,0:T(8,128)S(1)}, f32[32,256]{1,0:T(8,128)S(1)}, u32[]{:S(2)}, u32[]{:S(2)}) collective-permute-start(f32[32,256]{1,0:T(8,128)S(1)} %get-tuple-element.48), channel_id=1, source_target_pairs={{0,1},{1,0},{2,3},{3,2},{4,5},{5,4},{6,7},{7,6},{8,9},{9,8},{10,11... | collective-permute-start | bytes 98312 | tf_op jit(solution)/shard_map/ppermute | solution.py:473
  36.9 0.6 %collective-permute-done.7.refs_0_ = f32[32,256]{1,0:T(8,128)S(1)} collective-permute-done((f32[32,256]{1,0:T(8,128)S(1)}, f32[32,256]{1,0:T(8,128)S(1)}, u32[]{:S(2)}, u32[]{:S(2)}) %collective-permute-start.7) | collective-permute-done | bytes 32800 | tf_op jit(solution)/shard_map/ppermute | solution.py:473
  37.5 1.8 %collective-permute-done.8.refs_1_ = f32[32,256]{1,0:T(8,128)S(1)} collective-permute-done((f32[32,256]{1,0:T(8,128)S(1)}, f32[32,256]{1,0:T(8,128)S(1)}, u32[]{:S(2)}, u32[]{:S(2)}) %collective-permute-start.8) | collective-permute-done | bytes 32800 | tf_op jit(solution)/shard_map/ppermute | solution.py:473
  39.3 1.0 %collective-permute-done.9.refs_2_ = f32[32,256]{1,0:T(8,128)S(1)} collective-permute-done((f32[32,256]{1,0:T(8,128)S(1)}, f32[32,256]{1,0:T(8,128)S(1)}, u32[]{:S(2)}, u32[]{:S(2)}) %collective-permute-start.9) | collective-permute-done | bytes 32800 | tf_op jit(solution)/shard_map/ppermute | solution.py:473
  40.3 0.9 %finish.1 = (f32[8,128]{1,0:T(8,128)}, f32[8,128]{1,0:T(8,128)}, f32[3,2048]{1,0:T(4,128)}) custom-call(s32[8,128]{1,0:T(8,128)S(1)} %bitcast.8, f32[24,256]{1,0:T(8,128)S(1)} %get-tuple-element.47.kept_ref, f32[8,256]{1,0:T(8,128)S(1)} %slice_add_fusion.6.sums_ref, f32[32,256]{1,0:T(8,128)S(1)} %collective-permute-done.7.refs_0_, ...), custom_call_target="tpu_custom_call" | custom-call | tf_op jit(solution)/shard_map/finish/pallas_call | solution.py:438
  (21 shorter events, 0.1 us)
Async XLA Ops:
  0.6 4.7 %copy-start.2 = (s32[4096]{0:T(1024)S(1)}, s32[4096]{0:T(1024)}, u32[]{:S(2)}) copy-start(s32[4096]{0:T(1024)} %param.7) | copy-start | bytes 49156
  0.6 6.4 %collective-permute-start = (f32[8,128]{1,0:T(8,128)}, f32[8,128]{1,0:T(8,128)S(1)}, u32[]{:S(2)}, u32[]{:S(2)}) collective-permute-start(f32[8,128]{1,0:T(8,128)} %bitcast.10), channel_id=1, source_target_pairs={{0,4},{1,2},{2,1},{3,7},{4,0},{5,6},{6,5},{7,3},{8,12},{9,10},{10,... | collective-permute-start | bytes 12296 | tf_op jit(solution)/shard_map/ppermute | solution.py:485
  1.2 6.0 %collective-permute-start.1 = (f32[8,128]{1,0:T(8,128)}, f32[8,128]{1,0:T(8,128)S(1)}, u32[]{:S(2)}, u32[]{:S(2)}) collective-permute-start(f32[8,128]{1,0:T(8,128)} %bitcast.11), channel_id=1, source_target_pairs={{0,1},{1,0},{2,3},{3,2},{4,5},{5,4},{6,7},{7,6},{8,9},{9,8},{10,11... | collective-permute-start | bytes 12296 | tf_op jit(solution)/shard_map/ppermute | solution.py:473
  5.3 0.7 %copy-start.3 = (f32[1024]{0:T(1024)S(1)}, f32[1024]{0:T(1024)}, u32[]{:S(2)}) copy-start(f32[1024]{0:T(1024)} %param.6) | copy-start | bytes 12292
  5.3 0.7 %copy-start.4 = (s32[256]{0:T(256)S(1)}, s32[256]{0:T(256)}, u32[]{:S(2)}) copy-start(s32[256]{0:T(256)} %param.11) | copy-start | bytes 3076
  5.3 0.7 %copy-start.5 = (s32[1,16]{1,0:T(1,128)S(1)}, s32[1,16]{1,0:T(1,128)}, u32[]{:S(2)}) copy-start(s32[1,16]{1,0:T(1,128)} %len_ref.1) | copy-start | bytes 196
  7.1 5.2 %copy-start = (s32[1024,256]{1,0:T(8,128)S(1)}, s32[1024,256]{1,0:T(8,128)}, u32[]{:S(2)}) copy-start(s32[1024,256]{1,0:T(8,128)} %bins_ref.1) | copy-start | bytes 3145732
  12.3 0.7 %copy-start.1 = (s32[1024]{0:T(1024)S(1)}, s32[1024]{0:T(1024)}, u32[]{:S(2)}) copy-start(s32[1024]{0:T(1024)} %param.8) | copy-start | bytes 12292
  15.7 2.3 %collective-permute-start.2 = (f32[200,256]{1,0:T(8,128)S(1)}, f32[200,256]{1,0:T(8,128)S(1)}, u32[]{:S(2)}, u32[]{:S(2)}) collective-permute-start(f32[200,256]{1,0:T(8,128)S(1)} %histogram_part.7), channel_id=1, source_target_pairs={{0,4},{1,5},{2,6},{3,7},{4,0},{5,1},{6,2},{7,3},{8,12},{9,13},{10,... | collective-permute-start | bytes 614408 | tf_op jit(solution)/shard_map/ppermute | solution.py:473
  19.1 5.3 %collective-permute-start.4 = (f32[104,256]{1,0:T(8,128)S(1)}, f32[104,256]{1,0:T(8,128)S(1)}, u32[]{:S(2)}, u32[]{:S(2)}) collective-permute-start(f32[104,256]{1,0:T(8,128)S(1)} %pad_maximum_fusion), channel_id=1, source_target_pairs={{0,8},{1,9},{2,10},{3,11},{4,12},{5,13},{6,14},{7,15},{8,0},{9,1},... | collective-permute-start | bytes 319496 | tf_op jit(solution)/shard_map/ppermute | solution.py:473
  22.4 2.0 %collective-permute-start.3 = (f32[192,256]{1,0:T(8,128)S(1)}, f32[192,256]{1,0:T(8,128)S(1)}, u32[]{:S(2)}, u32[]{:S(2)}) collective-permute-start(f32[192,256]{1,0:T(8,128)S(1)} %histogram_part.10), channel_id=1, source_target_pairs={{0,4},{1,5},{2,6},{3,7},{4,0},{5,1},{6,2},{7,3},{8,12},{9,13},{10,... | collective-permute-start | bytes 589832 | tf_op jit(solution)/shard_map/ppermute | solution.py:473
  24.4 7.3 %collective-permute-start.6 = (f32[104,256]{1,0:T(8,128)S(1)}, f32[104,256]{1,0:T(8,128)S(1)}, u32[]{:S(2)}, u32[]{:S(2)}) collective-permute-start(f32[104,256]{1,0:T(8,128)S(1)} %pad_maximum_fusion.1), channel_id=1, source_target_pairs={{0,16},{1,17},{2,18},{3,19},{4,20},{5,21},{6,22},{7,23},{8,24},{9,... | collective-permute-start | bytes 319496 | tf_op jit(solution)/shard_map/ppermute | solution.py:473
  27.1 4.6 %collective-permute-start.5 = (f32[96,256]{1,0:T(8,128)S(1)}, f32[96,256]{1,0:T(8,128)S(1)}, u32[]{:S(2)}, u32[]{:S(2)}) collective-permute-start(f32[96,256]{1,0:T(8,128)S(1)} %slice_add_fusion.4), channel_id=1, source_target_pairs={{0,8},{1,9},{2,10},{3,11},{4,12},{5,13},{6,14},{7,15},{8,0},{9,1},... | collective-permute-start | bytes 294920 | tf_op jit(solution)/shard_map/ppermute | solution.py:473
  31.8 5.8 %collective-permute-start.7 = (f32[32,256]{1,0:T(8,128)S(1)}, f32[32,256]{1,0:T(8,128)S(1)}, u32[]{:S(2)}, u32[]{:S(2)}) collective-permute-start(f32[32,256]{1,0:T(8,128)S(1)} %get-tuple-element.50), channel_id=1, source_target_pairs={{0,3},{1,2},{2,1},{3,0},{4,7},{5,6},{6,5},{7,4},{8,11},{9,10},{10,... | collective-permute-start | bytes 98312 | tf_op jit(solution)/shard_map/ppermute | solution.py:473
  34.4 4.9 %collective-permute-start.8 = (f32[32,256]{1,0:T(8,128)S(1)}, f32[32,256]{1,0:T(8,128)S(1)}, u32[]{:S(2)}, u32[]{:S(2)}) collective-permute-start(f32[32,256]{1,0:T(8,128)S(1)} %get-tuple-element.49), channel_id=1, source_target_pairs={{0,2},{1,3},{2,0},{3,1},{4,6},{5,7},{6,4},{7,5},{8,10},{9,11},{10,... | collective-permute-start | bytes 98312 | tf_op jit(solution)/shard_map/ppermute | solution.py:473
  36.4 3.9 %collective-permute-start.9 = (f32[32,256]{1,0:T(8,128)S(1)}, f32[32,256]{1,0:T(8,128)S(1)}, u32[]{:S(2)}, u32[]{:S(2)}) collective-permute-start(f32[32,256]{1,0:T(8,128)S(1)} %get-tuple-element.48), channel_id=1, source_target_pairs={{0,1},{1,0},{2,3},{3,2},{4,5},{5,4},{6,7},{7,6},{8,9},{9,8},{10,11... | collective-permute-start | bytes 98312 | tf_op jit(solution)/shard_map/ppermute | solution.py:473

commit v15 on v14

--- a/solution.py
+++ b/solution.py
@@ -39,9 +39,10 @@
     return pl.BlockSpec(memory_space=pltpu.SMEM)
 
 
-def prepare_kernel(feat_count, masks, len_ref, pos_ref, lab_ref, owner_ref, score_ref,
-                   kept_ref, qid_ref, worth_ref, inv_ref, perm_ref, bounds_ref):
+def prepare_kernel(feat_count, masks, len_ref, pos_ref, lab_ref, owner_ref, score_ref, leaf_ref,
+                   kept_ref, leaf_out, qid_ref, worth_ref, inv_ref, perm_ref, bounds_ref):
     kept_ref[...] = score_ref[...]
+    leaf_out[...] = leaf_ref[...]
     queries = len_ref.shape[1]
     rows = lab_ref.shape[0]
     own = rows // feat_count
@@ -106,25 +107,26 @@
     perm_ref[...] = lax.dot_general(pick, holds, NT, preferred_element_type=F32).astype(BF16)
 
 
-def prepare(feat_count, masks, lengths, pos, labels, owner, scores):
+def prepare(feat_count, masks, lengths, pos, labels, owner, scores, leaves):
     rows = labels.shape[0]
     features = owner.shape[0] * LANES
     return pl.pallas_call(
         functools.partial(prepare_kernel, feat_count, masks),
         out_shape=(
             jax.ShapeDtypeStruct(scores.shape, F32),
+            jax.ShapeDtypeStruct(leaves.shape, jnp.int32),
             jax.ShapeDtypeStruct((rows, LANES), jnp.int32),
             jax.ShapeDtypeStruct((rows, LANES), F32),
             jax.ShapeDtypeStruct((1, rows // feat_count * LANES), F32),
             jax.ShapeDtypeStruct((features, features), BF16),
             jax.ShapeDtypeStruct((8, LANES), jnp.int32),
         ),
-        in_specs=[smem(), smem(), vmem(), vmem(), vmem()],
-        out_specs=(vmem(),) * 6,
+        in_specs=[smem(), smem(), vmem(), vmem(), vmem(), vmem()],
+        out_specs=(vmem(),) * 7,
         compiler_params=pltpu.CompilerParams(vmem_limit_bytes=VMEM_LIMIT),
         cost_estimate=pl.CostEstimate(flops=2_000_000_000, bytes_accessed=300_000, transcendentals=20_000),
         name="prepare",
-    )(lengths, pos, labels, owner, scores)
+    )(lengths, pos, labels, owner, scores, leaves)
 
 
 def split_terms(value, terms):
@@ -425,10 +427,19 @@
     step_ref[...] = shrinkage * step
     hist = add_up([kept_ref[...]] + [ref[:unit, :] for ref in arrived])
     if per_dev == GROUP:
+        shape = hist.shape
+        line, place = iota(shape, 0), iota(shape, 1) // LOW
+        step = 1
+        while step < GROUP:
+            down, across = (line // step) % 2, (place // step) % 2
+            shift = step * LOW
+            ahead = pltpu.roll(pltpu.roll(hist, shape[0] - step, 0), shift, 1)
+            behind = pltpu.roll(pltpu.roll(hist, step, 0), shape[1] - shift, 1)
+            hist = jnp.where(down == across, hist, jnp.where(across == 1, ahead, behind))
+            step *= 2
         for c in range(3):
             for f in range(GROUP):
-                line = [hist[c * HIGH + h:c * HIGH + h + 1, f * LOW:(f + 1) * LOW] for h in range(HIGH)]
-                hist_ref[c:c + 1, f * BINS:(f + 1) * BINS] = jnp.concatenate(line, axis=1)
+                hist_ref[c:c + 1, f * BINS:(f + 1) * BINS] = hist[c * HIGH + f:c * HIGH + f + 1, :]
     else:
         hist_ref[...] = hist
 
@@ -485,8 +496,8 @@
     score_parts.append(lax.ppermute(own_scores, axes, [(p, inner_partner(p)) for p in range(count)]))
     score_parts.append(swap(own_scores, 1))
     masks = feat_masks + query_masks[:0:-1] + query_masks[:1]
-    score_parts[0], qid, worth, inverse, perm, bounds = prepare(
-        feat_count, masks, lengths, pos, labels.reshape(-1, LANES), owner.reshape(-1, LANES), own_scores)
+    score_parts[0], leaf_rows, qid, worth, inverse, perm, bounds = prepare(
+        feat_count, masks, lengths, pos, labels.reshape(-1, LANES), owner.reshape(-1, LANES), own_scores, leaf_rows)
     lambdas, near_lambdas = pair_terms(feat_count, bounds, pos, score_parts, worth, qid, inverse)
     bins_t, tiles, sums = leaf_terms(perm, bins, leaf_rows, near_lambdas)
 
@@ -503,19 +514,19 @@
 
     eighth = features // GROUP // 8
     edge = count // 8 * unit
-    arrived = swap(part(tiles, 6 * eighth, 8 * eighth, sums), query_masks[0])
-    block = part(tiles, 3 * eighth, 4 * eighth) + arrived[edge:2 * edge]
-    sums = sums + arrived[2 * edge:]
+    arrived = swap(part(tiles, 7 * eighth, 8 * eighth, sums), query_masks[0])
+    block = part(tiles, 3 * eighth, 4 * eighth) + arrived[:edge]
+    sums = sums + arrived[edge:]
     message, tiles = lax.optimization_barrier((join(block, sums), tiles))
     crossed_far = swap(message, query_masks[1])
-    block = part(tiles, 2 * eighth, 3 * eighth) + arrived[:edge]
-    message, tiles = lax.optimization_barrier((block, tiles))
-    crossed_near = swap(message, query_masks[1])
-    arrived = swap(part(tiles, 4 * eighth, 6 * eighth), query_masks[0])
-    block = part(tiles, eighth, 2 * eighth) + arrived[edge:] + crossed_far[:edge]
+    arrived = swap(part(tiles, 4 * eighth, 7 * eighth), query_masks[0])
+    block = part(tiles, eighth, 2 * eighth) + arrived[edge:2 * edge] + crossed_far[:edge]
     sums = sums + crossed_far[edge:]
     message, tiles = lax.optimization_barrier((join(block, sums), tiles))
     turned = swap(message, query_masks[2])
+    block = part(tiles, 2 * eighth, 3 * eighth) + arrived[2 * edge:]
+    message, tiles = lax.optimization_barrier((block, tiles))
+    crossed_near = swap(message, query_masks[1])
     kept = part(tiles, 0, eighth) + arrived[:edge] + crossed_near + turned[:edge]
     sums = sums + turned[edge:]
     for mask in query_masks[3:]:

time: 41.6 us -> 41.2 us (level)
  starting transfers between devices: 15.6 us -> 14.3 us
  Pallas kernels: 16.3 us -> 17.1 us
    ppermute x9, starting transfers between devices: 15.1 us -> 13.8 us  [swap(): return lax.ppermute(value, axes, [(p, p ^ mask) for p in range(count)])]
    pallas_call x1, Pallas kernels: 5.19 us -> 6.04 us  [pair_terms(): pl.pallas_call(functools.partial(pairs_kernel, feat_count), out_shape=(ja...]
  transfers between devices with their start and end apart: 10 -> 10, of which waited for: 6 -> 6; matrix products, arithmetic and copies ran while one was open for 0% -> 0% of each run, Pallas kernels for 16% -> 21%
where the time goes in v15:
time: 41.2 us; the launch traced here: 40.6 us
  Pallas kernels  17.1 us (42%)
  starting transfers between devices  14.3 us (35%)
  waiting for transfers between devices  6.86 us (17%)
  local copies, waits for them, and re-layouts  1.42 us (3%)
  between operations  0.8 us (2%)
    ppermute x9, starting transfers between devices, swap(): return lax.ppermute(value, axes, [(p, p ^ mask) for p in range(count)])  13.8 us
    pallas_call x6, Pallas kernels, histogram_part(): pl.pallas_call(functools.partial(histogram_kernel, first, groups), out_sh...  8.8 us
    ppermute x9, waiting for transfers between devices, swap(): return lax.ppermute(value, axes, [(p, p ^ mask) for p in range(count)])  6.85 us
    pallas_call x1, Pallas kernels, pair_terms(): pl.pallas_call(functools.partial(pairs_kernel, feat_count), out_shape=(ja...  6.04 us
    unnamed x12, local copies, waits for them, and re-layouts  1.41 us
    pallas_call x1, Pallas kernels, prepare(): pl.pallas_call(functools.partial(prepare_kernel, feat_count, masks), out_...  1.01 us
  transfers between devices with their start and end apart: 10, of which 6 were waited for; matrix products, arithmetic and copies ran while one was open for 0% of the time, Pallas kernels for 21%

profile of v15, /device:TPU:0, one launch (start us, length us, event | category | flops | bytes accessed | tf_op | source)
XLA Modules:
  0.0 40.6 jit_solution(12679891783549516720)
XLA Ops:
  0.6 0.5 %collective-permute-start = (f32[8,128]{1,0:T(8,128)}, f32[8,128]{1,0:T(8,128)S(1)}, u32[]{:S(2)}, u32[]{:S(2)}) collective-permute-start(f32[8,128]{1,0:T(8,128)} %bitcast.9), channel_id=1, source_target_pairs={{0,4},{1,2},{2,1},{3,7},{4,0},{5,6},{6,5},{7,3},{8,12},{9,10},{10,... | collective-permute-start | bytes 12296 | tf_op jit(solution)/shard_map/ppermute | solution.py:496
  1.2 4.1 %collective-permute-start.1 = (f32[8,128]{1,0:T(8,128)}, f32[8,128]{1,0:T(8,128)S(1)}, u32[]{:S(2)}, u32[]{:S(2)}) collective-permute-start(f32[8,128]{1,0:T(8,128)} %bitcast.10), channel_id=1, source_target_pairs={{0,1},{1,0},{2,3},{3,2},{4,5},{5,4},{6,7},{7,6},{8,9},{9,8},{10,11... | collective-permute-start | bytes 12296 | tf_op jit(solution)/shard_map/ppermute | solution.py:484
  5.3 0.7 %copy-done.3 = f32[1024]{0:T(1024)S(1)} copy-done((f32[1024]{0:T(1024)S(1)}, f32[1024]{0:T(1024)}, u32[]{:S(2)}) %copy-start.3) | copy-done | bytes 4120
  6.0 0.7 %copy-done.4 = s32[256]{0:T(256)S(1)} copy-done((s32[256]{0:T(256)S(1)}, s32[256]{0:T(256)}, u32[]{:S(2)}) %copy-start.4) | copy-done | bytes 1048
  6.7 1.0 %prepare.1 = (f32[8,128]{1,0:T(8,128)S(1)}, s32[8,128]{1,0:T(8,128)S(1)}, s32[32,128]{1,0:T(8,128)S(1)}, f32[32,128]{1,0:T(8,128)S(1)}, f32[1,1024]{1,0:T(1,128)...) custom-call(s32[1,16]{1,0:T(1,128)S(1)} %copy-done.5, s32[1]{0:T(128)} %bitcast.pos_ref, s32[32,128]{1,0:T(8,128)S(1)} %bitcast.7, ...), custom_call_target="tpu_custom_call" | custom-call | flops 2000000000 | bytes 300000 | tf_op jit(solution)/shard_map/prepare/pallas_call | solution.py:113
  7.7 0.0 collective-permute-done.refs_1_
  7.8 0.0 copy-start
  7.8 6.0 %pair_terms.1 = (f32[2,1024]{1,0:T(2,128)}, f32[2,1024]{1,0:T(2,128)S(1)}) custom-call(s32[8,128]{1,0:T(8,128)S(1)} %get-tuple-element.25.bounds_ref, s32[1]{0:T(128)} %bitcast.pos_ref, f32[8,128]{1,0:T(8,128)S(1)} %get-tuple-element.26.refs_0_, f32[8,128]{1,0:T(8,128)S(1)} %collective-permute-done.refs_1_, f32[8,128]{1,0:T(8,128)S(1)} %collective-permute-done.1.refs_2_, ...), custom_call_target="tpu_custom_call" | custom-call | flops 8999999488 | bytes 200000 | tf_op jit(solution)/shard_map/pair_terms/pallas_call | solution.py:285
  13.8 0.4 %leaf_terms.1 = (f32[256,1024]{1,0:T(8,128)S(1)}, bf16[32,1024]{1,0:T(8,128)(2,1)S(1)}, f32[8,256]{1,0:T(8,128)S(1)}) custom-call(bf16[256,256]{1,0:T(8,128)(2,1)S(1)} %get-tuple-element.32.perm_ref, s32[1024,256]{1,0:T(8,128)S(1)} %copy-done, s32[8,128]{1,0:T(8,128)S(1)} %get-tuple-element.31.leaf_ref, f32[2,1024]{1,0:T(2,128)S(1)} %get-tuple-element.33.lam_ref), custom_call_target="tpu_custom_call" | custom-call | flops 200000000 | bytes 3000000 | tf_op jit(solution)/shard_map/leaf_terms/pallas_call | solution.py:326
  14.2 1.1 %histogram_part.7 = f32[104,256]{1,0:T(8,128)S(1)} custom-call(bf16[32,1024]{1,0:T(8,128)(2,1)S(1)} %get-tuple-element.40.tile_ref, f32[256,1024]{1,0:T(8,128)S(1)} %get-tuple-element.35.bins_ref, f32[8,256]{1,0:T(8,128)S(1)} %get-tuple-element.36.refs_0_), custom_call_target="tpu_custom_call" | custom-call | flops 4000000 | bytes 4000 | tf_op jit(solution)/shard_map/histogram_part/pallas_call | solution.py:400
  15.3 0.1 collective-permute-start.2
  15.4 1.1 %histogram_part.6 = f32[96,256]{1,0:T(8,128)S(1)} custom-call(bf16[32,1024]{1,0:T(8,128)(2,1)S(1)} %get-tuple-element.40.tile_ref, f32[256,1024]{1,0:T(8,128)S(1)} %get-tuple-element.35.bins_ref), custom_call_target="tpu_custom_call" | custom-call | flops 4000000 | bytes 4000 | tf_op jit(solution)/shard_map/histogram_part/pallas_call | solution.py:400
  16.5 0.2 collective-permute-done.2
  16.7 3.3 %collective-permute-start.4 = (f32[104,256]{1,0:T(8,128)S(1)}, f32[104,256]{1,0:T(8,128)S(1)}, u32[]{:S(2)}, u32[]{:S(2)}) collective-permute-start(f32[104,256]{1,0:T(8,128)S(1)} %pad_maximum_fusion), channel_id=1, source_target_pairs={{0,8},{1,9},{2,10},{3,11},{4,12},{5,13},{6,14},{7,15},{8,0},{9,1},... | collective-permute-start | bytes 319496 | tf_op jit(solution)/shard_map/ppermute | solution.py:484
  20.1 3.3 %histogram_part.9 = f32[288,256]{1,0:T(8,128)S(1)} custom-call(bf16[32,1024]{1,0:T(8,128)(2,1)S(1)} %get-tuple-element.40.tile_ref, f32[256,1024]{1,0:T(8,128)S(1)} %get-tuple-element.35.bins_ref), custom_call_target="tpu_custom_call" | custom-call | flops 12000000 | bytes 12000 | tf_op jit(solution)/shard_map/histogram_part/pallas_call | solution.py:400
  23.4 0.1 collective-permute-start.3
  23.5 1.1 %histogram_part.8 = f32[96,256]{1,0:T(8,128)S(1)} custom-call(bf16[32,1024]{1,0:T(8,128)(2,1)S(1)} %get-tuple-element.40.tile_ref, f32[256,1024]{1,0:T(8,128)S(1)} %get-tuple-element.35.bins_ref), custom_call_target="tpu_custom_call" | custom-call | flops 4000000 | bytes 4000 | tf_op jit(solution)/shard_map/histogram_part/pallas_call | solution.py:400
  24.6 0.0 collective-permute-done.4
  24.6 0.4 collective-permute-done.3
  25.1 1.4 %collective-permute-start.6 = (f32[104,256]{1,0:T(8,128)S(1)}, f32[104,256]{1,0:T(8,128)S(1)}, u32[]{:S(2)}, u32[]{:S(2)}) collective-permute-start(f32[104,256]{1,0:T(8,128)S(1)} %pad_maximum_fusion.1), channel_id=1, source_target_pairs={{0,16},{1,17},{2,18},{3,19},{4,20},{5,21},{6,22},{7,23},{8,24},{9,... | collective-permute-start | bytes 319496 | tf_op jit(solution)/shard_map/ppermute | solution.py:484
  26.5 1.1 %histogram_part.10 = f32[96,256]{1,0:T(8,128)S(1)} custom-call(bf16[32,1024]{1,0:T(8,128)(2,1)S(1)} %get-tuple-element.40.tile_ref, f32[256,1024]{1,0:T(8,128)S(1)} %get-tuple-element.35.bins_ref), custom_call_target="tpu_custom_call" | custom-call | flops 4000000 | bytes 4000 | tf_op jit(solution)/shard_map/histogram_part/pallas_call | solution.py:400
  27.6 0.3 collective-permute-start.5
  27.9 1.1 %histogram_part.11 = f32[96,256]{1,0:T(8,128)S(1)} custom-call(bf16[32,1024]{1,0:T(8,128)(2,1)S(1)} %get-tuple-element.40.tile_ref, f32[256,1024]{1,0:T(8,128)S(1)} %get-tuple-element.35.bins_ref), custom_call_target="tpu_custom_call" | custom-call | flops 4000000 | bytes 4000 | tf_op jit(solution)/shard_map/histogram_part/pallas_call | solution.py:400
  29.0 3.3 %collective-permute-done.5 = f32[96,256]{1,0:T(8,128)S(1)} collective-permute-done((f32[96,256]{1,0:T(8,128)S(1)}, f32[96,256]{1,0:T(8,128)S(1)}, u32[]{:S(2)}, u32[]{:S(2)}) %collective-permute-start.5) | collective-permute-done | bytes 98336 | tf_op jit(solution)/shard_map/ppermute | solution.py:484
  32.3 0.0 collective-permute-done.6
  32.4 0.6 %collective-permute-start.7 = (f32[32,256]{1,0:T(8,128)S(1)}, f32[32,256]{1,0:T(8,128)S(1)}, u32[]{:S(2)}, u32[]{:S(2)}) collective-permute-start(f32[32,256]{1,0:T(8,128)S(1)} %get-tuple-element.52), channel_id=1, source_target_pairs={{0,3},{1,2},{2,1},{3,0},{4,7},{5,6},{6,5},{7,4},{8,11},{9,10},{10,... | collective-permute-start | bytes 98312 | tf_op jit(solution)/shard_map/ppermute | solution.py:484
  32.9 3.0 %collective-permute-start.8 = (f32[32,256]{1,0:T(8,128)S(1)}, f32[32,256]{1,0:T(8,128)S(1)}, u32[]{:S(2)}, u32[]{:S(2)}) collective-permute-start(f32[32,256]{1,0:T(8,128)S(1)} %get-tuple-element.51), channel_id=1, source_target_pairs={{0,2},{1,3},{2,0},{3,1},{4,6},{5,7},{6,4},{7,5},{8,10},{9,11},{10,... | collective-permute-start | bytes 98312 | tf_op jit(solution)/shard_map/ppermute | solution.py:484
  35.9 0.9 %collective-permute-start.9 = (f32[32,256]{1,0:T(8,128)S(1)}, f32[32,256]{1,0:T(8,128)S(1)}, u32[]{:S(2)}, u32[]{:S(2)}) collective-permute-start(f32[32,256]{1,0:T(8,128)S(1)} %get-tuple-element.50), channel_id=1, source_target_pairs={{0,1},{1,0},{2,3},{3,2},{4,5},{5,4},{6,7},{7,6},{8,9},{9,8},{10,11... | collective-permute-start | bytes 98312 | tf_op jit(solution)/shard_map/ppermute | solution.py:484
  36.8 1.4 %collective-permute-done.7.refs_0_ = f32[32,256]{1,0:T(8,128)S(1)} collective-permute-done((f32[32,256]{1,0:T(8,128)S(1)}, f32[32,256]{1,0:T(8,128)S(1)}, u32[]{:S(2)}, u32[]{:S(2)}) %collective-permute-start.7) | collective-permute-done | bytes 32800 | tf_op jit(solution)/shard_map/ppermute | solution.py:484
  38.2 0.2 collective-permute-done.8.refs_1_
  38.5 1.3 %collective-permute-done.9.refs_2_ = f32[32,256]{1,0:T(8,128)S(1)} collective-permute-done((f32[32,256]{1,0:T(8,128)S(1)}, f32[32,256]{1,0:T(8,128)S(1)}, u32[]{:S(2)}, u32[]{:S(2)}) %collective-permute-start.9) | collective-permute-done | bytes 32800 | tf_op jit(solution)/shard_map/ppermute | solution.py:484
  39.8 0.8 %finish.1 = (f32[8,128]{1,0:T(8,128)}, f32[8,128]{1,0:T(8,128)}, f32[3,2048]{1,0:T(4,128)}) custom-call(s32[8,128]{1,0:T(8,128)S(1)} %get-tuple-element.31.leaf_ref, f32[24,256]{1,0:T(8,128)S(1)} %get-tuple-element.49.kept_ref, f32[8,256]{1,0:T(8,128)S(1)} %slice_add_fusion.6.sums_ref, f32[32,256]{1,0:T(8,128)S(1)} %collective-permute-done.7.refs_0_, ...), custom_call_target="tpu_custom_call" | custom-call | tf_op jit(solution)/shard_map/finish/pallas_call | solution.py:449
  (21 shorter events, 0.1 us)
Async XLA Ops:
  0.6 4.7 %copy-start.1 = (s32[4096]{0:T(1024)S(1)}, s32[4096]{0:T(1024)}, u32[]{:S(2)}) copy-start(s32[4096]{0:T(1024)} %param.7) | copy-start | bytes 49156
  0.6 7.1 %collective-permute-start = (f32[8,128]{1,0:T(8,128)}, f32[8,128]{1,0:T(8,128)S(1)}, u32[]{:S(2)}, u32[]{:S(2)}) collective-permute-start(f32[8,128]{1,0:T(8,128)} %bitcast.9), channel_id=1, source_target_pairs={{0,4},{1,2},{2,1},{3,7},{4,0},{5,6},{6,5},{7,3},{8,12},{9,10},{10,... | collective-permute-start | bytes 12296 | tf_op jit(solution)/shard_map/ppermute | solution.py:496
  1.2 6.6 %collective-permute-start.1 = (f32[8,128]{1,0:T(8,128)}, f32[8,128]{1,0:T(8,128)S(1)}, u32[]{:S(2)}, u32[]{:S(2)}) collective-permute-start(f32[8,128]{1,0:T(8,128)} %bitcast.10), channel_id=1, source_target_pairs={{0,1},{1,0},{2,3},{3,2},{4,5},{5,4},{6,7},{7,6},{8,9},{9,8},{10,11... | collective-permute-start | bytes 12296 | tf_op jit(solution)/shard_map/ppermute | solution.py:484
  5.3 0.7 %copy-start.3 = (f32[1024]{0:T(1024)S(1)}, f32[1024]{0:T(1024)}, u32[]{:S(2)}) copy-start(f32[1024]{0:T(1024)} %param.6) | copy-start | bytes 12292
  5.3 0.7 %copy-start.2 = (s32[1024]{0:T(1024)S(1)}, s32[1024]{0:T(1024)}, u32[]{:S(2)}) copy-start(s32[1024]{0:T(1024)} %param.8) | copy-start | bytes 12292
  5.3 0.7 %copy-start.5 = (s32[1,16]{1,0:T(1,128)S(1)}, s32[1,16]{1,0:T(1,128)}, u32[]{:S(2)}) copy-start(s32[1,16]{1,0:T(1,128)} %len_ref.1) | copy-start | bytes 196
  6.0 0.7 %copy-start.4 = (s32[256]{0:T(256)S(1)}, s32[256]{0:T(256)}, u32[]{:S(2)}) copy-start(s32[256]{0:T(256)} %param.11) | copy-start | bytes 3076
  7.8 6.1 %copy-start = (s32[1024,256]{1,0:T(8,128)S(1)}, s32[1024,256]{1,0:T(8,128)}, u32[]{:S(2)}) copy-start(s32[1024,256]{1,0:T(8,128)} %bins_ref.1) | copy-start | bytes 3145732
  15.3 1.4 %collective-permute-start.2 = (f32[104,256]{1,0:T(8,128)S(1)}, f32[104,256]{1,0:T(8,128)S(1)}, u32[]{:S(2)}, u32[]{:S(2)}) collective-permute-start(f32[104,256]{1,0:T(8,128)S(1)} %histogram_part.7), channel_id=1, source_target_pairs={{0,4},{1,5},{2,6},{3,7},{4,0},{5,1},{6,2},{7,3},{8,12},{9,13},{10,... | collective-permute-start | bytes 319496 | tf_op jit(solution)/shard_map/ppermute | solution.py:484
  16.7 7.9 %collective-permute-start.4 = (f32[104,256]{1,0:T(8,128)S(1)}, f32[104,256]{1,0:T(8,128)S(1)}, u32[]{:S(2)}, u32[]{:S(2)}) collective-permute-start(f32[104,256]{1,0:T(8,128)S(1)} %pad_maximum_fusion), channel_id=1, source_target_pairs={{0,8},{1,9},{2,10},{3,11},{4,12},{5,13},{6,14},{7,15},{8,0},{9,1},... | collective-permute-start | bytes 319496 | tf_op jit(solution)/shard_map/ppermute | solution.py:484
  23.4 1.6 %collective-permute-start.3 = (f32[288,256]{1,0:T(8,128)S(1)}, f32[288,256]{1,0:T(8,128)S(1)}, u32[]{:S(2)}, u32[]{:S(2)}) collective-permute-start(f32[288,256]{1,0:T(8,128)S(1)} %histogram_part.9), channel_id=1, source_target_pairs={{0,4},{1,5},{2,6},{3,7},{4,0},{5,1},{6,2},{7,3},{8,12},{9,13},{10,... | collective-permute-start | bytes 884744 | tf_op jit(solution)/shard_map/ppermute | solution.py:484
  25.1 7.2 %collective-permute-start.6 = (f32[104,256]{1,0:T(8,128)S(1)}, f32[104,256]{1,0:T(8,128)S(1)}, u32[]{:S(2)}, u32[]{:S(2)}) collective-permute-start(f32[104,256]{1,0:T(8,128)S(1)} %pad_maximum_fusion.1), channel_id=1, source_target_pairs={{0,16},{1,17},{2,18},{3,19},{4,20},{5,21},{6,22},{7,23},{8,24},{9,... | collective-permute-start | bytes 319496 | tf_op jit(solution)/shard_map/ppermute | solution.py:484
  27.6 4.7 %collective-permute-start.5 = (f32[96,256]{1,0:T(8,128)S(1)}, f32[96,256]{1,0:T(8,128)S(1)}, u32[]{:S(2)}, u32[]{:S(2)}) collective-permute-start(f32[96,256]{1,0:T(8,128)S(1)} %slice_add_fusion.2), channel_id=1, source_target_pairs={{0,8},{1,9},{2,10},{3,11},{4,12},{5,13},{6,14},{7,15},{8,0},{9,1},... | collective-permute-start | bytes 294920 | tf_op jit(solution)/shard_map/ppermute | solution.py:484
  32.4 5.9 %collective-permute-start.7 = (f32[32,256]{1,0:T(8,128)S(1)}, f32[32,256]{1,0:T(8,128)S(1)}, u32[]{:S(2)}, u32[]{:S(2)}) collective-permute-start(f32[32,256]{1,0:T(8,128)S(1)} %get-tuple-element.52), channel_id=1, source_target_pairs={{0,3},{1,2},{2,1},{3,0},{4,7},{5,6},{6,5},{7,4},{8,11},{9,10},{10,... | collective-permute-start | bytes 98312 | tf_op jit(solution)/shard_map/ppermute | solution.py:484
  32.9 5.6 %collective-permute-start.8 = (f32[32,256]{1,0:T(8,128)S(1)}, f32[32,256]{1,0:T(8,128)S(1)}, u32[]{:S(2)}, u32[]{:S(2)}) collective-permute-start(f32[32,256]{1,0:T(8,128)S(1)} %get-tuple-element.51), channel_id=1, source_target_pairs={{0,2},{1,3},{2,0},{3,1},{4,6},{5,7},{6,4},{7,5},{8,10},{9,11},{10,... | collective-permute-start | bytes 98312 | tf_op jit(solution)/shard_map/ppermute | solution.py:484
  35.9 3.9 %collective-permute-start.9 = (f32[32,256]{1,0:T(8,128)S(1)}, f32[32,256]{1,0:T(8,128)S(1)}, u32[]{:S(2)}, u32[]{:S(2)}) collective-permute-start(f32[32,256]{1,0:T(8,128)S(1)} %get-tuple-element.50), channel_id=1, source_target_pairs={{0,1},{1,0},{2,3},{3,2},{4,5},{5,4},{6,7},{7,6},{8,9},{9,8},{10,11... | collective-permute-start | bytes 98312 | tf_op jit(solution)/shard_map/ppermute | solution.py:484

commit v16 on v15

--- a/solution.py
+++ b/solution.py
@@ -519,15 +519,15 @@
     sums = sums + arrived[edge:]
     message, tiles = lax.optimization_barrier((join(block, sums), tiles))
     crossed_far = swap(message, query_masks[1])
-    arrived = swap(part(tiles, 4 * eighth, 7 * eighth), query_masks[0])
-    block = part(tiles, eighth, 2 * eighth) + arrived[edge:2 * edge] + crossed_far[:edge]
+    arrived = swap(part(tiles, 5 * eighth, 7 * eighth), query_masks[0])
+    both = part(tiles, eighth, 3 * eighth) + arrived
     sums = sums + crossed_far[edge:]
-    message, tiles = lax.optimization_barrier((join(block, sums), tiles))
+    message, rest, tiles = lax.optimization_barrier(
+        (join(both[:edge] + crossed_far[:edge], sums), join(both[edge:], sums), tiles))
     turned = swap(message, query_masks[2])
-    block = part(tiles, 2 * eighth, 3 * eighth) + arrived[2 * edge:]
-    message, tiles = lax.optimization_barrier((block, tiles))
-    crossed_near = swap(message, query_masks[1])
-    kept = part(tiles, 0, eighth) + arrived[:edge] + crossed_near + turned[:edge]
+    crossed_near = swap(rest, query_masks[1])
+    arrived = swap(part(tiles, 4 * eighth, 5 * eighth), query_masks[0])
+    kept = part(tiles, 0, eighth) + arrived + crossed_near[:edge] + turned[:edge]
     sums = sums + turned[edge:]
     for mask in query_masks[3:]:
         edge = edge // 2

time: 41.2 us -> 40.9 us (level); the launches traced: 40.6 us -> 41.6 us
  Pallas kernels: 17.1 us -> 18.1 us
  waiting for transfers between devices: 6.86 us -> 6.4 us
    pallas_call x1, Pallas kernels: 6.04 us -> 7.06 us  [pair_terms(): pl.pallas_call(functools.partial(pairs_kernel, feat_count), out_shape=(ja...]
    ppermute x9 -> x10, waiting for transfers between devices: 6.85 us -> 6.39 us  [swap(): return lax.ppermute(value, axes, [(p, p ^ mask) for p in range(count)])]
    ppermute x9 -> x10, starting transfers between devices: 13.8 us -> 14.2 us  [swap(): return lax.ppermute(value, axes, [(p, p ^ mask) for p in range(count)])]
  transfers between devices with their start and end apart: 10 -> 11, of which waited for: 6 -> 6; matrix products, arithmetic and copies ran while one was open for 0% -> 0% of each run, Pallas kernels for 21% -> 21%
where the time goes in v16:
time: 40.9 us; the launch traced here: 41.6 us
  Pallas kernels  18.1 us (44%)
  starting transfers between devices  14.7 us (36%)
  waiting for transfers between devices  6.4 us (16%)
  local copies, waits for them, and re-layouts  1.42 us (3%)
  between operations  0.8 us (2%)
    ppermute x10, starting transfers between devices, swap(): return lax.ppermute(value, axes, [(p, p ^ mask) for p in range(count)])  14.2 us
    pallas_call x6, Pallas kernels, histogram_part(): pl.pallas_call(functools.partial(histogram_kernel, first, groups), out_sh...  8.84 us
    pallas_call x1, Pallas kernels, pair_terms(): pl.pallas_call(functools.partial(pairs_kernel, feat_count), out_shape=(ja...  7.06 us
    ppermute x10, waiting for transfers between devices, swap(): return lax.ppermute(value, axes, [(p, p ^ mask) for p in range(count)])  6.39 us
    unnamed x12, local copies, waits for them, and re-layouts  1.41 us
    pallas_call x1, Pallas kernels, prepare(): pl.pallas_call(functools.partial(prepare_kernel, feat_count, masks), out_...  1.01 us
  transfers between devices with their start and end apart: 11, of which 6 were waited for; matrix products, arithmetic and copies ran while one was open for 0% of the time, Pallas kernels for 21%

profile of v16, /device:TPU:0, one launch (start us, length us, event | category | flops | bytes accessed | tf_op | source)
XLA Modules:
  0.0 41.6 jit_solution(10302529649562351362)
XLA Ops:
  0.6 0.5 %collective-permute-start = (f32[8,128]{1,0:T(8,128)}, f32[8,128]{1,0:T(8,128)S(1)}, u32[]{:S(2)}, u32[]{:S(2)}) collective-permute-start(f32[8,128]{1,0:T(8,128)} %bitcast.9), channel_id=1, source_target_pairs={{0,4},{1,2},{2,1},{3,7},{4,0},{5,6},{6,5},{7,3},{8,12},{9,10},{10,... | collective-permute-start | bytes 12296 | tf_op jit(solution)/shard_map/ppermute | solution.py:496
  1.2 4.1 %collective-permute-start.1 = (f32[8,128]{1,0:T(8,128)}, f32[8,128]{1,0:T(8,128)S(1)}, u32[]{:S(2)}, u32[]{:S(2)}) collective-permute-start(f32[8,128]{1,0:T(8,128)} %bitcast.10), channel_id=1, source_target_pairs={{0,1},{1,0},{2,3},{3,2},{4,5},{5,4},{6,7},{7,6},{8,9},{9,8},{10,11... | collective-permute-start | bytes 12296 | tf_op jit(solution)/shard_map/ppermute | solution.py:484
  5.3 0.7 %copy-done.3 = f32[1024]{0:T(1024)S(1)} copy-done((f32[1024]{0:T(1024)S(1)}, f32[1024]{0:T(1024)}, u32[]{:S(2)}) %copy-start.3) | copy-done | bytes 4120
  6.0 0.7 %copy-done.4 = s32[256]{0:T(256)S(1)} copy-done((s32[256]{0:T(256)S(1)}, s32[256]{0:T(256)}, u32[]{:S(2)}) %copy-start.4) | copy-done | bytes 1048
  6.7 1.0 %prepare.1 = (f32[8,128]{1,0:T(8,128)S(1)}, s32[8,128]{1,0:T(8,128)S(1)}, s32[32,128]{1,0:T(8,128)S(1)}, f32[32,128]{1,0:T(8,128)S(1)}, f32[1,1024]{1,0:T(1,128)...) custom-call(s32[1,16]{1,0:T(1,128)S(1)} %copy-done.5, s32[1]{0:T(128)} %bitcast.pos_ref, s32[32,128]{1,0:T(8,128)S(1)} %bitcast.7, ...), custom_call_target="tpu_custom_call" | custom-call | flops 2000000000 | bytes 300000 | tf_op jit(solution)/shard_map/prepare/pallas_call | solution.py:113
  7.7 0.0 collective-permute-done.1.refs_2_
  7.8 0.0 copy-start
  7.8 7.1 %pair_terms.1 = (f32[2,1024]{1,0:T(2,128)}, f32[2,1024]{1,0:T(2,128)S(1)}) custom-call(s32[8,128]{1,0:T(8,128)S(1)} %get-tuple-element.24.bounds_ref, s32[1]{0:T(128)} %bitcast.pos_ref, f32[8,128]{1,0:T(8,128)S(1)} %get-tuple-element.25.refs_0_, f32[8,128]{1,0:T(8,128)S(1)} %collective-permute-done.refs_1_, f32[8,128]{1,0:T(8,128)S(1)} %collective-permute-done.1.refs_2_, ...), custom_call_target="tpu_custom_call" | custom-call | flops 8999999488 | bytes 200000 | tf_op jit(solution)/shard_map/pair_terms/pallas_call | solution.py:285
  14.8 0.4 %leaf_terms.1 = (f32[256,1024]{1,0:T(8,128)S(1)}, bf16[32,1024]{1,0:T(8,128)(2,1)S(1)}, f32[8,256]{1,0:T(8,128)S(1)}) custom-call(bf16[256,256]{1,0:T(8,128)(2,1)S(1)} %get-tuple-element.31.perm_ref, s32[1024,256]{1,0:T(8,128)S(1)} %copy-done, s32[8,128]{1,0:T(8,128)S(1)} %get-tuple-element.30.leaf_ref, f32[2,1024]{1,0:T(2,128)S(1)} %get-tuple-element.32.lam_ref), custom_call_target="tpu_custom_call" | custom-call | flops 200000000 | bytes 3000000 | tf_op jit(solution)/shard_map/leaf_terms/pallas_call | solution.py:326
  15.3 1.1 %histogram_part.7 = f32[104,256]{1,0:T(8,128)S(1)} custom-call(bf16[32,1024]{1,0:T(8,128)(2,1)S(1)} %get-tuple-element.38.tile_ref, f32[256,1024]{1,0:T(8,128)S(1)} %get-tuple-element.34.bins_ref, f32[8,256]{1,0:T(8,128)S(1)} %get-tuple-element.35.refs_0_), custom_call_target="tpu_custom_call" | custom-call | flops 4000000 | bytes 4000 | tf_op jit(solution)/shard_map/histogram_part/pallas_call | solution.py:400
  16.4 0.1 collective-permute-start.2
  16.4 1.1 %histogram_part.6 = f32[96,256]{1,0:T(8,128)S(1)} custom-call(bf16[32,1024]{1,0:T(8,128)(2,1)S(1)} %get-tuple-element.38.tile_ref, f32[256,1024]{1,0:T(8,128)S(1)} %get-tuple-element.34.bins_ref), custom_call_target="tpu_custom_call" | custom-call | flops 4000000 | bytes 4000 | tf_op jit(solution)/shard_map/histogram_part/pallas_call | solution.py:400
  17.6 0.2 collective-permute-done.2
  17.8 0.7 %collective-permute-start.4 = (f32[104,256]{1,0:T(8,128)S(1)}, f32[104,256]{1,0:T(8,128)S(1)}, u32[]{:S(2)}, u32[]{:S(2)}) collective-permute-start(f32[104,256]{1,0:T(8,128)S(1)} %pad_maximum_fusion.2), channel_id=1, source_target_pairs={{0,8},{1,9},{2,10},{3,11},{4,12},{5,13},{6,14},{7,15},{8,0},{9,1},... | collective-permute-start | bytes 319496 | tf_op jit(solution)/shard_map/ppermute | solution.py:484
  18.5 2.2 %histogram_part.9 = f32[192,256]{1,0:T(8,128)S(1)} custom-call(bf16[32,1024]{1,0:T(8,128)(2,1)S(1)} %get-tuple-element.38.tile_ref, f32[256,1024]{1,0:T(8,128)S(1)} %get-tuple-element.34.bins_ref), custom_call_target="tpu_custom_call" | custom-call | flops 8000000 | bytes 8000 | tf_op jit(solution)/shard_map/histogram_part/pallas_call | solution.py:400
  20.7 0.1 collective-permute-start.3
  20.8 2.2 %histogram_part.8 = f32[192,256]{1,0:T(8,128)S(1)} custom-call(bf16[32,1024]{1,0:T(8,128)(2,1)S(1)} %get-tuple-element.38.tile_ref, f32[256,1024]{1,0:T(8,128)S(1)} %get-tuple-element.34.bins_ref), custom_call_target="tpu_custom_call" | custom-call | flops 8000000 | bytes 8000 | tf_op jit(solution)/shard_map/histogram_part/pallas_call | solution.py:400
  23.0 0.0 collective-permute-done.4
  23.1 0.0 collective-permute-done.3
  23.1 0.7 %collective-permute-start.7 = (f32[104,256]{1,0:T(8,128)S(1)}, f32[104,256]{1,0:T(8,128)S(1)}, u32[]{:S(2)}, u32[]{:S(2)}) collective-permute-start(f32[104,256]{1,0:T(8,128)S(1)} %get-tuple-element.40), channel_id=1, source_target_pairs={{0,16},{1,17},{2,18},{3,19},{4,20},{5,21},{6,22},{7,23},{8,24},{9,... | collective-permute-start | bytes 319496 | tf_op jit(solution)/shard_map/ppermute | solution.py:484
  23.8 1.4 %collective-permute-start.6 = (f32[104,256]{1,0:T(8,128)S(1)}, f32[104,256]{1,0:T(8,128)S(1)}, u32[]{:S(2)}, u32[]{:S(2)}) collective-permute-start(f32[104,256]{1,0:T(8,128)S(1)} %get-tuple-element.39), channel_id=1, source_target_pairs={{0,8},{1,9},{2,10},{3,11},{4,12},{5,13},{6,14},{7,15},{8,0},{9,1},... | collective-permute-start | bytes 319496 | tf_op jit(solution)/shard_map/ppermute | solution.py:484
  25.2 1.1 %histogram_part.11 = f32[96,256]{1,0:T(8,128)S(1)} custom-call(bf16[32,1024]{1,0:T(8,128)(2,1)S(1)} %get-tuple-element.38.tile_ref, f32[256,1024]{1,0:T(8,128)S(1)} %get-tuple-element.34.bins_ref), custom_call_target="tpu_custom_call" | custom-call | flops 4000000 | bytes 4000 | tf_op jit(solution)/shard_map/histogram_part/pallas_call | solution.py:400
  26.3 0.1 collective-permute-start.5
  26.4 1.1 %histogram_part.10 = f32[96,256]{1,0:T(8,128)S(1)} custom-call(bf16[32,1024]{1,0:T(8,128)(2,1)S(1)} %get-tuple-element.38.tile_ref, f32[256,1024]{1,0:T(8,128)S(1)} %get-tuple-element.34.bins_ref), custom_call_target="tpu_custom_call" | custom-call | flops 4000000 | bytes 4000 | tf_op jit(solution)/shard_map/histogram_part/pallas_call | solution.py:400
  27.5 0.2 collective-permute-done.5
  27.7 0.9 %collective-permute-done.7 = f32[104,256]{1,0:T(8,128)S(1)} collective-permute-done((f32[104,256]{1,0:T(8,128)S(1)}, f32[104,256]{1,0:T(8,128)S(1)}, u32[]{:S(2)}, u32[]{:S(2)}) %collective-permute-start.7) | collective-permute-done | bytes 106528 | tf_op jit(solution)/shard_map/ppermute | solution.py:484
  28.6 0.3 collective-permute-done.6
  28.9 3.3 %collective-permute-start.10 = (f32[32,256]{1,0:T(8,128)S(1)}, f32[32,256]{1,0:T(8,128)S(1)}, u32[]{:S(2)}, u32[]{:S(2)}) collective-permute-start(f32[32,256]{1,0:T(8,128)S(1)} %get-tuple-element.50), channel_id=1, source_target_pairs={{0,1},{1,0},{2,3},{3,2},{4,5},{5,4},{6,7},{7,6},{8,9},{9,8},{10,11... | collective-permute-start | bytes 98312 | tf_op jit(solution)/shard_map/ppermute | solution.py:484
  32.3 3.7 %collective-permute-start.8 = (f32[32,256]{1,0:T(8,128)S(1)}, f32[32,256]{1,0:T(8,128)S(1)}, u32[]{:S(2)}, u32[]{:S(2)}) collective-permute-start(f32[32,256]{1,0:T(8,128)S(1)} %get-tuple-element.52), channel_id=1, source_target_pairs={{0,3},{1,2},{2,1},{3,0},{4,7},{5,6},{6,5},{7,4},{8,11},{9,10},{10,... | collective-permute-start | bytes 98312 | tf_op jit(solution)/shard_map/ppermute | solution.py:484
  36.0 2.2 %collective-permute-done.8.refs_0_ = f32[32,256]{1,0:T(8,128)S(1)} collective-permute-done((f32[32,256]{1,0:T(8,128)S(1)}, f32[32,256]{1,0:T(8,128)S(1)}, u32[]{:S(2)}, u32[]{:S(2)}) %collective-permute-start.8) | collective-permute-done | bytes 32800 | tf_op jit(solution)/shard_map/ppermute | solution.py:484
  38.3 2.6 %collective-permute-done.9.refs_1_ = f32[32,256]{1,0:T(8,128)S(1)} collective-permute-done((f32[32,256]{1,0:T(8,128)S(1)}, f32[32,256]{1,0:T(8,128)S(1)}, u32[]{:S(2)}, u32[]{:S(2)}) %collective-permute-start.9) | collective-permute-done | bytes 32800 | tf_op jit(solution)/shard_map/ppermute | solution.py:484
  40.8 0.8 %finish.1 = (f32[8,128]{1,0:T(8,128)}, f32[8,128]{1,0:T(8,128)}, f32[3,2048]{1,0:T(4,128)}) custom-call(s32[8,128]{1,0:T(8,128)S(1)} %get-tuple-element.30.leaf_ref, f32[24,256]{1,0:T(8,128)S(1)} %get-tuple-element.49.kept_ref, f32[8,256]{1,0:T(8,128)S(1)} %slice_add_fusion.4.sums_ref, f32[32,256]{1,0:T(8,128)S(1)} %collective-permute-done.8.refs_0_, ...), custom_call_target="tpu_custom_call" | custom-call | tf_op jit(solution)/shard_map/finish/pallas_call | solution.py:449
  (23 shorter events, 0.2 us)
Async XLA Ops:
  0.6 4.7 %copy-start.1 = (s32[4096]{0:T(1024)S(1)}, s32[4096]{0:T(1024)}, u32[]{:S(2)}) copy-start(s32[4096]{0:T(1024)} %param.7) | copy-start | bytes 49156
  0.6 7.1 %collective-permute-start = (f32[8,128]{1,0:T(8,128)}, f32[8,128]{1,0:T(8,128)S(1)}, u32[]{:S(2)}, u32[]{:S(2)}) collective-permute-start(f32[8,128]{1,0:T(8,128)} %bitcast.9), channel_id=1, source_target_pairs={{0,4},{1,2},{2,1},{3,7},{4,0},{5,6},{6,5},{7,3},{8,12},{9,10},{10,... | collective-permute-start | bytes 12296 | tf_op jit(solution)/shard_map/ppermute | solution.py:496
  1.2 6.6 %collective-permute-start.1 = (f32[8,128]{1,0:T(8,128)}, f32[8,128]{1,0:T(8,128)S(1)}, u32[]{:S(2)}, u32[]{:S(2)}) collective-permute-start(f32[8,128]{1,0:T(8,128)} %bitcast.10), channel_id=1, source_target_pairs={{0,1},{1,0},{2,3},{3,2},{4,5},{5,4},{6,7},{7,6},{8,9},{9,8},{10,11... | collective-permute-start | bytes 12296 | tf_op jit(solution)/shard_map/ppermute | solution.py:484
  5.3 0.7 %copy-start.3 = (f32[1024]{0:T(1024)S(1)}, f32[1024]{0:T(1024)}, u32[]{:S(2)}) copy-start(f32[1024]{0:T(1024)} %param.6) | copy-start | bytes 12292
  5.3 0.7 %copy-start.2 = (s32[1024]{0:T(1024)S(1)}, s32[1024]{0:T(1024)}, u32[]{:S(2)}) copy-start(s32[1024]{0:T(1024)} %param.8) | copy-start | bytes 12292
  5.3 0.7 %copy-start.5 = (s32[1,16]{1,0:T(1,128)S(1)}, s32[1,16]{1,0:T(1,128)}, u32[]{:S(2)}) copy-start(s32[1,16]{1,0:T(1,128)} %len_ref.1) | copy-start | bytes 196
  6.0 0.7 %copy-start.4 = (s32[256]{0:T(256)S(1)}, s32[256]{0:T(256)}, u32[]{:S(2)}) copy-start(s32[256]{0:T(256)} %param.11) | copy-start | bytes 3076
  7.8 7.1 %copy-start = (s32[1024,256]{1,0:T(8,128)S(1)}, s32[1024,256]{1,0:T(8,128)}, u32[]{:S(2)}) copy-start(s32[1024,256]{1,0:T(8,128)} %bins_ref.1) | copy-start | bytes 3145732
  16.4 1.4 %collective-permute-start.2 = (f32[104,256]{1,0:T(8,128)S(1)}, f32[104,256]{1,0:T(8,128)S(1)}, u32[]{:S(2)}, u32[]{:S(2)}) collective-permute-start(f32[104,256]{1,0:T(8,128)S(1)} %histogram_part.7), channel_id=1, source_target_pairs={{0,4},{1,5},{2,6},{3,7},{4,0},{5,1},{6,2},{7,3},{8,12},{9,13},{10,... | collective-permute-start | bytes 319496 | tf_op jit(solution)/shard_map/ppermute | solution.py:484
  17.8 5.3 %collective-permute-start.4 = (f32[104,256]{1,0:T(8,128)S(1)}, f32[104,256]{1,0:T(8,128)S(1)}, u32[]{:S(2)}, u32[]{:S(2)}) collective-permute-start(f32[104,256]{1,0:T(8,128)S(1)} %pad_maximum_fusion.2), channel_id=1, source_target_pairs={{0,8},{1,9},{2,10},{3,11},{4,12},{5,13},{6,14},{7,15},{8,0},{9,1},... | collective-permute-start | bytes 319496 | tf_op jit(solution)/shard_map/ppermute | solution.py:484
  20.7 2.3 %collective-permute-start.3 = (f32[192,256]{1,0:T(8,128)S(1)}, f32[192,256]{1,0:T(8,128)S(1)}, u32[]{:S(2)}, u32[]{:S(2)}) collective-permute-start(f32[192,256]{1,0:T(8,128)S(1)} %histogram_part.9), channel_id=1, source_target_pairs={{0,4},{1,5},{2,6},{3,7},{4,0},{5,1},{6,2},{7,3},{8,12},{9,13},{10,... | collective-permute-start | bytes 589832 | tf_op jit(solution)/shard_map/ppermute | solution.py:484
  23.1 5.4 %collective-permute-start.7 = (f32[104,256]{1,0:T(8,128)S(1)}, f32[104,256]{1,0:T(8,128)S(1)}, u32[]{:S(2)}, u32[]{:S(2)}) collective-permute-start(f32[104,256]{1,0:T(8,128)S(1)} %get-tuple-element.40), channel_id=1, source_target_pairs={{0,16},{1,17},{2,18},{3,19},{4,20},{5,21},{6,22},{7,23},{8,24},{9,... | collective-permute-start | bytes 319496 | tf_op jit(solution)/shard_map/ppermute | solution.py:484
  23.8 5.1 %collective-permute-start.6 = (f32[104,256]{1,0:T(8,128)S(1)}, f32[104,256]{1,0:T(8,128)S(1)}, u32[]{:S(2)}, u32[]{:S(2)}) collective-permute-start(f32[104,256]{1,0:T(8,128)S(1)} %get-tuple-element.39), channel_id=1, source_target_pairs={{0,8},{1,9},{2,10},{3,11},{4,12},{5,13},{6,14},{7,15},{8,0},{9,1},... | collective-permute-start | bytes 319496 | tf_op jit(solution)/shard_map/ppermute | solution.py:484
  26.3 1.4 %collective-permute-start.5 = (f32[96,256]{1,0:T(8,128)S(1)}, f32[96,256]{1,0:T(8,128)S(1)}, u32[]{:S(2)}, u32[]{:S(2)}) collective-permute-start(f32[96,256]{1,0:T(8,128)S(1)} %histogram_part.11), channel_id=1, source_target_pairs={{0,4},{1,5},{2,6},{3,7},{4,0},{5,1},{6,2},{7,3},{8,12},{9,13},{10,... | collective-permute-start | bytes 294920 | tf_op jit(solution)/shard_map/ppermute | solution.py:484
  28.9 7.1 %collective-permute-start.10 = (f32[32,256]{1,0:T(8,128)S(1)}, f32[32,256]{1,0:T(8,128)S(1)}, u32[]{:S(2)}, u32[]{:S(2)}) collective-permute-start(f32[32,256]{1,0:T(8,128)S(1)} %get-tuple-element.50), channel_id=1, source_target_pairs={{0,1},{1,0},{2,3},{3,2},{4,5},{5,4},{6,7},{7,6},{8,9},{9,8},{10,11... | collective-permute-start | bytes 98312 | tf_op jit(solution)/shard_map/ppermute | solution.py:484
  32.3 6.0 %collective-permute-start.8 = (f32[32,256]{1,0:T(8,128)S(1)}, f32[32,256]{1,0:T(8,128)S(1)}, u32[]{:S(2)}, u32[]{:S(2)}) collective-permute-start(f32[32,256]{1,0:T(8,128)S(1)} %get-tuple-element.52), channel_id=1, source_target_pairs={{0,3},{1,2},{2,1},{3,0},{4,7},{5,6},{6,5},{7,4},{8,11},{9,10},{10,... | collective-permute-start | bytes 98312 | tf_op jit(solution)/shard_map/ppermute | solution.py:484
  36.0 4.8 %collective-permute-start.9 = (f32[32,256]{1,0:T(8,128)S(1)}, f32[32,256]{1,0:T(8,128)S(1)}, u32[]{:S(2)}, u32[]{:S(2)}) collective-permute-start(f32[32,256]{1,0:T(8,128)S(1)} %get-tuple-element.51), channel_id=1, source_target_pairs={{0,2},{1,3},{2,0},{3,1},{4,6},{5,7},{6,4},{7,5},{8,10},{9,11},{10,... | collective-permute-start | bytes 98312 | tf_op jit(solution)/shard_map/ppermute | solution.py:484

commit v17 on v16

--- a/solution.py
+++ b/solution.py
@@ -198,7 +198,8 @@
                     hit = test(other, g, u)
                     if masked:
                         hit = hit & (q_col[pl.ds(base + 8 * u, 8), :] == query[g])
-                    acc[2 * g + u % 2] = acc[2 * g + u % 2] + jnp.where(hit, 1.0, 0.0)
+                    k = 4 * g + u % 4
+                    acc[k] = acc[k] + jnp.where(hit, 1.0, 0.0)
             return tuple(acc)
 
         def ahead(other, g, u):
@@ -215,17 +216,24 @@
                 return (other > score[g]) | ((other == score[g]) & earlier)
             return test
 
-        acc = tuple(jnp.zeros((8, LANES), F32) for _ in range(4))
+        def twice(low, high, test, acc):
+            twos = (high - low) // 2
+            acc = lax.fori_loop(0, twos, lambda k, acc: gather(
+                low + 2 * k + 1, gather(low + 2 * k, acc, False, test), False, test), acc)
+            return lax.fori_loop(low + 2 * twos, high, lambda c, acc: gather(c, acc, False, test), acc)
+
+        acc = tuple(jnp.zeros((8, LANES), F32) for _ in range(8))
         low, inner_low, inner_high, high = spans(r)
         after = jnp.maximum(inner_high, r + 2)
         acc = lax.fori_loop(low, inner_low, lambda c, acc: gather(c, acc, True, ahead), acc)
-        acc = lax.fori_loop(inner_low, r, lambda c, acc: gather(c, acc, False, ahead), acc)
-        acc = lax.fori_loop(r + 2, after, lambda c, acc: gather(c, acc, False, behind), acc)
+        acc = twice(inner_low, r, ahead, acc)
+        acc = twice(r + 2, after, behind, acc)
         acc = lax.fori_loop(after, high, lambda c, acc: gather(c, acc, True, behind), acc)
         for mine in range(2):
             acc = gather(r + mine, acc, True, within(mine))
         for g in range(2):
-            d_row[pl.ds(r + g, 1), :] = jnp.sum(acc[2 * g] + acc[2 * g + 1], axis=0, keepdims=True)
+            total = (acc[4 * g] + acc[4 * g + 1]) + (acc[4 * g + 2] + acc[4 * g + 3])
+            d_row[pl.ds(r + g, 1), :] = jnp.sum(total, axis=0, keepdims=True)
         return carry
 
     lax.fori_loop(0, (window_high - window_low) // 2, rank_groups, 0)
@@ -409,7 +417,7 @@
 
 
 def finish_kernel(per_dev, leaf_ref, kept_ref, sums_ref, *refs):
-    arrived = refs[:-3][::-1]
+    arrived = list(refs[1::-1]) + list(refs[2:-3])
     value_ref, step_ref, hist_ref = refs[-3:]
     unit = kept_ref.shape[0]
     totals = add_up([sums_ref[...]] + [ref[unit:, :] for ref in arrived])
@@ -535,7 +543,8 @@
         kept = kept[:edge] + arrived[:edge]
         sums = sums + arrived[edge:]
     arrived = [swap(join(kept[m * unit:(m + 1) * unit], sums), m) for m in range(1, feat_count)]
-    values, step, histograms = finish(per_dev, leaf_rows, kept[:unit], sums, arrived[::-1])
+    arrived[:2] = arrived[1::-1]
+    values, step, histograms = finish(per_dev, leaf_rows, kept[:unit], sums, arrived)
     return lambdas, values.reshape(LEAVES), step.reshape(docs), histograms.reshape(3, per_dev * BINS)
 
 

time: 40.9 us -> 39.6 us (0.968); the launches traced: 41.6 us -> 38.8 us
  starting transfers between devices: 14.7 us -> 13.1 us
  waiting for transfers between devices: 6.4 us -> 5.48 us
    ppermute x10, starting transfers between devices: 14.2 us -> 12.6 us  [swap(): return lax.ppermute(value, axes, [(p, p ^ mask) for p in range(count)])]
    ppermute x10, waiting for transfers between devices: 6.39 us -> 5.47 us  [swap(): return lax.ppermute(value, axes, [(p, p ^ mask) for p in range(count)])]
  transfers between devices with their start and end apart: 11 -> 11, of which waited for: 6 -> 7; matrix products, arithmetic and copies ran while one was open for 0% -> 0% of each run, Pallas kernels for 21% -> 22%
where the time goes in v17:
time: 39.6 us; the launch traced here: 38.8 us
  Pallas kernels  17.9 us (45%)
  starting transfers between devices  13.1 us (33%)
  waiting for transfers between devices  5.48 us (14%)
  local copies, waits for them, and re-layouts  1.42 us (4%)
  between operations  0.79 us (2%)
    ppermute x10, starting transfers between devices, swap(): return lax.ppermute(value, axes, [(p, p ^ mask) for p in range(count)])  12.6 us
    pallas_call x6, Pallas kernels, histogram_part(): pl.pallas_call(functools.partial(histogram_kernel, first, groups), out_sh...  8.81 us
    pallas_call x1, Pallas kernels, pair_terms(): pl.pallas_call(functools.partial(pairs_kernel, feat_count), out_shape=(ja...  6.86 us
    ppermute x10, waiting for transfers between devices, swap(): return lax.ppermute(value, axes, [(p, p ^ mask) for p in range(count)])  5.47 us
    unnamed x12, local copies, waits for them, and re-layouts  1.41 us
    pallas_call x1, Pallas kernels, prepare(): pl.pallas_call(functools.partial(prepare_kernel, feat_count, masks), out_...  1.01 us
    pallas_call x1, Pallas kernels, finish(): pl.pallas_call(functools.partial(finish_kernel, per_dev), out_shape=(jax....  0.8 us
  transfers between devices with their start and end apart: 11, of which 7 were waited for; matrix products, arithmetic and copies ran while one was open for 0% of the time, Pallas kernels for 22%

profile of v17, /device:TPU:0, one launch (start us, length us, event | category | flops | bytes accessed | tf_op | source)
XLA Modules:
  0.0 38.8 jit_solution(760169734090323249)
XLA Ops:
  0.6 0.5 %collective-permute-start = (f32[8,128]{1,0:T(8,128)}, f32[8,128]{1,0:T(8,128)S(1)}, u32[]{:S(2)}, u32[]{:S(2)}) collective-permute-start(f32[8,128]{1,0:T(8,128)} %bitcast.9), channel_id=1, source_target_pairs={{0,4},{1,2},{2,1},{3,7},{4,0},{5,6},{6,5},{7,3},{8,12},{9,10},{10,... | collective-permute-start | bytes 12296 | tf_op jit(solution)/shard_map/ppermute | solution.py:504
  1.2 4.1 %collective-permute-start.1 = (f32[8,128]{1,0:T(8,128)}, f32[8,128]{1,0:T(8,128)S(1)}, u32[]{:S(2)}, u32[]{:S(2)}) collective-permute-start(f32[8,128]{1,0:T(8,128)} %bitcast.10), channel_id=1, source_target_pairs={{0,1},{1,0},{2,3},{3,2},{4,5},{5,4},{6,7},{7,6},{8,9},{9,8},{10,11... | collective-permute-start | bytes 12296 | tf_op jit(solution)/shard_map/ppermute | solution.py:492
  5.3 0.7 %copy-done.3 = f32[1024]{0:T(1024)S(1)} copy-done((f32[1024]{0:T(1024)S(1)}, f32[1024]{0:T(1024)}, u32[]{:S(2)}) %copy-start.3) | copy-done | bytes 4120
  6.0 0.7 %copy-done.4 = s32[256]{0:T(256)S(1)} copy-done((s32[256]{0:T(256)S(1)}, s32[256]{0:T(256)}, u32[]{:S(2)}) %copy-start.4) | copy-done | bytes 1048
  6.7 1.0 %prepare.1 = (f32[8,128]{1,0:T(8,128)S(1)}, s32[8,128]{1,0:T(8,128)S(1)}, s32[32,128]{1,0:T(8,128)S(1)}, f32[32,128]{1,0:T(8,128)S(1)}, f32[1,1024]{1,0:T(1,128)...) custom-call(s32[1,16]{1,0:T(1,128)S(1)} %copy-done.5, s32[1]{0:T(128)} %bitcast.pos_ref, s32[32,128]{1,0:T(8,128)S(1)} %bitcast.7, ...), custom_call_target="tpu_custom_call" | custom-call | flops 2000000000 | bytes 300000 | tf_op jit(solution)/shard_map/prepare/pallas_call | solution.py:113
  7.7 0.0 collective-permute-done.refs_1_
  7.8 0.0 copy-start
  7.8 6.9 %pair_terms.1 = (f32[2,1024]{1,0:T(2,128)}, f32[2,1024]{1,0:T(2,128)S(1)}) custom-call(s32[8,128]{1,0:T(8,128)S(1)} %get-tuple-element.24.bounds_ref, s32[1]{0:T(128)} %bitcast.pos_ref, f32[8,128]{1,0:T(8,128)S(1)} %get-tuple-element.25.refs_0_, f32[8,128]{1,0:T(8,128)S(1)} %collective-permute-done.refs_1_, f32[8,128]{1,0:T(8,128)S(1)} %collective-permute-done.1.refs_2_, ...), custom_call_target="tpu_custom_call" | custom-call | flops 8999999488 | bytes 200000 | tf_op jit(solution)/shard_map/pair_terms/pallas_call | solution.py:293
  14.6 0.4 %leaf_terms.1 = (f32[256,1024]{1,0:T(8,128)S(1)}, bf16[32,1024]{1,0:T(8,128)(2,1)S(1)}, f32[8,256]{1,0:T(8,128)S(1)}) custom-call(bf16[256,256]{1,0:T(8,128)(2,1)S(1)} %get-tuple-element.31.perm_ref, s32[1024,256]{1,0:T(8,128)S(1)} %copy-done, s32[8,128]{1,0:T(8,128)S(1)} %get-tuple-element.30.leaf_ref, f32[2,1024]{1,0:T(2,128)S(1)} %get-tuple-element.32.lam_ref), custom_call_target="tpu_custom_call" | custom-call | flops 200000000 | bytes 3000000 | tf_op jit(solution)/shard_map/leaf_terms/pallas_call | solution.py:334
  15.1 1.1 %histogram_part.7 = f32[104,256]{1,0:T(8,128)S(1)} custom-call(bf16[32,1024]{1,0:T(8,128)(2,1)S(1)} %get-tuple-element.38.tile_ref, f32[256,1024]{1,0:T(8,128)S(1)} %get-tuple-element.34.bins_ref, f32[8,256]{1,0:T(8,128)S(1)} %get-tuple-element.35.refs_0_), custom_call_target="tpu_custom_call" | custom-call | flops 4000000 | bytes 4000 | tf_op jit(solution)/shard_map/histogram_part/pallas_call | solution.py:408
  16.2 0.1 collective-permute-start.2
  16.2 1.1 %histogram_part.6 = f32[96,256]{1,0:T(8,128)S(1)} custom-call(bf16[32,1024]{1,0:T(8,128)(2,1)S(1)} %get-tuple-element.38.tile_ref, f32[256,1024]{1,0:T(8,128)S(1)} %get-tuple-element.34.bins_ref), custom_call_target="tpu_custom_call" | custom-call | flops 4000000 | bytes 4000 | tf_op jit(solution)/shard_map/histogram_part/pallas_call | solution.py:408
  17.4 0.2 collective-permute-done.2
  17.6 0.5 %collective-permute-start.4 = (f32[104,256]{1,0:T(8,128)S(1)}, f32[104,256]{1,0:T(8,128)S(1)}, u32[]{:S(2)}, u32[]{:S(2)}) collective-permute-start(f32[104,256]{1,0:T(8,128)S(1)} %pad_maximum_fusion.2), channel_id=1, source_target_pairs={{0,8},{1,9},{2,10},{3,11},{4,12},{5,13},{6,14},{7,15},{8,0},{9,1},... | collective-permute-start | bytes 319496 | tf_op jit(solution)/shard_map/ppermute | solution.py:492
  18.1 2.2 %histogram_part.9 = f32[192,256]{1,0:T(8,128)S(1)} custom-call(bf16[32,1024]{1,0:T(8,128)(2,1)S(1)} %get-tuple-element.38.tile_ref, f32[256,1024]{1,0:T(8,128)S(1)} %get-tuple-element.34.bins_ref), custom_call_target="tpu_custom_call" | custom-call | flops 8000000 | bytes 8000 | tf_op jit(solution)/shard_map/histogram_part/pallas_call | solution.py:408
  20.3 0.1 collective-permute-start.3
  20.4 2.2 %histogram_part.8 = f32[192,256]{1,0:T(8,128)S(1)} custom-call(bf16[32,1024]{1,0:T(8,128)(2,1)S(1)} %get-tuple-element.38.tile_ref, f32[256,1024]{1,0:T(8,128)S(1)} %get-tuple-element.34.bins_ref), custom_call_target="tpu_custom_call" | custom-call | flops 8000000 | bytes 8000 | tf_op jit(solution)/shard_map/histogram_part/pallas_call | solution.py:408
  22.6 0.3 collective-permute-done.4
  22.9 1.6 %collective-permute-start.7 = (f32[104,256]{1,0:T(8,128)S(1)}, f32[104,256]{1,0:T(8,128)S(1)}, u32[]{:S(2)}, u32[]{:S(2)}) collective-permute-start(f32[104,256]{1,0:T(8,128)S(1)} %get-tuple-element.40), channel_id=1, source_target_pairs={{0,16},{1,17},{2,18},{3,19},{4,20},{5,21},{6,22},{7,23},{8,24},{9,... | collective-permute-start | bytes 319496 | tf_op jit(solution)/shard_map/ppermute | solution.py:492
  24.6 1.2 %collective-permute-start.6 = (f32[104,256]{1,0:T(8,128)S(1)}, f32[104,256]{1,0:T(8,128)S(1)}, u32[]{:S(2)}, u32[]{:S(2)}) collective-permute-start(f32[104,256]{1,0:T(8,128)S(1)} %get-tuple-element.39), channel_id=1, source_target_pairs={{0,8},{1,9},{2,10},{3,11},{4,12},{5,13},{6,14},{7,15},{8,0},{9,1},... | collective-permute-start | bytes 319496 | tf_op jit(solution)/shard_map/ppermute | solution.py:492
  25.8 1.1 %histogram_part.11 = f32[96,256]{1,0:T(8,128)S(1)} custom-call(bf16[32,1024]{1,0:T(8,128)(2,1)S(1)} %get-tuple-element.38.tile_ref, f32[256,1024]{1,0:T(8,128)S(1)} %get-tuple-element.34.bins_ref), custom_call_target="tpu_custom_call" | custom-call | flops 4000000 | bytes 4000 | tf_op jit(solution)/shard_map/histogram_part/pallas_call | solution.py:408
  26.9 0.1 collective-permute-start.5
  26.9 1.1 %histogram_part.10 = f32[96,256]{1,0:T(8,128)S(1)} custom-call(bf16[32,1024]{1,0:T(8,128)(2,1)S(1)} %get-tuple-element.38.tile_ref, f32[256,1024]{1,0:T(8,128)S(1)} %get-tuple-element.34.bins_ref), custom_call_target="tpu_custom_call" | custom-call | flops 4000000 | bytes 4000 | tf_op jit(solution)/shard_map/histogram_part/pallas_call | solution.py:408
  28.1 0.2 collective-permute-done.5
  28.2 1.4 %collective-permute-done.6 = f32[104,256]{1,0:T(8,128)S(1)} collective-permute-done((f32[104,256]{1,0:T(8,128)S(1)}, f32[104,256]{1,0:T(8,128)S(1)}, u32[]{:S(2)}, u32[]{:S(2)}) %collective-permute-start.6) | collective-permute-done | bytes 106528 | tf_op jit(solution)/shard_map/ppermute | solution.py:492
  29.7 1.6 %collective-permute-start.10 = (f32[32,256]{1,0:T(8,128)S(1)}, f32[32,256]{1,0:T(8,128)S(1)}, u32[]{:S(2)}, u32[]{:S(2)}) collective-permute-start(f32[32,256]{1,0:T(8,128)S(1)} %get-tuple-element.50), channel_id=1, source_target_pairs={{0,3},{1,2},{2,1},{3,0},{4,7},{5,6},{6,5},{7,4},{8,11},{9,10},{10,... | collective-permute-start | bytes 98312 | tf_op jit(solution)/shard_map/ppermute | solution.py:492
  31.4 2.7 %collective-permute-start.8 = (f32[32,256]{1,0:T(8,128)S(1)}, f32[32,256]{1,0:T(8,128)S(1)}, u32[]{:S(2)}, u32[]{:S(2)}) collective-permute-start(f32[32,256]{1,0:T(8,128)S(1)} %get-tuple-element.52), channel_id=1, source_target_pairs={{0,2},{1,3},{2,0},{3,1},{4,6},{5,7},{6,4},{7,5},{8,10},{9,11},{10,... | collective-permute-start | bytes 98312 | tf_op jit(solution)/shard_map/ppermute | solution.py:492
  34.1 0.5 %collective-permute-start.9 = (f32[32,256]{1,0:T(8,128)S(1)}, f32[32,256]{1,0:T(8,128)S(1)}, u32[]{:S(2)}, u32[]{:S(2)}) collective-permute-start(f32[32,256]{1,0:T(8,128)S(1)} %get-tuple-element.51), channel_id=1, source_target_pairs={{0,1},{1,0},{2,3},{3,2},{4,5},{5,4},{6,7},{7,6},{8,9},{9,8},{10,11... | collective-permute-start | bytes 98312 | tf_op jit(solution)/shard_map/ppermute | solution.py:492
  34.6 0.9 %collective-permute-done.10.refs_2_ = f32[32,256]{1,0:T(8,128)S(1)} collective-permute-done((f32[32,256]{1,0:T(8,128)S(1)}, f32[32,256]{1,0:T(8,128)S(1)}, u32[]{:S(2)}, u32[]{:S(2)}) %collective-permute-start.10) | collective-permute-done | bytes 32800 | tf_op jit(solution)/shard_map/ppermute | solution.py:492
  35.5 0.9 %collective-permute-done.8.refs_0_ = f32[32,256]{1,0:T(8,128)S(1)} collective-permute-done((f32[32,256]{1,0:T(8,128)S(1)}, f32[32,256]{1,0:T(8,128)S(1)}, u32[]{:S(2)}, u32[]{:S(2)}) %collective-permute-start.8) | collective-permute-done | bytes 32800 | tf_op jit(solution)/shard_map/ppermute | solution.py:492
  36.4 1.6 %collective-permute-done.9.refs_1_ = f32[32,256]{1,0:T(8,128)S(1)} collective-permute-done((f32[32,256]{1,0:T(8,128)S(1)}, f32[32,256]{1,0:T(8,128)S(1)}, u32[]{:S(2)}, u32[]{:S(2)}) %collective-permute-start.9) | collective-permute-done | bytes 32800 | tf_op jit(solution)/shard_map/ppermute | solution.py:492
  38.0 0.8 %finish.1 = (f32[8,128]{1,0:T(8,128)}, f32[8,128]{1,0:T(8,128)}, f32[3,2048]{1,0:T(4,128)}) custom-call(s32[8,128]{1,0:T(8,128)S(1)} %get-tuple-element.30.leaf_ref, f32[24,256]{1,0:T(8,128)S(1)} %get-tuple-element.49.kept_ref, f32[8,256]{1,0:T(8,128)S(1)} %slice_add_fusion.4.sums_ref, f32[32,256]{1,0:T(8,128)S(1)} %collective-permute-done.8.refs_0_, ...), custom_call_target="tpu_custom_call" | custom-call | tf_op jit(solution)/shard_map/finish/pallas_call | solution.py:457
  (23 shorter events, 0.2 us)
Async XLA Ops:
  0.6 4.7 %copy-start.1 = (s32[4096]{0:T(1024)S(1)}, s32[4096]{0:T(1024)}, u32[]{:S(2)}) copy-start(s32[4096]{0:T(1024)} %param.7) | copy-start | bytes 49156
  0.6 7.1 %collective-permute-start = (f32[8,128]{1,0:T(8,128)}, f32[8,128]{1,0:T(8,128)S(1)}, u32[]{:S(2)}, u32[]{:S(2)}) collective-permute-start(f32[8,128]{1,0:T(8,128)} %bitcast.9), channel_id=1, source_target_pairs={{0,4},{1,2},{2,1},{3,7},{4,0},{5,6},{6,5},{7,3},{8,12},{9,10},{10,... | collective-permute-start | bytes 12296 | tf_op jit(solution)/shard_map/ppermute | solution.py:504
  1.2 6.6 %collective-permute-start.1 = (f32[8,128]{1,0:T(8,128)}, f32[8,128]{1,0:T(8,128)S(1)}, u32[]{:S(2)}, u32[]{:S(2)}) collective-permute-start(f32[8,128]{1,0:T(8,128)} %bitcast.10), channel_id=1, source_target_pairs={{0,1},{1,0},{2,3},{3,2},{4,5},{5,4},{6,7},{7,6},{8,9},{9,8},{10,11... | collective-permute-start | bytes 12296 | tf_op jit(solution)/shard_map/ppermute | solution.py:492
  5.3 0.7 %copy-start.3 = (f32[1024]{0:T(1024)S(1)}, f32[1024]{0:T(1024)}, u32[]{:S(2)}) copy-start(f32[1024]{0:T(1024)} %param.6) | copy-start | bytes 12292
  5.3 0.7 %copy-start.2 = (s32[1024]{0:T(1024)S(1)}, s32[1024]{0:T(1024)}, u32[]{:S(2)}) copy-start(s32[1024]{0:T(1024)} %param.8) | copy-start | bytes 12292
  5.3 0.7 %copy-start.5 = (s32[1,16]{1,0:T(1,128)S(1)}, s32[1,16]{1,0:T(1,128)}, u32[]{:S(2)}) copy-start(s32[1,16]{1,0:T(1,128)} %len_ref.1) | copy-start | bytes 196
  6.0 0.7 %copy-start.4 = (s32[256]{0:T(256)S(1)}, s32[256]{0:T(256)}, u32[]{:S(2)}) copy-start(s32[256]{0:T(256)} %param.11) | copy-start | bytes 3076
  7.8 6.9 %copy-start = (s32[1024,256]{1,0:T(8,128)S(1)}, s32[1024,256]{1,0:T(8,128)}, u32[]{:S(2)}) copy-start(s32[1024,256]{1,0:T(8,128)} %bins_ref.1) | copy-start | bytes 3145732
  16.2 1.4 %collective-permute-start.2 = (f32[104,256]{1,0:T(8,128)S(1)}, f32[104,256]{1,0:T(8,128)S(1)}, u32[]{:S(2)}, u32[]{:S(2)}) collective-permute-start(f32[104,256]{1,0:T(8,128)S(1)} %histogram_part.7), channel_id=1, source_target_pairs={{0,4},{1,5},{2,6},{3,7},{4,0},{5,1},{6,2},{7,3},{8,12},{9,13},{10,... | collective-permute-start | bytes 319496 | tf_op jit(solution)/shard_map/ppermute | solution.py:492
  17.6 5.3 %collective-permute-start.4 = (f32[104,256]{1,0:T(8,128)S(1)}, f32[104,256]{1,0:T(8,128)S(1)}, u32[]{:S(2)}, u32[]{:S(2)}) collective-permute-start(f32[104,256]{1,0:T(8,128)S(1)} %pad_maximum_fusion.2), channel_id=1, source_target_pairs={{0,8},{1,9},{2,10},{3,11},{4,12},{5,13},{6,14},{7,15},{8,0},{9,1},... | collective-permute-start | bytes 319496 | tf_op jit(solution)/shard_map/ppermute | solution.py:492
  20.3 2.6 %collective-permute-start.3 = (f32[192,256]{1,0:T(8,128)S(1)}, f32[192,256]{1,0:T(8,128)S(1)}, u32[]{:S(2)}, u32[]{:S(2)}) collective-permute-start(f32[192,256]{1,0:T(8,128)S(1)} %histogram_part.9), channel_id=1, source_target_pairs={{0,4},{1,5},{2,6},{3,7},{4,0},{5,1},{6,2},{7,3},{8,12},{9,13},{10,... | collective-permute-start | bytes 589832 | tf_op jit(solution)/shard_map/ppermute | solution.py:492
  22.9 5.3 %collective-permute-start.7 = (f32[104,256]{1,0:T(8,128)S(1)}, f32[104,256]{1,0:T(8,128)S(1)}, u32[]{:S(2)}, u32[]{:S(2)}) collective-permute-start(f32[104,256]{1,0:T(8,128)S(1)} %get-tuple-element.40), channel_id=1, source_target_pairs={{0,16},{1,17},{2,18},{3,19},{4,20},{5,21},{6,22},{7,23},{8,24},{9,... | collective-permute-start | bytes 319496 | tf_op jit(solution)/shard_map/ppermute | solution.py:492
  24.6 5.1 %collective-permute-start.6 = (f32[104,256]{1,0:T(8,128)S(1)}, f32[104,256]{1,0:T(8,128)S(1)}, u32[]{:S(2)}, u32[]{:S(2)}) collective-permute-start(f32[104,256]{1,0:T(8,128)S(1)} %get-tuple-element.39), channel_id=1, source_target_pairs={{0,8},{1,9},{2,10},{3,11},{4,12},{5,13},{6,14},{7,15},{8,0},{9,1},... | collective-permute-start | bytes 319496 | tf_op jit(solution)/shard_map/ppermute | solution.py:492
  26.9 1.4 %collective-permute-start.5 = (f32[96,256]{1,0:T(8,128)S(1)}, f32[96,256]{1,0:T(8,128)S(1)}, u32[]{:S(2)}, u32[]{:S(2)}) collective-permute-start(f32[96,256]{1,0:T(8,128)S(1)} %histogram_part.11), channel_id=1, source_target_pairs={{0,4},{1,5},{2,6},{3,7},{4,0},{5,1},{6,2},{7,3},{8,12},{9,13},{10,... | collective-permute-start | bytes 294920 | tf_op jit(solution)/shard_map/ppermute | solution.py:492
  29.7 5.8 %collective-permute-start.10 = (f32[32,256]{1,0:T(8,128)S(1)}, f32[32,256]{1,0:T(8,128)S(1)}, u32[]{:S(2)}, u32[]{:S(2)}) collective-permute-start(f32[32,256]{1,0:T(8,128)S(1)} %get-tuple-element.50), channel_id=1, source_target_pairs={{0,3},{1,2},{2,1},{3,0},{4,7},{5,6},{6,5},{7,4},{8,11},{9,10},{10,... | collective-permute-start | bytes 98312 | tf_op jit(solution)/shard_map/ppermute | solution.py:492
  31.4 5.0 %collective-permute-start.8 = (f32[32,256]{1,0:T(8,128)S(1)}, f32[32,256]{1,0:T(8,128)S(1)}, u32[]{:S(2)}, u32[]{:S(2)}) collective-permute-start(f32[32,256]{1,0:T(8,128)S(1)} %get-tuple-element.52), channel_id=1, source_target_pairs={{0,2},{1,3},{2,0},{3,1},{4,6},{5,7},{6,4},{7,5},{8,10},{9,11},{10,... | collective-permute-start | bytes 98312 | tf_op jit(solution)/shard_map/ppermute | solution.py:492
  34.1 3.9 %collective-permute-start.9 = (f32[32,256]{1,0:T(8,128)S(1)}, f32[32,256]{1,0:T(8,128)S(1)}, u32[]{:S(2)}, u32[]{:S(2)}) collective-permute-start(f32[32,256]{1,0:T(8,128)S(1)} %get-tuple-element.51), channel_id=1, source_target_pairs={{0,1},{1,0},{2,3},{3,2},{4,5},{5,4},{6,7},{7,6},{8,9},{9,8},{10,11... | collective-permute-start | bytes 98312 | tf_op jit(solution)/shard_map/ppermute | solution.py:492

commit v18 on v17

--- a/solution.py
+++ b/solution.py
@@ -47,7 +47,7 @@
     rows = lab_ref.shape[0]
     own = rows // feat_count
     spot = iota((rows, LANES), 0) * LANES + iota((rows, LANES), 1)
-    qid = jnp.zeros((rows, LANES), jnp.int32)
+    qid = jnp.zeros((rows, LANES), F32)
     begin = jnp.zeros((queries, LANES), jnp.int32)
     finish = jnp.zeros((queries, LANES), jnp.int32)
     which = iota((queries, LANES), 0)
@@ -57,7 +57,7 @@
     start = jnp.int32(0)
     for q in range(queries):
         end = start + len_ref[0, q]
-        qid = qid + jnp.where(spot >= end, 1, 0)
+        qid = qid + jnp.where(spot >= end, 1.0, 0.0)
         begin = jnp.where(which == q, start, begin)
         finish = jnp.where(which == q, end, finish)
 
@@ -115,7 +115,7 @@
         out_shape=(
             jax.ShapeDtypeStruct(scores.shape, F32),
             jax.ShapeDtypeStruct(leaves.shape, jnp.int32),
-            jax.ShapeDtypeStruct((rows, LANES), jnp.int32),
+            jax.ShapeDtypeStruct((rows, LANES), F32),
             jax.ShapeDtypeStruct((rows, LANES), F32),
             jax.ShapeDtypeStruct((1, rows // feat_count * LANES), F32),
             jax.ShapeDtypeStruct((features, features), BF16),
@@ -140,9 +140,9 @@
 
 
 def pairs_kernel(feat_count, bounds_ref, pos_ref, *refs):
-    scores = refs[:-20]
+    scores = refs[:-16]
     (worth_ref, qid_ref, inv_ref, lam_ref, near_ref,
-     s_row, a_row, d_row, s_turn, a_turn, w_turn, q_turn, d_turn, s_col, a_col, w_col, q_col, d_col, grad, curv) = refs[-20:]
+     s_row, a_row, d_row, turn, s_col, a_col, w_col, q_col, d_col, grad, curv) = refs[-16:]
     rows = worth_ref.shape[0]
     own = rows // feat_count
     docs = own * LANES
@@ -161,16 +161,20 @@
     stride = 4
 
     def widen(pairs):
-        for turn, source, _ in pairs:
-            turn[...] = jnp.transpose(source[...])
+        lines = jnp.concatenate([source[...] for source, _ in pairs], axis=0)
+        if lines.shape[0] % LANES:
+            lines = jnp.concatenate([lines, jnp.zeros((LANES - lines.shape[0] % LANES, LANES), F32)], axis=0)
+        for k in range(lines.shape[0] // LANES):
+            turn[:, k * LANES:(k + 1) * LANES] = jnp.transpose(lines[k * LANES:(k + 1) * LANES])
         for r in range(0, rows, stride):
             @pl.when((r + stride > window_low) & (r < window_high))
             def _(r=r):
-                for turn, _, col in pairs:
-                    for k in range(r, r + stride):
-                        col[k * LANES:(k + 1) * LANES, :] = jnp.broadcast_to(turn[:, k:k + 1], (LANES, LANES))
-
-    widen([(s_turn, s_row, s_col), (q_turn, qid_ref, q_col), (a_turn, a_row, a_col), (w_turn, worth_ref, w_col)])
+                for k, (_, col) in enumerate(pairs):
+                    for m in range(r, r + stride):
+                        at = k * rows + m
+                        col[m * LANES:(m + 1) * LANES, :] = jnp.broadcast_to(turn[:, at:at + 1], (LANES, LANES))
+
+    widen([(s_row, s_col), (qid_ref, q_col), (a_row, a_col), (worth_ref, w_col)])
 
     def rows_of(ref, r):
         return [jnp.broadcast_to(ref[pl.ds(r + g, 1), :], (8, LANES)) for g in range(2)]
@@ -238,7 +242,7 @@
 
     lax.fori_loop(0, (window_high - window_low) // 2, rank_groups, 0)
     d_row[...] = 1.0 / jnp.log2(2.0 + d_row[...])
-    widen([(d_turn, d_row, d_col)])
+    widen([(d_row, d_col)])
 
     def pair_groups(t, carry):
         r = first + 2 * t
@@ -287,7 +291,7 @@
     rows = worth.shape[0]
     docs = inverse.shape[1]
     row = pltpu.VMEM((rows, LANES), F32)
-    turn = pltpu.VMEM((LANES, rows), F32)
+    turn = pltpu.VMEM((LANES, 4 * rows), F32)
     col = pltpu.VMEM((rows * LANES, LANES), F32)
     mine = pltpu.VMEM((docs // LANES, LANES), F32)
     return pl.pallas_call(
@@ -295,8 +299,7 @@
         out_shape=(jax.ShapeDtypeStruct((2, docs), F32), jax.ShapeDtypeStruct((2, docs), F32)),
         in_specs=[smem(), smem()] + [vmem()] * (len(scores) + 3),
         out_specs=(vmem(), vmem()),
-        scratch_shapes=[row, row, row, turn, turn, turn, pltpu.VMEM((LANES, rows), jnp.int32), turn,
-                        col, col, col, pltpu.VMEM((rows * LANES, LANES), jnp.int32), col, mine, mine],
+        scratch_shapes=[row, row, row, turn, col, col, col, col, col, mine, mine],
         compiler_params=pltpu.CompilerParams(vmem_limit_bytes=VMEM_LIMIT),
         cost_estimate=pl.CostEstimate(flops=9_000_000_000, bytes_accessed=200_000, transcendentals=2_000_000),
         name="pair_terms",
@@ -400,7 +403,7 @@
 
     if len(refs) > 1:
         out_ref[groups * 3 * HIGH:, :] = refs[0][...]
-    lax.fori_loop(0, groups, one_group, 0, unroll=2)
+    lax.fori_loop(0, groups, one_group, 0, unroll=4)
 
 
 def histogram_part(first, groups, tiles, bins_t, *tail):

time: 39.6 us -> 38.8 us (0.980); the launches traced: 38.8 us -> 38.7 us
  waiting for transfers between devices: 5.48 us -> 7.58 us
  Pallas kernels: 17.9 us -> 16.6 us
  starting transfers between devices: 13.1 us -> 12.2 us
    ppermute x10, waiting for transfers between devices: 5.47 us -> 7.58 us  [swap(): return lax.ppermute(value, axes, [(p, p ^ mask) for p in range(count)])]
    pallas_call x6, Pallas kernels: 8.81 us -> 7.1 us  [histogram_part(): pl.pallas_call(functools.partial(histogram_kernel, first, groups), out_sh...]
    ppermute x10, starting transfers between devices: 12.6 us -> 11.7 us  [swap(): return lax.ppermute(value, axes, [(p, p ^ mask) for p in range(count)])]
  transfers between devices with their start and end apart: 11 -> 11, of which waited for: 7 -> 8; matrix products, arithmetic and copies ran while one was open for 0% -> 0% of each run, Pallas kernels for 22% -> 19%
where the time goes in v18:
time: 38.8 us; the launch traced here: 38.7 us
  Pallas kernels  16.6 us (43%)
  starting transfers between devices  12.2 us (31%)
  waiting for transfers between devices  7.58 us (20%)
  local copies, waits for them, and re-layouts  1.42 us (4%)
  between operations  0.8 us (2%)
    ppermute x10, starting transfers between devices, swap(): return lax.ppermute(value, axes, [(p, p ^ mask) for p in range(count)])  11.7 us
    ppermute x10, waiting for transfers between devices, swap(): return lax.ppermute(value, axes, [(p, p ^ mask) for p in range(count)])  7.58 us
    pallas_call x1, Pallas kernels, pair_terms(): pl.pallas_call(functools.partial(pairs_kernel, feat_count), out_shape=(ja...  7.23 us
    pallas_call x6, Pallas kernels, histogram_part(): pl.pallas_call(functools.partial(histogram_kernel, first, groups), out_sh...  7.1 us
    unnamed x12, local copies, waits for them, and re-layouts  1.41 us
    pallas_call x1, Pallas kernels, prepare(): pl.pallas_call(functools.partial(prepare_kernel, feat_count, masks), out_...  1.01 us
    pallas_call x1, Pallas kernels, finish(): pl.pallas_call(functools.partial(finish_kernel, per_dev), out_shape=(jax....  0.8 us
  transfers between devices with their start and end apart: 11, of which 8 were waited for; matrix products, arithmetic and copies ran while one was open for 0% of the time, Pallas kernels for 19%

profile of v18, /device:TPU:0, one launch (start us, length us, event | category | flops | bytes accessed | tf_op | source)
XLA Modules:
  0.0 38.7 jit_solution(7045309987695636192)
XLA Ops:
  0.6 0.5 %collective-permute-start = (f32[8,128]{1,0:T(8,128)}, f32[8,128]{1,0:T(8,128)S(1)}, u32[]{:S(2)}, u32[]{:S(2)}) collective-permute-start(f32[8,128]{1,0:T(8,128)} %bitcast.9), channel_id=1, source_target_pairs={{0,4},{1,2},{2,1},{3,7},{4,0},{5,6},{6,5},{7,3},{8,12},{9,10},{10,... | collective-permute-start | bytes 12296 | tf_op jit(solution)/shard_map/ppermute | solution.py:507
  1.2 4.1 %collective-permute-start.1 = (f32[8,128]{1,0:T(8,128)}, f32[8,128]{1,0:T(8,128)S(1)}, u32[]{:S(2)}, u32[]{:S(2)}) collective-permute-start(f32[8,128]{1,0:T(8,128)} %bitcast.10), channel_id=1, source_target_pairs={{0,1},{1,0},{2,3},{3,2},{4,5},{5,4},{6,7},{7,6},{8,9},{9,8},{10,11... | collective-permute-start | bytes 12296 | tf_op jit(solution)/shard_map/ppermute | solution.py:495
  5.3 0.7 %copy-done.3 = f32[1024]{0:T(1024)S(1)} copy-done((f32[1024]{0:T(1024)S(1)}, f32[1024]{0:T(1024)}, u32[]{:S(2)}) %copy-start.3) | copy-done | bytes 4120
  6.0 0.7 %copy-done.4 = s32[256]{0:T(256)S(1)} copy-done((s32[256]{0:T(256)S(1)}, s32[256]{0:T(256)}, u32[]{:S(2)}) %copy-start.4) | copy-done | bytes 1048
  6.7 1.0 %prepare.1 = (f32[8,128]{1,0:T(8,128)S(1)}, s32[8,128]{1,0:T(8,128)S(1)}, f32[32,128]{1,0:T(8,128)S(1)}, f32[32,128]{1,0:T(8,128)S(1)}, f32[1,1024]{1,0:T(1,128)...) custom-call(s32[1,16]{1,0:T(1,128)S(1)} %copy-done.5, s32[1]{0:T(128)} %bitcast.pos_ref, s32[32,128]{1,0:T(8,128)S(1)} %bitcast.7, ...), custom_call_target="tpu_custom_call" | custom-call | flops 2000000000 | bytes 300000 | tf_op jit(solution)/shard_map/prepare/pallas_call | solution.py:113
  7.7 0.0 collective-permute-done.refs_1_
  7.8 0.0 copy-start
  7.8 7.2 %pair_terms.1 = (f32[2,1024]{1,0:T(2,128)}, f32[2,1024]{1,0:T(2,128)S(1)}) custom-call(s32[8,128]{1,0:T(8,128)S(1)} %get-tuple-element.24.bounds_ref, s32[1]{0:T(128)} %bitcast.pos_ref, f32[8,128]{1,0:T(8,128)S(1)} %get-tuple-element.25.refs_0_, f32[8,128]{1,0:T(8,128)S(1)} %collective-permute-done.refs_1_, f32[8,128]{1,0:T(8,128)S(1)} %collective-permute-done.1.refs_2_, ...), custom_call_target="tpu_custom_call" | custom-call | flops 8999999488 | bytes 200000 | tf_op jit(solution)/shard_map/pair_terms/pallas_call | solution.py:297
  15.0 0.4 %leaf_terms.1 = (f32[256,1024]{1,0:T(8,128)S(1)}, bf16[32,1024]{1,0:T(8,128)(2,1)S(1)}, f32[8,256]{1,0:T(8,128)S(1)}) custom-call(bf16[256,256]{1,0:T(8,128)(2,1)S(1)} %get-tuple-element.31.perm_ref, s32[1024,256]{1,0:T(8,128)S(1)} %copy-done, s32[8,128]{1,0:T(8,128)S(1)} %get-tuple-element.30.leaf_ref, f32[2,1024]{1,0:T(2,128)S(1)} %get-tuple-element.32.lam_ref), custom_call_target="tpu_custom_call" | custom-call | flops 200000000 | bytes 3000000 | tf_op jit(solution)/shard_map/leaf_terms/pallas_call | solution.py:337
  15.4 0.9 %histogram_part.7 = f32[104,256]{1,0:T(8,128)S(1)} custom-call(bf16[32,1024]{1,0:T(8,128)(2,1)S(1)} %get-tuple-element.38.tile_ref, f32[256,1024]{1,0:T(8,128)S(1)} %get-tuple-element.34.bins_ref, f32[8,256]{1,0:T(8,128)S(1)} %get-tuple-element.35.refs_0_), custom_call_target="tpu_custom_call" | custom-call | flops 4000000 | bytes 4000 | tf_op jit(solution)/shard_map/histogram_part/pallas_call | solution.py:411
  16.3 0.1 collective-permute-start.2
  16.4 0.9 %histogram_part.6 = f32[96,256]{1,0:T(8,128)S(1)} custom-call(bf16[32,1024]{1,0:T(8,128)(2,1)S(1)} %get-tuple-element.38.tile_ref, f32[256,1024]{1,0:T(8,128)S(1)} %get-tuple-element.34.bins_ref), custom_call_target="tpu_custom_call" | custom-call | flops 4000000 | bytes 4000 | tf_op jit(solution)/shard_map/histogram_part/pallas_call | solution.py:411
  17.3 0.4 %collective-permute-done.2 = f32[104,256]{1,0:T(8,128)S(1)} collective-permute-done((f32[104,256]{1,0:T(8,128)S(1)}, f32[104,256]{1,0:T(8,128)S(1)}, u32[]{:S(2)}, u32[]{:S(2)}) %collective-permute-start.2) | collective-permute-done | bytes 106528 | tf_op jit(solution)/shard_map/ppermute | solution.py:495
  17.7 0.1 collective-permute-start.4
  17.8 1.8 %histogram_part.9 = f32[192,256]{1,0:T(8,128)S(1)} custom-call(bf16[32,1024]{1,0:T(8,128)(2,1)S(1)} %get-tuple-element.38.tile_ref, f32[256,1024]{1,0:T(8,128)S(1)} %get-tuple-element.34.bins_ref), custom_call_target="tpu_custom_call" | custom-call | flops 8000000 | bytes 8000 | tf_op jit(solution)/shard_map/histogram_part/pallas_call | solution.py:411
  19.6 0.2 collective-permute-start.3
  19.8 1.8 %histogram_part.8 = f32[192,256]{1,0:T(8,128)S(1)} custom-call(bf16[32,1024]{1,0:T(8,128)(2,1)S(1)} %get-tuple-element.38.tile_ref, f32[256,1024]{1,0:T(8,128)S(1)} %get-tuple-element.34.bins_ref), custom_call_target="tpu_custom_call" | custom-call | flops 8000000 | bytes 8000 | tf_op jit(solution)/shard_map/histogram_part/pallas_call | solution.py:411
  21.6 1.2 %collective-permute-done.4 = f32[104,256]{1,0:T(8,128)S(1)} collective-permute-done((f32[104,256]{1,0:T(8,128)S(1)}, f32[104,256]{1,0:T(8,128)S(1)}, u32[]{:S(2)}, u32[]{:S(2)}) %collective-permute-start.4) | collective-permute-done | bytes 106528 | tf_op jit(solution)/shard_map/ppermute | solution.py:495
  22.9 0.7 %collective-permute-start.7 = (f32[104,256]{1,0:T(8,128)S(1)}, f32[104,256]{1,0:T(8,128)S(1)}, u32[]{:S(2)}, u32[]{:S(2)}) collective-permute-start(f32[104,256]{1,0:T(8,128)S(1)} %get-tuple-element.40), channel_id=1, source_target_pairs={{0,16},{1,17},{2,18},{3,19},{4,20},{5,21},{6,22},{7,23},{8,24},{9,... | collective-permute-start | bytes 319496 | tf_op jit(solution)/shard_map/ppermute | solution.py:495
  23.6 0.8 %collective-permute-start.6 = (f32[104,256]{1,0:T(8,128)S(1)}, f32[104,256]{1,0:T(8,128)S(1)}, u32[]{:S(2)}, u32[]{:S(2)}) collective-permute-start(f32[104,256]{1,0:T(8,128)S(1)} %get-tuple-element.39), channel_id=1, source_target_pairs={{0,8},{1,9},{2,10},{3,11},{4,12},{5,13},{6,14},{7,15},{8,0},{9,1},... | collective-permute-start | bytes 319496 | tf_op jit(solution)/shard_map/ppermute | solution.py:495
  24.4 0.9 %histogram_part.11 = f32[96,256]{1,0:T(8,128)S(1)} custom-call(bf16[32,1024]{1,0:T(8,128)(2,1)S(1)} %get-tuple-element.38.tile_ref, f32[256,1024]{1,0:T(8,128)S(1)} %get-tuple-element.34.bins_ref), custom_call_target="tpu_custom_call" | custom-call | flops 4000000 | bytes 4000 | tf_op jit(solution)/shard_map/histogram_part/pallas_call | solution.py:411
  25.3 0.1 collective-permute-start.5
  25.4 0.9 %histogram_part.10 = f32[96,256]{1,0:T(8,128)S(1)} custom-call(bf16[32,1024]{1,0:T(8,128)(2,1)S(1)} %get-tuple-element.38.tile_ref, f32[256,1024]{1,0:T(8,128)S(1)} %get-tuple-element.34.bins_ref), custom_call_target="tpu_custom_call" | custom-call | flops 4000000 | bytes 4000 | tf_op jit(solution)/shard_map/histogram_part/pallas_call | solution.py:411
  26.3 0.4 %collective-permute-done.5 = f32[96,256]{1,0:T(8,128)S(1)} collective-permute-done((f32[96,256]{1,0:T(8,128)S(1)}, f32[96,256]{1,0:T(8,128)S(1)}, u32[]{:S(2)}, u32[]{:S(2)}) %collective-permute-start.5) | collective-permute-done | bytes 98336 | tf_op jit(solution)/shard_map/ppermute | solution.py:495
  26.7 1.0 %collective-permute-done.7 = f32[104,256]{1,0:T(8,128)S(1)} collective-permute-done((f32[104,256]{1,0:T(8,128)S(1)}, f32[104,256]{1,0:T(8,128)S(1)}, u32[]{:S(2)}, u32[]{:S(2)}) %collective-permute-start.7) | collective-permute-done | bytes 106528 | tf_op jit(solution)/shard_map/ppermute | solution.py:495
  27.7 0.6 %collective-permute-done.6 = f32[104,256]{1,0:T(8,128)S(1)} collective-permute-done((f32[104,256]{1,0:T(8,128)S(1)}, f32[104,256]{1,0:T(8,128)S(1)}, u32[]{:S(2)}, u32[]{:S(2)}) %collective-permute-start.6) | collective-permute-done | bytes 106528 | tf_op jit(solution)/shard_map/ppermute | solution.py:495
  28.4 3.1 %collective-permute-start.10 = (f32[32,256]{1,0:T(8,128)S(1)}, f32[32,256]{1,0:T(8,128)S(1)}, u32[]{:S(2)}, u32[]{:S(2)}) collective-permute-start(f32[32,256]{1,0:T(8,128)S(1)} %get-tuple-element.50), channel_id=1, source_target_pairs={{0,3},{1,2},{2,1},{3,0},{4,7},{5,6},{6,5},{7,4},{8,11},{9,10},{10,... | collective-permute-start | bytes 98312 | tf_op jit(solution)/shard_map/ppermute | solution.py:495
  31.5 2.5 %collective-permute-start.8 = (f32[32,256]{1,0:T(8,128)S(1)}, f32[32,256]{1,0:T(8,128)S(1)}, u32[]{:S(2)}, u32[]{:S(2)}) collective-permute-start(f32[32,256]{1,0:T(8,128)S(1)} %get-tuple-element.52), channel_id=1, source_target_pairs={{0,2},{1,3},{2,0},{3,1},{4,6},{5,7},{6,4},{7,5},{8,10},{9,11},{10,... | collective-permute-start | bytes 98312 | tf_op jit(solution)/shard_map/ppermute | solution.py:495
  34.0 0.2 collective-permute-done.10.refs_2_
  34.2 2.1 %collective-permute-done.8.refs_0_ = f32[32,256]{1,0:T(8,128)S(1)} collective-permute-done((f32[32,256]{1,0:T(8,128)S(1)}, f32[32,256]{1,0:T(8,128)S(1)}, u32[]{:S(2)}, u32[]{:S(2)}) %collective-permute-start.8) | collective-permute-done | bytes 32800 | tf_op jit(solution)/shard_map/ppermute | solution.py:495
  36.3 1.6 %collective-permute-done.9.refs_1_ = f32[32,256]{1,0:T(8,128)S(1)} collective-permute-done((f32[32,256]{1,0:T(8,128)S(1)}, f32[32,256]{1,0:T(8,128)S(1)}, u32[]{:S(2)}, u32[]{:S(2)}) %collective-permute-start.9) | collective-permute-done | bytes 32800 | tf_op jit(solution)/shard_map/ppermute | solution.py:495
  37.9 0.8 %finish.1 = (f32[8,128]{1,0:T(8,128)}, f32[8,128]{1,0:T(8,128)}, f32[3,2048]{1,0:T(4,128)}) custom-call(s32[8,128]{1,0:T(8,128)S(1)} %get-tuple-element.30.leaf_ref, f32[24,256]{1,0:T(8,128)S(1)} %get-tuple-element.49.kept_ref, f32[8,256]{1,0:T(8,128)S(1)} %slice_add_fusion.4.sums_ref, f32[32,256]{1,0:T(8,128)S(1)} %collective-permute-done.8.refs_0_, ...), custom_call_target="tpu_custom_call" | custom-call | tf_op jit(solution)/shard_map/finish/pallas_call | solution.py:460
  (23 shorter events, 0.2 us)
Async XLA Ops:
  0.6 4.7 %copy-start.1 = (s32[4096]{0:T(1024)S(1)}, s32[4096]{0:T(1024)}, u32[]{:S(2)}) copy-start(s32[4096]{0:T(1024)} %param.7) | copy-start | bytes 49156
  0.6 7.1 %collective-permute-start = (f32[8,128]{1,0:T(8,128)}, f32[8,128]{1,0:T(8,128)S(1)}, u32[]{:S(2)}, u32[]{:S(2)}) collective-permute-start(f32[8,128]{1,0:T(8,128)} %bitcast.9), channel_id=1, source_target_pairs={{0,4},{1,2},{2,1},{3,7},{4,0},{5,6},{6,5},{7,3},{8,12},{9,10},{10,... | collective-permute-start | bytes 12296 | tf_op jit(solution)/shard_map/ppermute | solution.py:507
  1.2 6.6 %collective-permute-start.1 = (f32[8,128]{1,0:T(8,128)}, f32[8,128]{1,0:T(8,128)S(1)}, u32[]{:S(2)}, u32[]{:S(2)}) collective-permute-start(f32[8,128]{1,0:T(8,128)} %bitcast.10), channel_id=1, source_target_pairs={{0,1},{1,0},{2,3},{3,2},{4,5},{5,4},{6,7},{7,6},{8,9},{9,8},{10,11... | collective-permute-start | bytes 12296 | tf_op jit(solution)/shard_map/ppermute | solution.py:495
  5.3 0.7 %copy-start.3 = (f32[1024]{0:T(1024)S(1)}, f32[1024]{0:T(1024)}, u32[]{:S(2)}) copy-start(f32[1024]{0:T(1024)} %param.6) | copy-start | bytes 12292
  5.3 0.7 %copy-start.2 = (s32[1024]{0:T(1024)S(1)}, s32[1024]{0:T(1024)}, u32[]{:S(2)}) copy-start(s32[1024]{0:T(1024)} %param.8) | copy-start | bytes 12292
  5.3 0.7 %copy-start.5 = (s32[1,16]{1,0:T(1,128)S(1)}, s32[1,16]{1,0:T(1,128)}, u32[]{:S(2)}) copy-start(s32[1,16]{1,0:T(1,128)} %len_ref.1) | copy-start | bytes 196
  6.0 0.7 %copy-start.4 = (s32[256]{0:T(256)S(1)}, s32[256]{0:T(256)}, u32[]{:S(2)}) copy-start(s32[256]{0:T(256)} %param.11) | copy-start | bytes 3076
  7.8 7.2 %copy-start = (s32[1024,256]{1,0:T(8,128)S(1)}, s32[1024,256]{1,0:T(8,128)}, u32[]{:S(2)}) copy-start(s32[1024,256]{1,0:T(8,128)} %bins_ref.1) | copy-start | bytes 3145732
  16.3 1.4 %collective-permute-start.2 = (f32[104,256]{1,0:T(8,128)S(1)}, f32[104,256]{1,0:T(8,128)S(1)}, u32[]{:S(2)}, u32[]{:S(2)}) collective-permute-start(f32[104,256]{1,0:T(8,128)S(1)} %histogram_part.7), channel_id=1, source_target_pairs={{0,4},{1,5},{2,6},{3,7},{4,0},{5,1},{6,2},{7,3},{8,12},{9,13},{10,... | collective-permute-start | bytes 319496 | tf_op jit(solution)/shard_map/ppermute | solution.py:495
  17.7 5.1 %collective-permute-start.4 = (f32[104,256]{1,0:T(8,128)S(1)}, f32[104,256]{1,0:T(8,128)S(1)}, u32[]{:S(2)}, u32[]{:S(2)}) collective-permute-start(f32[104,256]{1,0:T(8,128)S(1)} %pad_maximum_fusion.2), channel_id=1, source_target_pairs={{0,8},{1,9},{2,10},{3,11},{4,12},{5,13},{6,14},{7,15},{8,0},{9,1},... | collective-permute-start | bytes 319496 | tf_op jit(solution)/shard_map/ppermute | solution.py:495
  19.6 3.2 %collective-permute-start.3 = (f32[192,256]{1,0:T(8,128)S(1)}, f32[192,256]{1,0:T(8,128)S(1)}, u32[]{:S(2)}, u32[]{:S(2)}) collective-permute-start(f32[192,256]{1,0:T(8,128)S(1)} %histogram_part.9), channel_id=1, source_target_pairs={{0,4},{1,5},{2,6},{3,7},{4,0},{5,1},{6,2},{7,3},{8,12},{9,13},{10,... | collective-permute-start | bytes 589832 | tf_op jit(solution)/shard_map/ppermute | solution.py:495
  22.9 4.8 %collective-permute-start.7 = (f32[104,256]{1,0:T(8,128)S(1)}, f32[104,256]{1,0:T(8,128)S(1)}, u32[]{:S(2)}, u32[]{:S(2)}) collective-permute-start(f32[104,256]{1,0:T(8,128)S(1)} %get-tuple-element.40), channel_id=1, source_target_pairs={{0,16},{1,17},{2,18},{3,19},{4,20},{5,21},{6,22},{7,23},{8,24},{9,... | collective-permute-start | bytes 319496 | tf_op jit(solution)/shard_map/ppermute | solution.py:495
  23.6 4.7 %collective-permute-start.6 = (f32[104,256]{1,0:T(8,128)S(1)}, f32[104,256]{1,0:T(8,128)S(1)}, u32[]{:S(2)}, u32[]{:S(2)}) collective-permute-start(f32[104,256]{1,0:T(8,128)S(1)} %get-tuple-element.39), channel_id=1, source_target_pairs={{0,8},{1,9},{2,10},{3,11},{4,12},{5,13},{6,14},{7,15},{8,0},{9,1},... | collective-permute-start | bytes 319496 | tf_op jit(solution)/shard_map/ppermute | solution.py:495
  25.3 1.4 %collective-permute-start.5 = (f32[96,256]{1,0:T(8,128)S(1)}, f32[96,256]{1,0:T(8,128)S(1)}, u32[]{:S(2)}, u32[]{:S(2)}) collective-permute-start(f32[96,256]{1,0:T(8,128)S(1)} %histogram_part.11), channel_id=1, source_target_pairs={{0,4},{1,5},{2,6},{3,7},{4,0},{5,1},{6,2},{7,3},{8,12},{9,13},{10,... | collective-permute-start | bytes 294920 | tf_op jit(solution)/shard_map/ppermute | solution.py:495
  28.4 5.8 %collective-permute-start.10 = (f32[32,256]{1,0:T(8,128)S(1)}, f32[32,256]{1,0:T(8,128)S(1)}, u32[]{:S(2)}, u32[]{:S(2)}) collective-permute-start(f32[32,256]{1,0:T(8,128)S(1)} %get-tuple-element.50), channel_id=1, source_target_pairs={{0,3},{1,2},{2,1},{3,0},{4,7},{5,6},{6,5},{7,4},{8,11},{9,10},{10,... | collective-permute-start | bytes 98312 | tf_op jit(solution)/shard_map/ppermute | solution.py:495
  31.5 4.8 %collective-permute-start.8 = (f32[32,256]{1,0:T(8,128)S(1)}, f32[32,256]{1,0:T(8,128)S(1)}, u32[]{:S(2)}, u32[]{:S(2)}) collective-permute-start(f32[32,256]{1,0:T(8,128)S(1)} %get-tuple-element.52), channel_id=1, source_target_pairs={{0,2},{1,3},{2,0},{3,1},{4,6},{5,7},{6,4},{7,5},{8,10},{9,11},{10,... | collective-permute-start | bytes 98312 | tf_op jit(solution)/shard_map/ppermute | solution.py:495
  34.0 3.9 %collective-permute-start.9 = (f32[32,256]{1,0:T(8,128)S(1)}, f32[32,256]{1,0:T(8,128)S(1)}, u32[]{:S(2)}, u32[]{:S(2)}) collective-permute-start(f32[32,256]{1,0:T(8,128)S(1)} %get-tuple-element.51), channel_id=1, source_target_pairs={{0,1},{1,0},{2,3},{3,2},{4,5},{5,4},{6,7},{7,6},{8,9},{9,8},{10,11... | collective-permute-start | bytes 98312 | tf_op jit(solution)/shard_map/ppermute | solution.py:495

commit v19 on v18

--- a/solution.py
+++ b/solution.py
@@ -268,11 +268,19 @@
                 return tuple(acc)
             return step
 
+        def twice(low, high, step, acc):
+            twos = (high - low) // 2
+            acc = lax.fori_loop(0, twos, lambda k, acc: step(low + 2 * k + 1, step(low + 2 * k, acc)), acc)
+            return lax.fori_loop(low + 2 * twos, high, step, acc)
+
         acc = tuple(jnp.zeros((8, LANES), F32) for _ in range(8))
         low, inner_low, inner_high, high = spans(r)
+        whole = inner_low < inner_high
+        inner_low = jnp.where(whole, inner_low, low)
+        inner_high = jnp.where(whole, inner_high, low)
         acc = lax.fori_loop(low, inner_low, columns(True), acc)
-        acc = lax.fori_loop(inner_low, inner_high, columns(False), acc)
-        acc = lax.fori_loop(inner_high, high, columns(True), acc)
+        acc = twice(inner_low, inner_high, columns(False), acc)
+        acc = twice(inner_high, high, columns(True), acc)
         for g in range(2):
             at = pl.ds(2 * t + g, 1)
             grad[at, :] = -jnp.sum(acc[4 * g] + acc[4 * g + 1], axis=0, keepdims=True)
@@ -403,7 +411,7 @@
 
     if len(refs) > 1:
         out_ref[groups * 3 * HIGH:, :] = refs[0][...]
-    lax.fori_loop(0, groups, one_group, 0, unroll=4)
+    lax.fori_loop(0, groups, one_group, 0, unroll=min(groups, 8))
 
 
 def histogram_part(first, groups, tiles, bins_t, *tail):

time: 38.8 us -> 38.2 us (0.985)
  waiting for transfers between devices: 7.58 us -> 6.8 us
  Pallas kernels: 16.6 us -> 16.2 us
    ppermute x10, waiting for transfers between devices: 7.58 us -> 6.8 us  [swap(): return lax.ppermute(value, axes, [(p, p ^ mask) for p in range(count)])]
    pallas_call x6, Pallas kernels: 7.1 us -> 6.68 us  [histogram_part(): pl.pallas_call(functools.partial(histogram_kernel, first, groups), out_sh...]
  transfers between devices with their start and end apart: 11 -> 11, of which waited for: 8 -> 8; matrix products, arithmetic and copies ran while one was open for 0% -> 0% of each run, Pallas kernels for 19% -> 18%
where the time goes in v19:
time: 38.2 us; the launch traced here: 37.8 us
  Pallas kernels  16.2 us (42%)
  starting transfers between devices  12.4 us (32%)
  waiting for transfers between devices  6.8 us (18%)
  local copies, waits for them, and re-layouts  1.42 us (4%)
  between operations  0.79 us (2%)
    ppermute x10, starting transfers between devices, swap(): return lax.ppermute(value, axes, [(p, p ^ mask) for p in range(count)])  11.9 us
    pallas_call x1, Pallas kernels, pair_terms(): pl.pallas_call(functools.partial(pairs_kernel, feat_count), out_shape=(ja...  7.27 us
    ppermute x10, waiting for transfers between devices, swap(): return lax.ppermute(value, axes, [(p, p ^ mask) for p in range(count)])  6.8 us
    pallas_call x6, Pallas kernels, histogram_part(): pl.pallas_call(functools.partial(histogram_kernel, first, groups), out_sh...  6.68 us
    unnamed x12, local copies, waits for them, and re-layouts  1.41 us
    pallas_call x1, Pallas kernels, prepare(): pl.pallas_call(functools.partial(prepare_kernel, feat_count, masks), out_...  1.01 us
    pallas_call x1, Pallas kernels, finish(): pl.pallas_call(functools.partial(finish_kernel, per_dev), out_shape=(jax....  0.8 us
  transfers between devices with their start and end apart: 11, of which 8 were waited for; matrix products, arithmetic and copies ran while one was open for 0% of the time, Pallas kernels for 18%

profile of v19, /device:TPU:0, one launch (start us, length us, event | category | flops | bytes accessed | tf_op | source)
XLA Modules:
  0.0 37.8 jit_solution(279617738498244251)
XLA Ops:
  0.6 0.5 %collective-permute-start = (f32[8,128]{1,0:T(8,128)}, f32[8,128]{1,0:T(8,128)S(1)}, u32[]{:S(2)}, u32[]{:S(2)}) collective-permute-start(f32[8,128]{1,0:T(8,128)} %bitcast.9), channel_id=1, source_target_pairs={{0,4},{1,2},{2,1},{3,7},{4,0},{5,6},{6,5},{7,3},{8,12},{9,10},{10,... | collective-permute-start | bytes 12296 | tf_op jit(solution)/shard_map/ppermute | solution.py:515
  1.2 4.1 %collective-permute-start.1 = (f32[8,128]{1,0:T(8,128)}, f32[8,128]{1,0:T(8,128)S(1)}, u32[]{:S(2)}, u32[]{:S(2)}) collective-permute-start(f32[8,128]{1,0:T(8,128)} %bitcast.10), channel_id=1, source_target_pairs={{0,1},{1,0},{2,3},{3,2},{4,5},{5,4},{6,7},{7,6},{8,9},{9,8},{10,11... | collective-permute-start | bytes 12296 | tf_op jit(solution)/shard_map/ppermute | solution.py:503
  5.3 0.7 %copy-done.3 = f32[1024]{0:T(1024)S(1)} copy-done((f32[1024]{0:T(1024)S(1)}, f32[1024]{0:T(1024)}, u32[]{:S(2)}) %copy-start.3) | copy-done | bytes 4120
  6.0 0.7 %copy-done.4 = s32[256]{0:T(256)S(1)} copy-done((s32[256]{0:T(256)S(1)}, s32[256]{0:T(256)}, u32[]{:S(2)}) %copy-start.4) | copy-done | bytes 1048
  6.7 1.0 %prepare.1 = (f32[8,128]{1,0:T(8,128)S(1)}, s32[8,128]{1,0:T(8,128)S(1)}, f32[32,128]{1,0:T(8,128)S(1)}, f32[32,128]{1,0:T(8,128)S(1)}, f32[1,1024]{1,0:T(1,128)...) custom-call(s32[1,16]{1,0:T(1,128)S(1)} %copy-done.5, s32[1]{0:T(128)} %bitcast.pos_ref, s32[32,128]{1,0:T(8,128)S(1)} %bitcast.7, ...), custom_call_target="tpu_custom_call" | custom-call | flops 2000000000 | bytes 300000 | tf_op jit(solution)/shard_map/prepare/pallas_call | solution.py:113
  7.8 0.0 copy-start
  7.8 7.3 %pair_terms.1 = (f32[2,1024]{1,0:T(2,128)}, f32[2,1024]{1,0:T(2,128)S(1)}) custom-call(s32[8,128]{1,0:T(8,128)S(1)} %get-tuple-element.24.bounds_ref, s32[1]{0:T(128)} %bitcast.pos_ref, f32[8,128]{1,0:T(8,128)S(1)} %get-tuple-element.25.refs_0_, f32[8,128]{1,0:T(8,128)S(1)} %collective-permute-done.refs_1_, f32[8,128]{1,0:T(8,128)S(1)} %collective-permute-done.1.refs_2_, ...), custom_call_target="tpu_custom_call" | custom-call | flops 8999999488 | bytes 200000 | tf_op jit(solution)/shard_map/pair_terms/pallas_call | solution.py:305
  15.0 0.4 %leaf_terms.1 = (f32[256,1024]{1,0:T(8,128)S(1)}, bf16[32,1024]{1,0:T(8,128)(2,1)S(1)}, f32[8,256]{1,0:T(8,128)S(1)}) custom-call(bf16[256,256]{1,0:T(8,128)(2,1)S(1)} %get-tuple-element.31.perm_ref, s32[1024,256]{1,0:T(8,128)S(1)} %copy-done, s32[8,128]{1,0:T(8,128)S(1)} %get-tuple-element.30.leaf_ref, f32[2,1024]{1,0:T(2,128)S(1)} %get-tuple-element.32.lam_ref), custom_call_target="tpu_custom_call" | custom-call | flops 200000000 | bytes 3000000 | tf_op jit(solution)/shard_map/leaf_terms/pallas_call | solution.py:345
  15.5 0.9 %histogram_part.7 = f32[104,256]{1,0:T(8,128)S(1)} custom-call(bf16[32,1024]{1,0:T(8,128)(2,1)S(1)} %get-tuple-element.38.tile_ref, f32[256,1024]{1,0:T(8,128)S(1)} %get-tuple-element.34.bins_ref, f32[8,256]{1,0:T(8,128)S(1)} %get-tuple-element.35.refs_0_), custom_call_target="tpu_custom_call" | custom-call | flops 4000000 | bytes 4000 | tf_op jit(solution)/shard_map/histogram_part/pallas_call | solution.py:419
  16.4 0.1 collective-permute-start.2
  16.4 0.9 %histogram_part.6 = f32[96,256]{1,0:T(8,128)S(1)} custom-call(bf16[32,1024]{1,0:T(8,128)(2,1)S(1)} %get-tuple-element.38.tile_ref, f32[256,1024]{1,0:T(8,128)S(1)} %get-tuple-element.34.bins_ref), custom_call_target="tpu_custom_call" | custom-call | flops 4000000 | bytes 4000 | tf_op jit(solution)/shard_map/histogram_part/pallas_call | solution.py:419
  17.3 0.4 %collective-permute-done.2 = f32[104,256]{1,0:T(8,128)S(1)} collective-permute-done((f32[104,256]{1,0:T(8,128)S(1)}, f32[104,256]{1,0:T(8,128)S(1)}, u32[]{:S(2)}, u32[]{:S(2)}) %collective-permute-start.2) | collective-permute-done | bytes 106528 | tf_op jit(solution)/shard_map/ppermute | solution.py:503
  17.8 0.7 %collective-permute-start.4 = (f32[104,256]{1,0:T(8,128)S(1)}, f32[104,256]{1,0:T(8,128)S(1)}, u32[]{:S(2)}, u32[]{:S(2)}) collective-permute-start(f32[104,256]{1,0:T(8,128)S(1)} %pad_maximum_fusion.2), channel_id=1, source_target_pairs={{0,8},{1,9},{2,10},{3,11},{4,12},{5,13},{6,14},{7,15},{8,0},{9,1},... | collective-permute-start | bytes 319496 | tf_op jit(solution)/shard_map/ppermute | solution.py:503
  18.5 1.6 %histogram_part.9 = f32[192,256]{1,0:T(8,128)S(1)} custom-call(bf16[32,1024]{1,0:T(8,128)(2,1)S(1)} %get-tuple-element.38.tile_ref, f32[256,1024]{1,0:T(8,128)S(1)} %get-tuple-element.34.bins_ref), custom_call_target="tpu_custom_call" | custom-call | flops 8000000 | bytes 8000 | tf_op jit(solution)/shard_map/histogram_part/pallas_call | solution.py:419
  20.0 0.1 collective-permute-start.3
  20.1 1.6 %histogram_part.8 = f32[192,256]{1,0:T(8,128)S(1)} custom-call(bf16[32,1024]{1,0:T(8,128)(2,1)S(1)} %get-tuple-element.38.tile_ref, f32[256,1024]{1,0:T(8,128)S(1)} %get-tuple-element.34.bins_ref), custom_call_target="tpu_custom_call" | custom-call | flops 8000000 | bytes 8000 | tf_op jit(solution)/shard_map/histogram_part/pallas_call | solution.py:419
  21.7 1.2 %collective-permute-done.4 = f32[104,256]{1,0:T(8,128)S(1)} collective-permute-done((f32[104,256]{1,0:T(8,128)S(1)}, f32[104,256]{1,0:T(8,128)S(1)}, u32[]{:S(2)}, u32[]{:S(2)}) %collective-permute-start.4) | collective-permute-done | bytes 106528 | tf_op jit(solution)/shard_map/ppermute | solution.py:503
  23.0 2.0 %collective-permute-start.7 = (f32[104,256]{1,0:T(8,128)S(1)}, f32[104,256]{1,0:T(8,128)S(1)}, u32[]{:S(2)}, u32[]{:S(2)}) collective-permute-start(f32[104,256]{1,0:T(8,128)S(1)} %get-tuple-element.40), channel_id=1, source_target_pairs={{0,16},{1,17},{2,18},{3,19},{4,20},{5,21},{6,22},{7,23},{8,24},{9,... | collective-permute-start | bytes 319496 | tf_op jit(solution)/shard_map/ppermute | solution.py:503
  24.9 0.4 %collective-permute-start.6 = (f32[104,256]{1,0:T(8,128)S(1)}, f32[104,256]{1,0:T(8,128)S(1)}, u32[]{:S(2)}, u32[]{:S(2)}) collective-permute-start(f32[104,256]{1,0:T(8,128)S(1)} %get-tuple-element.39), channel_id=1, source_target_pairs={{0,8},{1,9},{2,10},{3,11},{4,12},{5,13},{6,14},{7,15},{8,0},{9,1},... | collective-permute-start | bytes 319496 | tf_op jit(solution)/shard_map/ppermute | solution.py:503
  25.4 0.9 %histogram_part.11 = f32[96,256]{1,0:T(8,128)S(1)} custom-call(bf16[32,1024]{1,0:T(8,128)(2,1)S(1)} %get-tuple-element.38.tile_ref, f32[256,1024]{1,0:T(8,128)S(1)} %get-tuple-element.34.bins_ref), custom_call_target="tpu_custom_call" | custom-call | flops 4000000 | bytes 4000 | tf_op jit(solution)/shard_map/histogram_part/pallas_call | solution.py:419
  26.3 0.1 collective-permute-start.5
  26.3 0.9 %histogram_part.10 = f32[96,256]{1,0:T(8,128)S(1)} custom-call(bf16[32,1024]{1,0:T(8,128)(2,1)S(1)} %get-tuple-element.38.tile_ref, f32[256,1024]{1,0:T(8,128)S(1)} %get-tuple-element.34.bins_ref), custom_call_target="tpu_custom_call" | custom-call | flops 4000000 | bytes 4000 | tf_op jit(solution)/shard_map/histogram_part/pallas_call | solution.py:419
  27.2 0.4 %collective-permute-done.5 = f32[96,256]{1,0:T(8,128)S(1)} collective-permute-done((f32[96,256]{1,0:T(8,128)S(1)}, f32[96,256]{1,0:T(8,128)S(1)}, u32[]{:S(2)}, u32[]{:S(2)}) %collective-permute-start.5) | collective-permute-done | bytes 98336 | tf_op jit(solution)/shard_map/ppermute | solution.py:503
  27.6 0.1 collective-permute-done.7
  27.7 1.9 %collective-permute-done.6 = f32[104,256]{1,0:T(8,128)S(1)} collective-permute-done((f32[104,256]{1,0:T(8,128)S(1)}, f32[104,256]{1,0:T(8,128)S(1)}, u32[]{:S(2)}, u32[]{:S(2)}) %collective-permute-start.6) | collective-permute-done | bytes 106528 | tf_op jit(solution)/shard_map/ppermute | solution.py:503
  29.7 1.8 %collective-permute-start.10 = (f32[32,256]{1,0:T(8,128)S(1)}, f32[32,256]{1,0:T(8,128)S(1)}, u32[]{:S(2)}, u32[]{:S(2)}) collective-permute-start(f32[32,256]{1,0:T(8,128)S(1)} %get-tuple-element.50), channel_id=1, source_target_pairs={{0,3},{1,2},{2,1},{3,0},{4,7},{5,6},{6,5},{7,4},{8,11},{9,10},{10,... | collective-permute-start | bytes 98312 | tf_op jit(solution)/shard_map/ppermute | solution.py:503
  31.6 1.4 %collective-permute-start.8 = (f32[32,256]{1,0:T(8,128)S(1)}, f32[32,256]{1,0:T(8,128)S(1)}, u32[]{:S(2)}, u32[]{:S(2)}) collective-permute-start(f32[32,256]{1,0:T(8,128)S(1)} %get-tuple-element.52), channel_id=1, source_target_pairs={{0,2},{1,3},{2,0},{3,1},{4,6},{5,7},{6,4},{7,5},{8,10},{9,11},{10,... | collective-permute-start | bytes 98312 | tf_op jit(solution)/shard_map/ppermute | solution.py:503
  32.9 1.2 %collective-permute-start.9 = (f32[32,256]{1,0:T(8,128)S(1)}, f32[32,256]{1,0:T(8,128)S(1)}, u32[]{:S(2)}, u32[]{:S(2)}) collective-permute-start(f32[32,256]{1,0:T(8,128)S(1)} %get-tuple-element.51), channel_id=1, source_target_pairs={{0,1},{1,0},{2,3},{3,2},{4,5},{5,4},{6,7},{7,6},{8,9},{9,8},{10,11... | collective-permute-start | bytes 98312 | tf_op jit(solution)/shard_map/ppermute | solution.py:503
  34.2 1.5 %collective-permute-done.10.refs_2_ = f32[32,256]{1,0:T(8,128)S(1)} collective-permute-done((f32[32,256]{1,0:T(8,128)S(1)}, f32[32,256]{1,0:T(8,128)S(1)}, u32[]{:S(2)}, u32[]{:S(2)}) %collective-permute-start.10) | collective-permute-done | bytes 32800 | tf_op jit(solution)/shard_map/ppermute | solution.py:503
  35.7 0.9 %collective-permute-done.8.refs_0_ = f32[32,256]{1,0:T(8,128)S(1)} collective-permute-done((f32[32,256]{1,0:T(8,128)S(1)}, f32[32,256]{1,0:T(8,128)S(1)}, u32[]{:S(2)}, u32[]{:S(2)}) %collective-permute-start.8) | collective-permute-done | bytes 32800 | tf_op jit(solution)/shard_map/ppermute | solution.py:503
  36.6 0.3 collective-permute-done.9.refs_1_
  37.0 0.8 %finish.1 = (f32[8,128]{1,0:T(8,128)}, f32[8,128]{1,0:T(8,128)}, f32[3,2048]{1,0:T(4,128)}) custom-call(s32[8,128]{1,0:T(8,128)S(1)} %get-tuple-element.30.leaf_ref, f32[24,256]{1,0:T(8,128)S(1)} %get-tuple-element.49.kept_ref, f32[8,256]{1,0:T(8,128)S(1)} %slice_add_fusion.4.sums_ref, f32[32,256]{1,0:T(8,128)S(1)} %collective-permute-done.8.refs_0_, ...), custom_call_target="tpu_custom_call" | custom-call | tf_op jit(solution)/shard_map/finish/pallas_call | solution.py:468
  (23 shorter events, 0.2 us)
Async XLA Ops:
  0.6 4.7 %copy-start.1 = (s32[4096]{0:T(1024)S(1)}, s32[4096]{0:T(1024)}, u32[]{:S(2)}) copy-start(s32[4096]{0:T(1024)} %param.7) | copy-start | bytes 49156
  0.6 7.1 %collective-permute-start = (f32[8,128]{1,0:T(8,128)}, f32[8,128]{1,0:T(8,128)S(1)}, u32[]{:S(2)}, u32[]{:S(2)}) collective-permute-start(f32[8,128]{1,0:T(8,128)} %bitcast.9), channel_id=1, source_target_pairs={{0,4},{1,2},{2,1},{3,7},{4,0},{5,6},{6,5},{7,3},{8,12},{9,10},{10,... | collective-permute-start | bytes 12296 | tf_op jit(solution)/shard_map/ppermute | solution.py:515
  1.2 6.6 %collective-permute-start.1 = (f32[8,128]{1,0:T(8,128)}, f32[8,128]{1,0:T(8,128)S(1)}, u32[]{:S(2)}, u32[]{:S(2)}) collective-permute-start(f32[8,128]{1,0:T(8,128)} %bitcast.10), channel_id=1, source_target_pairs={{0,1},{1,0},{2,3},{3,2},{4,5},{5,4},{6,7},{7,6},{8,9},{9,8},{10,11... | collective-permute-start | bytes 12296 | tf_op jit(solution)/shard_map/ppermute | solution.py:503
  5.3 0.7 %copy-start.3 = (f32[1024]{0:T(1024)S(1)}, f32[1024]{0:T(1024)}, u32[]{:S(2)}) copy-start(f32[1024]{0:T(1024)} %param.6) | copy-start | bytes 12292
  5.3 0.7 %copy-start.2 = (s32[1024]{0:T(1024)S(1)}, s32[1024]{0:T(1024)}, u32[]{:S(2)}) copy-start(s32[1024]{0:T(1024)} %param.8) | copy-start | bytes 12292
  5.3 0.7 %copy-start.5 = (s32[1,16]{1,0:T(1,128)S(1)}, s32[1,16]{1,0:T(1,128)}, u32[]{:S(2)}) copy-start(s32[1,16]{1,0:T(1,128)} %len_ref.1) | copy-start | bytes 196
  6.0 0.7 %copy-start.4 = (s32[256]{0:T(256)S(1)}, s32[256]{0:T(256)}, u32[]{:S(2)}) copy-start(s32[256]{0:T(256)} %param.11) | copy-start | bytes 3076
  7.8 7.3 %copy-start = (s32[1024,256]{1,0:T(8,128)S(1)}, s32[1024,256]{1,0:T(8,128)}, u32[]{:S(2)}) copy-start(s32[1024,256]{1,0:T(8,128)} %bins_ref.1) | copy-start | bytes 3145732
  16.4 1.4 %collective-permute-start.2 = (f32[104,256]{1,0:T(8,128)S(1)}, f32[104,256]{1,0:T(8,128)S(1)}, u32[]{:S(2)}, u32[]{:S(2)}) collective-permute-start(f32[104,256]{1,0:T(8,128)S(1)} %histogram_part.7), channel_id=1, source_target_pairs={{0,4},{1,5},{2,6},{3,7},{4,0},{5,1},{6,2},{7,3},{8,12},{9,13},{10,... | collective-permute-start | bytes 319496 | tf_op jit(solution)/shard_map/ppermute | solution.py:503
  17.8 5.1 %collective-permute-start.4 = (f32[104,256]{1,0:T(8,128)S(1)}, f32[104,256]{1,0:T(8,128)S(1)}, u32[]{:S(2)}, u32[]{:S(2)}) collective-permute-start(f32[104,256]{1,0:T(8,128)S(1)} %pad_maximum_fusion.2), channel_id=1, source_target_pairs={{0,8},{1,9},{2,10},{3,11},{4,12},{5,13},{6,14},{7,15},{8,0},{9,1},... | collective-permute-start | bytes 319496 | tf_op jit(solution)/shard_map/ppermute | solution.py:503
  20.0 2.8 %collective-permute-start.3 = (f32[192,256]{1,0:T(8,128)S(1)}, f32[192,256]{1,0:T(8,128)S(1)}, u32[]{:S(2)}, u32[]{:S(2)}) collective-permute-start(f32[192,256]{1,0:T(8,128)S(1)} %histogram_part.9), channel_id=1, source_target_pairs={{0,4},{1,5},{2,6},{3,7},{4,0},{5,1},{6,2},{7,3},{8,12},{9,13},{10,... | collective-permute-start | bytes 589832 | tf_op jit(solution)/shard_map/ppermute | solution.py:503
  23.0 4.8 %collective-permute-start.7 = (f32[104,256]{1,0:T(8,128)S(1)}, f32[104,256]{1,0:T(8,128)S(1)}, u32[]{:S(2)}, u32[]{:S(2)}) collective-permute-start(f32[104,256]{1,0:T(8,128)S(1)} %get-tuple-element.40), channel_id=1, source_target_pairs={{0,16},{1,17},{2,18},{3,19},{4,20},{5,21},{6,22},{7,23},{8,24},{9,... | collective-permute-start | bytes 319496 | tf_op jit(solution)/shard_map/ppermute | solution.py:503
  24.9 4.7 %collective-permute-start.6 = (f32[104,256]{1,0:T(8,128)S(1)}, f32[104,256]{1,0:T(8,128)S(1)}, u32[]{:S(2)}, u32[]{:S(2)}) collective-permute-start(f32[104,256]{1,0:T(8,128)S(1)} %get-tuple-element.39), channel_id=1, source_target_pairs={{0,8},{1,9},{2,10},{3,11},{4,12},{5,13},{6,14},{7,15},{8,0},{9,1},... | collective-permute-start | bytes 319496 | tf_op jit(solution)/shard_map/ppermute | solution.py:503
  26.3 1.4 %collective-permute-start.5 = (f32[96,256]{1,0:T(8,128)S(1)}, f32[96,256]{1,0:T(8,128)S(1)}, u32[]{:S(2)}, u32[]{:S(2)}) collective-permute-start(f32[96,256]{1,0:T(8,128)S(1)} %histogram_part.11), channel_id=1, source_target_pairs={{0,4},{1,5},{2,6},{3,7},{4,0},{5,1},{6,2},{7,3},{8,12},{9,13},{10,... | collective-permute-start | bytes 294920 | tf_op jit(solution)/shard_map/ppermute | solution.py:503
  29.7 6.0 %collective-permute-start.10 = (f32[32,256]{1,0:T(8,128)S(1)}, f32[32,256]{1,0:T(8,128)S(1)}, u32[]{:S(2)}, u32[]{:S(2)}) collective-permute-start(f32[32,256]{1,0:T(8,128)S(1)} %get-tuple-element.50), channel_id=1, source_target_pairs={{0,3},{1,2},{2,1},{3,0},{4,7},{5,6},{6,5},{7,4},{8,11},{9,10},{10,... | collective-permute-start | bytes 98312 | tf_op jit(solution)/shard_map/ppermute | solution.py:503
  31.6 5.1 %collective-permute-start.8 = (f32[32,256]{1,0:T(8,128)S(1)}, f32[32,256]{1,0:T(8,128)S(1)}, u32[]{:S(2)}, u32[]{:S(2)}) collective-permute-start(f32[32,256]{1,0:T(8,128)S(1)} %get-tuple-element.52), channel_id=1, source_target_pairs={{0,2},{1,3},{2,0},{3,1},{4,6},{5,7},{6,4},{7,5},{8,10},{9,11},{10,... | collective-permute-start | bytes 98312 | tf_op jit(solution)/shard_map/ppermute | solution.py:503
  32.9 4.0 %collective-permute-start.9 = (f32[32,256]{1,0:T(8,128)S(1)}, f32[32,256]{1,0:T(8,128)S(1)}, u32[]{:S(2)}, u32[]{:S(2)}) collective-permute-start(f32[32,256]{1,0:T(8,128)S(1)} %get-tuple-element.51), channel_id=1, source_target_pairs={{0,1},{1,0},{2,3},{3,2},{4,5},{5,4},{6,7},{7,6},{8,9},{9,8},{10,11... | collective-permute-start | bytes 98312 | tf_op jit(solution)/shard_map/ppermute | solution.py:503

commit v20 on v19

--- a/solution.py
+++ b/solution.py
@@ -179,14 +179,16 @@
     def rows_of(ref, r):
         return [jnp.broadcast_to(ref[pl.ds(r + g, 1), :], (8, LANES)) for g in range(2)]
 
+    per = LANES // CHUNK
+
     def spans(r):
         start, end = bounds_ref[0, r], bounds_ref[1, r + 1]
-        low = jnp.maximum(start // LANES, window_low)
-        high = jnp.minimum((end + LANES - 1) // LANES, window_high)
+        low = jnp.maximum(start // CHUNK, per * window_low)
+        high = jnp.minimum((end + CHUNK - 1) // CHUNK, per * window_high)
         single = bounds_ref[2, r] >= (r + 2) * LANES
-        inner_low = jnp.where(single, jnp.maximum((start + LANES - 1) // LANES, window_low), r)
-        inner_high = jnp.where(single, jnp.minimum(end // LANES, window_high), r)
-        return low, inner_low, inner_high, high
+        inner_low = jnp.maximum((start + LANES - 1) // LANES, window_low)
+        inner_high = jnp.minimum(end // LANES, window_high)
+        return low, high, single, inner_low, inner_high
 
     def rank_groups(k, carry):
         r = window_low + 2 * k
@@ -194,9 +196,10 @@
         query = rows_of(qid_ref, r)
 
         def gather(c, acc, masked, test):
-            base = pl.multiple_of(c * LANES, LANES)
+            size = CHUNK if masked else LANES
+            base = pl.multiple_of(c * size, size)
             acc = list(acc)
-            for u in range(LANES // 8):
+            for u in range(size // 8):
                 other = s_col[pl.ds(base + 8 * u, 8), :]
                 for g in range(2):
                     hit = test(other, g, u)
@@ -212,11 +215,11 @@
         def behind(other, g, u):
             return other > score[g]
 
-        def within(mine):
+        def within(mine, offset):
             def test(other, g, u):
                 if g != mine:
                     return ahead(other, g, u) if mine < g else behind(other, g, u)
-                earlier = iota((8, LANES), 0) + 8 * u < iota((8, LANES), 1)
+                earlier = iota((8, LANES), 0) + (offset + 8 * u) < iota((8, LANES), 1)
                 return (other > score[g]) | ((other == score[g]) & earlier)
             return test
 
@@ -227,14 +230,15 @@
             return lax.fori_loop(low + 2 * twos, high, lambda c, acc: gather(c, acc, False, test), acc)
 
         acc = tuple(jnp.zeros((8, LANES), F32) for _ in range(8))
-        low, inner_low, inner_high, high = spans(r)
-        after = jnp.maximum(inner_high, r + 2)
-        acc = lax.fori_loop(low, inner_low, lambda c, acc: gather(c, acc, True, ahead), acc)
+        low, high, single, inner_low, inner_high = spans(r)
+        inner_low = jnp.where(single, inner_low, r)
+        after = jnp.where(single, inner_high, r + 2)
+        acc = lax.fori_loop(low, per * inner_low, lambda c, acc: gather(c, acc, True, ahead), acc)
         acc = twice(inner_low, r, ahead, acc)
         acc = twice(r + 2, after, behind, acc)
-        acc = lax.fori_loop(after, high, lambda c, acc: gather(c, acc, True, behind), acc)
-        for mine in range(2):
-            acc = gather(r + mine, acc, True, within(mine))
+        acc = lax.fori_loop(per * after, high, lambda c, acc: gather(c, acc, True, behind), acc)
+        for c in range(2 * per):
+            acc = gather(per * r + c, acc, True, within(c // per, c % per * CHUNK))
         for g in range(2):
             total = (acc[4 * g] + acc[4 * g + 1]) + (acc[4 * g + 2] + acc[4 * g + 3])
             d_row[pl.ds(r + g, 1), :] = jnp.sum(total, axis=0, keepdims=True)
@@ -250,9 +254,10 @@
 
         def columns(masked):
             def step(c, acc):
-                base = pl.multiple_of(c * LANES, LANES)
+                size = CHUNK if masked else LANES
+                base = pl.multiple_of(c * size, size)
                 acc = list(acc)
-                for u in range(LANES // 8):
+                for u in range(size // 8):
                     at = pl.ds(base + 8 * u, 8)
                     a_j, w_j, d_j = a_col[at, :], w_col[at, :], d_col[at, :]
                     for g in range(2):
@@ -274,13 +279,10 @@
             return lax.fori_loop(low + 2 * twos, high, step, acc)
 
         acc = tuple(jnp.zeros((8, LANES), F32) for _ in range(8))
-        low, inner_low, inner_high, high = spans(r)
-        whole = inner_low < inner_high
-        inner_low = jnp.where(whole, inner_low, low)
-        inner_high = jnp.where(whole, inner_high, low)
-        acc = lax.fori_loop(low, inner_low, columns(True), acc)
-        acc = twice(inner_low, inner_high, columns(False), acc)
-        acc = twice(inner_high, high, columns(True), acc)
+        low, high, single, inner_low, inner_high = spans(r)
+        acc = lax.fori_loop(low, jnp.where(single, per * inner_low, low), columns(True), acc)
+        acc = twice(inner_low, jnp.where(single, inner_high, inner_low), columns(False), acc)
+        acc = twice(jnp.where(single, per * inner_high, low), high, columns(True), acc)
         for g in range(2):
             at = pl.ds(2 * t + g, 1)
             grad[at, :] = -jnp.sum(acc[4 * g] + acc[4 * g + 1], axis=0, keepdims=True)

time: 38.2 us -> 38.1 us (level); the launches traced: 37.8 us -> 38.4 us
  starting transfers between devices: 12.4 us -> 15.9 us
  Pallas kernels: 16.2 us -> 14.4 us
  waiting for transfers between devices: 6.8 us -> 5.85 us
    ppermute x10, starting transfers between devices: 11.9 us -> 15.3 us  [swap(): return lax.ppermute(value, axes, [(p, p ^ mask) for p in range(count)])]
    pallas_call x1, Pallas kernels: 7.27 us -> 5.48 us  [pair_terms(): pl.pallas_call(functools.partial(pairs_kernel, feat_count), out_shape=(ja...]
    ppermute x10, waiting for transfers between devices: 6.8 us -> 5.84 us  [swap(): return lax.ppermute(value, axes, [(p, p ^ mask) for p in range(count)])]
where the time goes in v20:
time: 38.1 us; the launch traced here: 38.4 us
  starting transfers between devices  15.9 us (42%)
  Pallas kernels  14.4 us (38%)
  waiting for transfers between devices  5.85 us (15%)
  local copies, waits for them, and re-layouts  1.42 us (4%)
  between operations  0.79 us (2%)
    ppermute x10, starting transfers between devices, swap(): return lax.ppermute(value, axes, [(p, p ^ mask) for p in range(count)])  15.3 us
    pallas_call x6, Pallas kernels, histogram_part(): pl.pallas_call(functools.partial(histogram_kernel, first, groups), out_sh...  6.68 us
    ppermute x10, waiting for transfers between devices, swap(): return lax.ppermute(value, axes, [(p, p ^ mask) for p in range(count)])  5.84 us
    pallas_call x1, Pallas kernels, pair_terms(): pl.pallas_call(functools.partial(pairs_kernel, feat_count), out_shape=(ja...  5.48 us
    unnamed x12, local copies, waits for them, and re-layouts  1.41 us
    pallas_call x1, Pallas kernels, prepare(): pl.pallas_call(functools.partial(prepare_kernel, feat_count, masks), out_...  1.01 us
    pallas_call x1, Pallas kernels, finish(): pl.pallas_call(functools.partial(finish_kernel, per_dev), out_shape=(jax....  0.8 us
  transfers between devices with their start and end apart: 11, of which 8 were waited for; matrix products, arithmetic and copies ran while one was open for 0% of the time, Pallas kernels for 18%

profile of v20, /device:TPU:0, one launch (start us, length us, event | category | flops | bytes accessed | tf_op | source)
XLA Modules:
  0.0 38.4 jit_solution(16531072628709807458)
XLA Ops:
  0.6 0.5 %collective-permute-start = (f32[8,128]{1,0:T(8,128)}, f32[8,128]{1,0:T(8,128)S(1)}, u32[]{:S(2)}, u32[]{:S(2)}) collective-permute-start(f32[8,128]{1,0:T(8,128)} %bitcast.9), channel_id=1, source_target_pairs={{0,4},{1,2},{2,1},{3,7},{4,0},{5,6},{6,5},{7,3},{8,12},{9,10},{10,... | collective-permute-start | bytes 12296 | tf_op jit(solution)/shard_map/ppermute | solution.py:517
  1.2 4.1 %collective-permute-start.1 = (f32[8,128]{1,0:T(8,128)}, f32[8,128]{1,0:T(8,128)S(1)}, u32[]{:S(2)}, u32[]{:S(2)}) collective-permute-start(f32[8,128]{1,0:T(8,128)} %bitcast.10), channel_id=1, source_target_pairs={{0,1},{1,0},{2,3},{3,2},{4,5},{5,4},{6,7},{7,6},{8,9},{9,8},{10,11... | collective-permute-start | bytes 12296 | tf_op jit(solution)/shard_map/ppermute | solution.py:505
  5.3 0.7 %copy-done.3 = f32[1024]{0:T(1024)S(1)} copy-done((f32[1024]{0:T(1024)S(1)}, f32[1024]{0:T(1024)}, u32[]{:S(2)}) %copy-start.3) | copy-done | bytes 4120
  6.0 0.7 %copy-done.4 = s32[256]{0:T(256)S(1)} copy-done((s32[256]{0:T(256)S(1)}, s32[256]{0:T(256)}, u32[]{:S(2)}) %copy-start.4) | copy-done | bytes 1048
  6.7 1.0 %prepare.1 = (f32[8,128]{1,0:T(8,128)S(1)}, s32[8,128]{1,0:T(8,128)S(1)}, f32[32,128]{1,0:T(8,128)S(1)}, f32[32,128]{1,0:T(8,128)S(1)}, f32[1,1024]{1,0:T(1,128)...) custom-call(s32[1,16]{1,0:T(1,128)S(1)} %copy-done.5, s32[1]{0:T(128)} %bitcast.pos_ref, s32[32,128]{1,0:T(8,128)S(1)} %bitcast.7, ...), custom_call_target="tpu_custom_call" | custom-call | flops 2000000000 | bytes 300000 | tf_op jit(solution)/shard_map/prepare/pallas_call | solution.py:113
  7.7 0.0 collective-permute-done.1.refs_2_
  7.8 0.0 copy-start
  7.8 5.5 %pair_terms.1 = (f32[2,1024]{1,0:T(2,128)}, f32[2,1024]{1,0:T(2,128)S(1)}) custom-call(s32[8,128]{1,0:T(8,128)S(1)} %get-tuple-element.24.bounds_ref, s32[1]{0:T(128)} %bitcast.pos_ref, f32[8,128]{1,0:T(8,128)S(1)} %get-tuple-element.25.refs_0_, f32[8,128]{1,0:T(8,128)S(1)} %collective-permute-done.refs_1_, f32[8,128]{1,0:T(8,128)S(1)} %collective-permute-done.1.refs_2_, ...), custom_call_target="tpu_custom_call" | custom-call | flops 8999999488 | bytes 200000 | tf_op jit(solution)/shard_map/pair_terms/pallas_call | solution.py:307
  13.2 0.4 %leaf_terms.1 = (f32[256,1024]{1,0:T(8,128)S(1)}, bf16[32,1024]{1,0:T(8,128)(2,1)S(1)}, f32[8,256]{1,0:T(8,128)S(1)}) custom-call(bf16[256,256]{1,0:T(8,128)(2,1)S(1)} %get-tuple-element.31.perm_ref, s32[1024,256]{1,0:T(8,128)S(1)} %copy-done, s32[8,128]{1,0:T(8,128)S(1)} %get-tuple-element.30.leaf_ref, f32[2,1024]{1,0:T(2,128)S(1)} %get-tuple-element.32.lam_ref), custom_call_target="tpu_custom_call" | custom-call | flops 200000000 | bytes 3000000 | tf_op jit(solution)/shard_map/leaf_terms/pallas_call | solution.py:347
  13.7 0.9 %histogram_part.7 = f32[104,256]{1,0:T(8,128)S(1)} custom-call(bf16[32,1024]{1,0:T(8,128)(2,1)S(1)} %get-tuple-element.38.tile_ref, f32[256,1024]{1,0:T(8,128)S(1)} %get-tuple-element.34.bins_ref, f32[8,256]{1,0:T(8,128)S(1)} %get-tuple-element.35.refs_0_), custom_call_target="tpu_custom_call" | custom-call | flops 4000000 | bytes 4000 | tf_op jit(solution)/shard_map/histogram_part/pallas_call | solution.py:421
  14.6 0.1 collective-permute-start.2
  14.6 0.9 %histogram_part.6 = f32[96,256]{1,0:T(8,128)S(1)} custom-call(bf16[32,1024]{1,0:T(8,128)(2,1)S(1)} %get-tuple-element.38.tile_ref, f32[256,1024]{1,0:T(8,128)S(1)} %get-tuple-element.34.bins_ref), custom_call_target="tpu_custom_call" | custom-call | flops 4000000 | bytes 4000 | tf_op jit(solution)/shard_map/histogram_part/pallas_call | solution.py:421
  15.5 0.4 %collective-permute-done.2 = f32[104,256]{1,0:T(8,128)S(1)} collective-permute-done((f32[104,256]{1,0:T(8,128)S(1)}, f32[104,256]{1,0:T(8,128)S(1)}, u32[]{:S(2)}, u32[]{:S(2)}) %collective-permute-start.2) | collective-permute-done | bytes 106528 | tf_op jit(solution)/shard_map/ppermute | solution.py:505
  16.0 3.5 %collective-permute-start.4 = (f32[104,256]{1,0:T(8,128)S(1)}, f32[104,256]{1,0:T(8,128)S(1)}, u32[]{:S(2)}, u32[]{:S(2)}) collective-permute-start(f32[104,256]{1,0:T(8,128)S(1)} %pad_maximum_fusion.2), channel_id=1, source_target_pairs={{0,8},{1,9},{2,10},{3,11},{4,12},{5,13},{6,14},{7,15},{8,0},{9,1},... | collective-permute-start | bytes 319496 | tf_op jit(solution)/shard_map/ppermute | solution.py:505
  19.5 1.6 %histogram_part.9 = f32[192,256]{1,0:T(8,128)S(1)} custom-call(bf16[32,1024]{1,0:T(8,128)(2,1)S(1)} %get-tuple-element.38.tile_ref, f32[256,1024]{1,0:T(8,128)S(1)} %get-tuple-element.34.bins_ref), custom_call_target="tpu_custom_call" | custom-call | flops 8000000 | bytes 8000 | tf_op jit(solution)/shard_map/histogram_part/pallas_call | solution.py:421
  21.0 0.1 collective-permute-start.3
  21.1 1.6 %histogram_part.8 = f32[192,256]{1,0:T(8,128)S(1)} custom-call(bf16[32,1024]{1,0:T(8,128)(2,1)S(1)} %get-tuple-element.38.tile_ref, f32[256,1024]{1,0:T(8,128)S(1)} %get-tuple-element.34.bins_ref), custom_call_target="tpu_custom_call" | custom-call | flops 8000000 | bytes 8000 | tf_op jit(solution)/shard_map/histogram_part/pallas_call | solution.py:421
  22.7 0.1 collective-permute-done.4
  22.8 0.8 %collective-permute-start.7 = (f32[104,256]{1,0:T(8,128)S(1)}, f32[104,256]{1,0:T(8,128)S(1)}, u32[]{:S(2)}, u32[]{:S(2)}) collective-permute-start(f32[104,256]{1,0:T(8,128)S(1)} %get-tuple-element.40), channel_id=1, source_target_pairs={{0,16},{1,17},{2,18},{3,19},{4,20},{5,21},{6,22},{7,23},{8,24},{9,... | collective-permute-start | bytes 319496 | tf_op jit(solution)/shard_map/ppermute | solution.py:505
  23.6 1.5 %collective-permute-start.6 = (f32[104,256]{1,0:T(8,128)S(1)}, f32[104,256]{1,0:T(8,128)S(1)}, u32[]{:S(2)}, u32[]{:S(2)}) collective-permute-start(f32[104,256]{1,0:T(8,128)S(1)} %get-tuple-element.39), channel_id=1, source_target_pairs={{0,8},{1,9},{2,10},{3,11},{4,12},{5,13},{6,14},{7,15},{8,0},{9,1},... | collective-permute-start | bytes 319496 | tf_op jit(solution)/shard_map/ppermute | solution.py:505
  25.1 0.9 %histogram_part.11 = f32[96,256]{1,0:T(8,128)S(1)} custom-call(bf16[32,1024]{1,0:T(8,128)(2,1)S(1)} %get-tuple-element.38.tile_ref, f32[256,1024]{1,0:T(8,128)S(1)} %get-tuple-element.34.bins_ref), custom_call_target="tpu_custom_call" | custom-call | flops 4000000 | bytes 4000 | tf_op jit(solution)/shard_map/histogram_part/pallas_call | solution.py:421
  26.0 0.1 collective-permute-start.5
  26.1 0.9 %histogram_part.10 = f32[96,256]{1,0:T(8,128)S(1)} custom-call(bf16[32,1024]{1,0:T(8,128)(2,1)S(1)} %get-tuple-element.38.tile_ref, f32[256,1024]{1,0:T(8,128)S(1)} %get-tuple-element.34.bins_ref), custom_call_target="tpu_custom_call" | custom-call | flops 4000000 | bytes 4000 | tf_op jit(solution)/shard_map/histogram_part/pallas_call | solution.py:421
  27.0 0.4 %collective-permute-done.5 = f32[96,256]{1,0:T(8,128)S(1)} collective-permute-done((f32[96,256]{1,0:T(8,128)S(1)}, f32[96,256]{1,0:T(8,128)S(1)}, u32[]{:S(2)}, u32[]{:S(2)}) %collective-permute-start.5) | collective-permute-done | bytes 98336 | tf_op jit(solution)/shard_map/ppermute | solution.py:505
  27.4 0.8 %collective-permute-done.7 = f32[104,256]{1,0:T(8,128)S(1)} collective-permute-done((f32[104,256]{1,0:T(8,128)S(1)}, f32[104,256]{1,0:T(8,128)S(1)}, u32[]{:S(2)}, u32[]{:S(2)}) %collective-permute-start.7) | collective-permute-done | bytes 106528 | tf_op jit(solution)/shard_map/ppermute | solution.py:505
  28.2 0.2 collective-permute-done.6
  28.5 2.3 %collective-permute-start.10 = (f32[32,256]{1,0:T(8,128)S(1)}, f32[32,256]{1,0:T(8,128)S(1)}, u32[]{:S(2)}, u32[]{:S(2)}) collective-permute-start(f32[32,256]{1,0:T(8,128)S(1)} %get-tuple-element.50), channel_id=1, source_target_pairs={{0,3},{1,2},{2,1},{3,0},{4,7},{5,6},{6,5},{7,4},{8,11},{9,10},{10,... | collective-permute-start | bytes 98312 | tf_op jit(solution)/shard_map/ppermute | solution.py:505
  30.8 2.9 %collective-permute-start.8 = (f32[32,256]{1,0:T(8,128)S(1)}, f32[32,256]{1,0:T(8,128)S(1)}, u32[]{:S(2)}, u32[]{:S(2)}) collective-permute-start(f32[32,256]{1,0:T(8,128)S(1)} %get-tuple-element.52), channel_id=1, source_target_pairs={{0,2},{1,3},{2,0},{3,1},{4,6},{5,7},{6,4},{7,5},{8,10},{9,11},{10,... | collective-permute-start | bytes 98312 | tf_op jit(solution)/shard_map/ppermute | solution.py:505
  33.7 0.7 %collective-permute-done.10.refs_2_ = f32[32,256]{1,0:T(8,128)S(1)} collective-permute-done((f32[32,256]{1,0:T(8,128)S(1)}, f32[32,256]{1,0:T(8,128)S(1)}, u32[]{:S(2)}, u32[]{:S(2)}) %collective-permute-start.10) | collective-permute-done | bytes 32800 | tf_op jit(solution)/shard_map/ppermute | solution.py:505
  34.4 1.5 %collective-permute-done.8.refs_0_ = f32[32,256]{1,0:T(8,128)S(1)} collective-permute-done((f32[32,256]{1,0:T(8,128)S(1)}, f32[32,256]{1,0:T(8,128)S(1)}, u32[]{:S(2)}, u32[]{:S(2)}) %collective-permute-start.8) | collective-permute-done | bytes 32800 | tf_op jit(solution)/shard_map/ppermute | solution.py:505
  36.0 1.7 %collective-permute-done.9.refs_1_ = f32[32,256]{1,0:T(8,128)S(1)} collective-permute-done((f32[32,256]{1,0:T(8,128)S(1)}, f32[32,256]{1,0:T(8,128)S(1)}, u32[]{:S(2)}, u32[]{:S(2)}) %collective-permute-start.9) | collective-permute-done | bytes 32800 | tf_op jit(solution)/shard_map/ppermute | solution.py:505
  37.6 0.8 %finish.1 = (f32[8,128]{1,0:T(8,128)}, f32[8,128]{1,0:T(8,128)}, f32[3,2048]{1,0:T(4,128)}) custom-call(s32[8,128]{1,0:T(8,128)S(1)} %get-tuple-element.30.leaf_ref, f32[24,256]{1,0:T(8,128)S(1)} %get-tuple-element.49.kept_ref, f32[8,256]{1,0:T(8,128)S(1)} %slice_add_fusion.4.sums_ref, f32[32,256]{1,0:T(8,128)S(1)} %collective-permute-done.8.refs_0_, ...), custom_call_target="tpu_custom_call" | custom-call | tf_op jit(solution)/shard_map/finish/pallas_call | solution.py:470
  (23 shorter events, 0.2 us)
Async XLA Ops:
  0.6 4.7 %copy-start.1 = (s32[4096]{0:T(1024)S(1)}, s32[4096]{0:T(1024)}, u32[]{:S(2)}) copy-start(s32[4096]{0:T(1024)} %param.7) | copy-start | bytes 49156
  0.6 7.1 %collective-permute-start = (f32[8,128]{1,0:T(8,128)}, f32[8,128]{1,0:T(8,128)S(1)}, u32[]{:S(2)}, u32[]{:S(2)}) collective-permute-start(f32[8,128]{1,0:T(8,128)} %bitcast.9), channel_id=1, source_target_pairs={{0,4},{1,2},{2,1},{3,7},{4,0},{5,6},{6,5},{7,3},{8,12},{9,10},{10,... | collective-permute-start | bytes 12296 | tf_op jit(solution)/shard_map/ppermute | solution.py:517
  1.2 6.6 %collective-permute-start.1 = (f32[8,128]{1,0:T(8,128)}, f32[8,128]{1,0:T(8,128)S(1)}, u32[]{:S(2)}, u32[]{:S(2)}) collective-permute-start(f32[8,128]{1,0:T(8,128)} %bitcast.10), channel_id=1, source_target_pairs={{0,1},{1,0},{2,3},{3,2},{4,5},{5,4},{6,7},{7,6},{8,9},{9,8},{10,11... | collective-permute-start | bytes 12296 | tf_op jit(solution)/shard_map/ppermute | solution.py:505
  5.3 0.7 %copy-start.3 = (f32[1024]{0:T(1024)S(1)}, f32[1024]{0:T(1024)}, u32[]{:S(2)}) copy-start(f32[1024]{0:T(1024)} %param.6) | copy-start | bytes 12292
  5.3 0.7 %copy-start.2 = (s32[1024]{0:T(1024)S(1)}, s32[1024]{0:T(1024)}, u32[]{:S(2)}) copy-start(s32[1024]{0:T(1024)} %param.8) | copy-start | bytes 12292
  5.3 0.7 %copy-start.5 = (s32[1,16]{1,0:T(1,128)S(1)}, s32[1,16]{1,0:T(1,128)}, u32[]{:S(2)}) copy-start(s32[1,16]{1,0:T(1,128)} %len_ref.1) | copy-start | bytes 196
  6.0 0.7 %copy-start.4 = (s32[256]{0:T(256)S(1)}, s32[256]{0:T(256)}, u32[]{:S(2)}) copy-start(s32[256]{0:T(256)} %param.11) | copy-start | bytes 3076
  7.8 5.5 %copy-start = (s32[1024,256]{1,0:T(8,128)S(1)}, s32[1024,256]{1,0:T(8,128)}, u32[]{:S(2)}) copy-start(s32[1024,256]{1,0:T(8,128)} %bins_ref.1) | copy-start | bytes 3145732
  14.6 1.4 %collective-permute-start.2 = (f32[104,256]{1,0:T(8,128)S(1)}, f32[104,256]{1,0:T(8,128)S(1)}, u32[]{:S(2)}, u32[]{:S(2)}) collective-permute-start(f32[104,256]{1,0:T(8,128)S(1)} %histogram_part.7), channel_id=1, source_target_pairs={{0,4},{1,5},{2,6},{3,7},{4,0},{5,1},{6,2},{7,3},{8,12},{9,13},{10,... | collective-permute-start | bytes 319496 | tf_op jit(solution)/shard_map/ppermute | solution.py:505
  16.0 6.8 %collective-permute-start.4 = (f32[104,256]{1,0:T(8,128)S(1)}, f32[104,256]{1,0:T(8,128)S(1)}, u32[]{:S(2)}, u32[]{:S(2)}) collective-permute-start(f32[104,256]{1,0:T(8,128)S(1)} %pad_maximum_fusion.2), channel_id=1, source_target_pairs={{0,8},{1,9},{2,10},{3,11},{4,12},{5,13},{6,14},{7,15},{8,0},{9,1},... | collective-permute-start | bytes 319496 | tf_op jit(solution)/shard_map/ppermute | solution.py:505
  21.0 1.7 %collective-permute-start.3 = (f32[192,256]{1,0:T(8,128)S(1)}, f32[192,256]{1,0:T(8,128)S(1)}, u32[]{:S(2)}, u32[]{:S(2)}) collective-permute-start(f32[192,256]{1,0:T(8,128)S(1)} %histogram_part.9), channel_id=1, source_target_pairs={{0,4},{1,5},{2,6},{3,7},{4,0},{5,1},{6,2},{7,3},{8,12},{9,13},{10,... | collective-permute-start | bytes 589832 | tf_op jit(solution)/shard_map/ppermute | solution.py:505
  22.8 5.4 %collective-permute-start.7 = (f32[104,256]{1,0:T(8,128)S(1)}, f32[104,256]{1,0:T(8,128)S(1)}, u32[]{:S(2)}, u32[]{:S(2)}) collective-permute-start(f32[104,256]{1,0:T(8,128)S(1)} %get-tuple-element.40), channel_id=1, source_target_pairs={{0,16},{1,17},{2,18},{3,19},{4,20},{5,21},{6,22},{7,23},{8,24},{9,... | collective-permute-start | bytes 319496 | tf_op jit(solution)/shard_map/ppermute | solution.py:505
  23.6 4.8 %collective-permute-start.6 = (f32[104,256]{1,0:T(8,128)S(1)}, f32[104,256]{1,0:T(8,128)S(1)}, u32[]{:S(2)}, u32[]{:S(2)}) collective-permute-start(f32[104,256]{1,0:T(8,128)S(1)} %get-tuple-element.39), channel_id=1, source_target_pairs={{0,8},{1,9},{2,10},{3,11},{4,12},{5,13},{6,14},{7,15},{8,0},{9,1},... | collective-permute-start | bytes 319496 | tf_op jit(solution)/shard_map/ppermute | solution.py:505
  26.0 1.4 %collective-permute-start.5 = (f32[96,256]{1,0:T(8,128)S(1)}, f32[96,256]{1,0:T(8,128)S(1)}, u32[]{:S(2)}, u32[]{:S(2)}) collective-permute-start(f32[96,256]{1,0:T(8,128)S(1)} %histogram_part.11), channel_id=1, source_target_pairs={{0,4},{1,5},{2,6},{3,7},{4,0},{5,1},{6,2},{7,3},{8,12},{9,13},{10,... | collective-permute-start | bytes 294920 | tf_op jit(solution)/shard_map/ppermute | solution.py:505
  28.5 5.9 %collective-permute-start.10 = (f32[32,256]{1,0:T(8,128)S(1)}, f32[32,256]{1,0:T(8,128)S(1)}, u32[]{:S(2)}, u32[]{:S(2)}) collective-permute-start(f32[32,256]{1,0:T(8,128)S(1)} %get-tuple-element.50), channel_id=1, source_target_pairs={{0,3},{1,2},{2,1},{3,0},{4,7},{5,6},{6,5},{7,4},{8,11},{9,10},{10,... | collective-permute-start | bytes 98312 | tf_op jit(solution)/shard_map/ppermute | solution.py:505
  30.8 5.1 %collective-permute-start.8 = (f32[32,256]{1,0:T(8,128)S(1)}, f32[32,256]{1,0:T(8,128)S(1)}, u32[]{:S(2)}, u32[]{:S(2)}) collective-permute-start(f32[32,256]{1,0:T(8,128)S(1)} %get-tuple-element.52), channel_id=1, source_target_pairs={{0,2},{1,3},{2,0},{3,1},{4,6},{5,7},{6,4},{7,5},{8,10},{9,11},{10,... | collective-permute-start | bytes 98312 | tf_op jit(solution)/shard_map/ppermute | solution.py:505
  33.7 3.9 %collective-permute-start.9 = (f32[32,256]{1,0:T(8,128)S(1)}, f32[32,256]{1,0:T(8,128)S(1)}, u32[]{:S(2)}, u32[]{:S(2)}) collective-permute-start(f32[32,256]{1,0:T(8,128)S(1)} %get-tuple-element.51), channel_id=1, source_target_pairs={{0,1},{1,0},{2,3},{3,2},{4,5},{5,4},{6,7},{7,6},{8,9},{9,8},{10,11... | collective-permute-start | bytes 98312 | tf_op jit(solution)/shard_map/ppermute | solution.py:505

commit v21 on v20

--- a/solution.py
+++ b/solution.py
@@ -540,15 +540,16 @@
     sums = sums + arrived[edge:]
     message, tiles = lax.optimization_barrier((join(block, sums), tiles))
     crossed_far = swap(message, query_masks[1])
-    arrived = swap(part(tiles, 5 * eighth, 7 * eighth), query_masks[0])
-    both = part(tiles, eighth, 3 * eighth) + arrived
+    arrived = swap(part(tiles, 6 * eighth, 7 * eighth), query_masks[0])
+    rest = part(tiles, 2 * eighth, 3 * eighth) + arrived
+    rest, tiles = lax.optimization_barrier((join(rest, sums), tiles))
+    crossed_near = swap(rest, query_masks[1])
+    arrived = swap(part(tiles, 4 * eighth, 6 * eighth), query_masks[0])
+    block = part(tiles, eighth, 2 * eighth) + arrived[edge:] + crossed_far[:edge]
     sums = sums + crossed_far[edge:]
-    message, rest, tiles = lax.optimization_barrier(
-        (join(both[:edge] + crossed_far[:edge], sums), join(both[edge:], sums), tiles))
+    message, tiles = lax.optimization_barrier((join(block, sums), tiles))
     turned = swap(message, query_masks[2])
-    crossed_near = swap(rest, query_masks[1])
-    arrived = swap(part(tiles, 4 * eighth, 5 * eighth), query_masks[0])
-    kept = part(tiles, 0, eighth) + arrived + crossed_near[:edge] + turned[:edge]
+    kept = part(tiles, 0, eighth) + arrived[:edge] + crossed_near[:edge] + turned[:edge]
     sums = sums + turned[edge:]
     for mask in query_masks[3:]:
         edge = edge // 2

time: 38.1 us -> 39.1 us (1.026)
  Pallas kernels: 14.4 us -> 15.8 us
  starting transfers between devices: 15.9 us -> 14.7 us
  waiting for transfers between devices: 5.85 us -> 6.74 us
    pallas_call x1, Pallas kernels: 5.48 us -> 6.7 us  [pair_terms(): pl.pallas_call(functools.partial(pairs_kernel, feat_count), out_shape=(ja...]
    ppermute x10, starting transfers between devices: 15.3 us -> 14.2 us  [swap(): return lax.ppermute(value, axes, [(p, p ^ mask) for p in range(count)])]
    ppermute x10, waiting for transfers between devices: 5.84 us -> 6.74 us  [swap(): return lax.ppermute(value, axes, [(p, p ^ mask) for p in range(count)])]
    pallas_call x6 -> x7, Pallas kernels: 6.68 us -> 6.88 us  [histogram_part(): pl.pallas_call(functools.partial(histogram_kernel, first, groups), out_sh...]
  transfers between devices with their start and end apart: 11 -> 11, of which waited for: 8 -> 6; matrix products, arithmetic and copies ran while one was open for 0% -> 0% of each run, Pallas kernels for 18% -> 15%
where the time goes in v21:
time: 39.1 us; the launch traced here: 39.7 us
  Pallas kernels  15.8 us (40%)
  starting transfers between devices  14.7 us (38%)
  waiting for transfers between devices  6.74 us (17%)
  local copies, waits for them, and re-layouts  1.42 us (4%)
  between operations  0.83 us (2%)
    ppermute x10, starting transfers between devices, swap(): return lax.ppermute(value, axes, [(p, p ^ mask) for p in range(count)])  14.2 us
    pallas_call x7, Pallas kernels, histogram_part(): pl.pallas_call(functools.partial(histogram_kernel, first, groups), out_sh...  6.88 us
    ppermute x10, waiting for transfers between devices, swap(): return lax.ppermute(value, axes, [(p, p ^ mask) for p in range(count)])  6.74 us
    pallas_call x1, Pallas kernels, pair_terms(): pl.pallas_call(functools.partial(pairs_kernel, feat_count), out_shape=(ja...  6.7 us
    unnamed x12, local copies, waits for them, and re-layouts  1.41 us
    pallas_call x1, Pallas kernels, prepare(): pl.pallas_call(functools.partial(prepare_kernel, feat_count, masks), out_...  1.01 us
    pallas_call x1, Pallas kernels, finish(): pl.pallas_call(functools.partial(finish_kernel, per_dev), out_shape=(jax....  0.8 us
  transfers between devices with their start and end apart: 11, of which 6 were waited for; matrix products, arithmetic and copies ran while one was open for 0% of the time, Pallas kernels for 15%

profile of v21, /device:TPU:0, one launch (start us, length us, event | category | flops | bytes accessed | tf_op | source)
XLA Modules:
  0.0 39.7 jit_solution(13961706700406561273)
XLA Ops:
  0.6 0.5 %collective-permute-start = (f32[8,128]{1,0:T(8,128)}, f32[8,128]{1,0:T(8,128)S(1)}, u32[]{:S(2)}, u32[]{:S(2)}) collective-permute-start(f32[8,128]{1,0:T(8,128)} %bitcast.9), channel_id=1, source_target_pairs={{0,4},{1,2},{2,1},{3,7},{4,0},{5,6},{6,5},{7,3},{8,12},{9,10},{10,... | collective-permute-start | bytes 12296 | tf_op jit(solution)/shard_map/ppermute | solution.py:517
  1.2 4.1 %collective-permute-start.1 = (f32[8,128]{1,0:T(8,128)}, f32[8,128]{1,0:T(8,128)S(1)}, u32[]{:S(2)}, u32[]{:S(2)}) collective-permute-start(f32[8,128]{1,0:T(8,128)} %bitcast.10), channel_id=1, source_target_pairs={{0,1},{1,0},{2,3},{3,2},{4,5},{5,4},{6,7},{7,6},{8,9},{9,8},{10,11... | collective-permute-start | bytes 12296 | tf_op jit(solution)/shard_map/ppermute | solution.py:505
  5.3 0.7 %copy-done.3 = f32[1024]{0:T(1024)S(1)} copy-done((f32[1024]{0:T(1024)S(1)}, f32[1024]{0:T(1024)}, u32[]{:S(2)}) %copy-start.3) | copy-done | bytes 4120
  6.0 0.7 %copy-done.4 = s32[256]{0:T(256)S(1)} copy-done((s32[256]{0:T(256)S(1)}, s32[256]{0:T(256)}, u32[]{:S(2)}) %copy-start.4) | copy-done | bytes 1048
  6.7 1.0 %prepare.1 = (f32[8,128]{1,0:T(8,128)S(1)}, s32[8,128]{1,0:T(8,128)S(1)}, f32[32,128]{1,0:T(8,128)S(1)}, f32[32,128]{1,0:T(8,128)S(1)}, f32[1,1024]{1,0:T(1,128)...) custom-call(s32[1,16]{1,0:T(1,128)S(1)} %copy-done.5, s32[1]{0:T(128)} %bitcast.pos_ref, s32[32,128]{1,0:T(8,128)S(1)} %bitcast.7, ...), custom_call_target="tpu_custom_call" | custom-call | flops 2000000000 | bytes 300000 | tf_op jit(solution)/shard_map/prepare/pallas_call | solution.py:113
  7.7 0.0 collective-permute-done.refs_1_
  7.8 0.0 copy-start
  7.8 6.7 %pair_terms.1 = (f32[2,1024]{1,0:T(2,128)}, f32[2,1024]{1,0:T(2,128)S(1)}) custom-call(s32[8,128]{1,0:T(8,128)S(1)} %get-tuple-element.25.bounds_ref, s32[1]{0:T(128)} %bitcast.pos_ref, f32[8,128]{1,0:T(8,128)S(1)} %get-tuple-element.26.refs_0_, f32[8,128]{1,0:T(8,128)S(1)} %collective-permute-done.refs_1_, f32[8,128]{1,0:T(8,128)S(1)} %collective-permute-done.1.refs_2_, ...), custom_call_target="tpu_custom_call" | custom-call | flops 8999999488 | bytes 200000 | tf_op jit(solution)/shard_map/pair_terms/pallas_call | solution.py:307
  14.5 0.4 %leaf_terms.1 = (f32[256,1024]{1,0:T(8,128)S(1)}, bf16[32,1024]{1,0:T(8,128)(2,1)S(1)}, f32[8,256]{1,0:T(8,128)S(1)}) custom-call(bf16[256,256]{1,0:T(8,128)(2,1)S(1)} %get-tuple-element.32.perm_ref, s32[1024,256]{1,0:T(8,128)S(1)} %copy-done, s32[8,128]{1,0:T(8,128)S(1)} %get-tuple-element.31.leaf_ref, f32[2,1024]{1,0:T(2,128)S(1)} %get-tuple-element.33.lam_ref), custom_call_target="tpu_custom_call" | custom-call | flops 200000000 | bytes 3000000 | tf_op jit(solution)/shard_map/leaf_terms/pallas_call | solution.py:347
  14.9 0.9 %histogram_part.8 = f32[104,256]{1,0:T(8,128)S(1)} custom-call(bf16[32,1024]{1,0:T(8,128)(2,1)S(1)} %get-tuple-element.40.tile_ref, f32[256,1024]{1,0:T(8,128)S(1)} %get-tuple-element.35.bins_ref, f32[8,256]{1,0:T(8,128)S(1)} %get-tuple-element.36.refs_0_), custom_call_target="tpu_custom_call" | custom-call | flops 4000000 | bytes 4000 | tf_op jit(solution)/shard_map/histogram_part/pallas_call | solution.py:421
  15.8 0.1 collective-permute-start.2
  15.9 0.9 %histogram_part.7 = f32[96,256]{1,0:T(8,128)S(1)} custom-call(bf16[32,1024]{1,0:T(8,128)(2,1)S(1)} %get-tuple-element.40.tile_ref, f32[256,1024]{1,0:T(8,128)S(1)} %get-tuple-element.35.bins_ref), custom_call_target="tpu_custom_call" | custom-call | flops 4000000 | bytes 4000 | tf_op jit(solution)/shard_map/histogram_part/pallas_call | solution.py:421
  16.8 0.4 %collective-permute-done.2 = f32[104,256]{1,0:T(8,128)S(1)} collective-permute-done((f32[104,256]{1,0:T(8,128)S(1)}, f32[104,256]{1,0:T(8,128)S(1)}, u32[]{:S(2)}, u32[]{:S(2)}) %collective-permute-start.2) | collective-permute-done | bytes 106528 | tf_op jit(solution)/shard_map/ppermute | solution.py:505
  17.2 0.9 %histogram_part.10 = f32[96,256]{1,0:T(8,128)S(1)} custom-call(bf16[32,1024]{1,0:T(8,128)(2,1)S(1)} %get-tuple-element.40.tile_ref, f32[256,1024]{1,0:T(8,128)S(1)} %get-tuple-element.35.bins_ref), custom_call_target="tpu_custom_call" | custom-call | flops 4000000 | bytes 4000 | tf_op jit(solution)/shard_map/histogram_part/pallas_call | solution.py:421
  18.1 0.2 collective-permute-start.3
  18.3 1.2 %collective-permute-start.5 = (f32[104,256]{1,0:T(8,128)S(1)}, f32[104,256]{1,0:T(8,128)S(1)}, u32[]{:S(2)}, u32[]{:S(2)}) collective-permute-start(f32[104,256]{1,0:T(8,128)S(1)} %pad_maximum_fusion.1), channel_id=1, source_target_pairs={{0,8},{1,9},{2,10},{3,11},{4,12},{5,13},{6,14},{7,15},{8,0},{9,1},... | collective-permute-start | bytes 319496 | tf_op jit(solution)/shard_map/ppermute | solution.py:505
  19.5 0.9 %histogram_part.9 = f32[96,256]{1,0:T(8,128)S(1)} custom-call(bf16[32,1024]{1,0:T(8,128)(2,1)S(1)} %get-tuple-element.40.tile_ref, f32[256,1024]{1,0:T(8,128)S(1)} %get-tuple-element.35.bins_ref), custom_call_target="tpu_custom_call" | custom-call | flops 4000000 | bytes 4000 | tf_op jit(solution)/shard_map/histogram_part/pallas_call | solution.py:421
  20.5 1.6 %histogram_part.12 = f32[192,256]{1,0:T(8,128)S(1)} custom-call(bf16[32,1024]{1,0:T(8,128)(2,1)S(1)} %get-tuple-element.40.tile_ref, f32[256,1024]{1,0:T(8,128)S(1)} %get-tuple-element.35.bins_ref), custom_call_target="tpu_custom_call" | custom-call | flops 8000000 | bytes 8000 | tf_op jit(solution)/shard_map/histogram_part/pallas_call | solution.py:421
  22.0 0.1 collective-permute-start.4
  22.1 0.9 %collective-permute-start.6 = (f32[104,256]{1,0:T(8,128)S(1)}, f32[104,256]{1,0:T(8,128)S(1)}, u32[]{:S(2)}, u32[]{:S(2)}) collective-permute-start(f32[104,256]{1,0:T(8,128)S(1)} %pad_maximum_fusion), channel_id=1, source_target_pairs={{0,8},{1,9},{2,10},{3,11},{4,12},{5,13},{6,14},{7,15},{8,0},{9,1},... | collective-permute-start | bytes 319496 | tf_op jit(solution)/shard_map/ppermute | solution.py:505
  23.0 0.9 %histogram_part.11 = f32[96,256]{1,0:T(8,128)S(1)} custom-call(bf16[32,1024]{1,0:T(8,128)(2,1)S(1)} %get-tuple-element.40.tile_ref, f32[256,1024]{1,0:T(8,128)S(1)} %get-tuple-element.35.bins_ref), custom_call_target="tpu_custom_call" | custom-call | flops 4000000 | bytes 4000 | tf_op jit(solution)/shard_map/histogram_part/pallas_call | solution.py:421
  23.9 0.0 collective-permute-done.4
  24.0 2.2 %collective-permute-start.7 = (f32[104,256]{1,0:T(8,128)S(1)}, f32[104,256]{1,0:T(8,128)S(1)}, u32[]{:S(2)}, u32[]{:S(2)}) collective-permute-start(f32[104,256]{1,0:T(8,128)S(1)} %pad_maximum_fusion.2), channel_id=1, source_target_pairs={{0,16},{1,17},{2,18},{3,19},{4,20},{5,21},{6,22},{7,23},{8,24},{9,... | collective-permute-start | bytes 319496 | tf_op jit(solution)/shard_map/ppermute | solution.py:505
  26.2 0.9 %histogram_part.13 = f32[96,256]{1,0:T(8,128)S(1)} custom-call(bf16[32,1024]{1,0:T(8,128)(2,1)S(1)} %get-tuple-element.40.tile_ref, f32[256,1024]{1,0:T(8,128)S(1)} %get-tuple-element.35.bins_ref), custom_call_target="tpu_custom_call" | custom-call | flops 4000000 | bytes 4000 | tf_op jit(solution)/shard_map/histogram_part/pallas_call | solution.py:421
  27.1 0.4 %collective-permute-done.6 = f32[104,256]{1,0:T(8,128)S(1)} collective-permute-done((f32[104,256]{1,0:T(8,128)S(1)}, f32[104,256]{1,0:T(8,128)S(1)}, u32[]{:S(2)}, u32[]{:S(2)}) %collective-permute-start.6) | collective-permute-done | bytes 106528 | tf_op jit(solution)/shard_map/ppermute | solution.py:505
  27.5 2.0 %collective-permute-done.7 = f32[104,256]{1,0:T(8,128)S(1)} collective-permute-done((f32[104,256]{1,0:T(8,128)S(1)}, f32[104,256]{1,0:T(8,128)S(1)}, u32[]{:S(2)}, u32[]{:S(2)}) %collective-permute-start.7) | collective-permute-done | bytes 106528 | tf_op jit(solution)/shard_map/ppermute | solution.py:505
  29.6 2.6 %collective-permute-start.10 = (f32[32,256]{1,0:T(8,128)S(1)}, f32[32,256]{1,0:T(8,128)S(1)}, u32[]{:S(2)}, u32[]{:S(2)}) collective-permute-start(f32[32,256]{1,0:T(8,128)S(1)} %get-tuple-element.50), channel_id=1, source_target_pairs={{0,3},{1,2},{2,1},{3,0},{4,7},{5,6},{6,5},{7,4},{8,11},{9,10},{10,... | collective-permute-start | bytes 98312 | tf_op jit(solution)/shard_map/ppermute | solution.py:505
  32.1 2.8 %collective-permute-start.8 = (f32[32,256]{1,0:T(8,128)S(1)}, f32[32,256]{1,0:T(8,128)S(1)}, u32[]{:S(2)}, u32[]{:S(2)}) collective-permute-start(f32[32,256]{1,0:T(8,128)S(1)} %get-tuple-element.52), channel_id=1, source_target_pairs={{0,2},{1,3},{2,0},{3,1},{4,6},{5,7},{6,4},{7,5},{8,10},{9,11},{10,... | collective-permute-start | bytes 98312 | tf_op jit(solution)/shard_map/ppermute | solution.py:505
  35.0 0.4 %collective-permute-done.10.refs_2_ = f32[32,256]{1,0:T(8,128)S(1)} collective-permute-done((f32[32,256]{1,0:T(8,128)S(1)}, f32[32,256]{1,0:T(8,128)S(1)}, u32[]{:S(2)}, u32[]{:S(2)}) %collective-permute-start.10) | collective-permute-done | bytes 32800 | tf_op jit(solution)/shard_map/ppermute | solution.py:505
  35.4 2.0 %collective-permute-done.8.refs_0_ = f32[32,256]{1,0:T(8,128)S(1)} collective-permute-done((f32[32,256]{1,0:T(8,128)S(1)}, f32[32,256]{1,0:T(8,128)S(1)}, u32[]{:S(2)}, u32[]{:S(2)}) %collective-permute-start.8) | collective-permute-done | bytes 32800 | tf_op jit(solution)/shard_map/ppermute | solution.py:505
  37.3 1.6 %collective-permute-done.9.refs_1_ = f32[32,256]{1,0:T(8,128)S(1)} collective-permute-done((f32[32,256]{1,0:T(8,128)S(1)}, f32[32,256]{1,0:T(8,128)S(1)}, u32[]{:S(2)}, u32[]{:S(2)}) %collective-permute-start.9) | collective-permute-done | bytes 32800 | tf_op jit(solution)/shard_map/ppermute | solution.py:505
  38.9 0.8 %finish.1 = (f32[8,128]{1,0:T(8,128)}, f32[8,128]{1,0:T(8,128)}, f32[3,2048]{1,0:T(4,128)}) custom-call(s32[8,128]{1,0:T(8,128)S(1)} %get-tuple-element.31.leaf_ref, f32[24,256]{1,0:T(8,128)S(1)} %get-tuple-element.49.kept_ref, f32[8,256]{1,0:T(8,128)S(1)} %slice_add_fusion.6.sums_ref, f32[32,256]{1,0:T(8,128)S(1)} %collective-permute-done.8.refs_0_, ...), custom_call_target="tpu_custom_call" | custom-call | tf_op jit(solution)/shard_map/finish/pallas_call | solution.py:470
  (25 shorter events, 0.2 us)
Async XLA Ops:
  0.6 4.7 %copy-start.1 = (s32[4096]{0:T(1024)S(1)}, s32[4096]{0:T(1024)}, u32[]{:S(2)}) copy-start(s32[4096]{0:T(1024)} %param.7) | copy-start | bytes 49156
  0.6 7.1 %collective-permute-start = (f32[8,128]{1,0:T(8,128)}, f32[8,128]{1,0:T(8,128)S(1)}, u32[]{:S(2)}, u32[]{:S(2)}) collective-permute-start(f32[8,128]{1,0:T(8,128)} %bitcast.9), channel_id=1, source_target_pairs={{0,4},{1,2},{2,1},{3,7},{4,0},{5,6},{6,5},{7,3},{8,12},{9,10},{10,... | collective-permute-start | bytes 12296 | tf_op jit(solution)/shard_map/ppermute | solution.py:517
  1.2 6.6 %collective-permute-start.1 = (f32[8,128]{1,0:T(8,128)}, f32[8,128]{1,0:T(8,128)S(1)}, u32[]{:S(2)}, u32[]{:S(2)}) collective-permute-start(f32[8,128]{1,0:T(8,128)} %bitcast.10), channel_id=1, source_target_pairs={{0,1},{1,0},{2,3},{3,2},{4,5},{5,4},{6,7},{7,6},{8,9},{9,8},{10,11... | collective-permute-start | bytes 12296 | tf_op jit(solution)/shard_map/ppermute | solution.py:505
  5.3 0.7 %copy-start.3 = (f32[1024]{0:T(1024)S(1)}, f32[1024]{0:T(1024)}, u32[]{:S(2)}) copy-start(f32[1024]{0:T(1024)} %param.6) | copy-start | bytes 12292
  5.3 0.7 %copy-start.2 = (s32[1024]{0:T(1024)S(1)}, s32[1024]{0:T(1024)}, u32[]{:S(2)}) copy-start(s32[1024]{0:T(1024)} %param.8) | copy-start | bytes 12292
  5.3 0.7 %copy-start.5 = (s32[1,16]{1,0:T(1,128)S(1)}, s32[1,16]{1,0:T(1,128)}, u32[]{:S(2)}) copy-start(s32[1,16]{1,0:T(1,128)} %len_ref.1) | copy-start | bytes 196
  6.0 0.7 %copy-start.4 = (s32[256]{0:T(256)S(1)}, s32[256]{0:T(256)}, u32[]{:S(2)}) copy-start(s32[256]{0:T(256)} %param.11) | copy-start | bytes 3076
  7.8 6.7 %copy-start = (s32[1024,256]{1,0:T(8,128)S(1)}, s32[1024,256]{1,0:T(8,128)}, u32[]{:S(2)}) copy-start(s32[1024,256]{1,0:T(8,128)} %bins_ref.1) | copy-start | bytes 3145732
  15.8 1.4 %collective-permute-start.2 = (f32[104,256]{1,0:T(8,128)S(1)}, f32[104,256]{1,0:T(8,128)S(1)}, u32[]{:S(2)}, u32[]{:S(2)}) collective-permute-start(f32[104,256]{1,0:T(8,128)S(1)} %histogram_part.8), channel_id=1, source_target_pairs={{0,4},{1,5},{2,6},{3,7},{4,0},{5,1},{6,2},{7,3},{8,12},{9,13},{10,... | collective-permute-start | bytes 319496 | tf_op jit(solution)/shard_map/ppermute | solution.py:505
  18.1 2.3 %collective-permute-start.3 = (f32[96,256]{1,0:T(8,128)S(1)}, f32[96,256]{1,0:T(8,128)S(1)}, u32[]{:S(2)}, u32[]{:S(2)}) collective-permute-start(f32[96,256]{1,0:T(8,128)S(1)} %histogram_part.10), channel_id=1, source_target_pairs={{0,4},{1,5},{2,6},{3,7},{4,0},{5,1},{6,2},{7,3},{8,12},{9,13},{10,... | collective-permute-start | bytes 294920 | tf_op jit(solution)/shard_map/ppermute | solution.py:505
  18.3 5.6 %collective-permute-start.5 = (f32[104,256]{1,0:T(8,128)S(1)}, f32[104,256]{1,0:T(8,128)S(1)}, u32[]{:S(2)}, u32[]{:S(2)}) collective-permute-start(f32[104,256]{1,0:T(8,128)S(1)} %pad_maximum_fusion.1), channel_id=1, source_target_pairs={{0,8},{1,9},{2,10},{3,11},{4,12},{5,13},{6,14},{7,15},{8,0},{9,1},... | collective-permute-start | bytes 319496 | tf_op jit(solution)/shard_map/ppermute | solution.py:505
  22.0 1.9 %collective-permute-start.4 = (f32[192,256]{1,0:T(8,128)S(1)}, f32[192,256]{1,0:T(8,128)S(1)}, u32[]{:S(2)}, u32[]{:S(2)}) collective-permute-start(f32[192,256]{1,0:T(8,128)S(1)} %histogram_part.12), channel_id=1, source_target_pairs={{0,4},{1,5},{2,6},{3,7},{4,0},{5,1},{6,2},{7,3},{8,12},{9,13},{10,... | collective-permute-start | bytes 589832 | tf_op jit(solution)/shard_map/ppermute | solution.py:505
  22.1 5.4 %collective-permute-start.6 = (f32[104,256]{1,0:T(8,128)S(1)}, f32[104,256]{1,0:T(8,128)S(1)}, u32[]{:S(2)}, u32[]{:S(2)}) collective-permute-start(f32[104,256]{1,0:T(8,128)S(1)} %pad_maximum_fusion), channel_id=1, source_target_pairs={{0,8},{1,9},{2,10},{3,11},{4,12},{5,13},{6,14},{7,15},{8,0},{9,1},... | collective-permute-start | bytes 319496 | tf_op jit(solution)/shard_map/ppermute | solution.py:505
  24.0 5.5 %collective-permute-start.7 = (f32[104,256]{1,0:T(8,128)S(1)}, f32[104,256]{1,0:T(8,128)S(1)}, u32[]{:S(2)}, u32[]{:S(2)}) collective-permute-start(f32[104,256]{1,0:T(8,128)S(1)} %pad_maximum_fusion.2), channel_id=1, source_target_pairs={{0,16},{1,17},{2,18},{3,19},{4,20},{5,21},{6,22},{7,23},{8,24},{9,... | collective-permute-start | bytes 319496 | tf_op jit(solution)/shard_map/ppermute | solution.py:505
  29.6 5.8 %collective-permute-start.10 = (f32[32,256]{1,0:T(8,128)S(1)}, f32[32,256]{1,0:T(8,128)S(1)}, u32[]{:S(2)}, u32[]{:S(2)}) collective-permute-start(f32[32,256]{1,0:T(8,128)S(1)} %get-tuple-element.50), channel_id=1, source_target_pairs={{0,3},{1,2},{2,1},{3,0},{4,7},{5,6},{6,5},{7,4},{8,11},{9,10},{10,... | collective-permute-start | bytes 98312 | tf_op jit(solution)/shard_map/ppermute | solution.py:505
  32.1 5.2 %collective-permute-start.8 = (f32[32,256]{1,0:T(8,128)S(1)}, f32[32,256]{1,0:T(8,128)S(1)}, u32[]{:S(2)}, u32[]{:S(2)}) collective-permute-start(f32[32,256]{1,0:T(8,128)S(1)} %get-tuple-element.52), channel_id=1, source_target_pairs={{0,2},{1,3},{2,0},{3,1},{4,6},{5,7},{6,4},{7,5},{8,10},{9,11},{10,... | collective-permute-start | bytes 98312 | tf_op jit(solution)/shard_map/ppermute | solution.py:505
  35.0 3.9 %collective-permute-start.9 = (f32[32,256]{1,0:T(8,128)S(1)}, f32[32,256]{1,0:T(8,128)S(1)}, u32[]{:S(2)}, u32[]{:S(2)}) collective-permute-start(f32[32,256]{1,0:T(8,128)S(1)} %get-tuple-element.51), channel_id=1, source_target_pairs={{0,1},{1,0},{2,3},{3,2},{4,5},{5,4},{6,7},{7,6},{8,9},{9,8},{10,11... | collective-permute-start | bytes 98312 | tf_op jit(solution)/shard_map/ppermute | solution.py:505

commit v22 on v20

--- a/solution.py
+++ b/solution.py
@@ -260,8 +260,10 @@
                 for u in range(size // 8):
                     at = pl.ds(base + 8 * u, 8)
                     a_j, w_j, d_j = a_col[at, :], w_col[at, :], d_col[at, :]
+                    totals = [a_i[g] + a_j for g in range(2)]
+                    product = pl.reciprocal(totals[0] * totals[1], approx=True)
                     for g in range(2):
-                        recip = pl.reciprocal(a_i[g] + a_j, approx=True)
+                        recip = product * totals[1 - g]
                         lift = w_i[g] - w_j
                         weight = jnp.abs(d_i[g] - d_j) * recip
                         if masked:

time: 38.1 us -> 38.2 us (level)
  starting transfers between devices: 15.9 us -> 11.4 us
  Pallas kernels: 14.4 us -> 17.1 us
  waiting for transfers between devices: 5.85 us -> 7.39 us
    ppermute x10, starting transfers between devices: 15.3 us -> 10.9 us  [swap(): return lax.ppermute(value, axes, [(p, p ^ mask) for p in range(count)])]
    pallas_call x1, Pallas kernels: 5.48 us -> 8.14 us  [pair_terms(): pl.pallas_call(functools.partial(pairs_kernel, feat_count), out_shape=(ja...]
    ppermute x10, waiting for transfers between devices: 5.84 us -> 7.39 us  [swap(): return lax.ppermute(value, axes, [(p, p ^ mask) for p in range(count)])]
where the time goes in v22:
time: 38.2 us
  Pallas kernels  17.1 us (45%)
  starting transfers between devices  11.4 us (30%)
  waiting for transfers between devices  7.39 us (19%)
  local copies, waits for them, and re-layouts  1.42 us (4%)
  between operations  0.79 us (2%)
    ppermute x10, starting transfers between devices, swap(): return lax.ppermute(value, axes, [(p, p ^ mask) for p in range(count)])  10.9 us
    pallas_call x1, Pallas kernels, pair_terms(): pl.pallas_call(functools.partial(pairs_kernel, feat_count), out_shape=(ja...  8.14 us
    ppermute x10, waiting for transfers between devices, swap(): return lax.ppermute(value, axes, [(p, p ^ mask) for p in range(count)])  7.39 us
    pallas_call x6, Pallas kernels, histogram_part(): pl.pallas_call(functools.partial(histogram_kernel, first, groups), out_sh...  6.68 us
    unnamed x12, local copies, waits for them, and re-layouts  1.41 us
    pallas_call x1, Pallas kernels, prepare(): pl.pallas_call(functools.partial(prepare_kernel, feat_count, masks), out_...  1.01 us
    pallas_call x1, Pallas kernels, finish(): pl.pallas_call(functools.partial(finish_kernel, per_dev), out_shape=(jax....  0.8 us
  transfers between devices with their start and end apart: 11, of which 8 were waited for; matrix products, arithmetic and copies ran while one was open for 0% of the time, Pallas kernels for 18%

profile of v22, /device:TPU:0, one launch (start us, length us, event | category | flops | bytes accessed | tf_op | source)
XLA Modules:
  0.0 38.2 jit_solution(10888915794402957370)
XLA Ops:
  0.6 0.5 %collective-permute-start = (f32[8,128]{1,0:T(8,128)}, f32[8,128]{1,0:T(8,128)S(1)}, u32[]{:S(2)}, u32[]{:S(2)}) collective-permute-start(f32[8,128]{1,0:T(8,128)} %bitcast.9), channel_id=1, source_target_pairs={{0,4},{1,2},{2,1},{3,7},{4,0},{5,6},{6,5},{7,3},{8,12},{9,10},{10,... | collective-permute-start | bytes 12296 | tf_op jit(solution)/shard_map/ppermute | solution.py:519
  1.2 4.1 %collective-permute-start.1 = (f32[8,128]{1,0:T(8,128)}, f32[8,128]{1,0:T(8,128)S(1)}, u32[]{:S(2)}, u32[]{:S(2)}) collective-permute-start(f32[8,128]{1,0:T(8,128)} %bitcast.10), channel_id=1, source_target_pairs={{0,1},{1,0},{2,3},{3,2},{4,5},{5,4},{6,7},{7,6},{8,9},{9,8},{10,11... | collective-permute-start | bytes 12296 | tf_op jit(solution)/shard_map/ppermute | solution.py:507
  5.3 0.7 %copy-done.3 = f32[1024]{0:T(1024)S(1)} copy-done((f32[1024]{0:T(1024)S(1)}, f32[1024]{0:T(1024)}, u32[]{:S(2)}) %copy-start.3) | copy-done | bytes 4120
  6.0 0.7 %copy-done.4 = s32[256]{0:T(256)S(1)} copy-done((s32[256]{0:T(256)S(1)}, s32[256]{0:T(256)}, u32[]{:S(2)}) %copy-start.4) | copy-done | bytes 1048
  6.7 1.0 %prepare.1 = (f32[8,128]{1,0:T(8,128)S(1)}, s32[8,128]{1,0:T(8,128)S(1)}, f32[32,128]{1,0:T(8,128)S(1)}, f32[32,128]{1,0:T(8,128)S(1)}, f32[1,1024]{1,0:T(1,128)...) custom-call(s32[1,16]{1,0:T(1,128)S(1)} %copy-done.5, s32[1]{0:T(128)} %bitcast.pos_ref, s32[32,128]{1,0:T(8,128)S(1)} %bitcast.7, ...), custom_call_target="tpu_custom_call" | custom-call | flops 2000000000 | bytes 300000 | tf_op jit(solution)/shard_map/prepare/pallas_call | solution.py:113
  7.8 0.0 copy-start
  7.8 8.1 %pair_terms.1 = (f32[2,1024]{1,0:T(2,128)}, f32[2,1024]{1,0:T(2,128)S(1)}) custom-call(s32[8,128]{1,0:T(8,128)S(1)} %get-tuple-element.24.bounds_ref, s32[1]{0:T(128)} %bitcast.pos_ref, f32[8,128]{1,0:T(8,128)S(1)} %get-tuple-element.25.refs_0_, f32[8,128]{1,0:T(8,128)S(1)} %collective-permute-done.refs_1_, f32[8,128]{1,0:T(8,128)S(1)} %collective-permute-done.1.refs_2_, ...), custom_call_target="tpu_custom_call" | custom-call | flops 8999999488 | bytes 200000 | tf_op jit(solution)/shard_map/pair_terms/pallas_call | solution.py:309
  15.9 0.4 %leaf_terms.1 = (f32[256,1024]{1,0:T(8,128)S(1)}, bf16[32,1024]{1,0:T(8,128)(2,1)S(1)}, f32[8,256]{1,0:T(8,128)S(1)}) custom-call(bf16[256,256]{1,0:T(8,128)(2,1)S(1)} %get-tuple-element.31.perm_ref, s32[1024,256]{1,0:T(8,128)S(1)} %copy-done, s32[8,128]{1,0:T(8,128)S(1)} %get-tuple-element.30.leaf_ref, f32[2,1024]{1,0:T(2,128)S(1)} %get-tuple-element.32.lam_ref), custom_call_target="tpu_custom_call" | custom-call | flops 200000000 | bytes 3000000 | tf_op jit(solution)/shard_map/leaf_terms/pallas_call | solution.py:349
  16.3 0.9 %histogram_part.7 = f32[104,256]{1,0:T(8,128)S(1)} custom-call(bf16[32,1024]{1,0:T(8,128)(2,1)S(1)} %get-tuple-element.38.tile_ref, f32[256,1024]{1,0:T(8,128)S(1)} %get-tuple-element.34.bins_ref, f32[8,256]{1,0:T(8,128)S(1)} %get-tuple-element.35.refs_0_), custom_call_target="tpu_custom_call" | custom-call | flops 4000000 | bytes 4000 | tf_op jit(solution)/shard_map/histogram_part/pallas_call | solution.py:423
  17.2 0.1 collective-permute-start.2
  17.3 0.9 %histogram_part.6 = f32[96,256]{1,0:T(8,128)S(1)} custom-call(bf16[32,1024]{1,0:T(8,128)(2,1)S(1)} %get-tuple-element.38.tile_ref, f32[256,1024]{1,0:T(8,128)S(1)} %get-tuple-element.34.bins_ref), custom_call_target="tpu_custom_call" | custom-call | flops 4000000 | bytes 4000 | tf_op jit(solution)/shard_map/histogram_part/pallas_call | solution.py:423
  18.2 0.4 %collective-permute-done.2 = f32[104,256]{1,0:T(8,128)S(1)} collective-permute-done((f32[104,256]{1,0:T(8,128)S(1)}, f32[104,256]{1,0:T(8,128)S(1)}, u32[]{:S(2)}, u32[]{:S(2)}) %collective-permute-start.2) | collective-permute-done | bytes 106528 | tf_op jit(solution)/shard_map/ppermute | solution.py:507
  18.6 0.1 collective-permute-start.4
  18.7 1.6 %histogram_part.9 = f32[192,256]{1,0:T(8,128)S(1)} custom-call(bf16[32,1024]{1,0:T(8,128)(2,1)S(1)} %get-tuple-element.38.tile_ref, f32[256,1024]{1,0:T(8,128)S(1)} %get-tuple-element.34.bins_ref), custom_call_target="tpu_custom_call" | custom-call | flops 8000000 | bytes 8000 | tf_op jit(solution)/shard_map/histogram_part/pallas_call | solution.py:423
  20.3 0.2 collective-permute-start.3
  20.5 1.6 %histogram_part.8 = f32[192,256]{1,0:T(8,128)S(1)} custom-call(bf16[32,1024]{1,0:T(8,128)(2,1)S(1)} %get-tuple-element.38.tile_ref, f32[256,1024]{1,0:T(8,128)S(1)} %get-tuple-element.34.bins_ref), custom_call_target="tpu_custom_call" | custom-call | flops 8000000 | bytes 8000 | tf_op jit(solution)/shard_map/histogram_part/pallas_call | solution.py:423
  22.1 1.7 %collective-permute-done.4 = f32[104,256]{1,0:T(8,128)S(1)} collective-permute-done((f32[104,256]{1,0:T(8,128)S(1)}, f32[104,256]{1,0:T(8,128)S(1)}, u32[]{:S(2)}, u32[]{:S(2)}) %collective-permute-start.4) | collective-permute-done | bytes 106528 | tf_op jit(solution)/shard_map/ppermute | solution.py:507
  23.8 0.1 collective-permute-start.7
  24.0 1.7 %collective-permute-start.6 = (f32[104,256]{1,0:T(8,128)S(1)}, f32[104,256]{1,0:T(8,128)S(1)}, u32[]{:S(2)}, u32[]{:S(2)}) collective-permute-start(f32[104,256]{1,0:T(8,128)S(1)} %get-tuple-element.39), channel_id=1, source_target_pairs={{0,8},{1,9},{2,10},{3,11},{4,12},{5,13},{6,14},{7,15},{8,0},{9,1},... | collective-permute-start | bytes 319496 | tf_op jit(solution)/shard_map/ppermute | solution.py:507
  25.7 0.9 %histogram_part.11 = f32[96,256]{1,0:T(8,128)S(1)} custom-call(bf16[32,1024]{1,0:T(8,128)(2,1)S(1)} %get-tuple-element.38.tile_ref, f32[256,1024]{1,0:T(8,128)S(1)} %get-tuple-element.34.bins_ref), custom_call_target="tpu_custom_call" | custom-call | flops 4000000 | bytes 4000 | tf_op jit(solution)/shard_map/histogram_part/pallas_call | solution.py:423
  26.6 0.1 collective-permute-start.5
  26.7 0.9 %histogram_part.10 = f32[96,256]{1,0:T(8,128)S(1)} custom-call(bf16[32,1024]{1,0:T(8,128)(2,1)S(1)} %get-tuple-element.38.tile_ref, f32[256,1024]{1,0:T(8,128)S(1)} %get-tuple-element.34.bins_ref), custom_call_target="tpu_custom_call" | custom-call | flops 4000000 | bytes 4000 | tf_op jit(solution)/shard_map/histogram_part/pallas_call | solution.py:423
  27.6 0.4 %collective-permute-done.5 = f32[96,256]{1,0:T(8,128)S(1)} collective-permute-done((f32[96,256]{1,0:T(8,128)S(1)}, f32[96,256]{1,0:T(8,128)S(1)}, u32[]{:S(2)}, u32[]{:S(2)}) %collective-permute-start.5) | collective-permute-done | bytes 98336 | tf_op jit(solution)/shard_map/ppermute | solution.py:507
  28.0 0.6 %collective-permute-done.7 = f32[104,256]{1,0:T(8,128)S(1)} collective-permute-done((f32[104,256]{1,0:T(8,128)S(1)}, f32[104,256]{1,0:T(8,128)S(1)}, u32[]{:S(2)}, u32[]{:S(2)}) %collective-permute-start.7) | collective-permute-done | bytes 106528 | tf_op jit(solution)/shard_map/ppermute | solution.py:507
  28.6 0.4 %collective-permute-done.6 = f32[104,256]{1,0:T(8,128)S(1)} collective-permute-done((f32[104,256]{1,0:T(8,128)S(1)}, f32[104,256]{1,0:T(8,128)S(1)}, u32[]{:S(2)}, u32[]{:S(2)}) %collective-permute-start.6) | collective-permute-done | bytes 106528 | tf_op jit(solution)/shard_map/ppermute | solution.py:507
  29.1 2.1 %collective-permute-start.10 = (f32[32,256]{1,0:T(8,128)S(1)}, f32[32,256]{1,0:T(8,128)S(1)}, u32[]{:S(2)}, u32[]{:S(2)}) collective-permute-start(f32[32,256]{1,0:T(8,128)S(1)} %get-tuple-element.50), channel_id=1, source_target_pairs={{0,3},{1,2},{2,1},{3,0},{4,7},{5,6},{6,5},{7,4},{8,11},{9,10},{10,... | collective-permute-start | bytes 98312 | tf_op jit(solution)/shard_map/ppermute | solution.py:507
  31.2 2.3 %collective-permute-start.8 = (f32[32,256]{1,0:T(8,128)S(1)}, f32[32,256]{1,0:T(8,128)S(1)}, u32[]{:S(2)}, u32[]{:S(2)}) collective-permute-start(f32[32,256]{1,0:T(8,128)S(1)} %get-tuple-element.52), channel_id=1, source_target_pairs={{0,2},{1,3},{2,0},{3,1},{4,6},{5,7},{6,4},{7,5},{8,10},{9,11},{10,... | collective-permute-start | bytes 98312 | tf_op jit(solution)/shard_map/ppermute | solution.py:507
  33.5 0.0 collective-permute-start.9
  33.5 1.6 %collective-permute-done.10.refs_2_ = f32[32,256]{1,0:T(8,128)S(1)} collective-permute-done((f32[32,256]{1,0:T(8,128)S(1)}, f32[32,256]{1,0:T(8,128)S(1)}, u32[]{:S(2)}, u32[]{:S(2)}) %collective-permute-start.10) | collective-permute-done | bytes 32800 | tf_op jit(solution)/shard_map/ppermute | solution.py:507
  35.2 0.9 %collective-permute-done.8.refs_0_ = f32[32,256]{1,0:T(8,128)S(1)} collective-permute-done((f32[32,256]{1,0:T(8,128)S(1)}, f32[32,256]{1,0:T(8,128)S(1)}, u32[]{:S(2)}, u32[]{:S(2)}) %collective-permute-start.8) | collective-permute-done | bytes 32800 | tf_op jit(solution)/shard_map/ppermute | solution.py:507
  36.0 1.4 %collective-permute-done.9.refs_1_ = f32[32,256]{1,0:T(8,128)S(1)} collective-permute-done((f32[32,256]{1,0:T(8,128)S(1)}, f32[32,256]{1,0:T(8,128)S(1)}, u32[]{:S(2)}, u32[]{:S(2)}) %collective-permute-start.9) | collective-permute-done | bytes 32800 | tf_op jit(solution)/shard_map/ppermute | solution.py:507
  37.4 0.8 %finish.1 = (f32[8,128]{1,0:T(8,128)}, f32[8,128]{1,0:T(8,128)}, f32[3,2048]{1,0:T(4,128)}) custom-call(s32[8,128]{1,0:T(8,128)S(1)} %get-tuple-element.30.leaf_ref, f32[24,256]{1,0:T(8,128)S(1)} %get-tuple-element.49.kept_ref, f32[8,256]{1,0:T(8,128)S(1)} %slice_add_fusion.4.sums_ref, f32[32,256]{1,0:T(8,128)S(1)} %collective-permute-done.8.refs_0_, ...), custom_call_target="tpu_custom_call" | custom-call | tf_op jit(solution)/shard_map/finish/pallas_call | solution.py:472
  (23 shorter events, 0.2 us)
Async XLA Ops:
  0.6 4.7 %copy-start.1 = (s32[4096]{0:T(1024)S(1)}, s32[4096]{0:T(1024)}, u32[]{:S(2)}) copy-start(s32[4096]{0:T(1024)} %param.7) | copy-start | bytes 49156
  0.6 7.1 %collective-permute-start = (f32[8,128]{1,0:T(8,128)}, f32[8,128]{1,0:T(8,128)S(1)}, u32[]{:S(2)}, u32[]{:S(2)}) collective-permute-start(f32[8,128]{1,0:T(8,128)} %bitcast.9), channel_id=1, source_target_pairs={{0,4},{1,2},{2,1},{3,7},{4,0},{5,6},{6,5},{7,3},{8,12},{9,10},{10,... | collective-permute-start | bytes 12296 | tf_op jit(solution)/shard_map/ppermute | solution.py:519
  1.2 6.6 %collective-permute-start.1 = (f32[8,128]{1,0:T(8,128)}, f32[8,128]{1,0:T(8,128)S(1)}, u32[]{:S(2)}, u32[]{:S(2)}) collective-permute-start(f32[8,128]{1,0:T(8,128)} %bitcast.10), channel_id=1, source_target_pairs={{0,1},{1,0},{2,3},{3,2},{4,5},{5,4},{6,7},{7,6},{8,9},{9,8},{10,11... | collective-permute-start | bytes 12296 | tf_op jit(solution)/shard_map/ppermute | solution.py:507
  5.3 0.7 %copy-start.3 = (f32[1024]{0:T(1024)S(1)}, f32[1024]{0:T(1024)}, u32[]{:S(2)}) copy-start(f32[1024]{0:T(1024)} %param.6) | copy-start | bytes 12292
  5.3 0.7 %copy-start.2 = (s32[1024]{0:T(1024)S(1)}, s32[1024]{0:T(1024)}, u32[]{:S(2)}) copy-start(s32[1024]{0:T(1024)} %param.8) | copy-start | bytes 12292
  5.3 0.7 %copy-start.5 = (s32[1,16]{1,0:T(1,128)S(1)}, s32[1,16]{1,0:T(1,128)}, u32[]{:S(2)}) copy-start(s32[1,16]{1,0:T(1,128)} %len_ref.1) | copy-start | bytes 196
  6.0 0.7 %copy-start.4 = (s32[256]{0:T(256)S(1)}, s32[256]{0:T(256)}, u32[]{:S(2)}) copy-start(s32[256]{0:T(256)} %param.11) | copy-start | bytes 3076
  7.8 8.2 %copy-start = (s32[1024,256]{1,0:T(8,128)S(1)}, s32[1024,256]{1,0:T(8,128)}, u32[]{:S(2)}) copy-start(s32[1024,256]{1,0:T(8,128)} %bins_ref.1) | copy-start | bytes 3145732
  17.2 1.4 %collective-permute-start.2 = (f32[104,256]{1,0:T(8,128)S(1)}, f32[104,256]{1,0:T(8,128)S(1)}, u32[]{:S(2)}, u32[]{:S(2)}) collective-permute-start(f32[104,256]{1,0:T(8,128)S(1)} %histogram_part.7), channel_id=1, source_target_pairs={{0,4},{1,5},{2,6},{3,7},{4,0},{5,1},{6,2},{7,3},{8,12},{9,13},{10,... | collective-permute-start | bytes 319496 | tf_op jit(solution)/shard_map/ppermute | solution.py:507
  18.6 5.1 %collective-permute-start.4 = (f32[104,256]{1,0:T(8,128)S(1)}, f32[104,256]{1,0:T(8,128)S(1)}, u32[]{:S(2)}, u32[]{:S(2)}) collective-permute-start(f32[104,256]{1,0:T(8,128)S(1)} %pad_maximum_fusion.2), channel_id=1, source_target_pairs={{0,8},{1,9},{2,10},{3,11},{4,12},{5,13},{6,14},{7,15},{8,0},{9,1},... | collective-permute-start | bytes 319496 | tf_op jit(solution)/shard_map/ppermute | solution.py:507
  20.3 3.5 %collective-permute-start.3 = (f32[192,256]{1,0:T(8,128)S(1)}, f32[192,256]{1,0:T(8,128)S(1)}, u32[]{:S(2)}, u32[]{:S(2)}) collective-permute-start(f32[192,256]{1,0:T(8,128)S(1)} %histogram_part.9), channel_id=1, source_target_pairs={{0,4},{1,5},{2,6},{3,7},{4,0},{5,1},{6,2},{7,3},{8,12},{9,13},{10,... | collective-permute-start | bytes 589832 | tf_op jit(solution)/shard_map/ppermute | solution.py:507
  23.8 4.8 %collective-permute-start.7 = (f32[104,256]{1,0:T(8,128)S(1)}, f32[104,256]{1,0:T(8,128)S(1)}, u32[]{:S(2)}, u32[]{:S(2)}) collective-permute-start(f32[104,256]{1,0:T(8,128)S(1)} %get-tuple-element.40), channel_id=1, source_target_pairs={{0,16},{1,17},{2,18},{3,19},{4,20},{5,21},{6,22},{7,23},{8,24},{9,... | collective-permute-start | bytes 319496 | tf_op jit(solution)/shard_map/ppermute | solution.py:507
  24.0 5.1 %collective-permute-start.6 = (f32[104,256]{1,0:T(8,128)S(1)}, f32[104,256]{1,0:T(8,128)S(1)}, u32[]{:S(2)}, u32[]{:S(2)}) collective-permute-start(f32[104,256]{1,0:T(8,128)S(1)} %get-tuple-element.39), channel_id=1, source_target_pairs={{0,8},{1,9},{2,10},{3,11},{4,12},{5,13},{6,14},{7,15},{8,0},{9,1},... | collective-permute-start | bytes 319496 | tf_op jit(solution)/shard_map/ppermute | solution.py:507
  26.6 1.4 %collective-permute-start.5 = (f32[96,256]{1,0:T(8,128)S(1)}, f32[96,256]{1,0:T(8,128)S(1)}, u32[]{:S(2)}, u32[]{:S(2)}) collective-permute-start(f32[96,256]{1,0:T(8,128)S(1)} %histogram_part.11), channel_id=1, source_target_pairs={{0,4},{1,5},{2,6},{3,7},{4,0},{5,1},{6,2},{7,3},{8,12},{9,13},{10,... | collective-permute-start | bytes 294920 | tf_op jit(solution)/shard_map/ppermute | solution.py:507
  29.1 6.1 %collective-permute-start.10 = (f32[32,256]{1,0:T(8,128)S(1)}, f32[32,256]{1,0:T(8,128)S(1)}, u32[]{:S(2)}, u32[]{:S(2)}) collective-permute-start(f32[32,256]{1,0:T(8,128)S(1)} %get-tuple-element.50), channel_id=1, source_target_pairs={{0,3},{1,2},{2,1},{3,0},{4,7},{5,6},{6,5},{7,4},{8,11},{9,10},{10,... | collective-permute-start | bytes 98312 | tf_op jit(solution)/shard_map/ppermute | solution.py:507
  31.2 4.8 %collective-permute-start.8 = (f32[32,256]{1,0:T(8,128)S(1)}, f32[32,256]{1,0:T(8,128)S(1)}, u32[]{:S(2)}, u32[]{:S(2)}) collective-permute-start(f32[32,256]{1,0:T(8,128)S(1)} %get-tuple-element.52), channel_id=1, source_target_pairs={{0,2},{1,3},{2,0},{3,1},{4,6},{5,7},{6,4},{7,5},{8,10},{9,11},{10,... | collective-permute-start | bytes 98312 | tf_op jit(solution)/shard_map/ppermute | solution.py:507
  33.5 3.9 %collective-permute-start.9 = (f32[32,256]{1,0:T(8,128)S(1)}, f32[32,256]{1,0:T(8,128)S(1)}, u32[]{:S(2)}, u32[]{:S(2)}) collective-permute-start(f32[32,256]{1,0:T(8,128)S(1)} %get-tuple-element.51), channel_id=1, source_target_pairs={{0,1},{1,0},{2,3},{3,2},{4,5},{5,4},{6,7},{7,6},{8,9},{9,8},{10,11... | collective-permute-start | bytes 98312 | tf_op jit(solution)/shard_map/ppermute | solution.py:507

commit v23 on v20

--- a/solution.py
+++ b/solution.py
@@ -140,9 +140,9 @@
 
 
 def pairs_kernel(feat_count, bounds_ref, pos_ref, *refs):
-    scores = refs[:-16]
-    (worth_ref, qid_ref, inv_ref, lam_ref, near_ref,
-     s_row, a_row, d_row, turn, s_col, a_col, w_col, q_col, d_col, grad, curv) = refs[-16:]
+    scores = refs[:-15]
+    (worth_ref, qid_ref, inv_ref, lam_ref,
+     s_row, a_row, d_row, turn, s_col, a_col, w_col, q_col, d_col, grad, curv) = refs[-15:]
     rows = worth_ref.shape[0]
     own = rows // feat_count
     docs = own * LANES
@@ -294,7 +294,6 @@
     terms = [inverse * jnp.concatenate([ref[t:t + 1, :] for t in range(own)], axis=1) for ref in (grad, curv)]
     for c in range(2):
         lam_ref[c:c + 1, :] = terms[c]
-        near_ref[c:c + 1, :] = terms[c]
 
 
 def pair_terms(feat_count, bounds, pos, scores, worth, qid, inverse):
@@ -306,9 +305,9 @@
     mine = pltpu.VMEM((docs // LANES, LANES), F32)
     return pl.pallas_call(
         functools.partial(pairs_kernel, feat_count),
-        out_shape=(jax.ShapeDtypeStruct((2, docs), F32), jax.ShapeDtypeStruct((2, docs), F32)),
+        out_shape=jax.ShapeDtypeStruct((2, docs), F32),
         in_specs=[smem(), smem()] + [vmem()] * (len(scores) + 3),
-        out_specs=(vmem(), vmem()),
+        out_specs=vmem(),
         scratch_shapes=[row, row, row, turn, col, col, col, col, col, mine, mine],
         compiler_params=pltpu.CompilerParams(vmem_limit_bytes=VMEM_LIMIT),
         cost_estimate=pl.CostEstimate(flops=9_000_000_000, bytes_accessed=200_000, transcendentals=2_000_000),
@@ -429,9 +428,10 @@
     )(tiles, bins_t, *tail)
 
 
-def finish_kernel(per_dev, leaf_ref, kept_ref, sums_ref, *refs):
-    arrived = list(refs[1::-1]) + list(refs[2:-3])
-    value_ref, step_ref, hist_ref = refs[-3:]
+def finish_kernel(per_dev, lam_ref, leaf_ref, kept_ref, sums_ref, *refs):
+    arrived = list(refs[1::-1]) + list(refs[2:-4])
+    lam_out, value_ref, step_ref, hist_ref = refs[-4:]
+    lam_out[...] = lam_ref[...]
     unit = kept_ref.shape[0]
     totals = add_up([sums_ref[...]] + [ref[unit:, :] for ref in arrived])
     highs = LEAVES // LANES
@@ -465,20 +465,21 @@
         hist_ref[...] = hist
 
 
-def finish(per_dev, leaves, kept, sums, arrived):
+def finish(per_dev, lambdas, leaves, kept, sums, arrived):
     out = (3, per_dev * BINS) if per_dev == GROUP else kept.shape
     return pl.pallas_call(
         functools.partial(finish_kernel, per_dev),
         out_shape=(
+            jax.ShapeDtypeStruct(lambdas.shape, F32),
             jax.ShapeDtypeStruct((LEAVES // LANES, LANES), F32),
             jax.ShapeDtypeStruct(leaves.shape, F32),
             jax.ShapeDtypeStruct(out, F32),
         ),
-        in_specs=[vmem()] * (3 + len(arrived)),
-        out_specs=(vmem(), vmem(), vmem()),
+        in_specs=[vmem()] * (4 + len(arrived)),
+        out_specs=(vmem(),) * 4,
         compiler_params=pltpu.CompilerParams(vmem_limit_bytes=VMEM_LIMIT),
         name="finish",
-    )(leaves, kept, sums, *arrived)
+    )(lambdas, leaves, kept, sums, *arrived)
 
 
 def add_up(parts):
@@ -519,8 +520,8 @@
     masks = feat_masks + query_masks[:0:-1] + query_masks[:1]
     score_parts[0], leaf_rows, qid, worth, inverse, perm, bounds = prepare(
         feat_count, masks, lengths, pos, labels.reshape(-1, LANES), owner.reshape(-1, LANES), own_scores, leaf_rows)
-    lambdas, near_lambdas = pair_terms(feat_count, bounds, pos, score_parts, worth, qid, inverse)
-    bins_t, tiles, sums = leaf_terms(perm, bins, leaf_rows, near_lambdas)
+    lambdas = pair_terms(feat_count, bounds, pos, score_parts, worth, qid, inverse)
+    bins_t, tiles, sums = leaf_terms(perm, bins, leaf_rows, lambdas)
 
     def part(tiles, low, high, *tail):
         if per_dev == GROUP:
@@ -557,7 +558,7 @@
         sums = sums + arrived[edge:]
     arrived = [swap(join(kept[m * unit:(m + 1) * unit], sums), m) for m in range(1, feat_count)]
     arrived[:2] = arrived[1::-1]
-    values, step, histograms = finish(per_dev, leaf_rows, kept[:unit], sums, arrived)
+    lambdas, values, step, histograms = finish(per_dev, lambdas, leaf_rows, kept[:unit], sums, arrived)
     return lambdas, values.reshape(LEAVES), step.reshape(docs), histograms.reshape(3, per_dev * BINS)
 
 

time: 38.1 us -> 37.9 us (level); the launches traced: 38.4 us -> 37.7 us
  starting transfers between devices: 15.9 us -> 13.4 us
  Pallas kernels: 14.4 us -> 15.9 us
    ppermute x10, starting transfers between devices: 15.3 us -> 12.9 us  [swap(): return lax.ppermute(value, axes, [(p, p ^ mask) for p in range(count)])]
    pallas_call x1, Pallas kernels: 5.48 us -> 6.95 us  [pair_terms(): pl.pallas_call(functools.partial(pairs_kernel, feat_count), out_shape=jax...]
  transfers between devices with their start and end apart: 11 -> 11, of which waited for: 8 -> 7; matrix products, arithmetic and copies ran while one was open for 0% -> 0% of each run, Pallas kernels for 18% -> 18%
where the time goes in v23:
time: 37.9 us; the launch traced here: 37.7 us
  Pallas kernels  15.9 us (42%)
  starting transfers between devices  13.4 us (35%)
  waiting for transfers between devices  6.01 us (16%)
  local copies, waits for them, and re-layouts  1.42 us (4%)
  between operations  0.8 us (2%)
    ppermute x10, starting transfers between devices, swap(): return lax.ppermute(value, axes, [(p, p ^ mask) for p in range(count)])  12.9 us
    pallas_call x1, Pallas kernels, pair_terms(): pl.pallas_call(functools.partial(pairs_kernel, feat_count), out_shape=jax...  6.95 us
    pallas_call x6, Pallas kernels, histogram_part(): pl.pallas_call(functools.partial(histogram_kernel, first, groups), out_sh...  6.68 us
    ppermute x10, waiting for transfers between devices, swap(): return lax.ppermute(value, axes, [(p, p ^ mask) for p in range(count)])  6.01 us
    unnamed x12, local copies, waits for them, and re-layouts  1.41 us
    pallas_call x1, Pallas kernels, prepare(): pl.pallas_call(functools.partial(prepare_kernel, feat_count, masks), out_...  1.01 us
    pallas_call x1, Pallas kernels, finish(): pl.pallas_call(functools.partial(finish_kernel, per_dev), out_shape=(jax....  0.8 us
  transfers between devices with their start and end apart: 11, of which 7 were waited for; matrix products, arithmetic and copies ran while one was open for 0% of the time, Pallas kernels for 18%

profile of v23, /device:TPU:0, one launch (start us, length us, event | category | flops | bytes accessed | tf_op | source)
XLA Modules:
  0.0 37.7 jit_solution(1474499923666048169)
XLA Ops:
  0.6 0.5 %collective-permute-start = (f32[8,128]{1,0:T(8,128)}, f32[8,128]{1,0:T(8,128)S(1)}, u32[]{:S(2)}, u32[]{:S(2)}) collective-permute-start(f32[8,128]{1,0:T(8,128)} %bitcast.9), channel_id=1, source_target_pairs={{0,4},{1,2},{2,1},{3,7},{4,0},{5,6},{6,5},{7,3},{8,12},{9,10},{10,... | collective-permute-start | bytes 12296 | tf_op jit(solution)/shard_map/ppermute | solution.py:518
  1.2 4.1 %collective-permute-start.1 = (f32[8,128]{1,0:T(8,128)}, f32[8,128]{1,0:T(8,128)S(1)}, u32[]{:S(2)}, u32[]{:S(2)}) collective-permute-start(f32[8,128]{1,0:T(8,128)} %bitcast.10), channel_id=1, source_target_pairs={{0,1},{1,0},{2,3},{3,2},{4,5},{5,4},{6,7},{7,6},{8,9},{9,8},{10,11... | collective-permute-start | bytes 12296 | tf_op jit(solution)/shard_map/ppermute | solution.py:506
  5.3 0.7 %copy-done.3 = f32[1024]{0:T(1024)S(1)} copy-done((f32[1024]{0:T(1024)S(1)}, f32[1024]{0:T(1024)}, u32[]{:S(2)}) %copy-start.3) | copy-done | bytes 4120
  6.0 0.7 %copy-done.4 = s32[256]{0:T(256)S(1)} copy-done((s32[256]{0:T(256)S(1)}, s32[256]{0:T(256)}, u32[]{:S(2)}) %copy-start.4) | copy-done | bytes 1048
  6.7 1.0 %prepare.1 = (f32[8,128]{1,0:T(8,128)S(1)}, s32[8,128]{1,0:T(8,128)S(1)}, f32[32,128]{1,0:T(8,128)S(1)}, f32[32,128]{1,0:T(8,128)S(1)}, f32[1,1024]{1,0:T(1,128)...) custom-call(s32[1,16]{1,0:T(1,128)S(1)} %copy-done.5, s32[1]{0:T(128)} %bitcast.pos_ref, s32[32,128]{1,0:T(8,128)S(1)} %bitcast.7, ...), custom_call_target="tpu_custom_call" | custom-call | flops 2000000000 | bytes 300000 | tf_op jit(solution)/shard_map/prepare/pallas_call | solution.py:113
  7.7 0.0 collective-permute-done.refs_1_
  7.8 0.0 copy-start
  7.8 7.0 %pair_terms.1.lam_ref = f32[2,1024]{1,0:T(2,128)S(1)} custom-call(s32[8,128]{1,0:T(8,128)S(1)} %get-tuple-element.23.bounds_ref, s32[1]{0:T(128)} %bitcast.pos_ref, f32[8,128]{1,0:T(8,128)S(1)} %get-tuple-element.24.refs_0_, f32[8,128]{1,0:T(8,128)S(1)} %collective-permute-done.refs_1_, f32[8,128]{1,0:T(8,128)S(1)} %collective-permute-done.1.refs_2_, ...), custom_call_target="tpu_custom_call" | custom-call | flops 8999999488 | bytes 200000 | tf_op jit(solution)/shard_map/pair_terms/pallas_call | solution.py:306
  14.7 0.4 %leaf_terms.1 = (f32[256,1024]{1,0:T(8,128)S(1)}, bf16[32,1024]{1,0:T(8,128)(2,1)S(1)}, f32[8,256]{1,0:T(8,128)S(1)}) custom-call(bf16[256,256]{1,0:T(8,128)(2,1)S(1)} %get-tuple-element.29.perm_ref, s32[1024,256]{1,0:T(8,128)S(1)} %copy-done, s32[8,128]{1,0:T(8,128)S(1)} %get-tuple-element.28.leaf_ref, f32[2,1024]{1,0:T(2,128)S(1)} %pair_terms.1.lam_ref), custom_call_target="tpu_custom_call" | custom-call | flops 200000000 | bytes 3000000 | tf_op jit(solution)/shard_map/leaf_terms/pallas_call | solution.py:346
  15.2 0.9 %histogram_part.7 = f32[104,256]{1,0:T(8,128)S(1)} custom-call(bf16[32,1024]{1,0:T(8,128)(2,1)S(1)} %get-tuple-element.35.tile_ref, f32[256,1024]{1,0:T(8,128)S(1)} %get-tuple-element.31.bins_ref, f32[8,256]{1,0:T(8,128)S(1)} %get-tuple-element.32.refs_0_), custom_call_target="tpu_custom_call" | custom-call | flops 4000000 | bytes 4000 | tf_op jit(solution)/shard_map/histogram_part/pallas_call | solution.py:420
  16.0 0.1 collective-permute-start.2
  16.1 0.9 %histogram_part.6 = f32[96,256]{1,0:T(8,128)S(1)} custom-call(bf16[32,1024]{1,0:T(8,128)(2,1)S(1)} %get-tuple-element.35.tile_ref, f32[256,1024]{1,0:T(8,128)S(1)} %get-tuple-element.31.bins_ref), custom_call_target="tpu_custom_call" | custom-call | flops 4000000 | bytes 4000 | tf_op jit(solution)/shard_map/histogram_part/pallas_call | solution.py:420
  17.0 0.4 %collective-permute-done.2 = f32[104,256]{1,0:T(8,128)S(1)} collective-permute-done((f32[104,256]{1,0:T(8,128)S(1)}, f32[104,256]{1,0:T(8,128)S(1)}, u32[]{:S(2)}, u32[]{:S(2)}) %collective-permute-start.2) | collective-permute-done | bytes 106528 | tf_op jit(solution)/shard_map/ppermute | solution.py:506
  17.5 1.2 %collective-permute-start.4 = (f32[104,256]{1,0:T(8,128)S(1)}, f32[104,256]{1,0:T(8,128)S(1)}, u32[]{:S(2)}, u32[]{:S(2)}) collective-permute-start(f32[104,256]{1,0:T(8,128)S(1)} %pad_maximum_fusion.2), channel_id=1, source_target_pairs={{0,8},{1,9},{2,10},{3,11},{4,12},{5,13},{6,14},{7,15},{8,0},{9,1},... | collective-permute-start | bytes 319496 | tf_op jit(solution)/shard_map/ppermute | solution.py:506
  18.7 1.6 %histogram_part.9 = f32[192,256]{1,0:T(8,128)S(1)} custom-call(bf16[32,1024]{1,0:T(8,128)(2,1)S(1)} %get-tuple-element.35.tile_ref, f32[256,1024]{1,0:T(8,128)S(1)} %get-tuple-element.31.bins_ref), custom_call_target="tpu_custom_call" | custom-call | flops 8000000 | bytes 8000 | tf_op jit(solution)/shard_map/histogram_part/pallas_call | solution.py:420
  20.2 0.1 collective-permute-start.3
  20.3 1.6 %histogram_part.8 = f32[192,256]{1,0:T(8,128)S(1)} custom-call(bf16[32,1024]{1,0:T(8,128)(2,1)S(1)} %get-tuple-element.35.tile_ref, f32[256,1024]{1,0:T(8,128)S(1)} %get-tuple-element.31.bins_ref), custom_call_target="tpu_custom_call" | custom-call | flops 8000000 | bytes 8000 | tf_op jit(solution)/shard_map/histogram_part/pallas_call | solution.py:420
  21.9 0.7 %collective-permute-done.4 = f32[104,256]{1,0:T(8,128)S(1)} collective-permute-done((f32[104,256]{1,0:T(8,128)S(1)}, f32[104,256]{1,0:T(8,128)S(1)}, u32[]{:S(2)}, u32[]{:S(2)}) %collective-permute-start.4) | collective-permute-done | bytes 106528 | tf_op jit(solution)/shard_map/ppermute | solution.py:506
  22.6 1.1 %collective-permute-start.7 = (f32[104,256]{1,0:T(8,128)S(1)}, f32[104,256]{1,0:T(8,128)S(1)}, u32[]{:S(2)}, u32[]{:S(2)}) collective-permute-start(f32[104,256]{1,0:T(8,128)S(1)} %get-tuple-element.37), channel_id=1, source_target_pairs={{0,16},{1,17},{2,18},{3,19},{4,20},{5,21},{6,22},{7,23},{8,24},{9,... | collective-permute-start | bytes 319496 | tf_op jit(solution)/shard_map/ppermute | solution.py:506
  23.8 1.7 %collective-permute-start.6 = (f32[104,256]{1,0:T(8,128)S(1)}, f32[104,256]{1,0:T(8,128)S(1)}, u32[]{:S(2)}, u32[]{:S(2)}) collective-permute-start(f32[104,256]{1,0:T(8,128)S(1)} %get-tuple-element.36), channel_id=1, source_target_pairs={{0,8},{1,9},{2,10},{3,11},{4,12},{5,13},{6,14},{7,15},{8,0},{9,1},... | collective-permute-start | bytes 319496 | tf_op jit(solution)/shard_map/ppermute | solution.py:506
  25.5 0.9 %histogram_part.11 = f32[96,256]{1,0:T(8,128)S(1)} custom-call(bf16[32,1024]{1,0:T(8,128)(2,1)S(1)} %get-tuple-element.35.tile_ref, f32[256,1024]{1,0:T(8,128)S(1)} %get-tuple-element.31.bins_ref), custom_call_target="tpu_custom_call" | custom-call | flops 4000000 | bytes 4000 | tf_op jit(solution)/shard_map/histogram_part/pallas_call | solution.py:420
  26.4 0.1 collective-permute-start.5
  26.5 0.9 %histogram_part.10 = f32[96,256]{1,0:T(8,128)S(1)} custom-call(bf16[32,1024]{1,0:T(8,128)(2,1)S(1)} %get-tuple-element.35.tile_ref, f32[256,1024]{1,0:T(8,128)S(1)} %get-tuple-element.31.bins_ref), custom_call_target="tpu_custom_call" | custom-call | flops 4000000 | bytes 4000 | tf_op jit(solution)/shard_map/histogram_part/pallas_call | solution.py:420
  27.4 0.4 %collective-permute-done.5 = f32[96,256]{1,0:T(8,128)S(1)} collective-permute-done((f32[96,256]{1,0:T(8,128)S(1)}, f32[96,256]{1,0:T(8,128)S(1)}, u32[]{:S(2)}, u32[]{:S(2)}) %collective-permute-start.5) | collective-permute-done | bytes 98336 | tf_op jit(solution)/shard_map/ppermute | solution.py:506
  27.8 1.0 %collective-permute-done.6 = f32[104,256]{1,0:T(8,128)S(1)} collective-permute-done((f32[104,256]{1,0:T(8,128)S(1)}, f32[104,256]{1,0:T(8,128)S(1)}, u32[]{:S(2)}, u32[]{:S(2)}) %collective-permute-start.6) | collective-permute-done | bytes 106528 | tf_op jit(solution)/shard_map/ppermute | solution.py:506
  28.9 1.8 %collective-permute-start.10 = (f32[32,256]{1,0:T(8,128)S(1)}, f32[32,256]{1,0:T(8,128)S(1)}, u32[]{:S(2)}, u32[]{:S(2)}) collective-permute-start(f32[32,256]{1,0:T(8,128)S(1)} %get-tuple-element.48), channel_id=1, source_target_pairs={{0,3},{1,2},{2,1},{3,0},{4,7},{5,6},{6,5},{7,4},{8,11},{9,10},{10,... | collective-permute-start | bytes 98312 | tf_op jit(solution)/shard_map/ppermute | solution.py:506
  30.7 2.2 %collective-permute-start.8 = (f32[32,256]{1,0:T(8,128)S(1)}, f32[32,256]{1,0:T(8,128)S(1)}, u32[]{:S(2)}, u32[]{:S(2)}) collective-permute-start(f32[32,256]{1,0:T(8,128)S(1)} %get-tuple-element.50), channel_id=1, source_target_pairs={{0,2},{1,3},{2,0},{3,1},{4,6},{5,7},{6,4},{7,5},{8,10},{9,11},{10,... | collective-permute-start | bytes 98312 | tf_op jit(solution)/shard_map/ppermute | solution.py:506
  32.9 0.4 %collective-permute-start.9 = (f32[32,256]{1,0:T(8,128)S(1)}, f32[32,256]{1,0:T(8,128)S(1)}, u32[]{:S(2)}, u32[]{:S(2)}) collective-permute-start(f32[32,256]{1,0:T(8,128)S(1)} %get-tuple-element.49), channel_id=1, source_target_pairs={{0,1},{1,0},{2,3},{3,2},{4,5},{5,4},{6,7},{7,6},{8,9},{9,8},{10,11... | collective-permute-start | bytes 98312 | tf_op jit(solution)/shard_map/ppermute | solution.py:506
  33.4 1.7 %collective-permute-done.10.refs_2_ = f32[32,256]{1,0:T(8,128)S(1)} collective-permute-done((f32[32,256]{1,0:T(8,128)S(1)}, f32[32,256]{1,0:T(8,128)S(1)}, u32[]{:S(2)}, u32[]{:S(2)}) %collective-permute-start.10) | collective-permute-done | bytes 32800 | tf_op jit(solution)/shard_map/ppermute | solution.py:506
  35.0 0.5 %collective-permute-done.8.refs_0_ = f32[32,256]{1,0:T(8,128)S(1)} collective-permute-done((f32[32,256]{1,0:T(8,128)S(1)}, f32[32,256]{1,0:T(8,128)S(1)}, u32[]{:S(2)}, u32[]{:S(2)}) %collective-permute-start.8) | collective-permute-done | bytes 32800 | tf_op jit(solution)/shard_map/ppermute | solution.py:506
  35.5 1.3 %collective-permute-done.9.refs_1_ = f32[32,256]{1,0:T(8,128)S(1)} collective-permute-done((f32[32,256]{1,0:T(8,128)S(1)}, f32[32,256]{1,0:T(8,128)S(1)}, u32[]{:S(2)}, u32[]{:S(2)}) %collective-permute-start.9) | collective-permute-done | bytes 32800 | tf_op jit(solution)/shard_map/ppermute | solution.py:506
  36.9 0.8 %finish.1 = (f32[2,1024]{1,0:T(2,128)}, f32[8,128]{1,0:T(8,128)}, f32[8,128]{1,0:T(8,128)}, f32[3,2048]{1,0:T(4,128)}) custom-call(f32[2,1024]{1,0:T(2,128)S(1)} %pair_terms.1.lam_ref, s32[8,128]{1,0:T(8,128)S(1)} %get-tuple-element.28.leaf_ref, f32[24,256]{1,0:T(8,128)S(1)} %get-tuple-element.47.kept_ref, f32[8,256]{1,0:T(8,128)S(1)} %slice_add_fusion.4.sums_ref, ...), custom_call_target="tpu_custom_call" | custom-call | tf_op jit(solution)/shard_map/finish/pallas_call | solution.py:470
  (23 shorter events, 0.2 us)
Async XLA Ops:
  0.6 4.7 %copy-start.1 = (s32[4096]{0:T(1024)S(1)}, s32[4096]{0:T(1024)}, u32[]{:S(2)}) copy-start(s32[4096]{0:T(1024)} %param.7) | copy-start | bytes 49156
  0.6 7.1 %collective-permute-start = (f32[8,128]{1,0:T(8,128)}, f32[8,128]{1,0:T(8,128)S(1)}, u32[]{:S(2)}, u32[]{:S(2)}) collective-permute-start(f32[8,128]{1,0:T(8,128)} %bitcast.9), channel_id=1, source_target_pairs={{0,4},{1,2},{2,1},{3,7},{4,0},{5,6},{6,5},{7,3},{8,12},{9,10},{10,... | collective-permute-start | bytes 12296 | tf_op jit(solution)/shard_map/ppermute | solution.py:518
  1.2 6.6 %collective-permute-start.1 = (f32[8,128]{1,0:T(8,128)}, f32[8,128]{1,0:T(8,128)S(1)}, u32[]{:S(2)}, u32[]{:S(2)}) collective-permute-start(f32[8,128]{1,0:T(8,128)} %bitcast.10), channel_id=1, source_target_pairs={{0,1},{1,0},{2,3},{3,2},{4,5},{5,4},{6,7},{7,6},{8,9},{9,8},{10,11... | collective-permute-start | bytes 12296 | tf_op jit(solution)/shard_map/ppermute | solution.py:506
  5.3 0.7 %copy-start.3 = (f32[1024]{0:T(1024)S(1)}, f32[1024]{0:T(1024)}, u32[]{:S(2)}) copy-start(f32[1024]{0:T(1024)} %param.6) | copy-start | bytes 12292
  5.3 0.7 %copy-start.2 = (s32[1024]{0:T(1024)S(1)}, s32[1024]{0:T(1024)}, u32[]{:S(2)}) copy-start(s32[1024]{0:T(1024)} %param.8) | copy-start | bytes 12292
  5.3 0.7 %copy-start.5 = (s32[1,16]{1,0:T(1,128)S(1)}, s32[1,16]{1,0:T(1,128)}, u32[]{:S(2)}) copy-start(s32[1,16]{1,0:T(1,128)} %len_ref.1) | copy-start | bytes 196
  6.0 0.7 %copy-start.4 = (s32[256]{0:T(256)S(1)}, s32[256]{0:T(256)}, u32[]{:S(2)}) copy-start(s32[256]{0:T(256)} %param.11) | copy-start | bytes 3076
  7.8 7.0 %copy-start = (s32[1024,256]{1,0:T(8,128)S(1)}, s32[1024,256]{1,0:T(8,128)}, u32[]{:S(2)}) copy-start(s32[1024,256]{1,0:T(8,128)} %bins_ref.1) | copy-start | bytes 3145732
  16.0 1.4 %collective-permute-start.2 = (f32[104,256]{1,0:T(8,128)S(1)}, f32[104,256]{1,0:T(8,128)S(1)}, u32[]{:S(2)}, u32[]{:S(2)}) collective-permute-start(f32[104,256]{1,0:T(8,128)S(1)} %histogram_part.7), channel_id=1, source_target_pairs={{0,4},{1,5},{2,6},{3,7},{4,0},{5,1},{6,2},{7,3},{8,12},{9,13},{10,... | collective-permute-start | bytes 319496 | tf_op jit(solution)/shard_map/ppermute | solution.py:506
  17.5 5.1 %collective-permute-start.4 = (f32[104,256]{1,0:T(8,128)S(1)}, f32[104,256]{1,0:T(8,128)S(1)}, u32[]{:S(2)}, u32[]{:S(2)}) collective-permute-start(f32[104,256]{1,0:T(8,128)S(1)} %pad_maximum_fusion.2), channel_id=1, source_target_pairs={{0,8},{1,9},{2,10},{3,11},{4,12},{5,13},{6,14},{7,15},{8,0},{9,1},... | collective-permute-start | bytes 319496 | tf_op jit(solution)/shard_map/ppermute | solution.py:506
  20.2 2.3 %collective-permute-start.3 = (f32[192,256]{1,0:T(8,128)S(1)}, f32[192,256]{1,0:T(8,128)S(1)}, u32[]{:S(2)}, u32[]{:S(2)}) collective-permute-start(f32[192,256]{1,0:T(8,128)S(1)} %histogram_part.9), channel_id=1, source_target_pairs={{0,4},{1,5},{2,6},{3,7},{4,0},{5,1},{6,2},{7,3},{8,12},{9,13},{10,... | collective-permute-start | bytes 589832 | tf_op jit(solution)/shard_map/ppermute | solution.py:506
  22.6 5.1 %collective-permute-start.7 = (f32[104,256]{1,0:T(8,128)S(1)}, f32[104,256]{1,0:T(8,128)S(1)}, u32[]{:S(2)}, u32[]{:S(2)}) collective-permute-start(f32[104,256]{1,0:T(8,128)S(1)} %get-tuple-element.37), channel_id=1, source_target_pairs={{0,16},{1,17},{2,18},{3,19},{4,20},{5,21},{6,22},{7,23},{8,24},{9,... | collective-permute-start | bytes 319496 | tf_op jit(solution)/shard_map/ppermute | solution.py:506
  23.8 5.0 %collective-permute-start.6 = (f32[104,256]{1,0:T(8,128)S(1)}, f32[104,256]{1,0:T(8,128)S(1)}, u32[]{:S(2)}, u32[]{:S(2)}) collective-permute-start(f32[104,256]{1,0:T(8,128)S(1)} %get-tuple-element.36), channel_id=1, source_target_pairs={{0,8},{1,9},{2,10},{3,11},{4,12},{5,13},{6,14},{7,15},{8,0},{9,1},... | collective-permute-start | bytes 319496 | tf_op jit(solution)/shard_map/ppermute | solution.py:506
  26.4 1.4 %collective-permute-start.5 = (f32[96,256]{1,0:T(8,128)S(1)}, f32[96,256]{1,0:T(8,128)S(1)}, u32[]{:S(2)}, u32[]{:S(2)}) collective-permute-start(f32[96,256]{1,0:T(8,128)S(1)} %histogram_part.11), channel_id=1, source_target_pairs={{0,4},{1,5},{2,6},{3,7},{4,0},{5,1},{6,2},{7,3},{8,12},{9,13},{10,... | collective-permute-start | bytes 294920 | tf_op jit(solution)/shard_map/ppermute | solution.py:506
  28.9 6.1 %collective-permute-start.10 = (f32[32,256]{1,0:T(8,128)S(1)}, f32[32,256]{1,0:T(8,128)S(1)}, u32[]{:S(2)}, u32[]{:S(2)}) collective-permute-start(f32[32,256]{1,0:T(8,128)S(1)} %get-tuple-element.48), channel_id=1, source_target_pairs={{0,3},{1,2},{2,1},{3,0},{4,7},{5,6},{6,5},{7,4},{8,11},{9,10},{10,... | collective-permute-start | bytes 98312 | tf_op jit(solution)/shard_map/ppermute | solution.py:506
  30.7 4.8 %collective-permute-start.8 = (f32[32,256]{1,0:T(8,128)S(1)}, f32[32,256]{1,0:T(8,128)S(1)}, u32[]{:S(2)}, u32[]{:S(2)}) collective-permute-start(f32[32,256]{1,0:T(8,128)S(1)} %get-tuple-element.50), channel_id=1, source_target_pairs={{0,2},{1,3},{2,0},{3,1},{4,6},{5,7},{6,4},{7,5},{8,10},{9,11},{10,... | collective-permute-start | bytes 98312 | tf_op jit(solution)/shard_map/ppermute | solution.py:506
  32.9 3.9 %collective-permute-start.9 = (f32[32,256]{1,0:T(8,128)S(1)}, f32[32,256]{1,0:T(8,128)S(1)}, u32[]{:S(2)}, u32[]{:S(2)}) collective-permute-start(f32[32,256]{1,0:T(8,128)S(1)} %get-tuple-element.49), channel_id=1, source_target_pairs={{0,1},{1,0},{2,3},{3,2},{4,5},{5,4},{6,7},{7,6},{8,9},{9,8},{10,11... | collective-permute-start | bytes 98312 | tf_op jit(solution)/shard_map/ppermute | solution.py:506

commit v24 on v23

--- a/solution.py
+++ b/solution.py
@@ -158,7 +158,7 @@
     first = me * own
     window_low = bounds_ref[0, first] // (2 * LANES) * 2
     window_high = (bounds_ref[1, first + own - 1] + 2 * LANES - 1) // (2 * LANES) * 2
-    stride = 4
+    stride = 2
 
     def widen(pairs):
         lines = jnp.concatenate([source[...] for source, _ in pairs], axis=0)

time: 37.9 us -> 38.4 us (1.013)
  starting transfers between devices: 13.4 us -> 17 us
  Pallas kernels: 15.9 us -> 13.8 us
  waiting for transfers between devices: 6.01 us -> 5.15 us
    ppermute x10, starting transfers between devices: 12.9 us -> 16.5 us  [swap(): return lax.ppermute(value, axes, [(p, p ^ mask) for p in range(count)])]
    pallas_call x1, Pallas kernels: 6.95 us -> 4.94 us  [pair_terms(): pl.pallas_call(functools.partial(pairs_kernel, feat_count), out_shape=jax...]
    ppermute x10, waiting for transfers between devices: 6.01 us -> 5.15 us  [swap(): return lax.ppermute(value, axes, [(p, p ^ mask) for p in range(count)])]
  transfers between devices with their start and end apart: 11 -> 11, of which waited for: 7 -> 8; matrix products, arithmetic and copies ran while one was open for 0% -> 0% of each run, Pallas kernels for 18% -> 18%
where the time goes in v24:
time: 38.4 us
  starting transfers between devices  17 us (44%)
  Pallas kernels  13.8 us (36%)
  waiting for transfers between devices  5.15 us (13%)
  local copies, waits for them, and re-layouts  1.42 us (4%)
  between operations  0.79 us (2%)
    ppermute x10, starting transfers between devices, swap(): return lax.ppermute(value, axes, [(p, p ^ mask) for p in range(count)])  16.5 us
    pallas_call x6, Pallas kernels, histogram_part(): pl.pallas_call(functools.partial(histogram_kernel, first, groups), out_sh...  6.68 us
    ppermute x10, waiting for transfers between devices, swap(): return lax.ppermute(value, axes, [(p, p ^ mask) for p in range(count)])  5.15 us
    pallas_call x1, Pallas kernels, pair_terms(): pl.pallas_call(functools.partial(pairs_kernel, feat_count), out_shape=jax...  4.94 us
    unnamed x12, local copies, waits for them, and re-layouts  1.41 us
    pallas_call x1, Pallas kernels, prepare(): pl.pallas_call(functools.partial(prepare_kernel, feat_count, masks), out_...  1.01 us
    pallas_call x1, Pallas kernels, finish(): pl.pallas_call(functools.partial(finish_kernel, per_dev), out_shape=(jax....  0.8 us
  transfers between devices with their start and end apart: 11, of which 8 were waited for; matrix products, arithmetic and copies ran while one was open for 0% of the time, Pallas kernels for 18%

profile of v24, /device:TPU:0, one launch (start us, length us, event | category | flops | bytes accessed | tf_op | source)
XLA Modules:
  0.0 38.4 jit_solution(16666970398877510048)
XLA Ops:
  0.6 0.5 %collective-permute-start = (f32[8,128]{1,0:T(8,128)}, f32[8,128]{1,0:T(8,128)S(1)}, u32[]{:S(2)}, u32[]{:S(2)}) collective-permute-start(f32[8,128]{1,0:T(8,128)} %bitcast.9), channel_id=1, source_target_pairs={{0,4},{1,2},{2,1},{3,7},{4,0},{5,6},{6,5},{7,3},{8,12},{9,10},{10,... | collective-permute-start | bytes 12296 | tf_op jit(solution)/shard_map/ppermute | solution.py:518
  1.2 4.1 %collective-permute-start.1 = (f32[8,128]{1,0:T(8,128)}, f32[8,128]{1,0:T(8,128)S(1)}, u32[]{:S(2)}, u32[]{:S(2)}) collective-permute-start(f32[8,128]{1,0:T(8,128)} %bitcast.10), channel_id=1, source_target_pairs={{0,1},{1,0},{2,3},{3,2},{4,5},{5,4},{6,7},{7,6},{8,9},{9,8},{10,11... | collective-permute-start | bytes 12296 | tf_op jit(solution)/shard_map/ppermute | solution.py:506
  5.3 0.7 %copy-done.3 = f32[1024]{0:T(1024)S(1)} copy-done((f32[1024]{0:T(1024)S(1)}, f32[1024]{0:T(1024)}, u32[]{:S(2)}) %copy-start.3) | copy-done | bytes 4120
  6.0 0.7 %copy-done.4 = s32[256]{0:T(256)S(1)} copy-done((s32[256]{0:T(256)S(1)}, s32[256]{0:T(256)}, u32[]{:S(2)}) %copy-start.4) | copy-done | bytes 1048
  6.7 1.0 %prepare.1 = (f32[8,128]{1,0:T(8,128)S(1)}, s32[8,128]{1,0:T(8,128)S(1)}, f32[32,128]{1,0:T(8,128)S(1)}, f32[32,128]{1,0:T(8,128)S(1)}, f32[1,1024]{1,0:T(1,128)...) custom-call(s32[1,16]{1,0:T(1,128)S(1)} %copy-done.5, s32[1]{0:T(128)} %bitcast.pos_ref, s32[32,128]{1,0:T(8,128)S(1)} %bitcast.7, ...), custom_call_target="tpu_custom_call" | custom-call | flops 2000000000 | bytes 300000 | tf_op jit(solution)/shard_map/prepare/pallas_call | solution.py:113
  7.8 0.0 copy-start
  7.8 4.9 %pair_terms.1.lam_ref = f32[2,1024]{1,0:T(2,128)S(1)} custom-call(s32[8,128]{1,0:T(8,128)S(1)} %get-tuple-element.23.bounds_ref, s32[1]{0:T(128)} %bitcast.pos_ref, f32[8,128]{1,0:T(8,128)S(1)} %get-tuple-element.24.refs_0_, f32[8,128]{1,0:T(8,128)S(1)} %collective-permute-done.refs_1_, f32[8,128]{1,0:T(8,128)S(1)} %collective-permute-done.1.refs_2_, ...), custom_call_target="tpu_custom_call" | custom-call | flops 8999999488 | bytes 200000 | tf_op jit(solution)/shard_map/pair_terms/pallas_call | solution.py:306
  12.7 0.4 %leaf_terms.1 = (f32[256,1024]{1,0:T(8,128)S(1)}, bf16[32,1024]{1,0:T(8,128)(2,1)S(1)}, f32[8,256]{1,0:T(8,128)S(1)}) custom-call(bf16[256,256]{1,0:T(8,128)(2,1)S(1)} %get-tuple-element.29.perm_ref, s32[1024,256]{1,0:T(8,128)S(1)} %copy-done, s32[8,128]{1,0:T(8,128)S(1)} %get-tuple-element.28.leaf_ref, f32[2,1024]{1,0:T(2,128)S(1)} %pair_terms.1.lam_ref), custom_call_target="tpu_custom_call" | custom-call | flops 200000000 | bytes 3000000 | tf_op jit(solution)/shard_map/leaf_terms/pallas_call | solution.py:346
  13.1 0.9 %histogram_part.7 = f32[104,256]{1,0:T(8,128)S(1)} custom-call(bf16[32,1024]{1,0:T(8,128)(2,1)S(1)} %get-tuple-element.35.tile_ref, f32[256,1024]{1,0:T(8,128)S(1)} %get-tuple-element.31.bins_ref, f32[8,256]{1,0:T(8,128)S(1)} %get-tuple-element.32.refs_0_), custom_call_target="tpu_custom_call" | custom-call | flops 4000000 | bytes 4000 | tf_op jit(solution)/shard_map/histogram_part/pallas_call | solution.py:420
  14.0 0.9 %collective-permute-start.2 = (f32[104,256]{1,0:T(8,128)S(1)}, f32[104,256]{1,0:T(8,128)S(1)}, u32[]{:S(2)}, u32[]{:S(2)}) collective-permute-start(f32[104,256]{1,0:T(8,128)S(1)} %histogram_part.7), channel_id=1, source_target_pairs={{0,4},{1,5},{2,6},{3,7},{4,0},{5,1},{6,2},{7,3},{8,12},{9,13},{10,... | collective-permute-start | bytes 319496 | tf_op jit(solution)/shard_map/ppermute | solution.py:506
  14.9 0.9 %histogram_part.6 = f32[96,256]{1,0:T(8,128)S(1)} custom-call(bf16[32,1024]{1,0:T(8,128)(2,1)S(1)} %get-tuple-element.35.tile_ref, f32[256,1024]{1,0:T(8,128)S(1)} %get-tuple-element.31.bins_ref), custom_call_target="tpu_custom_call" | custom-call | flops 4000000 | bytes 4000 | tf_op jit(solution)/shard_map/histogram_part/pallas_call | solution.py:420
  15.8 0.1 collective-permute-done.2
  15.9 2.9 %collective-permute-start.4 = (f32[104,256]{1,0:T(8,128)S(1)}, f32[104,256]{1,0:T(8,128)S(1)}, u32[]{:S(2)}, u32[]{:S(2)}) collective-permute-start(f32[104,256]{1,0:T(8,128)S(1)} %pad_maximum_fusion.2), channel_id=1, source_target_pairs={{0,8},{1,9},{2,10},{3,11},{4,12},{5,13},{6,14},{7,15},{8,0},{9,1},... | collective-permute-start | bytes 319496 | tf_op jit(solution)/shard_map/ppermute | solution.py:506
  18.8 1.6 %histogram_part.9 = f32[192,256]{1,0:T(8,128)S(1)} custom-call(bf16[32,1024]{1,0:T(8,128)(2,1)S(1)} %get-tuple-element.35.tile_ref, f32[256,1024]{1,0:T(8,128)S(1)} %get-tuple-element.31.bins_ref), custom_call_target="tpu_custom_call" | custom-call | flops 8000000 | bytes 8000 | tf_op jit(solution)/shard_map/histogram_part/pallas_call | solution.py:420
  20.4 0.1 collective-permute-start.3
  20.4 1.6 %histogram_part.8 = f32[192,256]{1,0:T(8,128)S(1)} custom-call(bf16[32,1024]{1,0:T(8,128)(2,1)S(1)} %get-tuple-element.35.tile_ref, f32[256,1024]{1,0:T(8,128)S(1)} %get-tuple-element.31.bins_ref), custom_call_target="tpu_custom_call" | custom-call | flops 8000000 | bytes 8000 | tf_op jit(solution)/shard_map/histogram_part/pallas_call | solution.py:420
  22.0 0.1 collective-permute-done.4
  22.2 0.9 %collective-permute-start.7 = (f32[104,256]{1,0:T(8,128)S(1)}, f32[104,256]{1,0:T(8,128)S(1)}, u32[]{:S(2)}, u32[]{:S(2)}) collective-permute-start(f32[104,256]{1,0:T(8,128)S(1)} %get-tuple-element.37), channel_id=1, source_target_pairs={{0,16},{1,17},{2,18},{3,19},{4,20},{5,21},{6,22},{7,23},{8,24},{9,... | collective-permute-start | bytes 319496 | tf_op jit(solution)/shard_map/ppermute | solution.py:506
  23.1 1.7 %collective-permute-start.6 = (f32[104,256]{1,0:T(8,128)S(1)}, f32[104,256]{1,0:T(8,128)S(1)}, u32[]{:S(2)}, u32[]{:S(2)}) collective-permute-start(f32[104,256]{1,0:T(8,128)S(1)} %get-tuple-element.36), channel_id=1, source_target_pairs={{0,8},{1,9},{2,10},{3,11},{4,12},{5,13},{6,14},{7,15},{8,0},{9,1},... | collective-permute-start | bytes 319496 | tf_op jit(solution)/shard_map/ppermute | solution.py:506
  24.8 0.9 %histogram_part.11 = f32[96,256]{1,0:T(8,128)S(1)} custom-call(bf16[32,1024]{1,0:T(8,128)(2,1)S(1)} %get-tuple-element.35.tile_ref, f32[256,1024]{1,0:T(8,128)S(1)} %get-tuple-element.31.bins_ref), custom_call_target="tpu_custom_call" | custom-call | flops 4000000 | bytes 4000 | tf_op jit(solution)/shard_map/histogram_part/pallas_call | solution.py:420
  25.7 0.1 collective-permute-start.5
  25.8 0.9 %histogram_part.10 = f32[96,256]{1,0:T(8,128)S(1)} custom-call(bf16[32,1024]{1,0:T(8,128)(2,1)S(1)} %get-tuple-element.35.tile_ref, f32[256,1024]{1,0:T(8,128)S(1)} %get-tuple-element.31.bins_ref), custom_call_target="tpu_custom_call" | custom-call | flops 4000000 | bytes 4000 | tf_op jit(solution)/shard_map/histogram_part/pallas_call | solution.py:420
  26.7 0.4 %collective-permute-done.5 = f32[96,256]{1,0:T(8,128)S(1)} collective-permute-done((f32[96,256]{1,0:T(8,128)S(1)}, f32[96,256]{1,0:T(8,128)S(1)}, u32[]{:S(2)}, u32[]{:S(2)}) %collective-permute-start.5) | collective-permute-done | bytes 98336 | tf_op jit(solution)/shard_map/ppermute | solution.py:506
  27.1 0.5 %collective-permute-done.7 = f32[104,256]{1,0:T(8,128)S(1)} collective-permute-done((f32[104,256]{1,0:T(8,128)S(1)}, f32[104,256]{1,0:T(8,128)S(1)}, u32[]{:S(2)}, u32[]{:S(2)}) %collective-permute-start.7) | collective-permute-done | bytes 106528 | tf_op jit(solution)/shard_map/ppermute | solution.py:506
  27.6 0.6 %collective-permute-done.6 = f32[104,256]{1,0:T(8,128)S(1)} collective-permute-done((f32[104,256]{1,0:T(8,128)S(1)}, f32[104,256]{1,0:T(8,128)S(1)}, u32[]{:S(2)}, u32[]{:S(2)}) %collective-permute-start.6) | collective-permute-done | bytes 106528 | tf_op jit(solution)/shard_map/ppermute | solution.py:506
  28.2 2.5 %collective-permute-start.10 = (f32[32,256]{1,0:T(8,128)S(1)}, f32[32,256]{1,0:T(8,128)S(1)}, u32[]{:S(2)}, u32[]{:S(2)}) collective-permute-start(f32[32,256]{1,0:T(8,128)S(1)} %get-tuple-element.48), channel_id=1, source_target_pairs={{0,3},{1,2},{2,1},{3,0},{4,7},{5,6},{6,5},{7,4},{8,11},{9,10},{10,... | collective-permute-start | bytes 98312 | tf_op jit(solution)/shard_map/ppermute | solution.py:506
  30.8 2.9 %collective-permute-start.8 = (f32[32,256]{1,0:T(8,128)S(1)}, f32[32,256]{1,0:T(8,128)S(1)}, u32[]{:S(2)}, u32[]{:S(2)}) collective-permute-start(f32[32,256]{1,0:T(8,128)S(1)} %get-tuple-element.50), channel_id=1, source_target_pairs={{0,2},{1,3},{2,0},{3,1},{4,6},{5,7},{6,4},{7,5},{8,10},{9,11},{10,... | collective-permute-start | bytes 98312 | tf_op jit(solution)/shard_map/ppermute | solution.py:506
  33.6 0.3 collective-permute-start.9
  34.0 0.1 collective-permute-done.10.refs_2_
  34.1 1.8 %collective-permute-done.8.refs_0_ = f32[32,256]{1,0:T(8,128)S(1)} collective-permute-done((f32[32,256]{1,0:T(8,128)S(1)}, f32[32,256]{1,0:T(8,128)S(1)}, u32[]{:S(2)}, u32[]{:S(2)}) %collective-permute-start.8) | collective-permute-done | bytes 32800 | tf_op jit(solution)/shard_map/ppermute | solution.py:506
  35.9 1.7 %collective-permute-done.9.refs_1_ = f32[32,256]{1,0:T(8,128)S(1)} collective-permute-done((f32[32,256]{1,0:T(8,128)S(1)}, f32[32,256]{1,0:T(8,128)S(1)}, u32[]{:S(2)}, u32[]{:S(2)}) %collective-permute-start.9) | collective-permute-done | bytes 32800 | tf_op jit(solution)/shard_map/ppermute | solution.py:506
  37.6 0.8 %finish.1 = (f32[2,1024]{1,0:T(2,128)}, f32[8,128]{1,0:T(8,128)}, f32[8,128]{1,0:T(8,128)}, f32[3,2048]{1,0:T(4,128)}) custom-call(f32[2,1024]{1,0:T(2,128)S(1)} %pair_terms.1.lam_ref, s32[8,128]{1,0:T(8,128)S(1)} %get-tuple-element.28.leaf_ref, f32[24,256]{1,0:T(8,128)S(1)} %get-tuple-element.47.kept_ref, f32[8,256]{1,0:T(8,128)S(1)} %slice_add_fusion.4.sums_ref, ...), custom_call_target="tpu_custom_call" | custom-call | tf_op jit(solution)/shard_map/finish/pallas_call | solution.py:470
  (23 shorter events, 0.2 us)
Async XLA Ops:
  0.6 4.7 %copy-start.1 = (s32[4096]{0:T(1024)S(1)}, s32[4096]{0:T(1024)}, u32[]{:S(2)}) copy-start(s32[4096]{0:T(1024)} %param.7) | copy-start | bytes 49156
  0.6 7.1 %collective-permute-start = (f32[8,128]{1,0:T(8,128)}, f32[8,128]{1,0:T(8,128)S(1)}, u32[]{:S(2)}, u32[]{:S(2)}) collective-permute-start(f32[8,128]{1,0:T(8,128)} %bitcast.9), channel_id=1, source_target_pairs={{0,4},{1,2},{2,1},{3,7},{4,0},{5,6},{6,5},{7,3},{8,12},{9,10},{10,... | collective-permute-start | bytes 12296 | tf_op jit(solution)/shard_map/ppermute | solution.py:518
  1.2 6.6 %collective-permute-start.1 = (f32[8,128]{1,0:T(8,128)}, f32[8,128]{1,0:T(8,128)S(1)}, u32[]{:S(2)}, u32[]{:S(2)}) collective-permute-start(f32[8,128]{1,0:T(8,128)} %bitcast.10), channel_id=1, source_target_pairs={{0,1},{1,0},{2,3},{3,2},{4,5},{5,4},{6,7},{7,6},{8,9},{9,8},{10,11... | collective-permute-start | bytes 12296 | tf_op jit(solution)/shard_map/ppermute | solution.py:506
  5.3 0.7 %copy-start.3 = (f32[1024]{0:T(1024)S(1)}, f32[1024]{0:T(1024)}, u32[]{:S(2)}) copy-start(f32[1024]{0:T(1024)} %param.6) | copy-start | bytes 12292
  5.3 0.7 %copy-start.2 = (s32[1024]{0:T(1024)S(1)}, s32[1024]{0:T(1024)}, u32[]{:S(2)}) copy-start(s32[1024]{0:T(1024)} %param.8) | copy-start | bytes 12292
  5.3 0.7 %copy-start.5 = (s32[1,16]{1,0:T(1,128)S(1)}, s32[1,16]{1,0:T(1,128)}, u32[]{:S(2)}) copy-start(s32[1,16]{1,0:T(1,128)} %len_ref.1) | copy-start | bytes 196
  6.0 0.7 %copy-start.4 = (s32[256]{0:T(256)S(1)}, s32[256]{0:T(256)}, u32[]{:S(2)}) copy-start(s32[256]{0:T(256)} %param.11) | copy-start | bytes 3076
  7.8 5.0 %copy-start = (s32[1024,256]{1,0:T(8,128)S(1)}, s32[1024,256]{1,0:T(8,128)}, u32[]{:S(2)}) copy-start(s32[1024,256]{1,0:T(8,128)} %bins_ref.1) | copy-start | bytes 3145732
  14.0 1.8 %collective-permute-start.2 = (f32[104,256]{1,0:T(8,128)S(1)}, f32[104,256]{1,0:T(8,128)S(1)}, u32[]{:S(2)}, u32[]{:S(2)}) collective-permute-start(f32[104,256]{1,0:T(8,128)S(1)} %histogram_part.7), channel_id=1, source_target_pairs={{0,4},{1,5},{2,6},{3,7},{4,0},{5,1},{6,2},{7,3},{8,12},{9,13},{10,... | collective-permute-start | bytes 319496 | tf_op jit(solution)/shard_map/ppermute | solution.py:506
  15.9 6.2 %collective-permute-start.4 = (f32[104,256]{1,0:T(8,128)S(1)}, f32[104,256]{1,0:T(8,128)S(1)}, u32[]{:S(2)}, u32[]{:S(2)}) collective-permute-start(f32[104,256]{1,0:T(8,128)S(1)} %pad_maximum_fusion.2), channel_id=1, source_target_pairs={{0,8},{1,9},{2,10},{3,11},{4,12},{5,13},{6,14},{7,15},{8,0},{9,1},... | collective-permute-start | bytes 319496 | tf_op jit(solution)/shard_map/ppermute | solution.py:506
  20.4 1.7 %collective-permute-start.3 = (f32[192,256]{1,0:T(8,128)S(1)}, f32[192,256]{1,0:T(8,128)S(1)}, u32[]{:S(2)}, u32[]{:S(2)}) collective-permute-start(f32[192,256]{1,0:T(8,128)S(1)} %histogram_part.9), channel_id=1, source_target_pairs={{0,4},{1,5},{2,6},{3,7},{4,0},{5,1},{6,2},{7,3},{8,12},{9,13},{10,... | collective-permute-start | bytes 589832 | tf_op jit(solution)/shard_map/ppermute | solution.py:506
  22.2 5.4 %collective-permute-start.7 = (f32[104,256]{1,0:T(8,128)S(1)}, f32[104,256]{1,0:T(8,128)S(1)}, u32[]{:S(2)}, u32[]{:S(2)}) collective-permute-start(f32[104,256]{1,0:T(8,128)S(1)} %get-tuple-element.37), channel_id=1, source_target_pairs={{0,16},{1,17},{2,18},{3,19},{4,20},{5,21},{6,22},{7,23},{8,24},{9,... | collective-permute-start | bytes 319496 | tf_op jit(solution)/shard_map/ppermute | solution.py:506
  23.1 5.0 %collective-permute-start.6 = (f32[104,256]{1,0:T(8,128)S(1)}, f32[104,256]{1,0:T(8,128)S(1)}, u32[]{:S(2)}, u32[]{:S(2)}) collective-permute-start(f32[104,256]{1,0:T(8,128)S(1)} %get-tuple-element.36), channel_id=1, source_target_pairs={{0,8},{1,9},{2,10},{3,11},{4,12},{5,13},{6,14},{7,15},{8,0},{9,1},... | collective-permute-start | bytes 319496 | tf_op jit(solution)/shard_map/ppermute | solution.py:506
  25.7 1.4 %collective-permute-start.5 = (f32[96,256]{1,0:T(8,128)S(1)}, f32[96,256]{1,0:T(8,128)S(1)}, u32[]{:S(2)}, u32[]{:S(2)}) collective-permute-start(f32[96,256]{1,0:T(8,128)S(1)} %histogram_part.11), channel_id=1, source_target_pairs={{0,4},{1,5},{2,6},{3,7},{4,0},{5,1},{6,2},{7,3},{8,12},{9,13},{10,... | collective-permute-start | bytes 294920 | tf_op jit(solution)/shard_map/ppermute | solution.py:506
  28.2 5.9 %collective-permute-start.10 = (f32[32,256]{1,0:T(8,128)S(1)}, f32[32,256]{1,0:T(8,128)S(1)}, u32[]{:S(2)}, u32[]{:S(2)}) collective-permute-start(f32[32,256]{1,0:T(8,128)S(1)} %get-tuple-element.48), channel_id=1, source_target_pairs={{0,3},{1,2},{2,1},{3,0},{4,7},{5,6},{6,5},{7,4},{8,11},{9,10},{10,... | collective-permute-start | bytes 98312 | tf_op jit(solution)/shard_map/ppermute | solution.py:506
  30.8 5.1 %collective-permute-start.8 = (f32[32,256]{1,0:T(8,128)S(1)}, f32[32,256]{1,0:T(8,128)S(1)}, u32[]{:S(2)}, u32[]{:S(2)}) collective-permute-start(f32[32,256]{1,0:T(8,128)S(1)} %get-tuple-element.50), channel_id=1, source_target_pairs={{0,2},{1,3},{2,0},{3,1},{4,6},{5,7},{6,4},{7,5},{8,10},{9,11},{10,... | collective-permute-start | bytes 98312 | tf_op jit(solution)/shard_map/ppermute | solution.py:506
  33.6 3.9 %collective-permute-start.9 = (f32[32,256]{1,0:T(8,128)S(1)}, f32[32,256]{1,0:T(8,128)S(1)}, u32[]{:S(2)}, u32[]{:S(2)}) collective-permute-start(f32[32,256]{1,0:T(8,128)S(1)} %get-tuple-element.49), channel_id=1, source_target_pairs={{0,1},{1,0},{2,3},{3,2},{4,5},{5,4},{6,7},{7,6},{8,9},{9,8},{10,11... | collective-permute-start | bytes 98312 | tf_op jit(solution)/shard_map/ppermute | solution.py:506
